TPU v7x, 32 devices: a whole 2x2x4 slice. The times are simulated.
32 devices in a mesh: head: 4 (over x, core), blk: 8 (over z, y).
Axes of the slice: x: 2, y: 2, z: 4, core: 2. Of those that a mesh axis runs over, the one named last changes fastest.
Arguments:
- queries: bfloat16 [4096, 24, 128], P(('head', 'blk')), may hold values from -5 to 5
- keys: bfloat16 [4096, 24, 128], P(('head', 'blk')), may hold values from -4 to 4
- values: bfloat16 [4096, 24, 128], P(('head', 'blk')), may hold values from -6 to 6
- block_mask: int32 [24, 32, 32], replicated, may hold values from 0 to 1, as said below
- out_weight: bfloat16 [3072, 3072], replicated, may hold values from -0.109375 to 0.109375
Outputs:
- projected: bfloat16 [4096, 3072], P(('head', 'blk'))
Inputs may be any that keep to these rules, and one draw needn't show every extreme that they name: Every diagonal entry block_mask[h, b, b] is 1; other entries are 0 or 1.
All inputs are finite; a program needn't handle non-finite values.
Results may differ from a plain program's by a relative error of at most 0.008.
Values may be sent and summed in bfloat16 or wider, within the bound.
No kernel may reach another device: no remote copies, remote signals or barrier semaphores. Data moves between devices by JAX's collectives and lax.ppermute only.
A program may use at most 128 MiB of HBM per device.

v0:
```python
import functools
import math

import jax
import jax.numpy as jnp
import numpy as np
from jax import lax
from jax.experimental import pallas as pl
from jax.experimental.pallas import tpu as pltpu
from jax.sharding import Mesh
from jax.sharding import PartitionSpec as P

BLOCK = 128
NEG = -1e30
CORES = 2
PLANES = 4


def swap(size, bit):
    return [(i, i ^ bit) for i in range(size)]


def attend_kernel(picks, widths, rows, scale, first, last, *refs):
    bias_ref, q_ref = refs[:2]
    kv_refs = refs[2 : 2 + len(widths)]
    rest = refs[2 + len(widths) :]
    if not first:
        m_in, acc_in = rest[:2]
        rest = rest[2:]
    groups, _, block, hdim = q_ref.shape
    qb = rows // block

    def tile(index, carry):
        q = q_ref[pl.ds(index * qb, qb), 0].reshape(rows, hdim)
        if first:
            m = jnp.full((rows, 1), NEG, jnp.float32)
            acc = jnp.zeros((rows, 2 * hdim), jnp.float32)
        else:
            m = m_in[pl.ds(index * rows, rows), :1]
            acc = acc_in[pl.ds(index * rows, rows), :]
        for number, (which, kpart, vpart) in enumerate(picks):
            ref = kv_refs[which]
            span = ref.shape[0] * block
            k = ref[:, kpart].reshape(span, hdim)
            v = ref[:, vpart].reshape(span, hdim)
            v = jnp.concatenate([v, jnp.ones((span, hdim), v.dtype)], axis=1)
            s = lax.dot_general(q, k, (((1,), (1,)), ((), ())), preferred_element_type=jnp.float32)
            bias = bias_ref[pl.ds(index * qb, qb), :, number * span : (number + 1) * span]
            s = (s.reshape(qb, block, span) * scale + bias).reshape(rows, span)
            m_next = jnp.maximum(m, jnp.max(s, axis=1, keepdims=True))
            p = jnp.exp2(s - m_next).astype(jnp.bfloat16)
            acc = acc * jnp.exp2(m - m_next) + jnp.dot(p, v, preferred_element_type=jnp.float32)
            m = m_next
        if last:
            out = (acc[:, :hdim] / acc[:, hdim:]).astype(jnp.bfloat16)
            rest[0][pl.ds(index * qb, qb)] = out.reshape(qb, block, hdim)
        else:
            rest[0][pl.ds(index * rows, rows), :] = jnp.broadcast_to(m, (rows, hdim))
            rest[1][pl.ds(index * rows, rows), :] = acc
        return carry

    lax.fori_loop(0, groups // qb, tile, 0)


def attend(bias, q, arrays, picks, state, last):
    groups, _, block, hdim = q.shape
    rows = 2 * block if groups % 2 == 0 else block
    total = groups * block
    first = state is None
    widths = [a.shape[0] * block for a in arrays]
    vmem = pl.BlockSpec(memory_space=pltpu.VMEM)
    if last:
        out_shape = jax.ShapeDtypeStruct((groups, block, hdim), jnp.bfloat16)
        out_specs = vmem
    else:
        out_shape = (
            jax.ShapeDtypeStruct((total, hdim), jnp.float32),
            jax.ShapeDtypeStruct((total, 2 * hdim), jnp.float32),
        )
        out_specs = (vmem, vmem)
    args = [bias, q, *arrays, *(() if first else state)]
    scale = hdim**-0.5 * math.log2(math.e)
    keys = sum(widths[w] for w, _, _ in picks)
    return pl.pallas_call(
        functools.partial(attend_kernel, picks, widths, rows, scale, first, last),
        out_shape=out_shape,
        in_specs=[vmem] * len(args),
        out_specs=out_specs,
        compiler_params=pltpu.CompilerParams(vmem_limit_bytes=40 * 1024 * 1024),
        cost_estimate=pl.CostEstimate(
            flops=4 * total * keys * hdim, bytes_accessed=4 * keys * hdim, transcendentals=total * keys
        ),
    )(*args)


def shards(split, gather, queries, keys, values, block_mask, out_weight):
    sizes = {a: lax.axis_size(a) for a in ("x", "c", "zh", "zl", "y")}
    n_split = math.prod(sizes[a] for a in split)
    tok, heads, hdim = queries.shape
    chunks = heads // n_split
    width = n_split * hdim
    cols = out_weight.shape[1]

    grid = tuple(sizes.values())
    mask = block_mask.reshape((chunks, n_split) + grid + grid)
    mask = lax.dynamic_index_in_dim(mask, lax.axis_index(split), 1, keepdims=False)
    names = list(sizes)
    for a in ("c", "zh") + gather:
        mask = lax.dynamic_index_in_dim(mask, lax.axis_index(a), 1 + names.index(a), keepdims=True)
    mask = mask.reshape((chunks, n_split) + grid)
    order = ("zh",) + gather + ("c",)
    pieces = [mask]
    for a in order:
        d = 2 + names.index(a)
        here = lax.axis_index(a)
        pieces = [
            lax.dynamic_index_in_dim(p, here ^ bit, d, keepdims=True) for bit in range(sizes[a]) for p in pieces
        ]
    mask = jnp.stack([p.reshape(chunks, n_split, n_split) for p in pieces], axis=2)
    mask = mask.reshape(chunks, n_split, 1, -1)
    bias = jnp.repeat(jnp.where(mask > 0, 0.0, NEG).astype(jnp.float32), BLOCK, axis=3)

    def across(a, axis, bit):
        return lax.ppermute(a, axis, swap(sizes[axis], bit))

    def spread(a):
        return lax.all_to_all(a, split, split_axis=0, concat_axis=0, tiled=True)

    def chunk(a, j):
        return jnp.transpose(a[:, j * n_split : (j + 1) * n_split], (1, 0, 2))

    def gathered(arrays, axes):
        for a in axes:
            arrays = [
                p if bit == 0 else across(p, a, bit) for bit in range(sizes[a]) for p in arrays
            ]
        return arrays

    far = across(jnp.stack([chunk(keys, 0), chunk(values, 0)], axis=1), "zh", 1)
    outs = []
    states = []
    for j in range(1, chunks):
        own = jnp.stack([chunk(queries, j), chunk(keys, j), chunk(values, j)], axis=1)
        got = spread(own)
        q, near = got[:, :1], got[:, 1:]
        states.append((q, near, across(near, "zh", 1)))
    own = jnp.stack([chunk(queries, 0), chunk(keys, 0), chunk(values, 0)], axis=1)
    got = spread(jnp.concatenate([own, far], axis=1))
    arrays = gathered([got[:, 1:]], gather + ("c",))
    half = len(arrays)
    picks = []
    for number in range(2 * half):
        which, side = number // 2, number % 2
        picks.append((which, 2 * side, 2 * side + 1))
    outs.append(attend(bias[0], got[:, :1], arrays, tuple(picks), None, True))
    for j, (q, near, far) in enumerate(states, 1):
        near_all = gathered([near], gather + ("c",))
        far_all = gathered([far], gather + ("c",))
        b = bias[j].reshape(n_split, 1, half, 2, -1)
        near_bias = b[:, :, :, 0].reshape(n_split, 1, -1)
        far_bias = b[:, :, :, 1].reshape(n_split, 1, -1)
        pick = tuple((i, 0, 1) for i in range(half))
        state = attend(near_bias, q, near_all, pick, None, False)
        outs.append(attend(far_bias, q, far_all, pick, state, True))

    def project(part, j):
        flat = jnp.transpose(part, (1, 0, 2)).reshape(tok, width)
        rows = out_weight[j * width : (j + 1) * width]
        return jnp.dot(flat, rows, preferred_element_type=jnp.float32)

    early = spread(jnp.stack(outs[:-1], axis=1))
    total = sum(project(early[:, j], j) for j in range(chunks - 1))
    late = spread(outs[-1])
    return (total + project(late, chunks - 1)).astype(jnp.bfloat16)


def solution(mesh):
    n_head, n_blk = mesh.shape["head"], mesh.shape["blk"]
    x, y = n_head // CORES, n_blk // PLANES
    shape = (x, CORES, 2, PLANES // 2, y)
    wide = Mesh(np.asarray(mesh.devices).reshape(shape), ("x", "c", "zh", "zl", "y"))
    split, gather = (("x", "zl", "y"), ()) if x * y * 2 <= 8 else (("x", "zl"), ("y",))
    every = ("x", "c", "zh", "zl", "y")
    spec = P(every, None, None)
    return jax.shard_map(
        functools.partial(shards, split, gather),
        mesh=wide,
        in_specs=(spec, spec, spec, P(), P()),
        out_specs=P(every, None),
        check_vma=False,
    )
```

profile of v0, /device:TPU:0, one launch (start us, length us, event | category | flops | bytes accessed | tf_op | source)
XLA Modules:
  0.0 166.8 jit_solution(1827692231821673595)
XLA Ops:
  0.0 1.3 fusion.17
  1.9 1.0 pad_maximum_fusion.1
  2.9 6.2 %all-to-all-start.1 = ((bf16[8,3,128,128]{3,2,1,0:T(8,128)(2,1)}), bf16[8,3,128,128]{3,2,1,0:T(8,128)(2,1)S(1)}, u32[]{:S(2)}, u32[]{:S(2)}) async-start(bf16[8,3,128,128]{3,2,1,0:T(8,128)(2,1)} %pad_maximum_fusion.1), calls=%async_computation.1 | async-start | bytes 1572864 | tf_op jit(solution)/shard_map/all_to_all | solution.py:127
  9.2 1.0 pad_maximum_fusion.2
  10.2 11.5 %all-to-all-done.1 = bf16[8,3,128,128]{3,2,1,0:T(8,128)(2,1)S(1)} async-done(((bf16[8,3,128,128]{3,2,1,0:T(8,128)(2,1)}), bf16[8,3,128,128]{3,2,1,0:T(8,128)(2,1)S(1)}, u32[]{:S(2)}, u32[]{:S(2)}) %all-to-all-start.1) | async-done | bytes 786464 | tf_op jit(solution)/shard_map/all_to_all | solution.py:127
  21.6 3.5 %all-to-all-start.3 = ((bf16[8,3,128,128]{3,2,1,0:T(8,128)(2,1)}), bf16[8,3,128,128]{3,2,1,0:T(8,128)(2,1)S(1)}, u32[]{:S(2)}, u32[]{:S(2)}) async-start(bf16[8,3,128,128]{3,2,1,0:T(8,128)(2,1)} %pad_maximum_fusion.2), calls=%async_computation.3 | async-start | bytes 1572864 | tf_op jit(solution)/shard_map/all_to_all | solution.py:127
  25.4 2.7 %collective-permute-start = (bf16[8,2,128,128]{3,2,1,0:T(8,128)(2,1)S(1)}, bf16[8,2,128,128]{3,2,1,0:T(8,128)(2,1)S(1)}, u32[]{:S(2)}, u32[]{:S(2)}) collective-permute-start(bf16[8,2,128,128]{3,2,1,0:T(8,128)(2,1)S(1)} %pad_maximum_fusion.3), channel_id=1, source_target_pairs={{0,4},{4,0},{1,5},{5,1},{2,6},{6,2},{3,7},{7,3},{8,12},{12,8},{9,1... | collective-permute-start | bytes 1572872 | tf_op jit(solution)/shard_map/ppermute | solution.py:124
  28.1 21.8 %collective-permute-done = bf16[8,2,128,128]{3,2,1,0:T(8,128)(2,1)S(1)} collective-permute-done((bf16[8,2,128,128]{3,2,1,0:T(8,128)(2,1)S(1)}, bf16[8,2,128,128]{3,2,1,0:T(8,128)(2,1)S(1)}, u32[]{:S(2)}, u32[]{:S(2)}) %collective-permute-start) | collective-permute-done | bytes 524320 | tf_op jit(solution)/shard_map/ppermute | solution.py:124
  49.8 1.2 pad_maximum_fusion
  51.0 4.4 %all-to-all-start = ((bf16[8,5,128,128]{3,2,1,0:T(8,128)(2,1)}), bf16[8,5,128,128]{3,2,1,0:T(8,128)(2,1)}, u32[]{:S(2)}, u32[]{:S(2)}) async-start(bf16[8,5,128,128]{3,2,1,0:T(8,128)(2,1)} %pad_maximum_fusion), calls=%async_computation | async-start | bytes 2621440 | tf_op jit(solution)/shard_map/all_to_all | solution.py:127
  55.5 3.1 %collective-permute-start.5 = (bf16[8,2,128,128]{3,2,1,0:T(8,128)(2,1)S(1)}, bf16[8,2,128,128]{3,2,1,0:T(8,128)(2,1)}, u32[]{:S(2)}, u32[]{:S(2)}) collective-permute-start(bf16[8,2,128,128]{3,2,1,0:T(8,128)(2,1)S(1)} %slice.141.refs_2_), channel_id=1, source_target_pairs={{0,4},{4,0},{1,5},{5,1},{2,6},{6,2},{3,7},{7,3},{8,12},{12,8},{9,1... | collective-permute-start | bytes 1572872 | tf_op jit(solution)/shard_map/ppermute | solution.py:124
  59.8 4.9 %dynamic-slice_reduce_fusion = s32[3,2,2,2,2,2,2,2,2]{0,8,7,6,5,4,3,2,1:T(2,128)S(1)} fusion(s32[3,8,2,2,2,2,2,2,2,2,2,2]{1,0,11,10,9,8,7,6,5,4,3,2:T(4,128)S(1)} %reshape.61, s32[]{:T(128)S(6)} %select_n.43, s32[]{:T(128)S(6)} %select_n.45, s32[]{:T(128)S(6)} %select_n.47), kind=kLoop, calls=%fused_computation.14 | loop fusion | bytes 6156 | tf_op jit(solution)/shard_map/jit(dynamic_index_in_dim)/dynamic_slice | solution.py:109
  65.2 1.1 slice.134.refs_2_
  66.5 19.6 %all-to-all-done = bf16[8,5,128,128]{3,2,1,0:T(8,128)(2,1)} async-done(((bf16[8,5,128,128]{3,2,1,0:T(8,128)(2,1)}), bf16[8,5,128,128]{3,2,1,0:T(8,128)(2,1)}, u32[]{:S(2)}, u32[]{:S(2)}) %all-to-all-start) | async-done | bytes 1310752 | tf_op jit(solution)/shard_map/all_to_all | solution.py:127
  86.2 1.3 slice.130.refs_2_
  88.9 12.6 %collective-permute-done.2.refs_2_ = bf16[8,2,128,128]{3,2,1,0:T(8,128)(2,1)} collective-permute-done((bf16[8,2,128,128]{3,2,1,0:T(8,128)(2,1)S(1)}, bf16[8,2,128,128]{3,2,1,0:T(8,128)(2,1)}, u32[]{:S(2)}, u32[]{:S(2)}) %collective-permute-start.2) | collective-permute-done | bytes 524320 | tf_op jit(solution)/shard_map/ppermute | solution.py:124
  101.6 1.0 slice.133.refs_1_
  102.6 1.0 slice.140.refs_1_
  103.6 5.6 %shard_map.58 = (f32[1024,128]{1,0:T(8,128)S(1)}, f32[1024,256]{1,0:T(8,128)S(1)}) custom-call(f32[8,1,2048]{2,1,0:T(1,128)S(1)} %bitcast.80, bf16[8,1,128,128]{3,2,1,0:T(8,128)(2,1)S(1)} %slice.140.refs_1_, bf16[8,2,128,128]{3,2,1,0:T(8,128)(2,1)S(1)} %slice.141.refs_2_, bf16[8,2,128,128]{3,2,1,0:T(8,128)(2,1)} %collective-permute-done.7.refs_3_), custom_call_target="tpu_custom_call" | custom-call | flops 1073741824 | bytes 1048576 | tf_op jit(solution)/shard_map/pallas_call | solution.py:84
  109.2 7.1 %shard_map.59 = bf16[8,128,128]{2,1,0:T(8,128)(2,1)} custom-call(f32[8,1,2048]{2,1,0:T(1,128)S(1)} %bitcast.79, bf16[8,1,128,128]{3,2,1,0:T(8,128)(2,1)S(1)} %slice.140.refs_1_, bf16[8,2,128,128]{3,2,1,0:T(8,128)(2,1)} %collective-permute-done.5.refs_2_, bf16[8,2,128,128]{3,2,1,0:T(8,128)(2,1)} %collective-permute-done.6.refs_3_, ...), custom_call_target="tpu_custom_call" | custom-call | flops 1073741824 | bytes 1048576 | tf_op jit(solution)/shard_map/pallas_call | solution.py:84
  116.3 4.0 %all-to-all-start.4 = ((bf16[8,128,128]{2,1,0:T(8,128)(2,1)}), bf16[8,128,128]{2,1,0:T(8,128)(2,1)S(1)}, u32[]{:S(2)}, u32[]{:S(2)}) async-start(bf16[8,128,128]{2,1,0:T(8,128)(2,1)} %shard_map.59), calls=%async_computation.4 | async-start | bytes 524288 | tf_op jit(solution)/shard_map/all_to_all | solution.py:127
  120.3 5.6 %shard_map.56 = (f32[1024,128]{1,0:T(8,128)S(1)}, f32[1024,256]{1,0:T(8,128)S(1)}) custom-call(f32[8,1,2048]{2,1,0:T(1,128)S(1)} %bitcast.78, bf16[8,1,128,128]{3,2,1,0:T(8,128)(2,1)S(1)} %slice.133.refs_1_, bf16[8,2,128,128]{3,2,1,0:T(8,128)(2,1)S(1)} %slice.134.refs_2_, bf16[8,2,128,128]{3,2,1,0:T(8,128)(2,1)} %collective-permute-done.4.refs_3_), custom_call_target="tpu_custom_call" | custom-call | flops 1073741824 | bytes 1048576 | tf_op jit(solution)/shard_map/pallas_call | solution.py:84
  125.9 6.4 %shard_map.57 = bf16[8,128,128]{2,1,0:T(8,128)(2,1)S(1)} custom-call(f32[8,1,2048]{2,1,0:T(1,128)S(1)} %bitcast.77, bf16[8,1,128,128]{3,2,1,0:T(8,128)(2,1)S(1)} %slice.133.refs_1_, bf16[8,2,128,128]{3,2,1,0:T(8,128)(2,1)} %collective-permute-done.2.refs_2_, bf16[8,2,128,128]{3,2,1,0:T(8,128)(2,1)} %collective-permute-done.3.refs_3_, ...), custom_call_target="tpu_custom_call" | custom-call | flops 1073741824 | bytes 1048576 | tf_op jit(solution)/shard_map/pallas_call | solution.py:84
  132.3 1.0 slice.129.refs_1_
  133.4 7.0 %shard_map.55 = bf16[8,128,128]{2,1,0:T(8,128)(2,1)S(1)} custom-call(f32[8,1,4096]{2,1,0:T(1,128)S(1)} %bitcast.76, bf16[8,1,128,128]{3,2,1,0:T(8,128)(2,1)S(1)} %slice.129.refs_1_, bf16[8,4,128,128]{3,2,1,0:T(8,128)(2,1)S(1)} %slice.130.refs_2_, bf16[8,4,128,128]{3,2,1,0:T(8,128)(2,1)S(1)} %collective-permute-done.1.refs_3_), custom_call_target="tpu_custom_call" | custom-call | flops 2147483648 | bytes 2097152 | tf_op jit(solution)/shard_map/pallas_call | solution.py:84
  140.4 0.8 copy.58
  141.3 5.1 %all-to-all-start.2 = ((bf16[8,2,128,128]{3,2,1,0:T(8,128)(2,1)}), bf16[8,2,128,128]{3,2,1,0:T(8,128)(2,1)S(1)}, u32[]{:S(2)}, u32[]{:S(2)}) async-start(bf16[8,2,128,128]{3,2,1,0:T(8,128)(2,1)} %copy.58), calls=%async_computation.2 | async-start | bytes 1048576 | tf_op jit(solution)/shard_map/all_to_all | solution.py:127
  146.5 3.8 %fusion = f32[128,3072]{1,0:T(8,128)S(1)} fusion(bf16[128,1024]{0,1:T(8,128)(2,1)S(1)} %bitcast.83, bf16[3072,3072]{1,0:T(8,128)(2,1)} %param.9), kind=kOutput, calls=%fused_computation | convolution fusion | flops 805306368 | bytes 8126464 | tf_op jit(solution)/shard_map/dot_general | solution.py:169
  150.3 5.9 %all-to-all-done.2 = bf16[8,2,128,128]{3,2,1,0:T(8,128)(2,1)S(1)} async-done(((bf16[8,2,128,128]{3,2,1,0:T(8,128)(2,1)}), bf16[8,2,128,128]{3,2,1,0:T(8,128)(2,1)S(1)}, u32[]{:S(2)}, u32[]{:S(2)}) %all-to-all-start.2) | async-done | bytes 524320 | tf_op jit(solution)/shard_map/all_to_all | solution.py:127
  157.2 3.8 %fusion.2 = f32[128,3072]{1,0:T(8,128)S(1)} fusion(bf16[128,1024]{0,1:T(8,128)(2,1)S(1)} %bitcast.84, bf16[3072,3072]{1,0:T(8,128)(2,1)} %param.9), kind=kOutput, calls=%fused_computation.2 | convolution fusion | flops 805306368 | bytes 8126464 | tf_op jit(solution)/shard_map/dot_general | solution.py:169
  161.0 1.1 copy.77
  162.1 4.7 %fusion.12 = bf16[128,3072]{1,0:T(8,128)(2,1)} fusion(f32[128,3072]{1,0:T(8,128)S(1)} %fusion, f32[128,3072]{1,0:T(8,128)S(1)} %fusion.2, bf16[128,1024]{0,1:T(8,128)(2,1)S(1)} %bitcast.82, bf16[3072,3072]{1,0:T(8,128)(2,1)} %param.9), kind=kOutput, calls=%fused_computation.8 | convolution fusion | flops 806486016 | bytes 10485760 | tf_op jit(solution)/shard_map/dot_general | solution.py:169
  (57 shorter events, 5.5 us)
Async XLA Ops:
  0.0 1.4 copy-start.2
  0.0 1.6 copy-start.3
  2.9 18.8 %all-to-all-start.1 = ((bf16[8,3,128,128]{3,2,1,0:T(8,128)(2,1)}), bf16[8,3,128,128]{3,2,1,0:T(8,128)(2,1)S(1)}, u32[]{:S(2)}, u32[]{:S(2)}) async-start(bf16[8,3,128,128]{3,2,1,0:T(8,128)(2,1)} %pad_maximum_fusion.1), calls=%async_computation.1 | async-start | bytes 1572864 | tf_op jit(solution)/shard_map/all_to_all | solution.py:127
  21.6 3.7 %copy-start = (bf16[8,3,128,128]{3,2,1,0:T(8,128)(2,1)}, bf16[8,3,128,128]{3,2,1,0:T(8,128)(2,1)S(1)}, u32[]{:S(2)}) copy-start(bf16[8,3,128,128]{3,2,1,0:T(8,128)(2,1)S(1)} %all-to-all-done.1) | copy-start | bytes 2359300
  21.6 29.4 %all-to-all-start.3 = ((bf16[8,3,128,128]{3,2,1,0:T(8,128)(2,1)}), bf16[8,3,128,128]{3,2,1,0:T(8,128)(2,1)S(1)}, u32[]{:S(2)}, u32[]{:S(2)}) async-start(bf16[8,3,128,128]{3,2,1,0:T(8,128)(2,1)} %pad_maximum_fusion.2), calls=%async_computation.3 | async-start | bytes 1572864 | tf_op jit(solution)/shard_map/all_to_all | solution.py:127
  25.4 24.4 %collective-permute-start = (bf16[8,2,128,128]{3,2,1,0:T(8,128)(2,1)S(1)}, bf16[8,2,128,128]{3,2,1,0:T(8,128)(2,1)S(1)}, u32[]{:S(2)}, u32[]{:S(2)}) collective-permute-start(bf16[8,2,128,128]{3,2,1,0:T(8,128)(2,1)S(1)} %pad_maximum_fusion.3), channel_id=1, source_target_pairs={{0,4},{4,0},{1,5},{5,1},{2,6},{6,2},{3,7},{7,3},{8,12},{12,8},{9,1... | collective-permute-start | bytes 1572872 | tf_op jit(solution)/shard_map/ppermute | solution.py:124
  51.0 7.6 %copy-start.4 = (s32[24,32,32]{2,1,0:T(8,128)S(1)}, s32[24,32,32]{2,1,0:T(8,128)}, u32[]{:S(2)}) copy-start(s32[24,32,32]{2,1,0:T(8,128)} %param.8) | copy-start | bytes 294916
  51.0 4.5 %copy-start.1 = (bf16[8,3,128,128]{3,2,1,0:T(8,128)(2,1)}, bf16[8,3,128,128]{3,2,1,0:T(8,128)(2,1)S(1)}, u32[]{:S(2)}) copy-start(bf16[8,3,128,128]{3,2,1,0:T(8,128)(2,1)S(1)} %all-to-all-done.3) | copy-start | bytes 2359300
  51.0 35.1 %all-to-all-start = ((bf16[8,5,128,128]{3,2,1,0:T(8,128)(2,1)}), bf16[8,5,128,128]{3,2,1,0:T(8,128)(2,1)}, u32[]{:S(2)}, u32[]{:S(2)}) async-start(bf16[8,5,128,128]{3,2,1,0:T(8,128)(2,1)} %pad_maximum_fusion), calls=%async_computation | async-start | bytes 2621440 | tf_op jit(solution)/shard_map/all_to_all | solution.py:127
  55.5 32.9 %collective-permute-start.5 = (bf16[8,2,128,128]{3,2,1,0:T(8,128)(2,1)S(1)}, bf16[8,2,128,128]{3,2,1,0:T(8,128)(2,1)}, u32[]{:S(2)}, u32[]{:S(2)}) collective-permute-start(bf16[8,2,128,128]{3,2,1,0:T(8,128)(2,1)S(1)} %slice.141.refs_2_), channel_id=1, source_target_pairs={{0,4},{4,0},{1,5},{5,1},{2,6},{6,2},{3,7},{7,3},{8,12},{12,8},{9,1... | collective-permute-start | bytes 1572872 | tf_op jit(solution)/shard_map/ppermute | solution.py:124
  66.3 35.2 %collective-permute-start.2 = (bf16[8,2,128,128]{3,2,1,0:T(8,128)(2,1)S(1)}, bf16[8,2,128,128]{3,2,1,0:T(8,128)(2,1)}, u32[]{:S(2)}, u32[]{:S(2)}) collective-permute-start(bf16[8,2,128,128]{3,2,1,0:T(8,128)(2,1)S(1)} %slice.134.refs_2_), channel_id=1, source_target_pairs={{0,4},{4,0},{1,5},{5,1},{2,6},{6,2},{3,7},{7,3},{8,12},{12,8},{9,1... | collective-permute-start | bytes 1572872 | tf_op jit(solution)/shard_map/ppermute | solution.py:124
  66.5 37.1 %collective-permute-start.7 = (bf16[8,2,128,128]{3,2,1,0:T(8,128)(2,1)S(1)}, bf16[8,2,128,128]{3,2,1,0:T(8,128)(2,1)}, u32[]{:S(2)}, u32[]{:S(2)}) collective-permute-start(bf16[8,2,128,128]{3,2,1,0:T(8,128)(2,1)S(1)} %slice.141.refs_2_), channel_id=1, source_target_pairs={{0,8},{8,0},{1,9},{9,1},{2,10},{10,2},{3,11},{11,3},{4,12},{12,4},... | collective-permute-start | bytes 1572872 | tf_op jit(solution)/shard_map/ppermute | solution.py:124
  87.5 45.8 %collective-permute-start.1 = (bf16[8,4,128,128]{3,2,1,0:T(8,128)(2,1)S(1)}, bf16[8,4,128,128]{3,2,1,0:T(8,128)(2,1)S(1)}, u32[]{:S(2)}, u32[]{:S(2)}) collective-permute-start(bf16[8,4,128,128]{3,2,1,0:T(8,128)(2,1)S(1)} %slice.130.refs_2_), channel_id=1, source_target_pairs={{0,8},{8,0},{1,9},{9,1},{2,10},{10,2},{3,11},{11,3},{4,12},{12,4},... | collective-permute-start | bytes 3145736 | tf_op jit(solution)/shard_map/ppermute | solution.py:124
  87.8 32.5 %collective-permute-start.4 = (bf16[8,2,128,128]{3,2,1,0:T(8,128)(2,1)S(1)}, bf16[8,2,128,128]{3,2,1,0:T(8,128)(2,1)}, u32[]{:S(2)}, u32[]{:S(2)}) collective-permute-start(bf16[8,2,128,128]{3,2,1,0:T(8,128)(2,1)S(1)} %slice.134.refs_2_), channel_id=1, source_target_pairs={{0,8},{8,0},{1,9},{9,1},{2,10},{10,2},{3,11},{11,3},{4,12},{12,4},... | collective-permute-start | bytes 1572872 | tf_op jit(solution)/shard_map/ppermute | solution.py:124
  88.3 20.8 %collective-permute-start.6 = (bf16[8,2,128,128]{3,2,1,0:T(8,128)(2,1)}, bf16[8,2,128,128]{3,2,1,0:T(8,128)(2,1)}, u32[]{:S(2)}, u32[]{:S(2)}) collective-permute-start(bf16[8,2,128,128]{3,2,1,0:T(8,128)(2,1)} %collective-permute-done.5.refs_2_), channel_id=1, source_target_pairs={{0,8},{8,0},{1,9},{9,1},{2,10},{10,2},{3,11},{11,3},{4,12},{12,4},... | collective-permute-start | bytes 1572872 | tf_op jit(solution)/shard_map/ppermute | solution.py:124
  101.5 24.4 %collective-permute-start.3 = (bf16[8,2,128,128]{3,2,1,0:T(8,128)(2,1)}, bf16[8,2,128,128]{3,2,1,0:T(8,128)(2,1)}, u32[]{:S(2)}, u32[]{:S(2)}) collective-permute-start(bf16[8,2,128,128]{3,2,1,0:T(8,128)(2,1)} %collective-permute-done.2.refs_2_), channel_id=1, source_target_pairs={{0,8},{8,0},{1,9},{9,1},{2,10},{10,2},{3,11},{11,3},{4,12},{12,4},... | collective-permute-start | bytes 1572872 | tf_op jit(solution)/shard_map/ppermute | solution.py:124
  116.3 25.0 %all-to-all-start.4 = ((bf16[8,128,128]{2,1,0:T(8,128)(2,1)}), bf16[8,128,128]{2,1,0:T(8,128)(2,1)S(1)}, u32[]{:S(2)}, u32[]{:S(2)}) async-start(bf16[8,128,128]{2,1,0:T(8,128)(2,1)} %shard_map.59), calls=%async_computation.4 | async-start | bytes 524288 | tf_op jit(solution)/shard_map/all_to_all | solution.py:127
  141.3 15.0 %all-to-all-start.2 = ((bf16[8,2,128,128]{3,2,1,0:T(8,128)(2,1)}), bf16[8,2,128,128]{3,2,1,0:T(8,128)(2,1)S(1)}, u32[]{:S(2)}, u32[]{:S(2)}) async-start(bf16[8,2,128,128]{3,2,1,0:T(8,128)(2,1)} %copy.58), calls=%async_computation.2 | async-start | bytes 1048576 | tf_op jit(solution)/shard_map/all_to_all | solution.py:127
where the time goes:
time: 168 us; the launch traced here: 167 us
  waiting for transfers between devices  71.4 us (43%)
  Pallas kernels  31.7 us (19%)
  starting transfers between devices  29.9 us (18%)
  local copies, waits for them, and re-layouts  17.9 us (11%)
  matrix products  12.3 us (7%)
  other arithmetic  3.28 us (2%)
    all_to_all x5, waiting for transfers between devices, spread(): return lax.all_to_all(a, split, split_axis=0, concat_axis=0, tiled=True)  37 us
    ppermute x8, waiting for transfers between devices, across(): return lax.ppermute(a, axis, swap(sizes[axis], bit))  34.4 us
    pallas_call x5, Pallas kernels, attend(): pl.pallas_call(functools.partial(attend_kernel, picks, widths, rows, scal...  31.7 us
    all_to_all x5, starting transfers between devices, spread(): return lax.all_to_all(a, split, split_axis=0, concat_axis=0, tiled=True)  23.2 us
    dot_general x3, matrix products, project(): return jnp.dot(flat, rows, preferred_element_type=jnp.float32)  12.3 us
    ppermute x8, starting transfers between devices, across(): return lax.ppermute(a, axis, swap(sizes[axis], bit))  6.69 us
    dynamic_slice x1, local copies, waits for them, and re-layouts, shards(): lax.dynamic_index_in_dim(mask, lax.axis_index(a), 1 + names.index(a), kee...  4.91 us
  transfers between devices with their start and end apart: 13, of which 5 were waited for; matrix products, arithmetic and copies ran while one was open for 12% of the time, Pallas kernels for 19%

commit v1 on v0

v1 whole, which is shorter than its diff:
```python
import functools
import math

import jax
import jax.numpy as jnp
import numpy as np
from jax import lax
from jax.experimental import pallas as pl
from jax.experimental.pallas import tpu as pltpu
from jax.sharding import Mesh
from jax.sharding import PartitionSpec as P

BLOCK = 128
NEG = -1e30
CORES = 2
PLANES = 4
AXES = ("x", "c", "zh", "zl", "y")
VMEM = pl.BlockSpec(memory_space=pltpu.VMEM)
SMEM = pl.BlockSpec(memory_space=pltpu.SMEM)
PARAMS = pltpu.CompilerParams(vmem_limit_bytes=40 * 1024 * 1024)


def swap(size, bit):
    return [(i, i ^ bit) for i in range(size)]


def after(value, *others):
    return lax.optimization_barrier((value, *others))[0]


def bias_kernel(sources, place_ref, mask_ref, rows_ref, cols_ref, bias_ref):
    chunks, tiles, qb, _ = bias_ref.shape
    blocks = mask_ref.shape[1]
    span = cols_ref.shape[1]
    groups = tiles * qb
    group = place_ref[sources]
    lanes = lax.broadcasted_iota(jnp.int32, (groups, blocks), 1)
    mine = (lanes == rows_ref[...] + place_ref[0]).astype(jnp.bfloat16)
    rows = []
    for j in range(chunks):
        mask = (mask_ref[j * groups + group] > 0).astype(jnp.bfloat16)
        rows.append(jnp.dot(mine, mask, preferred_element_type=jnp.float32))
    rows = jnp.concatenate(rows, axis=0).astype(jnp.bfloat16)
    depth = lax.broadcasted_iota(jnp.int32, (blocks, span), 0)
    for n in range(sources):
        pick = (depth == cols_ref[...] + place_ref[n]).astype(jnp.bfloat16)
        seen = jnp.dot(rows, pick, preferred_element_type=jnp.float32)
        bias = jnp.where(seen > 0.5, 0.0, NEG)
        bias_ref[:, :, :, n * span : (n + 1) * span] = bias.reshape(chunks, tiles, qb, span)


def attend_kernel(picks, count, chunk, sub, scale, first, last, *refs):
    bias_ref, q_ref = refs[:2]
    kv_refs = refs[2 : 2 + count]
    rest = refs[2 + count :]
    if not first:
        m_in, acc_in = rest[:2]
        rest = rest[2:]
    _, tiles, qb, _ = bias_ref.shape
    block, hdim = q_ref.shape[2:]
    rows = qb * block

    def tile(index, carry):
        q = q_ref[pl.ds(index * qb, qb), 0].reshape(rows, hdim)
        if first:
            m = jnp.full((rows, 1), NEG, jnp.float32)
            acc = jnp.zeros((rows, 2 * hdim), jnp.float32)
        else:
            m = m_in[pl.ds(index * rows, rows), :1]
            acc = acc_in[pl.ds(index * rows, rows), :]
        for kref, kpart, vref, vpart, source in picks:
            span = kv_refs[kref].shape[0] * block
            for start in range(0, span, sub):
                some = slice(start // block, (start + sub) // block)
                k = kv_refs[kref][some, kpart].reshape(sub, hdim)
                v = kv_refs[vref][some, vpart].reshape(sub, hdim)
                v = jnp.concatenate([v, jnp.ones((sub, hdim), v.dtype)], axis=1)
                s = lax.dot_general(q, k, (((1,), (1,)), ((), ())), preferred_element_type=jnp.float32)
                at = source * span + start
                bias = bias_ref[chunk, index, :, at : at + sub]
                s = (s.reshape(qb, block, sub) * scale + bias[:, None, :]).reshape(rows, sub)
                m_next = jnp.maximum(m, jnp.max(s, axis=1, keepdims=True))
                p = jnp.exp2(s - m_next).astype(jnp.bfloat16)
                acc = acc * jnp.exp2(m - m_next) + jnp.dot(p, v, preferred_element_type=jnp.float32)
                m = m_next
        if last:
            out = (acc[:, :hdim] / acc[:, hdim:]).astype(jnp.bfloat16)
            rest[0][pl.ds(index * qb, qb)] = out.reshape(qb, block, hdim)
        else:
            rest[0][pl.ds(index * rows, rows), :] = jnp.broadcast_to(m, (rows, hdim))
            rest[1][pl.ds(index * rows, rows), :] = acc
        return carry

    lax.fori_loop(0, tiles, tile, 0)


def attend(bias, chunk, q, arrays, picks, state, last):
    groups, _, block, hdim = q.shape
    total = groups * block
    first = state is None
    if last:
        out_shape = jax.ShapeDtypeStruct((groups, block, hdim), jnp.bfloat16)
        out_specs = VMEM
    else:
        out_shape = (
            jax.ShapeDtypeStruct((total, hdim), jnp.float32),
            jax.ShapeDtypeStruct((total, 2 * hdim), jnp.float32),
        )
        out_specs = (VMEM, VMEM)
    args = [bias, q, *arrays, *(() if first else state)]
    scale = hdim**-0.5 * math.log2(math.e)
    keys = len(picks) * total
    sub = min(4, groups) * block
    return pl.pallas_call(
        functools.partial(attend_kernel, picks, len(arrays), chunk, sub, scale, first, last),
        out_shape=out_shape,
        in_specs=[VMEM] * len(args),
        out_specs=out_specs,
        compiler_params=PARAMS,
        cost_estimate=pl.CostEstimate(
            flops=total, bytes_accessed=4 * keys, transcendentals=0
        ),
    )(*args)


def shards(split, gather, queries, keys, values, block_mask, out_weight):
    sizes = {a: lax.axis_size(a) for a in AXES}
    stride = {a: math.prod(list(sizes.values())[i + 1 :]) for i, a in enumerate(AXES)}
    n_split = math.prod(sizes[a] for a in split)
    tok, heads, hdim = queries.shape
    chunks = heads // n_split
    width = n_split * hdim

    order = ("zh",) + gather + ("c",)
    bits = [dict(zip(reversed(order), b)) for b in np.ndindex(*(sizes[a] for a in reversed(order)))]
    sources = len(bits)
    half = sources // 2
    place = sum(
        (lax.axis_index(a) ^ np.array([b[a] for b in bits] + [0], np.int32)) * stride[a] for a in order
    )
    place = jnp.where(np.arange(sources + 1) == sources, lax.axis_index(split), place).astype(jnp.int32)
    local = np.zeros(1, np.int32)
    for a in split:
        local = (local[:, None] + np.arange(sizes[a], dtype=np.int32) * stride[a]).reshape(-1)
    qb = min(4, n_split)

    def across(a, axis, bit):
        return lax.ppermute(a, axis, swap(sizes[axis], bit))

    def spread(a):
        return lax.all_to_all(a, split, split_axis=0, concat_axis=0, tiled=True)

    def chunk(a, j):
        return jnp.transpose(a[:, j * n_split : (j + 1) * n_split], (1, 0, 2))

    def gathered(array, axes):
        arrays = [array]
        for a in axes:
            arrays = [p if bit == 0 else across(p, a, bit) for bit in range(sizes[a]) for p in arrays]
        return arrays

    first = jnp.stack([chunk(keys, 0), chunk(values, 0)], axis=1)
    far0 = across(first, "zh", 1)
    keys1, queries1, values1 = after((keys, queries, values), first)
    own = [jnp.stack([chunk(a, j) for a in (queries1, keys1, values1)], axis=1) for j in range(chunks)]
    own = [after(o, own[1]) if j != 1 else o for j, o in enumerate(own)]
    bias = pl.pallas_call(
        functools.partial(bias_kernel, sources),
        out_shape=jax.ShapeDtypeStruct((chunks, n_split // qb, qb, sources * n_split * BLOCK), jnp.float32),
        in_specs=[SMEM, VMEM, VMEM, VMEM],
        out_specs=VMEM,
        compiler_params=PARAMS,
    )(place, after(block_mask, own[0]), local[:, None], np.repeat(local, BLOCK)[None, :])

    near_pick = tuple((i, 0, i, 1, 2 * i) for i in range(half))
    far_pick = tuple((i, 0, i, 1, 2 * i + 1) for i in range(half))
    both_pick = tuple((2 * i, 0, 2 * i + 1, 0, i) for i in range(sources))
    outs = [None] * chunks
    waiting = []
    gate = None
    for j in range(1, chunks):
        got = spread(own[j] if gate is None else after(own[j], *gate))
        kv = got[:, 1:]
        far = across(kv if gate is None else after(kv, waiting[-1][1]), "zh", 1)
        near = gathered(kv, gather + ("c",))
        state = attend(bias, j, got[:, :1], near, near_pick, None, False)
        waiting.append((got, far, state))
        gate = (kv, far0)
    got = spread(after(jnp.concatenate([own[0], far0], axis=1), *waiting[-2][1:], kv))
    for j, (mine, far, state) in enumerate(waiting[:-1], 1):
        outs[j] = attend(bias, j, mine[:, :1], gathered(far, gather + ("c",)), far_pick, state, True)
    mine, far, state = waiting[-1]
    got = after(got, state, outs[-2])
    parts = [gathered(got[:, p : p + 1], gather + ("c",)) for p in range(1, 5)]
    all0 = [a for part in zip(*parts) for a in part]
    outs[0] = attend(bias, 0, after(got, far)[:, :1], all0, both_pick, None, True)
    ready = jnp.stack(outs[:-1], axis=1)
    early = spread(ready)
    far_all = gathered(far, gather + ("c",))
    outs[-1] = attend(bias, chunks - 1, mine[:, :1], far_all, far_pick, after(state, ready), True)
    late = spread(after(outs[-1], early))

    def project(part, j):
        flat = jnp.transpose(part, (1, 0, 2)).reshape(tok, width)
        rows = out_weight[j * width : (j + 1) * width]
        return jnp.dot(flat, rows, preferred_element_type=jnp.float32)

    early = after(early, outs[-1])
    total = sum(project(early[:, j], j) for j in range(chunks - 1))
    return (total + project(late, chunks - 1)).astype(jnp.bfloat16)


def solution(mesh):
    n_head, n_blk = mesh.shape["head"], mesh.shape["blk"]
    x, y = n_head // CORES, n_blk // PLANES
    shape = (x, CORES, 2, PLANES // 2, y)
    wide = Mesh(np.asarray(mesh.devices).reshape(shape), AXES)
    split, gather = (("x", "zl", "y"), ()) if x * y * 2 <= 8 else (("x", "zl"), ("y",))
    spec = P(AXES, None, None)
    return jax.shard_map(
        functools.partial(shards, split, gather),
        mesh=wide,
        in_specs=(spec, spec, spec, P(), P()),
        out_specs=P(AXES, None),
        check_vma=False,
    )
```

time: 168 us -> 150 us (0.89)
  waiting for transfers between devices: 71.4 us -> 54.6 us
  Pallas kernels: 31.7 us -> 26 us
  starting transfers between devices: 29.9 us -> 33.3 us
  other arithmetic: 3.28 us -> 6.33 us
  local copies, waits for them, and re-layouts: 17.9 us -> 15.8 us
    ppermute x8 -> x11, waiting for transfers between devices: 34.4 us -> 12.8 us  [across(): return lax.ppermute(a, axis, swap(sizes[axis], bit))]
    pallas_call x5 -> x6, Pallas kernels: 31.7 us -> 26 us  [the longest x5 25.1 us: attend(): pl.pallas_call(functools.partial(attend_kernel, picks, len(arrays), chunk...]
    dynamic_slice x2 -> x0, local copies, waits for them, and re-layouts: 4.95 us -> none  [the longest x1 4.91 us: shards(): lax.dynamic_index_in_dim(mask, lax.axis_index(a), 1 + names.index(a), kee...]
    all_to_all x5, waiting for transfers between devices: 37 us -> 41.8 us  [spread(): return lax.all_to_all(a, split, split_axis=0, concat_axis=0, tiled=True)]
    ppermute x8 -> x11, starting transfers between devices: 6.69 us -> 11.1 us  [across(): return lax.ppermute(a, axis, swap(sizes[axis], bit))]
    unnamed x20 -> x30, local copies, waits for them, and re-layouts: 2.42 us -> 6.4 us
    another operation x4 -> x5, other arithmetic: 2.06 us -> 3.81 us  [the longest x3 2.91 us: shards(): jnp.stack([chunk(a, j) for a in (queries1, keys1, values1)], axis=1)]
    slice x12 -> x6, local copies, waits for them, and re-layouts: 5.74 us -> 5.31 us  [the longest x2 1.94 us: shards(): state = attend(bias, j, got[:, :1], near, near_pick, None, False)]
  transfers between devices with their start and end apart: 13 -> 16, of which waited for: 5 -> 10; matrix products, arithmetic and copies ran while one was open for 12% -> 9% of each run, Pallas kernels for 19% -> 14%
where the time goes in v1:
time: 150 us; the launch traced here: 149 us
  waiting for transfers between devices  54.6 us (36%)
  starting transfers between devices  33.3 us (22%)
  Pallas kernels  26 us (17%)
  local copies, waits for them, and re-layouts  15.8 us (11%)
  matrix products  12.3 us (8%)
  other arithmetic  6.33 us (4%)
    all_to_all x5, waiting for transfers between devices, spread(): return lax.all_to_all(a, split, split_axis=0, concat_axis=0, tiled=True)  41.8 us
    pallas_call x5, Pallas kernels, attend(): pl.pallas_call(functools.partial(attend_kernel, picks, len(arrays), chunk...  25.1 us
    all_to_all x5, starting transfers between devices, spread(): return lax.all_to_all(a, split, split_axis=0, concat_axis=0, tiled=True)  22.3 us
    ppermute x11, waiting for transfers between devices, across(): return lax.ppermute(a, axis, swap(sizes[axis], bit))  12.8 us
    dot_general x3, matrix products, project(): return jnp.dot(flat, rows, preferred_element_type=jnp.float32)  12.3 us
    ppermute x11, starting transfers between devices, across(): return lax.ppermute(a, axis, swap(sizes[axis], bit))  11.1 us
    unnamed x30, local copies, waits for them, and re-layouts  6.4 us
  transfers between devices with their start and end apart: 16, of which 10 were waited for; matrix products, arithmetic and copies ran while one was open for 9% of the time, Pallas kernels for 14%

profile of v1, /device:TPU:0, one launch (start us, length us, event | category | flops | bytes accessed | tf_op | source)
XLA Modules:
  0.0 148.7 jit_solution(7013314171121527098)
XLA Ops:
  0.0 1.0 slice.77
  5.5 1.0 pad_maximum_fusion.2
  6.5 6.2 %all-to-all-start = ((bf16[8,3,128,128]{3,2,1,0:T(8,128)(2,1)}), bf16[8,3,128,128]{3,2,1,0:T(8,128)(2,1)S(1)}, u32[]{:S(2)}, u32[]{:S(2)}) async-start(bf16[8,3,128,128]{3,2,1,0:T(8,128)(2,1)} %pad_maximum_fusion.2), calls=%async_computation | async-start | bytes 1572864 | tf_op jit(solution)/shard_map/all_to_all | solution.py:151
  12.6 2.6 %collective-permute-start = (bf16[8,2,128,128]{3,2,1,0:T(8,128)(2,1)}, bf16[8,2,128,128]{3,2,1,0:T(8,128)(2,1)S(1)}, u32[]{:S(2)}, u32[]{:S(2)}) collective-permute-start(bf16[8,2,128,128]{3,2,1,0:T(8,128)(2,1)} %pad_maximum_fusion.4), channel_id=1, source_target_pairs={{0,4},{4,0},{1,5},{5,1},{2,6},{6,2},{3,7},{7,3},{8,12},{12,8},{9,1... | collective-permute-start | bytes 1572872 | tf_op jit(solution)/shard_map/ppermute | solution.py:148
  16.2 18.4 %all-to-all-done = bf16[8,3,128,128]{3,2,1,0:T(8,128)(2,1)S(1)} async-done(((bf16[8,3,128,128]{3,2,1,0:T(8,128)(2,1)}), bf16[8,3,128,128]{3,2,1,0:T(8,128)(2,1)S(1)}, u32[]{:S(2)}, u32[]{:S(2)}) %all-to-all-start) | async-done | bytes 786464 | tf_op jit(solution)/shard_map/all_to_all | solution.py:151
  35.6 2.9 %collective-permute-done = bf16[8,2,128,128]{3,2,1,0:T(8,128)(2,1)S(1)} collective-permute-done((bf16[8,2,128,128]{3,2,1,0:T(8,128)(2,1)}, bf16[8,2,128,128]{3,2,1,0:T(8,128)(2,1)S(1)}, u32[]{:S(2)}, u32[]{:S(2)}) %collective-permute-start) | collective-permute-done | bytes 524320 | tf_op jit(solution)/shard_map/ppermute | solution.py:148
  38.4 4.2 %all-to-all-start.1 = ((bf16[8,3,128,128]{3,2,1,0:T(8,128)(2,1)}), bf16[8,3,128,128]{3,2,1,0:T(8,128)(2,1)}, u32[]{:S(2)}, u32[]{:S(2)}) async-start(bf16[8,3,128,128]{3,2,1,0:T(8,128)(2,1)} %pad_maximum_fusion.3), calls=%async_computation.1 | async-start | bytes 1572864 | tf_op jit(solution)/shard_map/all_to_all | solution.py:151
  42.7 3.3 %collective-permute-start.1 = (bf16[8,2,128,128]{3,2,1,0:T(8,128)(2,1)S(1)}, bf16[8,2,128,128]{3,2,1,0:T(8,128)(2,1)S(1)}, u32[]{:S(2)}, u32[]{:S(2)}) collective-permute-start(bf16[8,2,128,128]{3,2,1,0:T(8,128)(2,1)S(1)} %slice.108.refs_2_), channel_id=1, source_target_pairs={{0,4},{4,0},{1,5},{5,1},{2,6},{6,2},{3,7},{7,3},{8,12},{12,8},{9,1... | collective-permute-start | bytes 1572872 | tf_op jit(solution)/shard_map/ppermute | solution.py:148
  47.9 2.5 %pad_maximum_fusion = bf16[8,5,128,128]{3,2,1,0:T(8,128)(2,1)} fusion(bf16[8,2,128,128]{3,2,1,0:T(8,128)(2,1)} %copy-done.11, bf16[8,3,128,128]{3,2,1,0:T(8,128)(2,1)} %pad_maximum_fusion.1), kind=kLoop, calls=%fused_computation.9 | loop fusion | flops 655360 | bytes 2621440 | tf_op jit(solution)/shard_map/concatenate | solution.py:189
  52.2 1.0 copy-done.3
  53.3 3.5 %shard_map.101 = (f32[1024,128]{1,0:T(8,128)S(1)}, f32[1024,256]{1,0:T(8,128)S(1)}) custom-call(f32[3,2,4,4096]{3,2,1,0:T(4,128)S(1)} %shard_map.100.refs_0_, bf16[8,1,128,128]{3,2,1,0:T(8,128)(2,1)S(1)} %slice.109.refs_1_, bf16[8,2,128,128]{3,2,1,0:T(8,128)(2,1)S(1)} %slice.108.refs_2_, bf16[8,2,128,128]{3,2,1,0:T(8,128)(2,1)S(1)} %copy-done.3), custom_call_target="tpu_custom_call" | custom-call | flops 1024 | bytes 8192 | tf_op jit(solution)/shard_map/pallas_call | solution.py:114
  57.5 3.9 %all-to-all-done.1 = bf16[8,3,128,128]{3,2,1,0:T(8,128)(2,1)} async-done(((bf16[8,3,128,128]{3,2,1,0:T(8,128)(2,1)}), bf16[8,3,128,128]{3,2,1,0:T(8,128)(2,1)}, u32[]{:S(2)}, u32[]{:S(2)}) %all-to-all-start.1) | async-done | bytes 786464 | tf_op jit(solution)/shard_map/all_to_all | solution.py:151
  61.4 1.1 slice.113.refs_2_
  62.5 7.3 %collective-permute-done.1.refs_2_ = bf16[8,2,128,128]{3,2,1,0:T(8,128)(2,1)S(1)} collective-permute-done((bf16[8,2,128,128]{3,2,1,0:T(8,128)(2,1)S(1)}, bf16[8,2,128,128]{3,2,1,0:T(8,128)(2,1)S(1)}, u32[]{:S(2)}, u32[]{:S(2)}) %collective-permute-start.1) | collective-permute-done | bytes 524320 | tf_op jit(solution)/shard_map/ppermute | solution.py:148
  69.8 4.3 %all-to-all-start.2 = ((bf16[8,5,128,128]{3,2,1,0:T(8,128)(2,1)}), bf16[8,5,128,128]{3,2,1,0:T(8,128)(2,1)}, u32[]{:S(2)}, u32[]{:S(2)}) async-start(bf16[8,5,128,128]{3,2,1,0:T(8,128)(2,1)} %pad_maximum_fusion), calls=%async_computation.2 | async-start | bytes 2621440 | tf_op jit(solution)/shard_map/all_to_all | solution.py:151
  74.6 3.3 %collective-permute-start.5 = (bf16[8,2,128,128]{3,2,1,0:T(8,128)(2,1)S(1)}, bf16[8,2,128,128]{3,2,1,0:T(8,128)(2,1)}, u32[]{:S(2)}, u32[]{:S(2)}) collective-permute-start(bf16[8,2,128,128]{3,2,1,0:T(8,128)(2,1)S(1)} %slice.113.refs_2_), channel_id=1, source_target_pairs={{0,4},{4,0},{1,5},{5,1},{2,6},{6,2},{3,7},{7,3},{8,12},{12,8},{9,1... | collective-permute-start | bytes 1572872 | tf_op jit(solution)/shard_map/ppermute | solution.py:148
  78.0 1.0 copy-done.1
  79.0 5.3 %shard_map.103 = bf16[8,128,128]{2,1,0:T(8,128)(2,1)S(1)} custom-call(f32[3,2,4,4096]{3,2,1,0:T(4,128)S(1)} %shard_map.100.refs_0_, bf16[8,1,128,128]{3,2,1,0:T(8,128)(2,1)S(1)} %slice.109.refs_1_, bf16[8,2,128,128]{3,2,1,0:T(8,128)(2,1)S(1)} %collective-permute-done.1.refs_2_, bf16[8,2,128,128]{3,2,1,0:T(8,128)(2,1)S(1)} %collective-permute-done.4.refs_3_, ...), custom_call_target="tpu_custom_call" | custom-call | flops 1024 | bytes 8192 | tf_op jit(solution)/shard_map/pallas_call | solution.py:114
  84.3 1.0 slice.114.refs_1_
  85.3 3.5 %shard_map.102 = (f32[1024,128]{1,0:T(8,128)S(1)}, f32[1024,256]{1,0:T(8,128)S(1)}) custom-call(f32[3,2,4,4096]{3,2,1,0:T(4,128)S(1)} %shard_map.100.refs_0_, bf16[8,1,128,128]{3,2,1,0:T(8,128)(2,1)S(1)} %slice.114.refs_1_, bf16[8,2,128,128]{3,2,1,0:T(8,128)(2,1)S(1)} %slice.113.refs_2_, bf16[8,2,128,128]{3,2,1,0:T(8,128)(2,1)S(1)} %collective-permute-done.3.refs_3_), custom_call_target="tpu_custom_call" | custom-call | flops 1024 | bytes 8192 | tf_op jit(solution)/shard_map/pallas_call | solution.py:114
  88.7 15.1 %all-to-all-done.2 = bf16[8,5,128,128]{3,2,1,0:T(8,128)(2,1)} async-done(((bf16[8,5,128,128]{3,2,1,0:T(8,128)(2,1)}), bf16[8,5,128,128]{3,2,1,0:T(8,128)(2,1)}, u32[]{:S(2)}, u32[]{:S(2)}) %all-to-all-start.2) | async-done | bytes 1310752 | tf_op jit(solution)/shard_map/all_to_all | solution.py:151
  103.8 1.3 fusion.15
  107.8 5.8 %shard_map.104 = bf16[8,128,128]{2,1,0:T(8,128)(2,1)S(1)} custom-call(f32[3,2,4,4096]{3,2,1,0:T(4,128)S(1)} %shard_map.100.refs_0_, bf16[8,1,128,128]{3,2,1,0:T(8,128)(2,1)S(1)} %slice.92.refs_1_, bf16[8,1,128,128]{3,2,1,0:T(8,128)(2,1)S(1)} %get-tuple-element.46.refs_2_, bf16[8,1,128,128]{3,2,1,0:T(8,128)(2,1)S(1)} %get-tuple-element.45.refs_3_, ...), custom_call_target="tpu_custom_call" | custom-call | flops 1024 | bytes 16384 | tf_op jit(solution)/shard_map/pallas_call | solution.py:114
  114.6 3.7 %all-to-all-start.3 = ((bf16[8,2,128,128]{3,2,1,0:T(8,128)(2,1)}), bf16[8,2,128,128]{3,2,1,0:T(8,128)(2,1)S(1)}, u32[]{:S(2)}, u32[]{:S(2)}) async-start(bf16[8,2,128,128]{3,2,1,0:T(8,128)(2,1)} %copy.47), calls=%async_computation.3 | async-start | bytes 1048576 | tf_op jit(solution)/shard_map/all_to_all | solution.py:151
  118.5 2.0 %collective-permute-done.10.refs_3_ = bf16[8,2,128,128]{3,2,1,0:T(8,128)(2,1)S(1)} collective-permute-done((bf16[8,2,128,128]{3,2,1,0:T(8,128)(2,1)}, bf16[8,2,128,128]{3,2,1,0:T(8,128)(2,1)S(1)}, u32[]{:S(2)}, u32[]{:S(2)}) %collective-permute-start.10) | collective-permute-done | bytes 524320 | tf_op jit(solution)/shard_map/ppermute | solution.py:148
  120.4 7.0 %shard_map.105 = bf16[8,128,128]{2,1,0:T(8,128)(2,1)} custom-call(f32[3,2,4,4096]{3,2,1,0:T(4,128)S(1)} %shard_map.100.refs_0_, bf16[8,1,128,128]{3,2,1,0:T(8,128)(2,1)S(1)} %slice.114.refs_1_, bf16[8,2,128,128]{3,2,1,0:T(8,128)(2,1)} %collective-permute-done.5.refs_2_, bf16[8,2,128,128]{3,2,1,0:T(8,128)(2,1)S(1)} %collective-permute-done.10.refs_3_, ...), custom_call_target="tpu_custom_call" | custom-call | flops 1024 | bytes 8192 | tf_op jit(solution)/shard_map/pallas_call | solution.py:114
  127.5 1.1 all-to-all-done.3
  128.9 3.9 %all-to-all-start.4 = ((bf16[8,128,128]{2,1,0:T(8,128)(2,1)}), bf16[8,128,128]{2,1,0:T(8,128)(2,1)S(1)}, u32[]{:S(2)}, u32[]{:S(2)}) async-start(bf16[8,128,128]{2,1,0:T(8,128)(2,1)} %shard_map.105), calls=%async_computation.4 | async-start | bytes 524288 | tf_op jit(solution)/shard_map/all_to_all | solution.py:151
  132.8 3.8 %fusion.2 = f32[128,3072]{1,0:T(8,128)S(1)} fusion(bf16[128,1024]{0,1:T(8,128)(2,1)S(1)} %bitcast.66, bf16[3072,3072]{1,0:T(8,128)(2,1)} %param.14), kind=kOutput, calls=%fused_computation.2 | convolution fusion | flops 805306368 | bytes 8126464 | tf_op jit(solution)/shard_map/dot_general | solution.py:206
  136.6 3.5 %all-to-all-done.4 = bf16[8,128,128]{2,1,0:T(8,128)(2,1)S(1)} async-done(((bf16[8,128,128]{2,1,0:T(8,128)(2,1)}), bf16[8,128,128]{2,1,0:T(8,128)(2,1)S(1)}, u32[]{:S(2)}, u32[]{:S(2)}) %all-to-all-start.4) | async-done | bytes 262176 | tf_op jit(solution)/shard_map/all_to_all | solution.py:151
  140.2 3.8 %fusion = f32[128,3072]{1,0:T(8,128)S(1)} fusion(bf16[128,1024]{0,1:T(8,128)(2,1)S(1)} %bitcast.63, bf16[3072,3072]{1,0:T(8,128)(2,1)} %param.14), kind=kOutput, calls=%fused_computation | convolution fusion | flops 805306368 | bytes 8126464 | tf_op jit(solution)/shard_map/dot_general | solution.py:206
  144.0 4.7 %fusion.12 = bf16[128,3072]{1,0:T(8,128)(2,1)} fusion(f32[128,3072]{1,0:T(8,128)S(1)} %fusion, f32[128,3072]{1,0:T(8,128)S(1)} %fusion.2, bf16[128,1024]{0,1:T(8,128)(2,1)S(1)} %bitcast.64, bf16[3072,3072]{1,0:T(8,128)(2,1)} %param.14), kind=kOutput, calls=%fused_computation.8 | convolution fusion | flops 806486016 | bytes 10485760 | tf_op jit(solution)/shard_map/dot_general | solution.py:206
  (65 shorter events, 15.7 us)
Async XLA Ops:
  0.0 3.0 %copy-start.10 = (bf16[128,24,128]{2,1,0:T(8,128)(2,1)S(1)}, bf16[128,24,128]{2,1,0:T(8,128)(2,1)}, u32[]{:S(2)}) copy-start(bf16[128,24,128]{2,1,0:T(8,128)(2,1)} %param.10) | copy-start | bytes 2359300
  3.0 1.1 copy-start.8
  4.1 1.1 copy-start.9
  6.5 28.1 %all-to-all-start = ((bf16[8,3,128,128]{3,2,1,0:T(8,128)(2,1)}), bf16[8,3,128,128]{3,2,1,0:T(8,128)(2,1)S(1)}, u32[]{:S(2)}, u32[]{:S(2)}) async-start(bf16[8,3,128,128]{3,2,1,0:T(8,128)(2,1)} %pad_maximum_fusion.2), calls=%async_computation | async-start | bytes 1572864 | tf_op jit(solution)/shard_map/all_to_all | solution.py:151
  12.6 25.8 %collective-permute-start = (bf16[8,2,128,128]{3,2,1,0:T(8,128)(2,1)}, bf16[8,2,128,128]{3,2,1,0:T(8,128)(2,1)S(1)}, u32[]{:S(2)}, u32[]{:S(2)}) collective-permute-start(bf16[8,2,128,128]{3,2,1,0:T(8,128)(2,1)} %pad_maximum_fusion.4), channel_id=1, source_target_pairs={{0,4},{4,0},{1,5},{5,1},{2,6},{6,2},{3,7},{7,3},{8,12},{12,8},{9,1... | collective-permute-start | bytes 1572872 | tf_op jit(solution)/shard_map/ppermute | solution.py:148
  34.5 0.9 copy-start.7
  35.5 11.5 %copy-start.12 = (s32[5]{0:T(128)S(1)}, s32[5]{0:T(128)}, u32[]{:S(2)}) copy-start(s32[5]{0:T(128)} %constant.35.clone) | copy-start | bytes 64
  35.5 11.4 %copy-start.13 = (s32[5]{0:T(128)S(1)}, s32[5]{0:T(128)}, u32[]{:S(2)}) copy-start(s32[5]{0:T(128)} %constant.36.clone) | copy-start | bytes 64
  35.5 11.4 %copy-start.14 = (pred[5]{0:T(512)(128)(4,1)S(1)}, pred[5]{0:T(512)(128)(4,1)}, u32[]{:S(2)}) copy-start(pred[5]{0:T(512)(128)(4,1)} %constant.37.clone) | copy-start | bytes 19
  35.5 11.4 %copy-start.4 = (s32[24,32,32]{2,1,0:T(8,128)S(1)}, s32[24,32,32]{2,1,0:T(8,128)}, u32[]{:S(2)}) copy-start(s32[24,32,32]{2,1,0:T(8,128)} %mask_ref) | copy-start | bytes 294916
  35.5 11.4 %copy-start.5 = (s32[8,1]{1,0:T(8,128)S(1)}, s32[8,1]{1,0:T(8,128)}, u32[]{:S(2)}) copy-start(s32[8,1]{1,0:T(8,128)} %constant.38.clone.rows_ref) | copy-start | bytes 100
  35.5 11.4 %copy-start.6 = (s32[1,1024]{1,0:T(1,128)S(1)}, s32[1,1024]{1,0:T(1,128)}, u32[]{:S(2)}) copy-start(s32[1,1024]{1,0:T(1,128)} %constant.39.clone.cols_ref) | copy-start | bytes 12292
  38.4 4.2 %copy-start.11 = (bf16[8,2,128,128]{3,2,1,0:T(8,128)(2,1)}, bf16[8,2,128,128]{3,2,1,0:T(8,128)(2,1)S(1)}, u32[]{:S(2)}) copy-start(bf16[8,2,128,128]{3,2,1,0:T(8,128)(2,1)S(1)} %collective-permute-done) | copy-start | bytes 1572868
  38.4 23.0 %all-to-all-start.1 = ((bf16[8,3,128,128]{3,2,1,0:T(8,128)(2,1)}), bf16[8,3,128,128]{3,2,1,0:T(8,128)(2,1)}, u32[]{:S(2)}, u32[]{:S(2)}) async-start(bf16[8,3,128,128]{3,2,1,0:T(8,128)(2,1)} %pad_maximum_fusion.3), calls=%async_computation.1 | async-start | bytes 1572864 | tf_op jit(solution)/shard_map/all_to_all | solution.py:151
  42.6 8.8 %collective-permute-start.2 = (bf16[8,2,128,128]{3,2,1,0:T(8,128)(2,1)S(1)}, bf16[8,2,128,128]{3,2,1,0:T(8,128)(2,1)S(1)}, u32[]{:S(2)}, u32[]{:S(2)}) collective-permute-start(bf16[8,2,128,128]{3,2,1,0:T(8,128)(2,1)S(1)} %slice.108.refs_2_), channel_id=1, source_target_pairs={{0,8},{8,0},{1,9},{9,1},{2,10},{10,2},{3,11},{11,3},{4,12},{12,4},... | collective-permute-start | bytes 1572872 | tf_op jit(solution)/shard_map/ppermute | solution.py:148
  42.7 27.0 %collective-permute-start.1 = (bf16[8,2,128,128]{3,2,1,0:T(8,128)(2,1)S(1)}, bf16[8,2,128,128]{3,2,1,0:T(8,128)(2,1)S(1)}, u32[]{:S(2)}, u32[]{:S(2)}) collective-permute-start(bf16[8,2,128,128]{3,2,1,0:T(8,128)(2,1)S(1)} %slice.108.refs_2_), channel_id=1, source_target_pairs={{0,4},{4,0},{1,5},{5,1},{2,6},{6,2},{3,7},{7,3},{8,12},{12,8},{9,1... | collective-permute-start | bytes 1572872 | tf_op jit(solution)/shard_map/ppermute | solution.py:148
  51.4 0.8 copy-start.2
  52.2 1.0 copy-start.3
  56.7 0.8 copy-start
  69.8 34.0 %all-to-all-start.2 = ((bf16[8,5,128,128]{3,2,1,0:T(8,128)(2,1)}), bf16[8,5,128,128]{3,2,1,0:T(8,128)(2,1)}, u32[]{:S(2)}, u32[]{:S(2)}) async-start(bf16[8,5,128,128]{3,2,1,0:T(8,128)(2,1)} %pad_maximum_fusion), calls=%async_computation.2 | async-start | bytes 2621440 | tf_op jit(solution)/shard_map/all_to_all | solution.py:151
  74.1 3.9 %collective-permute-start.4 = (bf16[8,2,128,128]{3,2,1,0:T(8,128)(2,1)S(1)}, bf16[8,2,128,128]{3,2,1,0:T(8,128)(2,1)S(1)}, u32[]{:S(2)}, u32[]{:S(2)}) collective-permute-start(bf16[8,2,128,128]{3,2,1,0:T(8,128)(2,1)S(1)} %collective-permute-done.1.refs_2_), channel_id=1, source_target_pairs={{0,8},{8,0},{1,9},{9,1},{2,10},{10,2},{3,11},{11,3},{4,12},{12,4},... | collective-permute-start | bytes 1572872 | tf_op jit(solution)/shard_map/ppermute | solution.py:148
  74.1 11.1 %collective-permute-start.3 = (bf16[8,2,128,128]{3,2,1,0:T(8,128)(2,1)S(1)}, bf16[8,2,128,128]{3,2,1,0:T(8,128)(2,1)S(1)}, u32[]{:S(2)}, u32[]{:S(2)}) collective-permute-start(bf16[8,2,128,128]{3,2,1,0:T(8,128)(2,1)S(1)} %slice.113.refs_2_), channel_id=1, source_target_pairs={{0,8},{8,0},{1,9},{9,1},{2,10},{10,2},{3,11},{11,3},{4,12},{12,4},... | collective-permute-start | bytes 1572872 | tf_op jit(solution)/shard_map/ppermute | solution.py:148
  74.6 31.6 %collective-permute-start.5 = (bf16[8,2,128,128]{3,2,1,0:T(8,128)(2,1)S(1)}, bf16[8,2,128,128]{3,2,1,0:T(8,128)(2,1)}, u32[]{:S(2)}, u32[]{:S(2)}) collective-permute-start(bf16[8,2,128,128]{3,2,1,0:T(8,128)(2,1)S(1)} %slice.113.refs_2_), channel_id=1, source_target_pairs={{0,4},{4,0},{1,5},{5,1},{2,6},{6,2},{3,7},{7,3},{8,12},{12,8},{9,1... | collective-permute-start | bytes 1572872 | tf_op jit(solution)/shard_map/ppermute | solution.py:148
  78.0 1.0 copy-start.1
  105.1 2.1 %collective-permute-start.6 = (bf16[8,1,128,128]{3,2,1,0:T(8,128)(2,1)S(1)}, bf16[8,1,128,128]{3,2,1,0:T(8,128)(2,1)S(1)}, u32[]{:S(2)}, u32[]{:S(2)}) collective-permute-start(bf16[8,1,128,128]{3,2,1,0:T(8,128)(2,1)S(1)} %get-tuple-element.46.refs_2_), channel_id=1, source_target_pairs={{0,8},{8,0},{1,9},{9,1},{2,10},{10,2},{3,11},{11,3},{4,12},{12,4},... | collective-permute-start | bytes 786440 | tf_op jit(solution)/shard_map/ppermute | solution.py:148
  105.2 2.0 %collective-permute-start.7 = (bf16[8,1,128,128]{3,2,1,0:T(8,128)(2,1)S(1)}, bf16[8,1,128,128]{3,2,1,0:T(8,128)(2,1)S(1)}, u32[]{:S(2)}, u32[]{:S(2)}) collective-permute-start(bf16[8,1,128,128]{3,2,1,0:T(8,128)(2,1)S(1)} %get-tuple-element.45.refs_3_), channel_id=1, source_target_pairs={{0,8},{8,0},{1,9},{9,1},{2,10},{10,2},{3,11},{11,3},{4,12},{12,4},... | collective-permute-start | bytes 786440 | tf_op jit(solution)/shard_map/ppermute | solution.py:148
  105.7 1.8 %collective-permute-start.8 = (bf16[8,1,128,128]{3,2,1,0:T(8,128)(2,1)S(1)}, bf16[8,1,128,128]{3,2,1,0:T(8,128)(2,1)S(1)}, u32[]{:S(2)}, u32[]{:S(2)}) collective-permute-start(bf16[8,1,128,128]{3,2,1,0:T(8,128)(2,1)S(1)} %get-tuple-element.44.refs_4_), channel_id=1, source_target_pairs={{0,8},{8,0},{1,9},{9,1},{2,10},{10,2},{3,11},{11,3},{4,12},{12,4},... | collective-permute-start | bytes 786440 | tf_op jit(solution)/shard_map/ppermute | solution.py:148
  105.8 2.1 %collective-permute-start.9 = (bf16[8,1,128,128]{3,2,1,0:T(8,128)(2,1)S(1)}, bf16[8,1,128,128]{3,2,1,0:T(8,128)(2,1)S(1)}, u32[]{:S(2)}, u32[]{:S(2)}) collective-permute-start(bf16[8,1,128,128]{3,2,1,0:T(8,128)(2,1)S(1)} %get-tuple-element.43.refs_5_), channel_id=1, source_target_pairs={{0,8},{8,0},{1,9},{9,1},{2,10},{10,2},{3,11},{11,3},{4,12},{12,4},... | collective-permute-start | bytes 786440 | tf_op jit(solution)/shard_map/ppermute | solution.py:148
  114.6 14.0 %all-to-all-start.3 = ((bf16[8,2,128,128]{3,2,1,0:T(8,128)(2,1)}), bf16[8,2,128,128]{3,2,1,0:T(8,128)(2,1)S(1)}, u32[]{:S(2)}, u32[]{:S(2)}) async-start(bf16[8,2,128,128]{3,2,1,0:T(8,128)(2,1)} %copy.47), calls=%async_computation.3 | async-start | bytes 1048576 | tf_op jit(solution)/shard_map/all_to_all | solution.py:151
  118.3 2.2 %collective-permute-start.10 = (bf16[8,2,128,128]{3,2,1,0:T(8,128)(2,1)}, bf16[8,2,128,128]{3,2,1,0:T(8,128)(2,1)S(1)}, u32[]{:S(2)}, u32[]{:S(2)}) collective-permute-start(bf16[8,2,128,128]{3,2,1,0:T(8,128)(2,1)} %collective-permute-done.5.refs_2_), channel_id=1, source_target_pairs={{0,8},{8,0},{1,9},{9,1},{2,10},{10,2},{3,11},{11,3},{4,12},{12,4},... | collective-permute-start | bytes 1572872 | tf_op jit(solution)/shard_map/ppermute | solution.py:148
  128.9 11.2 %all-to-all-start.4 = ((bf16[8,128,128]{2,1,0:T(8,128)(2,1)}), bf16[8,128,128]{2,1,0:T(8,128)(2,1)S(1)}, u32[]{:S(2)}, u32[]{:S(2)}) async-start(bf16[8,128,128]{2,1,0:T(8,128)(2,1)} %shard_map.105), calls=%async_computation.4 | async-start | bytes 524288 | tf_op jit(solution)/shard_map/all_to_all | solution.py:151

commit v2 on v1

--- a/solution.py
+++ b/solution.py
@@ -17,7 +17,6 @@
 AXES = ("x", "c", "zh", "zl", "y")
 VMEM = pl.BlockSpec(memory_space=pltpu.VMEM)
 SMEM = pl.BlockSpec(memory_space=pltpu.SMEM)
-PARAMS = pltpu.CompilerParams(vmem_limit_bytes=40 * 1024 * 1024)
 
 
 def swap(size, bit):
@@ -28,35 +27,37 @@
     return lax.optimization_barrier((value, *others))[0]
 
 
-def bias_kernel(sources, place_ref, mask_ref, rows_ref, cols_ref, bias_ref):
-    chunks, tiles, qb, _ = bias_ref.shape
+def grant(*arrays):
+    held = sum(math.prod(a.shape) * a.dtype.itemsize for a in arrays)
+    return pltpu.CompilerParams(vmem_limit_bytes=10 * 2**20 + 2 * held)
+
+
+def bias_kernel(sources, chunk, place_ref, mask_ref, rows_ref, cols_ref, bias_ref):
+    tiles, qb, _ = bias_ref.shape
     blocks = mask_ref.shape[1]
     span = cols_ref.shape[1]
     groups = tiles * qb
     group = place_ref[sources]
     lanes = lax.broadcasted_iota(jnp.int32, (groups, blocks), 1)
     mine = (lanes == rows_ref[...] + place_ref[0]).astype(jnp.bfloat16)
-    rows = []
-    for j in range(chunks):
-        mask = (mask_ref[j * groups + group] > 0).astype(jnp.bfloat16)
-        rows.append(jnp.dot(mine, mask, preferred_element_type=jnp.float32))
-    rows = jnp.concatenate(rows, axis=0).astype(jnp.bfloat16)
+    mask = (mask_ref[chunk * groups + group] > 0).astype(jnp.bfloat16)
+    rows = jnp.dot(mine, mask, preferred_element_type=jnp.float32).astype(jnp.bfloat16)
     depth = lax.broadcasted_iota(jnp.int32, (blocks, span), 0)
     for n in range(sources):
         pick = (depth == cols_ref[...] + place_ref[n]).astype(jnp.bfloat16)
         seen = jnp.dot(rows, pick, preferred_element_type=jnp.float32)
         bias = jnp.where(seen > 0.5, 0.0, NEG)
-        bias_ref[:, :, :, n * span : (n + 1) * span] = bias.reshape(chunks, tiles, qb, span)
-
-
-def attend_kernel(picks, count, chunk, sub, scale, first, last, *refs):
+        bias_ref[:, :, n * span : (n + 1) * span] = bias.reshape(tiles, qb, span)
+
+
+def attend_kernel(picks, count, sub, scale, first, last, *refs):
     bias_ref, q_ref = refs[:2]
     kv_refs = refs[2 : 2 + count]
     rest = refs[2 + count :]
     if not first:
         m_in, acc_in = rest[:2]
         rest = rest[2:]
-    _, tiles, qb, _ = bias_ref.shape
+    tiles, qb, _ = bias_ref.shape
     block, hdim = q_ref.shape[2:]
     rows = qb * block
 
@@ -66,7 +67,7 @@
             m = jnp.full((rows, 1), NEG, jnp.float32)
             acc = jnp.zeros((rows, 2 * hdim), jnp.float32)
         else:
-            m = m_in[pl.ds(index * rows, rows), :1]
+            m = jnp.max(m_in[pl.ds(index * rows, rows), :], axis=1, keepdims=True)
             acc = acc_in[pl.ds(index * rows, rows), :]
         for kref, kpart, vref, vpart, source in picks:
             span = kv_refs[kref].shape[0] * block
@@ -77,7 +78,7 @@
                 v = jnp.concatenate([v, jnp.ones((sub, hdim), v.dtype)], axis=1)
                 s = lax.dot_general(q, k, (((1,), (1,)), ((), ())), preferred_element_type=jnp.float32)
                 at = source * span + start
-                bias = bias_ref[chunk, index, :, at : at + sub]
+                bias = bias_ref[index, :, at : at + sub]
                 s = (s.reshape(qb, block, sub) * scale + bias[:, None, :]).reshape(rows, sub)
                 m_next = jnp.maximum(m, jnp.max(s, axis=1, keepdims=True))
                 p = jnp.exp2(s - m_next).astype(jnp.bfloat16)
@@ -94,7 +95,7 @@
     lax.fori_loop(0, tiles, tile, 0)
 
 
-def attend(bias, chunk, q, arrays, picks, state, last):
+def attend(bias, q, arrays, picks, state, last):
     groups, _, block, hdim = q.shape
     total = groups * block
     first = state is None
@@ -112,11 +113,11 @@
     keys = len(picks) * total
     sub = min(4, groups) * block
     return pl.pallas_call(
-        functools.partial(attend_kernel, picks, len(arrays), chunk, sub, scale, first, last),
+        functools.partial(attend_kernel, picks, len(arrays), sub, scale, first, last),
         out_shape=out_shape,
         in_specs=[VMEM] * len(args),
         out_specs=out_specs,
-        compiler_params=PARAMS,
+        compiler_params=grant(*args),
         cost_estimate=pl.CostEstimate(
             flops=total, bytes_accessed=4 * keys, transcendentals=0
         ),
@@ -164,40 +165,45 @@
     keys1, queries1, values1 = after((keys, queries, values), first)
     own = [jnp.stack([chunk(a, j) for a in (queries1, keys1, values1)], axis=1) for j in range(chunks)]
     own = [after(o, own[1]) if j != 1 else o for j, o in enumerate(own)]
-    bias = pl.pallas_call(
-        functools.partial(bias_kernel, sources),
-        out_shape=jax.ShapeDtypeStruct((chunks, n_split // qb, qb, sources * n_split * BLOCK), jnp.float32),
-        in_specs=[SMEM, VMEM, VMEM, VMEM],
-        out_specs=VMEM,
-        compiler_params=PARAMS,
-    )(place, after(block_mask, own[0]), local[:, None], np.repeat(local, BLOCK)[None, :])
+    out = jax.ShapeDtypeStruct((n_split // qb, qb, sources * n_split * BLOCK), jnp.float32)
+
+    def bias_of(j, *before):
+        return pl.pallas_call(
+            functools.partial(bias_kernel, sources, j),
+            out_shape=out,
+            in_specs=[SMEM, VMEM, VMEM, VMEM],
+            out_specs=VMEM,
+            compiler_params=grant(out, block_mask),
+            cost_estimate=pl.CostEstimate(flops=10**11, bytes_accessed=0, transcendentals=0),
+        )(place, after(block_mask, *before), local[:, None], np.repeat(local, BLOCK)[None, :])
 
     near_pick = tuple((i, 0, i, 1, 2 * i) for i in range(half))
     far_pick = tuple((i, 0, i, 1, 2 * i + 1) for i in range(half))
-    both_pick = tuple((2 * i, 0, 2 * i + 1, 0, i) for i in range(sources))
+    both_pick = tuple((i, 1 + 2 * z, i, 2 + 2 * z, 2 * i + z) for i in range(half) for z in range(2))
     outs = [None] * chunks
     waiting = []
-    gate = None
+    far, gate = far0, ()
     for j in range(1, chunks):
-        got = spread(own[j] if gate is None else after(own[j], *gate))
+        got = spread(after(own[j], *gate))
+        bias = bias_of(j, far)
+        got = after(got, bias)
         kv = got[:, 1:]
-        far = across(kv if gate is None else after(kv, waiting[-1][1]), "zh", 1)
+        gate = (kv,)
+        far = across(kv, "zh", 1)
         near = gathered(kv, gather + ("c",))
-        state = attend(bias, j, got[:, :1], near, near_pick, None, False)
-        waiting.append((got, far, state))
-        gate = (kv, far0)
-    got = spread(after(jnp.concatenate([own[0], far0], axis=1), *waiting[-2][1:], kv))
-    for j, (mine, far, state) in enumerate(waiting[:-1], 1):
-        outs[j] = attend(bias, j, mine[:, :1], gathered(far, gather + ("c",)), far_pick, state, True)
-    mine, far, state = waiting[-1]
-    got = after(got, state, outs[-2])
-    parts = [gathered(got[:, p : p + 1], gather + ("c",)) for p in range(1, 5)]
-    all0 = [a for part in zip(*parts) for a in part]
-    outs[0] = attend(bias, 0, after(got, far)[:, :1], all0, both_pick, None, True)
+        state = attend(bias, got[:, :1], near, near_pick, None, False)
+        waiting.append((bias, got, far, state))
+    got = spread(after(jnp.concatenate([own[0], far0], axis=1), kv))
+    for j, (bias, mine, far, state) in enumerate(waiting[:-1], 1):
+        outs[j] = attend(bias, mine[:, :1], gathered(far, gather + ("c",)), far_pick, state, True)
+    bias, mine, far, state = waiting[-1]
+    bias0 = bias_of(0, far)
+    got = after(got, bias0, state, outs[-2])
+    outs[0] = attend(bias0, got[:, :1], gathered(got, gather + ("c",)), both_pick, None, True)
     ready = jnp.stack(outs[:-1], axis=1)
     early = spread(ready)
     far_all = gathered(far, gather + ("c",))
-    outs[-1] = attend(bias, chunks - 1, mine[:, :1], far_all, far_pick, after(state, ready), True)
+    outs[-1] = attend(bias, mine[:, :1], far_all, far_pick, after(state, ready), True)
     late = spread(after(outs[-1], early))
 
     def project(part, j):

time: 150 us -> 157 us (1.047)
  waiting for transfers between devices: 54.6 us -> 70.9 us
  starting transfers between devices: 33.3 us -> 25.6 us
  local copies, waits for them, and re-layouts: 15.8 us -> 19.3 us
  Pallas kernels: 26 us -> 23.2 us
  other arithmetic: 6.33 us -> 4.46 us
    ppermute x11 -> x8, waiting for transfers between devices: 12.8 us -> 39.8 us  [across(): return lax.ppermute(a, axis, swap(sizes[axis], bit))]
    all_to_all x5, waiting for transfers between devices: 41.8 us -> 31 us  [spread(): return lax.all_to_all(a, split, split_axis=0, concat_axis=0, tiled=True)]
    ppermute x11 -> x8, starting transfers between devices: 11.1 us -> 4.63 us  [across(): return lax.ppermute(a, axis, swap(sizes[axis], bit))]
    pallas_call x6 -> x8, Pallas kernels: 26 us -> 23.2 us  [the longest x5 20.5 us: attend(): pl.pallas_call(functools.partial(attend_kernel, picks, len(arrays), sub,...]
    unnamed x30 -> x50, local copies, waits for them, and re-layouts: 6.4 us -> 8.88 us
    slice x4 -> x3, local copies, waits for them, and re-layouts: 4.19 us -> 1.95 us  [the longest x1 0.97 us: shards(): mine[:, :1]]
    another operation x3, local copies, waits for them, and re-layouts: 0.17 us -> 2.33 us  [shards(): jnp.stack([chunk(a, j) for a in (queries1, keys1, values1)], axis=1)]
  transfers between devices with their start and end apart: 16 -> 13, of which waited for: 10 -> 10; matrix products, arithmetic and copies ran while one was open for 9% -> 9% of each run, Pallas kernels for 14% -> 11%
where the time goes in v2:
time: 157 us; the launch traced here: 156 us
  waiting for transfers between devices  70.9 us (45%)
  starting transfers between devices  25.6 us (16%)
  Pallas kernels  23.2 us (15%)
  local copies, waits for them, and re-layouts  19.3 us (12%)
  matrix products  12.3 us (8%)
  other arithmetic  4.46 us (3%)
    ppermute x8, waiting for transfers between devices, across(): return lax.ppermute(a, axis, swap(sizes[axis], bit))  39.8 us
    all_to_all x5, waiting for transfers between devices, spread(): return lax.all_to_all(a, split, split_axis=0, concat_axis=0, tiled=True)  31 us
    all_to_all x5, starting transfers between devices, spread(): return lax.all_to_all(a, split, split_axis=0, concat_axis=0, tiled=True)  21 us
    pallas_call x5, Pallas kernels, attend(): pl.pallas_call(functools.partial(attend_kernel, picks, len(arrays), sub,...  20.5 us
    dot_general x3, matrix products, project(): return jnp.dot(flat, rows, preferred_element_type=jnp.float32)  12.3 us
    unnamed x50, local copies, waits for them, and re-layouts  8.88 us
    ppermute x8, starting transfers between devices, across(): return lax.ppermute(a, axis, swap(sizes[axis], bit))  4.63 us
  transfers between devices with their start and end apart: 13, of which 10 were waited for; matrix products, arithmetic and copies ran while one was open for 9% of the time, Pallas kernels for 11%

profile of v2, /device:TPU:0, one launch (start us, length us, event | category | flops | bytes accessed | tf_op | source)
XLA Modules:
  0.0 156.1 jit_solution(17504541331050014816)
XLA Ops:
  0.0 1.0 slice.65
  2.2 4.1 %collective-permute-start = (bf16[8,2,128,128]{3,2,1,0:T(8,128)(2,1)S(1)}, bf16[8,2,128,128]{3,2,1,0:T(8,128)(2,1)S(1)}, u32[]{:S(2)}, u32[]{:S(2)}) collective-permute-start(bf16[8,2,128,128]{3,2,1,0:T(8,128)(2,1)S(1)} %pad_maximum_fusion.4), channel_id=1, source_target_pairs={{0,4},{4,0},{1,5},{5,1},{2,6},{6,2},{3,7},{7,3},{8,12},{12,8},{9,1... | collective-permute-start | bytes 1572872 | tf_op jit(solution)/shard_map/ppermute | solution.py:149
  10.3 4.9 %all-to-all-start = ((bf16[8,3,128,128]{3,2,1,0:T(8,128)(2,1)}), bf16[8,3,128,128]{3,2,1,0:T(8,128)(2,1)S(1)}, u32[]{:S(2)}, u32[]{:S(2)}) async-start(bf16[8,3,128,128]{3,2,1,0:T(8,128)(2,1)} %pad_maximum_fusion.2), calls=%async_computation | async-start | bytes 1572864 | tf_op jit(solution)/shard_map/all_to_all | solution.py:152
  15.2 14.3 %collective-permute-done = bf16[8,2,128,128]{3,2,1,0:T(8,128)(2,1)S(1)} collective-permute-done((bf16[8,2,128,128]{3,2,1,0:T(8,128)(2,1)S(1)}, bf16[8,2,128,128]{3,2,1,0:T(8,128)(2,1)S(1)}, u32[]{:S(2)}, u32[]{:S(2)}) %collective-permute-start) | collective-permute-done | bytes 524320 | tf_op jit(solution)/shard_map/ppermute | solution.py:149
  30.5 9.5 %all-to-all-done = bf16[8,3,128,128]{3,2,1,0:T(8,128)(2,1)S(1)} async-done(((bf16[8,3,128,128]{3,2,1,0:T(8,128)(2,1)}), bf16[8,3,128,128]{3,2,1,0:T(8,128)(2,1)S(1)}, u32[]{:S(2)}, u32[]{:S(2)}) %all-to-all-start) | async-done | bytes 786464 | tf_op jit(solution)/shard_map/all_to_all | solution.py:152
  41.8 4.2 %all-to-all-start.1 = ((bf16[8,3,128,128]{3,2,1,0:T(8,128)(2,1)}), bf16[8,3,128,128]{3,2,1,0:T(8,128)(2,1)}, u32[]{:S(2)}, u32[]{:S(2)}) async-start(bf16[8,3,128,128]{3,2,1,0:T(8,128)(2,1)} %pad_maximum_fusion.1), calls=%async_computation.1 | async-start | bytes 1572864 | tf_op jit(solution)/shard_map/all_to_all | solution.py:152
  46.1 14.0 %collective-permute-done.1.refs_2_ = bf16[8,2,128,128]{3,2,1,0:T(8,128)(2,1)S(1)} collective-permute-done((bf16[8,2,128,128]{3,2,1,0:T(8,128)(2,1)S(1)}, bf16[8,2,128,128]{3,2,1,0:T(8,128)(2,1)S(1)}, u32[]{:S(2)}, u32[]{:S(2)}) %collective-permute-start.1) | collective-permute-done | bytes 524320 | tf_op jit(solution)/shard_map/ppermute | solution.py:149
  60.9 8.4 %all-to-all-done.1 = bf16[8,3,128,128]{3,2,1,0:T(8,128)(2,1)} async-done(((bf16[8,3,128,128]{3,2,1,0:T(8,128)(2,1)}), bf16[8,3,128,128]{3,2,1,0:T(8,128)(2,1)}, u32[]{:S(2)}, u32[]{:S(2)}) %all-to-all-start.1) | async-done | bytes 786464 | tf_op jit(solution)/shard_map/all_to_all | solution.py:152
  69.4 1.1 slice.74.refs_2_
  70.6 1.2 pad_maximum_fusion.3
  71.8 1.2 pad_maximum_fusion
  74.8 1.0 copy-done.5
  75.9 3.5 %shard_map.140 = (f32[1024,128]{1,0:T(8,128)S(1)}, f32[1024,256]{1,0:T(8,128)S(1)}) custom-call(f32[2,4,4096]{2,1,0:T(4,128)S(1)} %shard_map.136.refs_0_, bf16[8,1,128,128]{3,2,1,0:T(8,128)(2,1)S(1)} %slice.79.refs_1_, bf16[8,2,128,128]{3,2,1,0:T(8,128)(2,1)S(1)} %slice.73.refs_2_, bf16[8,2,128,128]{3,2,1,0:T(8,128)(2,1)S(1)} %copy-done.5), custom_call_target="tpu_custom_call" | custom-call | flops 1024 | bytes 8192 | tf_op jit(solution)/shard_map/pallas_call | solution.py:115
  80.2 3.5 %shard_map.141 = bf16[8,128,128]{2,1,0:T(8,128)(2,1)S(1)} custom-call(f32[2,4,4096]{2,1,0:T(4,128)S(1)} %copy-done.9, bf16[8,1,128,128]{3,2,1,0:T(8,128)(2,1)S(1)} %slice.79.refs_1_, bf16[8,2,128,128]{3,2,1,0:T(8,128)(2,1)S(1)} %collective-permute-done.1.refs_2_, bf16[8,2,128,128]{3,2,1,0:T(8,128)(2,1)S(1)} %collective-permute-done.4.refs_3_, ...), custom_call_target="tpu_custom_call" | custom-call | flops 1024 | bytes 8192 | tf_op jit(solution)/shard_map/pallas_call | solution.py:115
  84.9 4.1 %all-to-all-start.2 = ((bf16[8,5,128,128]{3,2,1,0:T(8,128)(2,1)}), bf16[8,5,128,128]{3,2,1,0:T(8,128)(2,1)S(1)}, u32[]{:S(2)}, u32[]{:S(2)}) async-start(bf16[8,5,128,128]{3,2,1,0:T(8,128)(2,1)} %pad_maximum_fusion), calls=%async_computation.2 | async-start | bytes 2621440 | tf_op jit(solution)/shard_map/all_to_all | solution.py:152
  89.0 6.8 %collective-permute-done.2.refs_2_ = bf16[8,2,128,128]{3,2,1,0:T(8,128)(2,1)S(1)} collective-permute-done((bf16[8,2,128,128]{3,2,1,0:T(8,128)(2,1)S(1)}, bf16[8,2,128,128]{3,2,1,0:T(8,128)(2,1)S(1)}, u32[]{:S(2)}, u32[]{:S(2)}) %collective-permute-start.2) | collective-permute-done | bytes 524320 | tf_op jit(solution)/shard_map/ppermute | solution.py:149
  95.8 1.0 copy-done.13
  99.1 1.0 copy-done.7
  100.1 3.5 %shard_map.139 = (f32[1024,128]{1,0:T(8,128)S(1)}, f32[1024,256]{1,0:T(8,128)S(1)}) custom-call(f32[2,4,4096]{2,1,0:T(4,128)S(1)} %shard_map.137.refs_0_, bf16[8,1,128,128]{3,2,1,0:T(8,128)(2,1)S(1)} %slice.78.refs_1_, bf16[8,2,128,128]{3,2,1,0:T(8,128)(2,1)S(1)} %slice.74.refs_2_, bf16[8,2,128,128]{3,2,1,0:T(8,128)(2,1)S(1)} %copy-done.7), custom_call_target="tpu_custom_call" | custom-call | flops 1024 | bytes 8192 | tf_op jit(solution)/shard_map/pallas_call | solution.py:115
  104.4 6.0 %all-to-all-done.2.refs_2_ = bf16[8,5,128,128]{3,2,1,0:T(8,128)(2,1)S(1)} async-done(((bf16[8,5,128,128]{3,2,1,0:T(8,128)(2,1)}), bf16[8,5,128,128]{3,2,1,0:T(8,128)(2,1)S(1)}, u32[]{:S(2)}, u32[]{:S(2)}) %all-to-all-start.2) | async-done | bytes 1310752 | tf_op jit(solution)/shard_map/all_to_all | solution.py:152
  110.5 3.0 %collective-permute-done.6.refs_3_ = bf16[8,5,128,128]{3,2,1,0:T(8,128)(2,1)S(1)} collective-permute-done((bf16[8,5,128,128]{3,2,1,0:T(8,128)(2,1)S(1)}, bf16[8,5,128,128]{3,2,1,0:T(8,128)(2,1)S(1)}, u32[]{:S(2)}, u32[]{:S(2)}) %collective-permute-start.6) | collective-permute-done | bytes 1310752 | tf_op jit(solution)/shard_map/ppermute | solution.py:149
  114.4 5.8 %shard_map.142 = bf16[8,128,128]{2,1,0:T(8,128)(2,1)S(1)} custom-call(f32[2,4,4096]{2,1,0:T(4,128)S(1)} %copy-done.11, bf16[8,1,128,128]{3,2,1,0:T(8,128)(2,1)S(1)} %slice.80.refs_1_, bf16[8,5,128,128]{3,2,1,0:T(8,128)(2,1)S(1)} %all-to-all-done.2.refs_2_, bf16[8,5,128,128]{3,2,1,0:T(8,128)(2,1)S(1)} %collective-permute-done.6.refs_3_), custom_call_target="tpu_custom_call" | custom-call | flops 1024 | bytes 16384 | tf_op jit(solution)/shard_map/pallas_call | solution.py:115
  121.2 4.3 %all-to-all-start.3 = ((bf16[8,2,128,128]{3,2,1,0:T(8,128)(2,1)}), bf16[8,2,128,128]{3,2,1,0:T(8,128)(2,1)}, u32[]{:S(2)}, u32[]{:S(2)}) async-start(bf16[8,2,128,128]{3,2,1,0:T(8,128)(2,1)} %copy.51), calls=%async_computation.3 | async-start | bytes 1048576 | tf_op jit(solution)/shard_map/all_to_all | solution.py:152
  125.7 1.8 %collective-permute-done.7.refs_3_ = bf16[8,2,128,128]{3,2,1,0:T(8,128)(2,1)S(1)} collective-permute-done((bf16[8,2,128,128]{3,2,1,0:T(8,128)(2,1)S(1)}, bf16[8,2,128,128]{3,2,1,0:T(8,128)(2,1)S(1)}, u32[]{:S(2)}, u32[]{:S(2)}) %collective-permute-start.7) | collective-permute-done | bytes 524320 | tf_op jit(solution)/shard_map/ppermute | solution.py:149
  127.5 4.2 %shard_map.143 = bf16[8,128,128]{2,1,0:T(8,128)(2,1)} custom-call(f32[2,4,4096]{2,1,0:T(4,128)S(1)} %shard_map.137.refs_0_, bf16[8,1,128,128]{3,2,1,0:T(8,128)(2,1)S(1)} %slice.78.refs_1_, bf16[8,2,128,128]{3,2,1,0:T(8,128)(2,1)S(1)} %copy-done.1, bf16[8,2,128,128]{3,2,1,0:T(8,128)(2,1)S(1)} %collective-permute-done.7.refs_3_, f32[1024,128]{1,0:T(8,128)S(1)} %copy-done.3, ...), custom_call_target="tpu_custom_call" | custom-call | flops 1024 | bytes 8192 | tf_op jit(solution)/shard_map/pallas_call | solution.py:115
  131.7 4.0 %all-to-all-done.3 = bf16[8,2,128,128]{3,2,1,0:T(8,128)(2,1)} async-done(((bf16[8,2,128,128]{3,2,1,0:T(8,128)(2,1)}), bf16[8,2,128,128]{3,2,1,0:T(8,128)(2,1)}, u32[]{:S(2)}, u32[]{:S(2)}) %all-to-all-start.3) | async-done | bytes 524320 | tf_op jit(solution)/shard_map/all_to_all | solution.py:152
  135.7 1.3 copy.52
  137.0 3.4 %all-to-all-start.4 = ((bf16[8,128,128]{2,1,0:T(8,128)(2,1)}), bf16[8,128,128]{2,1,0:T(8,128)(2,1)S(1)}, u32[]{:S(2)}, u32[]{:S(2)}) async-start(bf16[8,128,128]{2,1,0:T(8,128)(2,1)} %shard_map.143), calls=%async_computation.4 | async-start | bytes 524288 | tf_op jit(solution)/shard_map/all_to_all | solution.py:152
  140.5 3.8 %fusion.2 = f32[128,3072]{1,0:T(8,128)S(1)} fusion(bf16[128,1024]{0,1:T(8,128)(2,1)S(1)} %bitcast.66, bf16[3072,3072]{1,0:T(8,128)(2,1)} %param.18), kind=kOutput, calls=%fused_computation.2 | convolution fusion | flops 805306368 | bytes 8126464 | tf_op jit(solution)/shard_map/dot_general | solution.py:212
  144.3 3.1 %all-to-all-done.4 = bf16[8,128,128]{2,1,0:T(8,128)(2,1)S(1)} async-done(((bf16[8,128,128]{2,1,0:T(8,128)(2,1)}), bf16[8,128,128]{2,1,0:T(8,128)(2,1)S(1)}, u32[]{:S(2)}, u32[]{:S(2)}) %all-to-all-start.4) | async-done | bytes 262176 | tf_op jit(solution)/shard_map/all_to_all | solution.py:152
  147.6 3.8 %fusion = f32[128,3072]{1,0:T(8,128)S(1)} fusion(bf16[128,1024]{0,1:T(8,128)(2,1)S(1)} %bitcast.63, bf16[3072,3072]{1,0:T(8,128)(2,1)} %param.18), kind=kOutput, calls=%fused_computation | convolution fusion | flops 805306368 | bytes 8126464 | tf_op jit(solution)/shard_map/dot_general | solution.py:212
  151.4 4.7 %fusion.12 = bf16[128,3072]{1,0:T(8,128)(2,1)} fusion(f32[128,3072]{1,0:T(8,128)S(1)} %fusion, f32[128,3072]{1,0:T(8,128)S(1)} %fusion.2, bf16[128,1024]{0,1:T(8,128)(2,1)S(1)} %bitcast.64, bf16[3072,3072]{1,0:T(8,128)(2,1)} %param.18), kind=kOutput, calls=%fused_computation.8 | convolution fusion | flops 806486016 | bytes 10485760 | tf_op jit(solution)/shard_map/dot_general | solution.py:212
  (80 shorter events, 18.0 us)
Async XLA Ops:
  0.0 6.3 %copy-start.19 = (bf16[128,24,128]{2,1,0:T(8,128)(2,1)S(1)}, bf16[128,24,128]{2,1,0:T(8,128)(2,1)}, u32[]{:S(2)}) copy-start(bf16[128,24,128]{2,1,0:T(8,128)(2,1)} %param.14) | copy-start | bytes 2359300
  2.2 5.1 %copy-start.17 = (bf16[128,24,128]{2,1,0:T(8,128)(2,1)S(1)}, bf16[128,24,128]{2,1,0:T(8,128)(2,1)}, u32[]{:S(2)}) copy-start(bf16[128,24,128]{2,1,0:T(8,128)(2,1)} %param.15) | copy-start | bytes 2359300
  2.2 27.4 %collective-permute-start = (bf16[8,2,128,128]{3,2,1,0:T(8,128)(2,1)S(1)}, bf16[8,2,128,128]{3,2,1,0:T(8,128)(2,1)S(1)}, u32[]{:S(2)}, u32[]{:S(2)}) collective-permute-start(bf16[8,2,128,128]{3,2,1,0:T(8,128)(2,1)S(1)} %pad_maximum_fusion.4), channel_id=1, source_target_pairs={{0,4},{4,0},{1,5},{5,1},{2,6},{6,2},{3,7},{7,3},{8,12},{12,8},{9,1... | collective-permute-start | bytes 1572872 | tf_op jit(solution)/shard_map/ppermute | solution.py:149
  7.2 1.1 copy-start.18
  9.3 5.8 %copy-start.22 = (s32[5]{0:T(128)S(1)}, s32[5]{0:T(128)}, u32[]{:S(2)}) copy-start(s32[5]{0:T(128)} %constant.35.clone) | copy-start | bytes 64
  9.3 20.2 %copy-start.12 = (s32[24,32,32]{2,1,0:T(8,128)S(1)}, s32[24,32,32]{2,1,0:T(8,128)}, u32[]{:S(2)}) copy-start(s32[24,32,32]{2,1,0:T(8,128)} %mask_ref.2) | copy-start | bytes 294916
  9.3 20.2 %copy-start.14 = (s32[8,1]{1,0:T(8,128)S(1)}, s32[8,1]{1,0:T(8,128)}, u32[]{:S(2)}) copy-start(s32[8,1]{1,0:T(8,128)} %constant.38.clone.rows_ref) | copy-start | bytes 100
  9.3 20.2 %copy-start.15 = (s32[1,1024]{1,0:T(1,128)S(1)}, s32[1,1024]{1,0:T(1,128)}, u32[]{:S(2)}) copy-start(s32[1,1024]{1,0:T(1,128)} %constant.39.clone.cols_ref) | copy-start | bytes 12292
  10.3 4.9 %copy-start.23 = (s32[5]{0:T(128)S(1)}, s32[5]{0:T(128)}, u32[]{:S(2)}) copy-start(s32[5]{0:T(128)} %constant.36.clone) | copy-start | bytes 64
  10.3 4.9 %copy-start.24 = (pred[5]{0:T(512)(128)(4,1)S(1)}, pred[5]{0:T(512)(128)(4,1)}, u32[]{:S(2)}) copy-start(pred[5]{0:T(512)(128)(4,1)} %constant.37.clone) | copy-start | bytes 19
  10.3 29.7 %all-to-all-start = ((bf16[8,3,128,128]{3,2,1,0:T(8,128)(2,1)}), bf16[8,3,128,128]{3,2,1,0:T(8,128)(2,1)S(1)}, u32[]{:S(2)}, u32[]{:S(2)}) async-start(bf16[8,3,128,128]{3,2,1,0:T(8,128)(2,1)} %pad_maximum_fusion.2), calls=%async_computation | async-start | bytes 1572864 | tf_op jit(solution)/shard_map/all_to_all | solution.py:152
  29.6 0.9 copy-start.20
  30.5 43.5 %copy-start.8 = (f32[2,4,4096]{2,1,0:T(4,128)}, f32[2,4,4096]{2,1,0:T(4,128)S(1)}, u32[]{:S(2)}) copy-start(f32[2,4,4096]{2,1,0:T(4,128)S(1)} %shard_map.136.refs_0_) | copy-start | bytes 393220
  40.0 20.0 %collective-permute-start.1 = (bf16[8,2,128,128]{3,2,1,0:T(8,128)(2,1)S(1)}, bf16[8,2,128,128]{3,2,1,0:T(8,128)(2,1)S(1)}, u32[]{:S(2)}, u32[]{:S(2)}) collective-permute-start(bf16[8,2,128,128]{3,2,1,0:T(8,128)(2,1)S(1)} %slice.73.refs_2_), channel_id=1, source_target_pairs={{0,4},{4,0},{1,5},{5,1},{2,6},{6,2},{3,7},{7,3},{8,12},{12,8},{9,1... | collective-permute-start | bytes 1572872 | tf_op jit(solution)/shard_map/ppermute | solution.py:149
  41.8 32.2 %collective-permute-start.5 = (bf16[8,2,128,128]{3,2,1,0:T(8,128)(2,1)S(1)}, bf16[8,2,128,128]{3,2,1,0:T(8,128)(2,1)S(1)}, u32[]{:S(2)}, u32[]{:S(2)}) collective-permute-start(bf16[8,2,128,128]{3,2,1,0:T(8,128)(2,1)S(1)} %slice.73.refs_2_), channel_id=1, source_target_pairs={{0,8},{8,0},{1,9},{9,1},{2,10},{10,2},{3,11},{11,3},{4,12},{12,4},... | collective-permute-start | bytes 1572872 | tf_op jit(solution)/shard_map/ppermute | solution.py:149
  41.8 27.6 %all-to-all-start.1 = ((bf16[8,3,128,128]{3,2,1,0:T(8,128)(2,1)}), bf16[8,3,128,128]{3,2,1,0:T(8,128)(2,1)}, u32[]{:S(2)}, u32[]{:S(2)}) async-start(bf16[8,3,128,128]{3,2,1,0:T(8,128)(2,1)} %pad_maximum_fusion.1), calls=%async_computation.1 | async-start | bytes 1572864 | tf_op jit(solution)/shard_map/all_to_all | solution.py:152
  60.0 19.3 %collective-permute-start.4 = (bf16[8,2,128,128]{3,2,1,0:T(8,128)(2,1)S(1)}, bf16[8,2,128,128]{3,2,1,0:T(8,128)(2,1)S(1)}, u32[]{:S(2)}, u32[]{:S(2)}) collective-permute-start(bf16[8,2,128,128]{3,2,1,0:T(8,128)(2,1)S(1)} %collective-permute-done.1.refs_2_), channel_id=1, source_target_pairs={{0,8},{8,0},{1,9},{9,1},{2,10},{10,2},{3,11},{11,3},{4,12},{12,4},... | collective-permute-start | bytes 1572872 | tf_op jit(solution)/shard_map/ppermute | solution.py:149
  69.4 2.4 %copy-start.21 = (bf16[8,2,128,128]{3,2,1,0:T(8,128)(2,1)S(1)}, bf16[8,2,128,128]{3,2,1,0:T(8,128)(2,1)}, u32[]{:S(2)}) copy-start(bf16[8,2,128,128]{3,2,1,0:T(8,128)(2,1)} %copy-done.20) | copy-start | bytes 1572868
  70.5 25.2 %collective-permute-start.2 = (bf16[8,2,128,128]{3,2,1,0:T(8,128)(2,1)S(1)}, bf16[8,2,128,128]{3,2,1,0:T(8,128)(2,1)S(1)}, u32[]{:S(2)}, u32[]{:S(2)}) collective-permute-start(bf16[8,2,128,128]{3,2,1,0:T(8,128)(2,1)S(1)} %slice.74.refs_2_), channel_id=1, source_target_pairs={{0,4},{4,0},{1,5},{5,1},{2,6},{6,2},{3,7},{7,3},{8,12},{12,8},{9,1... | collective-permute-start | bytes 1572872 | tf_op jit(solution)/shard_map/ppermute | solution.py:149
  74.8 1.0 copy-start.5
  79.3 0.9 copy-start.9
  83.8 14.5 %collective-permute-start.3 = (bf16[8,2,128,128]{3,2,1,0:T(8,128)(2,1)S(1)}, bf16[8,2,128,128]{3,2,1,0:T(8,128)(2,1)S(1)}, u32[]{:S(2)}, u32[]{:S(2)}) collective-permute-start(bf16[8,2,128,128]{3,2,1,0:T(8,128)(2,1)S(1)} %slice.74.refs_2_), channel_id=1, source_target_pairs={{0,8},{8,0},{1,9},{9,1},{2,10},{10,2},{3,11},{11,3},{4,12},{12,4},... | collective-permute-start | bytes 1572872 | tf_op jit(solution)/shard_map/ppermute | solution.py:149
  84.9 25.5 %all-to-all-start.2 = ((bf16[8,5,128,128]{3,2,1,0:T(8,128)(2,1)}), bf16[8,5,128,128]{3,2,1,0:T(8,128)(2,1)S(1)}, u32[]{:S(2)}, u32[]{:S(2)}) async-start(bf16[8,5,128,128]{3,2,1,0:T(8,128)(2,1)} %pad_maximum_fusion), calls=%async_computation.2 | async-start | bytes 2621440 | tf_op jit(solution)/shard_map/all_to_all | solution.py:152
  95.8 1.0 copy-start.13
  99.1 1.0 copy-start.7
  110.4 3.0 %collective-permute-start.6 = (bf16[8,5,128,128]{3,2,1,0:T(8,128)(2,1)S(1)}, bf16[8,5,128,128]{3,2,1,0:T(8,128)(2,1)S(1)}, u32[]{:S(2)}, u32[]{:S(2)}) collective-permute-start(bf16[8,5,128,128]{3,2,1,0:T(8,128)(2,1)S(1)} %all-to-all-done.2.refs_2_), channel_id=1, source_target_pairs={{0,8},{8,0},{1,9},{9,1},{2,10},{10,2},{3,11},{11,3},{4,12},{12,4},... | collective-permute-start | bytes 3932168 | tf_op jit(solution)/shard_map/ppermute | solution.py:149
  113.5 0.9 copy-start.11
  120.2 5.3 %copy-start.1 = (bf16[8,2,128,128]{3,2,1,0:T(8,128)(2,1)S(1)}, bf16[8,2,128,128]{3,2,1,0:T(8,128)(2,1)}, u32[]{:S(2)}) copy-start(bf16[8,2,128,128]{3,2,1,0:T(8,128)(2,1)} %copy-done) | copy-start | bytes 1572868
  120.2 7.2 %copy-start.3 = (f32[1024,128]{1,0:T(8,128)S(1)}, f32[1024,128]{1,0:T(8,128)}, u32[]{:S(2)}) copy-start(f32[1024,128]{1,0:T(8,128)} %copy-done.2) | copy-start | bytes 1572868
  121.2 14.5 %all-to-all-start.3 = ((bf16[8,2,128,128]{3,2,1,0:T(8,128)(2,1)}), bf16[8,2,128,128]{3,2,1,0:T(8,128)(2,1)}, u32[]{:S(2)}, u32[]{:S(2)}) async-start(bf16[8,2,128,128]{3,2,1,0:T(8,128)(2,1)} %copy.51), calls=%async_computation.3 | async-start | bytes 1048576 | tf_op jit(solution)/shard_map/all_to_all | solution.py:152
  125.5 2.0 %collective-permute-start.7 = (bf16[8,2,128,128]{3,2,1,0:T(8,128)(2,1)S(1)}, bf16[8,2,128,128]{3,2,1,0:T(8,128)(2,1)S(1)}, u32[]{:S(2)}, u32[]{:S(2)}) collective-permute-start(bf16[8,2,128,128]{3,2,1,0:T(8,128)(2,1)S(1)} %copy-done.1), channel_id=1, source_target_pairs={{0,8},{8,0},{1,9},{9,1},{2,10},{10,2},{3,11},{11,3},{4,12},{12,4},... | collective-permute-start | bytes 1572872 | tf_op jit(solution)/shard_map/ppermute | solution.py:149
  137.0 10.3 %all-to-all-start.4 = ((bf16[8,128,128]{2,1,0:T(8,128)(2,1)}), bf16[8,128,128]{2,1,0:T(8,128)(2,1)S(1)}, u32[]{:S(2)}, u32[]{:S(2)}) async-start(bf16[8,128,128]{2,1,0:T(8,128)(2,1)} %shard_map.143), calls=%async_computation.4 | async-start | bytes 524288 | tf_op jit(solution)/shard_map/all_to_all | solution.py:152
  (6 other events, 4.8 us)

commit v3 on v2

v3 whole, which is shorter than its diff:
```python
import functools
import math

import jax
import jax.numpy as jnp
import numpy as np
from jax import lax
from jax.experimental import pallas as pl
from jax.experimental.pallas import tpu as pltpu
from jax.sharding import Mesh
from jax.sharding import PartitionSpec as P

BLOCK = 128
NEG = -1e30
CORES = 2
PLANES = 4
AXES = ("x", "c", "zh", "zl", "y")
VMEM = pl.BlockSpec(memory_space=pltpu.VMEM)
SMEM = pl.BlockSpec(memory_space=pltpu.SMEM)


def swap(size, bit):
    return [(i, i ^ bit) for i in range(size)]


def after(value, *others):
    return lax.optimization_barrier((value, *others))[0]


def grant(*arrays):
    held = sum(math.prod(a.shape) * a.dtype.itemsize for a in arrays)
    return pltpu.CompilerParams(vmem_limit_bytes=10 * 2**20 + 2 * held)


def bias_kernel(sources, chunk, place_ref, mask_ref, rows_ref, cols_ref, bias_ref):
    tiles, qb, _ = bias_ref.shape
    blocks = mask_ref.shape[1]
    span = cols_ref.shape[1]
    mask = (mask_ref[chunk * tiles * qb + place_ref[sources]] > 0).astype(jnp.bfloat16)
    lanes = lax.broadcasted_iota(jnp.int32, (qb, blocks), 1)
    depth = lax.broadcasted_iota(jnp.int32, (blocks, span), 0)
    rows = []
    for tile in range(tiles):
        mine = (lanes == rows_ref[...] + place_ref[tile]).astype(jnp.bfloat16)
        rows.append(jnp.dot(mine, mask, preferred_element_type=jnp.float32).astype(jnp.bfloat16))
    for n in range(sources):
        pick = (depth == cols_ref[...] + place_ref[n]).astype(jnp.bfloat16)
        for tile in range(tiles):
            seen = jnp.dot(rows[tile], pick, preferred_element_type=jnp.float32)
            bias_ref[tile, :, n * span : (n + 1) * span] = jnp.where(seen > 0.5, 0.0, NEG)


def attend_kernel(picks, count, scale, first, last, place_ref, bias_ref, q_ref, *refs):
    kv_refs, rest = refs[:count], refs[count:]
    if not first:
        m_in, acc_in = rest[:2]
        rest = rest[2:]
    tiles, qb, _ = bias_ref.shape
    block, hdim = q_ref.shape[2:]
    rows = qb * block

    def tile(index, carry):
        q = q_ref[:, 3 * index].reshape(rows, hdim)
        if first:
            m = jnp.full((rows, 1), NEG, jnp.float32)
            acc = jnp.zeros((rows, 2 * hdim), jnp.float32)
        else:
            m = jnp.max(m_in[pl.ds(index * rows, rows), :], axis=1, keepdims=True)
            acc = acc_in[pl.ds(index * rows, rows), :]
        for which, kpart, vpart, source in picks:
            k = kv_refs[which][:, kpart].reshape(rows, hdim)
            v = kv_refs[which][:, vpart].reshape(rows, hdim)
            v = jnp.concatenate([v, jnp.ones((rows, hdim), v.dtype)], axis=1)
            s = lax.dot_general(q, k, (((1,), (1,)), ((), ())), preferred_element_type=jnp.float32)
            bias = bias_ref[index, :, source * rows : (source + 1) * rows]
            s = (s.reshape(qb, block, rows) * scale + bias[:, None, :]).reshape(rows, rows)
            m_next = jnp.maximum(m, jnp.max(s, axis=1, keepdims=True))
            p = jnp.exp2(s - m_next).astype(jnp.bfloat16)
            acc = acc * jnp.exp2(m - m_next) + jnp.dot(p, v, preferred_element_type=jnp.float32)
            m = m_next
        if last:
            out = (acc[:, :hdim] / acc[:, hdim:]).astype(jnp.bfloat16)
            for row in range(qb):
                rest[0][place_ref[index * qb + row]] = out[row * block : (row + 1) * block]
        else:
            rest[0][pl.ds(index * rows, rows), :] = jnp.broadcast_to(m, (rows, hdim))
            rest[1][pl.ds(index * rows, rows), :] = acc
        return carry

    lax.fori_loop(0, tiles, tile, 0)


def attend(place, bias, q, arrays, picks, state, last):
    tiles, qb, _ = bias.shape
    block, hdim = q.shape[2:]
    groups = tiles * qb
    total = groups * block
    first = state is None
    if last:
        out_shape = jax.ShapeDtypeStruct((groups, block, hdim), jnp.bfloat16)
        out_specs = VMEM
    else:
        out_shape = (
            jax.ShapeDtypeStruct((total, hdim), jnp.float32),
            jax.ShapeDtypeStruct((total, 2 * hdim), jnp.float32),
        )
        out_specs = (VMEM, VMEM)
    args = [place, bias, q, *arrays, *(() if first else state)]
    scale = hdim**-0.5 * math.log2(math.e)
    return pl.pallas_call(
        functools.partial(attend_kernel, picks, len(arrays), scale, first, last),
        out_shape=out_shape,
        in_specs=[SMEM] + [VMEM] * (len(args) - 1),
        out_specs=out_specs,
        compiler_params=grant(*args),
        cost_estimate=pl.CostEstimate(flops=total, bytes_accessed=4 * total, transcendentals=0),
    )(*args)


def shards(split, gather, queries, keys, values, block_mask, out_weight):
    sizes = {a: lax.axis_size(a) for a in AXES}
    stride = {a: math.prod(list(sizes.values())[i + 1 :]) for i, a in enumerate(AXES)}
    flat = tuple(a for a in split if a != "zl")
    n_split = math.prod(sizes[a] for a in split)
    n_flat = math.prod(sizes[a] for a in flat)
    tok, heads, hdim = queries.shape
    chunks = heads // n_split
    width = n_split * hdim
    here = lax.axis_index("zl")

    order = ("zl", "zh") + gather + ("c",)
    bits = [dict(zip(reversed(order), b)) for b in np.ndindex(*(sizes[a] for a in reversed(order)))]
    sources = len(bits)
    half = sources // 4
    place = sum(
        (lax.axis_index(a) ^ np.array([b[a] for b in bits] + [0], np.int32)) * stride[a] for a in order
    )
    place = jnp.where(np.arange(sources + 1) == sources, lax.axis_index(split), place).astype(jnp.int32)
    local = np.zeros(1, np.int32)
    for a in flat:
        local = (local[:, None] + np.arange(sizes[a], dtype=np.int32) * stride[a]).reshape(-1)
    spot = np.arange(n_split).reshape([sizes[a] for a in split])
    spot = np.moveaxis(spot, split.index("zl"), 0).reshape(2, n_flat).astype(np.int32)
    home = jnp.where(here == 0, spot, spot[::-1]).reshape(-1)

    def across(a, axis, bit):
        n = math.prod(sizes[x] for x in axis) if isinstance(axis, tuple) else sizes[axis]
        return lax.ppermute(a, axis, swap(n, bit))

    def spread(a, axes):
        return lax.all_to_all(a, axes, split_axis=0, concat_axis=0, tiled=True)

    def pieces(arrays, j, bit):
        out = []
        for a in arrays:
            a = jnp.transpose(a[:, j * n_split : (j + 1) * n_split], (1, 0, 2))
            a = a.reshape([sizes[x] for x in split] + [tok, hdim])
            a = lax.dynamic_index_in_dim(a, here ^ bit, split.index("zl"), keepdims=False)
            out.append(a.reshape(n_flat, tok, hdim))
        return jnp.stack(out, axis=1)

    def gathered(array, axes):
        arrays = [array]
        for a in axes:
            arrays = [p if bit == 0 else across(p, a, bit) for bit in range(sizes[a]) for p in arrays]
        return arrays

    out = jax.ShapeDtypeStruct((2, n_flat, sources * n_flat * BLOCK), jnp.float32)

    def bias_of(j, *before):
        return pl.pallas_call(
            functools.partial(bias_kernel, sources, j),
            out_shape=out,
            in_specs=[SMEM, VMEM, VMEM, VMEM],
            out_specs=VMEM,
            compiler_params=grant(out, block_mask),
            cost_estimate=pl.CostEstimate(flops=3 * 10**9 if j else 8 * 10**9, bytes_accessed=0, transcendentals=0),
        )(place, after(block_mask, *before), local[:, None], np.repeat(local, BLOCK)[None, :])

    far0 = [across(pieces((keys, values), 0, b), ("zh", "zl"), 2 + b) for b in range(2)]
    trio = (queries, keys, values)
    own = []
    for j in (1, 2, 0) if chunks == 3 else range(chunks):
        own.append((j, pieces(trio, j, 0), across(pieces(trio, j, 1), "zl", 1)))
    own = {j: jnp.concatenate([mine, got], axis=1) for j, mine, got in own}

    near_pick = tuple((i, 2 * r, 2 * r + 1, 4 * i + r) for i in range(half) for r in range(2))
    far_pick = tuple((i, 2 * r, 2 * r + 1, 4 * i + 2 + r) for i in range(half) for r in range(2))
    both_pick = tuple((i, 1 + 3 * r, 2 + 3 * r, 4 * i + r) for i in range(half) for r in range(2))
    both_pick += tuple((i, 6 + 2 * r, 7 + 2 * r, 4 * i + 2 + r) for i in range(half) for r in range(2))
    axes = gather + ("c",)
    outs = [None] * chunks
    waiting = []
    far, gate = far0, ()
    for j in range(1, chunks):
        got = spread(after(own[j], *gate), flat)
        bias = bias_of(j, far)
        got = after(got, bias)
        kv = jnp.concatenate([got[:, 1:3], got[:, 4:6]], axis=1)
        gate = (kv,)
        far = across(kv, "zh", 1)
        near = gathered(kv, axes)
        state = attend(home, bias, got, near, near_pick, None, False)
        waiting.append((bias, got, far, state))
    got = spread(after(jnp.concatenate([own[0], *far0], axis=1), kv), flat)
    for j, (bias, mine, far, state) in enumerate(waiting[:-1], 1):
        outs[j] = attend(home, bias, mine, gathered(far, axes), far_pick, state, True)
    bias, mine, far, state = waiting[-1]
    bias0 = bias_of(0, far)
    got = after(got, bias0, state, outs[-2])
    outs[0] = attend(home, bias0, got, gathered(got, axes), both_pick, None, True)
    ready = jnp.stack(outs[:-1], axis=1)
    early = spread(ready, split)
    far_all = gathered(far, axes)
    outs[-1] = attend(home, bias, mine, far_all, far_pick, after(state, ready), True)
    late = spread(after(outs[-1], early), split)

    def project(part, j):
        joined = jnp.transpose(part, (1, 0, 2)).reshape(tok, width)
        rows = out_weight[j * width : (j + 1) * width]
        return jnp.dot(joined, rows, preferred_element_type=jnp.float32)

    early = after(early, outs[-1])
    total = sum(project(early[:, j], j) for j in range(chunks - 1))
    return (total + project(late, chunks - 1)).astype(jnp.bfloat16)


def solution(mesh):
    n_head, n_blk = mesh.shape["head"], mesh.shape["blk"]
    x, y = n_head // CORES, n_blk // PLANES
    shape = (x, CORES, 2, PLANES // 2, y)
    wide = Mesh(np.asarray(mesh.devices).reshape(shape), AXES)
    split, gather = (("x", "zl", "y"), ()) if x * y * 2 <= 8 else (("x", "zl"), ("y",))
    spec = P(AXES, None, None)
    return jax.shard_map(
        functools.partial(shards, split, gather),
        mesh=wide,
        in_specs=(spec, spec, spec, P(), P()),
        out_specs=P(AXES, None),
        check_vma=False,
    )
```

time: 157 us -> 137 us (0.87)
  waiting for transfers between devices: 70.9 us -> 41.7 us
  Pallas kernels: 23.2 us -> 28.6 us
  starting transfers between devices: 25.6 us -> 30.8 us
  local copies, waits for them, and re-layouts: 19.3 us -> 15.6 us
  other arithmetic: 4.46 us -> 6.83 us
    all_to_all x5, waiting for transfers between devices: 31 us -> 11.8 us  [spread(): return lax.all_to_all(a, axes, split_axis=0, concat_axis=0, tiled=True)]
    ppermute x8 -> x12, waiting for transfers between devices: 39.8 us -> 29.9 us  [across(): return lax.ppermute(a, axis, swap(n, bit))]
    ppermute x8 -> x12, starting transfers between devices: 4.63 us -> 10.3 us  [across(): return lax.ppermute(a, axis, swap(n, bit))]
    pallas_call x5, Pallas kernels: 20.5 us -> 25.8 us  [attend(): pl.pallas_call(functools.partial(attend_kernel, picks, len(arrays), scale...]
    slice x7 -> x5, local copies, waits for them, and re-layouts: 5.14 us -> 1.62 us  [the longest x3 1.55 us: pieces(): a = jnp.transpose(a[:, j * n_split:(j + 1) * n_split], (1, 0, 2))]
    concatenate x1 -> x4, other arithmetic: 1.22 us -> 3.82 us  [the longest x2 2.93 us: shards(): own = {j: jnp.concatenate([mine, got], axis=1) for j, mine, got in own}]
    another operation x4 -> x0, local copies, waits for them, and re-layouts: 2.42 us -> none  [the longest x3 2.33 us: shards(): jnp.stack([chunk(a, j) for a in (queries1, keys1, values1)], axis=1)]
    dynamic_slice x0 -> x5, local copies, waits for them, and re-layouts: none -> 2.33 us  [pieces(): lax.dynamic_index_in_dim(a, here ^ bit, split.index('zl'), keepdims=False)]
  transfers between devices with their start and end apart: 13 -> 17, of which waited for: 10 -> 9; matrix products, arithmetic and copies ran while one was open for 9% -> 14% of each run, Pallas kernels for 11% -> 16%
where the time goes in v3:
time: 137 us; the launch traced here: 136 us
  waiting for transfers between devices  41.7 us (30%)
  starting transfers between devices  30.8 us (22%)
  Pallas kernels  28.6 us (21%)
  local copies, waits for them, and re-layouts  15.6 us (11%)
  matrix products  12.3 us (9%)
  other arithmetic  6.83 us (5%)
    ppermute x12, waiting for transfers between devices, across(): return lax.ppermute(a, axis, swap(n, bit))  29.9 us
    pallas_call x5, Pallas kernels, attend(): pl.pallas_call(functools.partial(attend_kernel, picks, len(arrays), scale...  25.8 us
    all_to_all x5, starting transfers between devices, spread(): return lax.all_to_all(a, axes, split_axis=0, concat_axis=0, tiled=True)  20.5 us
    dot_general x3, matrix products, project(): return jnp.dot(joined, rows, preferred_element_type=jnp.float32)  12.3 us
    all_to_all x5, waiting for transfers between devices, spread(): return lax.all_to_all(a, axes, split_axis=0, concat_axis=0, tiled=True)  11.8 us
    ppermute x12, starting transfers between devices, across(): return lax.ppermute(a, axis, swap(n, bit))  10.3 us
    unnamed x59, local copies, waits for them, and re-layouts  6.89 us
    concatenate x2, other arithmetic, shards(): own = {j: jnp.concatenate([mine, got], axis=1) for j, mine, got in own}  2.93 us
  transfers between devices with their start and end apart: 17, of which 9 were waited for; matrix products, arithmetic and copies ran while one was open for 14% of the time, Pallas kernels for 16%

profile of v3, /device:TPU:0, one launch (start us, length us, event | category | flops | bytes accessed | tf_op | source)
XLA Modules:
  0.0 136.5 jit_solution(7929618197256049482)
XLA Ops:
  0.0 1.3 fusion.18
  2.6 3.1 %collective-permute-start.1 = (bf16[4,3,128,128]{3,2,1,0:T(8,128)(2,1)S(1)}, bf16[4,3,128,128]{3,2,1,0:T(8,128)(2,1)S(1)}, u32[]{:S(2)}, u32[]{:S(2)}) collective-permute-start(bf16[4,3,128,128]{3,2,1,0:T(8,128)(2,1)S(1)} %pad_maximum_fusion.6), channel_id=1, source_target_pairs={{0,2},{2,0},{1,3},{3,1},{4,6},{6,4},{5,7},{7,5},{8,10},{10,8},{9,1... | collective-permute-start | bytes 1179656 | tf_op jit(solution)/shard_map/ppermute | solution.py:148
  6.2 2.7 %collective-permute-start.2 = (bf16[4,2,128,128]{3,2,1,0:T(8,128)(2,1)S(1)}, bf16[4,2,128,128]{3,2,1,0:T(8,128)(2,1)S(1)}, u32[]{:S(2)}, u32[]{:S(2)}) collective-permute-start(bf16[4,2,128,128]{3,2,1,0:T(8,128)(2,1)S(1)} %pad_maximum_fusion.8), channel_id=1, source_target_pairs={{0,4},{2,6},{4,0},{6,2},{1,5},{3,7},{5,1},{7,3},{8,12},{10,14},{12... | collective-permute-start | bytes 786440 | tf_op jit(solution)/shard_map/ppermute | solution.py:148
  11.0 9.4 %collective-permute-done.1 = bf16[4,3,128,128]{3,2,1,0:T(8,128)(2,1)S(1)} collective-permute-done((bf16[4,3,128,128]{3,2,1,0:T(8,128)(2,1)S(1)}, bf16[4,3,128,128]{3,2,1,0:T(8,128)(2,1)S(1)}, u32[]{:S(2)}, u32[]{:S(2)}) %collective-permute-start.1) | collective-permute-done | bytes 393248 | tf_op jit(solution)/shard_map/ppermute | solution.py:148
  20.5 1.0 pad_maximum_fusion.1
  21.5 4.0 %all-to-all-start = ((bf16[4,6,128,128]{3,2,1,0:T(8,128)(2,1)}), bf16[4,6,128,128]{3,2,1,0:T(8,128)(2,1)S(1)}, u32[]{:S(2)}, u32[]{:S(2)}) async-start(bf16[4,6,128,128]{3,2,1,0:T(8,128)(2,1)} %pad_maximum_fusion.1), calls=%async_computation | async-start | bytes 1572864 | tf_op jit(solution)/shard_map/all_to_all | solution.py:151
  26.4 2.1 %collective-permute-done.3 = bf16[4,2,128,128]{3,2,1,0:T(8,128)(2,1)} collective-permute-done((bf16[4,2,128,128]{3,2,1,0:T(8,128)(2,1)}, bf16[4,2,128,128]{3,2,1,0:T(8,128)(2,1)}, u32[]{:S(2)}, u32[]{:S(2)}) %collective-permute-start.3) | collective-permute-done | bytes 262176 | tf_op jit(solution)/shard_map/ppermute | solution.py:148
  29.5 6.2 %all-to-all-done.q_ref = bf16[4,6,128,128]{3,2,1,0:T(8,128)(2,1)S(1)} async-done(((bf16[4,6,128,128]{3,2,1,0:T(8,128)(2,1)}), bf16[4,6,128,128]{3,2,1,0:T(8,128)(2,1)S(1)}, u32[]{:S(2)}, u32[]{:S(2)}) %all-to-all-start) | async-done | bytes 786464 | tf_op jit(solution)/shard_map/all_to_all | solution.py:151
  35.8 1.4 %collective-permute-start.4 = (bf16[4,4,128,128]{3,2,1,0:T(8,128)(2,1)S(1)}, bf16[4,4,128,128]{3,2,1,0:T(8,128)(2,1)}, u32[]{:S(2)}, u32[]{:S(2)}) collective-permute-start(bf16[4,4,128,128]{3,2,1,0:T(8,128)(2,1)S(1)} %pad_maximum_fusion.2.refs_0_), channel_id=1, source_target_pairs={{0,4},{4,0},{1,5},{5,1},{2,6},{6,2},{3,7},{7,3},{8,12},{12,8},{9,1... | collective-permute-start | bytes 1572872 | tf_op jit(solution)/shard_map/ppermute | solution.py:148
  38.0 2.5 %collective-permute-start.6 = (bf16[4,3,128,128]{3,2,1,0:T(8,128)(2,1)}, bf16[4,3,128,128]{3,2,1,0:T(8,128)(2,1)}, u32[]{:S(2)}, u32[]{:S(2)}) collective-permute-start(bf16[4,3,128,128]{3,2,1,0:T(8,128)(2,1)} %pad_maximum_fusion.7), channel_id=1, source_target_pairs={{0,2},{2,0},{1,3},{3,1},{4,6},{6,4},{5,7},{7,5},{8,10},{10,8},{9,1... | collective-permute-start | bytes 1179656 | tf_op jit(solution)/shard_map/ppermute | solution.py:148
  40.6 2.0 %pad_maximum_fusion = bf16[4,6,128,128]{3,2,1,0:T(8,128)(2,1)} fusion(bf16[4,3,128,128]{3,2,1,0:T(8,128)(2,1)} %collective-permute-done, bf16[4,1,128,128]{3,2,1,0:T(8,128)(2,1)S(1)} %bitcast.88, bf16[4,1,128,128]{3,2,1,0:T(8,128)(2,1)S(1)} %bitcast.86, bf16[4,1,128,128]{3,2,1,0:T(8,128)(2,1)S(1)} %bitcast.90), kind=kLoop, calls=%fused_computation.9 | loop fusion | flops 1179648 | bytes 1572864 | tf_op jit(solution)/shard_map/concatenate | solution.py:185
  42.6 3.5 %all-to-all-start.1 = ((bf16[4,6,128,128]{3,2,1,0:T(8,128)(2,1)}), bf16[4,6,128,128]{3,2,1,0:T(8,128)(2,1)S(1)}, u32[]{:S(2)}, u32[]{:S(2)}) async-start(bf16[4,6,128,128]{3,2,1,0:T(8,128)(2,1)} %pad_maximum_fusion), calls=%async_computation.1 | async-start | bytes 1572864 | tf_op jit(solution)/shard_map/all_to_all | solution.py:151
  48.1 12.4 %collective-permute-done.4.refs_0_ = bf16[4,4,128,128]{3,2,1,0:T(8,128)(2,1)} collective-permute-done((bf16[4,4,128,128]{3,2,1,0:T(8,128)(2,1)S(1)}, bf16[4,4,128,128]{3,2,1,0:T(8,128)(2,1)}, u32[]{:S(2)}, u32[]{:S(2)}) %collective-permute-start.4) | collective-permute-done | bytes 524320 | tf_op jit(solution)/shard_map/ppermute | solution.py:148
  63.5 1.8 %constant_dynamic-update-slice_fusion.2 = bf16[4,10,128,128]{3,2,1,0:T(8,128)(2,1)} fusion(bf16[4,10,128,128]{3,2,1,0:T(8,128)(2,1)} %constant_dynamic-update-slice_fusion.3, bf16[4,3,128,128]{3,2,1,0:T(8,128)(2,1)} %collective-permute-done.6), kind=kLoop, calls=%fused_computation.21 | loop fusion | bytes 786432
  66.1 1.7 %constant_dynamic-update-slice_fusion = bf16[4,10,128,128]{3,2,1,0:T(8,128)(2,1)} fusion(bf16[4,10,128,128]{3,2,1,0:T(8,128)(2,1)} %constant_dynamic-update-slice_fusion.1, bf16[4,2,128,128]{3,2,1,0:T(8,128)(2,1)} %collective-permute-done.3), kind=kLoop, calls=%fused_computation.19 | loop fusion | bytes 524288 | tf_op jit(solution)/shard_map/concatenate | solution.py:205
  67.8 3.7 %all-to-all-start.2 = ((bf16[4,10,128,128]{3,2,1,0:T(8,128)(2,1)}), bf16[4,10,128,128]{3,2,1,0:T(8,128)(2,1)S(1)}, u32[]{:S(2)}, u32[]{:S(2)}) async-start(bf16[4,10,128,128]{3,2,1,0:T(8,128)(2,1)} %constant_dynamic-update-slice_fusion), calls=%async_computation.2 | async-start | bytes 2621440 | tf_op jit(solution)/shard_map/all_to_all | solution.py:151
  72.9 4.5 %shard_map.167 = (f32[1024,128]{1,0:T(8,128)S(1)}, f32[1024,256]{1,0:T(8,128)S(1)}) custom-call(s32[8]{0:T(128)S(1)} %reshape.70.place_ref, f32[2,4,4096]{2,1,0:T(4,128)S(1)} %shard_map.163.bias_ref, bf16[4,6,128,128]{3,2,1,0:T(8,128)(2,1)S(1)} %all-to-all-done.q_ref, bf16[4,4,128,128]{3,2,1,0:T(8,128)(2,1)S(1)} %pad_maximum_fusion.2.refs_0_, ...), custom_call_target="tpu_custom_call" | custom-call | flops 1024 | bytes 4096 | tf_op jit(solution)/shard_map/pallas_call | solution.py:110
  77.4 4.8 %shard_map.168 = bf16[8,128,128]{2,1,0:T(8,128)(2,1)S(1)} custom-call(s32[8]{0:T(128)S(1)} %reshape.70.place_ref, f32[2,4,4096]{2,1,0:T(4,128)S(1)} %shard_map.163.bias_ref, bf16[4,6,128,128]{3,2,1,0:T(8,128)(2,1)S(1)} %all-to-all-done.q_ref, bf16[4,4,128,128]{3,2,1,0:T(8,128)(2,1)} %collective-permute-done.4.refs_0_, ...), custom_call_target="tpu_custom_call" | custom-call | flops 1024 | bytes 4096 | tf_op jit(solution)/shard_map/pallas_call | solution.py:110
  82.3 4.7 %shard_map.166 = (f32[1024,128]{1,0:T(8,128)S(1)}, f32[1024,256]{1,0:T(8,128)S(1)}) custom-call(s32[8]{0:T(128)S(1)} %reshape.70.place_ref, f32[2,4,4096]{2,1,0:T(4,128)S(1)} %copy-done.3, bf16[4,6,128,128]{3,2,1,0:T(8,128)(2,1)S(1)} %all-to-all-done.1.q_ref, bf16[4,4,128,128]{3,2,1,0:T(8,128)(2,1)} %pad_maximum_fusion.3.refs_0_, ...), custom_call_target="tpu_custom_call" | custom-call | flops 1024 | bytes 4096 | tf_op jit(solution)/shard_map/pallas_call | solution.py:110
  87.0 1.0 copy-done
  89.9 3.0 %collective-permute-done.10.refs_1_ = bf16[4,10,128,128]{3,2,1,0:T(8,128)(2,1)S(1)} collective-permute-done((bf16[4,10,128,128]{3,2,1,0:T(8,128)(2,1)S(1)}, bf16[4,10,128,128]{3,2,1,0:T(8,128)(2,1)S(1)}, u32[]{:S(2)}, u32[]{:S(2)}) %collective-permute-start.10) | collective-permute-done | bytes 1310752 | tf_op jit(solution)/shard_map/ppermute | solution.py:148
  92.9 6.4 %shard_map.169 = bf16[8,128,128]{2,1,0:T(8,128)(2,1)S(1)} custom-call(s32[8]{0:T(128)S(1)} %reshape.70.place_ref, f32[2,4,4096]{2,1,0:T(4,128)S(1)} %shard_map.165.bias_ref, bf16[4,10,128,128]{3,2,1,0:T(8,128)(2,1)S(1)} %all-to-all-done.2.q_ref.refs_0_, bf16[4,10,128,128]{3,2,1,0:T(8,128)(2,1)S(1)} %all-to-all-done.2.q_ref.refs_0_, ...), custom_call_target="tpu_custom_call" | custom-call | flops 1024 | bytes 4096 | tf_op jit(solution)/shard_map/pallas_call | solution.py:110
  100.3 5.6 %all-to-all-start.3 = ((bf16[8,2,128,128]{3,2,1,0:T(8,128)(2,1)}), bf16[8,2,128,128]{3,2,1,0:T(8,128)(2,1)}, u32[]{:S(2)}, u32[]{:S(2)}) async-start(bf16[8,2,128,128]{3,2,1,0:T(8,128)(2,1)} %copy.75), calls=%async_computation.3 | async-start | bytes 1048576 | tf_op jit(solution)/shard_map/all_to_all | solution.py:151
  105.9 2.1 %collective-permute-done.11.refs_1_ = bf16[4,4,128,128]{3,2,1,0:T(8,128)(2,1)S(1)} collective-permute-done((bf16[4,4,128,128]{3,2,1,0:T(8,128)(2,1)}, bf16[4,4,128,128]{3,2,1,0:T(8,128)(2,1)S(1)}, u32[]{:S(2)}, u32[]{:S(2)}) %collective-permute-start.11) | collective-permute-done | bytes 524320 | tf_op jit(solution)/shard_map/ppermute | solution.py:148
  108.0 5.3 %shard_map.170 = bf16[8,128,128]{2,1,0:T(8,128)(2,1)} custom-call(s32[8]{0:T(128)S(1)} %reshape.70.place_ref, f32[2,4,4096]{2,1,0:T(4,128)S(1)} %copy-done.3, bf16[4,6,128,128]{3,2,1,0:T(8,128)(2,1)S(1)} %all-to-all-done.1.q_ref, bf16[4,4,128,128]{3,2,1,0:T(8,128)(2,1)} %collective-permute-done.5.refs_0_, ...), custom_call_target="tpu_custom_call" | custom-call | flops 1024 | bytes 4096 | tf_op jit(solution)/shard_map/pallas_call | solution.py:110
  113.3 2.7 %all-to-all-done.3 = bf16[8,2,128,128]{3,2,1,0:T(8,128)(2,1)} async-done(((bf16[8,2,128,128]{3,2,1,0:T(8,128)(2,1)}), bf16[8,2,128,128]{3,2,1,0:T(8,128)(2,1)}, u32[]{:S(2)}, u32[]{:S(2)}) %all-to-all-start.3) | async-done | bytes 524320 | tf_op jit(solution)/shard_map/all_to_all | solution.py:151
  116.1 1.3 copy.76
  117.4 3.6 %all-to-all-start.4 = ((bf16[8,128,128]{2,1,0:T(8,128)(2,1)}), bf16[8,128,128]{2,1,0:T(8,128)(2,1)S(1)}, u32[]{:S(2)}, u32[]{:S(2)}) async-start(bf16[8,128,128]{2,1,0:T(8,128)(2,1)} %shard_map.170), calls=%async_computation.4 | async-start | bytes 524288 | tf_op jit(solution)/shard_map/all_to_all | solution.py:151
  121.1 3.8 %fusion.2 = f32[128,3072]{1,0:T(8,128)S(1)} fusion(bf16[128,1024]{0,1:T(8,128)(2,1)S(1)} %bitcast.83, bf16[3072,3072]{1,0:T(8,128)(2,1)} %param.21), kind=kOutput, calls=%fused_computation.2 | convolution fusion | flops 805306368 | bytes 8126464 | tf_op jit(solution)/shard_map/dot_general | solution.py:221
  124.9 2.9 %all-to-all-done.4 = bf16[8,128,128]{2,1,0:T(8,128)(2,1)S(1)} async-done(((bf16[8,128,128]{2,1,0:T(8,128)(2,1)}), bf16[8,128,128]{2,1,0:T(8,128)(2,1)S(1)}, u32[]{:S(2)}, u32[]{:S(2)}) %all-to-all-start.4) | async-done | bytes 262176 | tf_op jit(solution)/shard_map/all_to_all | solution.py:151
  128.0 3.8 %fusion = f32[128,3072]{1,0:T(8,128)S(1)} fusion(bf16[128,1024]{0,1:T(8,128)(2,1)S(1)} %bitcast.72, bf16[3072,3072]{1,0:T(8,128)(2,1)} %param.21), kind=kOutput, calls=%fused_computation | convolution fusion | flops 805306368 | bytes 8126464 | tf_op jit(solution)/shard_map/dot_general | solution.py:221
  131.8 4.7 %fusion.12 = bf16[128,3072]{1,0:T(8,128)(2,1)} fusion(f32[128,3072]{1,0:T(8,128)S(1)} %fusion, f32[128,3072]{1,0:T(8,128)S(1)} %fusion.2, bf16[128,1024]{0,1:T(8,128)(2,1)S(1)} %bitcast.80, bf16[3072,3072]{1,0:T(8,128)(2,1)} %param.21), kind=kOutput, calls=%fused_computation.8 | convolution fusion | flops 806486016 | bytes 10485760 | tf_op jit(solution)/shard_map/dot_general | solution.py:221
  (100 shorter events, 16.7 us)
Async XLA Ops:
  0.0 1.6 %copy-start.9 = (bf16[128,24,128]{2,1,0:T(8,128)(2,1)S(1)}, bf16[128,24,128]{2,1,0:T(8,128)(2,1)}, u32[]{:S(2)}) copy-start(bf16[128,24,128]{2,1,0:T(8,128)(2,1)} %param.17) | copy-start | bytes 2359300
  2.6 17.8 %collective-permute-start.1 = (bf16[4,3,128,128]{3,2,1,0:T(8,128)(2,1)S(1)}, bf16[4,3,128,128]{3,2,1,0:T(8,128)(2,1)S(1)}, u32[]{:S(2)}, u32[]{:S(2)}) collective-permute-start(bf16[4,3,128,128]{3,2,1,0:T(8,128)(2,1)S(1)} %pad_maximum_fusion.6), channel_id=1, source_target_pairs={{0,2},{2,0},{1,3},{3,1},{4,6},{6,4},{5,7},{7,5},{8,10},{10,8},{9,1... | collective-permute-start | bytes 1179656 | tf_op jit(solution)/shard_map/ppermute | solution.py:148
  6.2 20.2 %collective-permute-start.2 = (bf16[4,2,128,128]{3,2,1,0:T(8,128)(2,1)S(1)}, bf16[4,2,128,128]{3,2,1,0:T(8,128)(2,1)S(1)}, u32[]{:S(2)}, u32[]{:S(2)}) collective-permute-start(bf16[4,2,128,128]{3,2,1,0:T(8,128)(2,1)S(1)} %pad_maximum_fusion.8), channel_id=1, source_target_pairs={{0,4},{2,6},{4,0},{6,2},{1,5},{3,7},{5,1},{7,3},{8,12},{10,14},{12... | collective-permute-start | bytes 786440 | tf_op jit(solution)/shard_map/ppermute | solution.py:148
  9.6 18.9 %collective-permute-start.3 = (bf16[4,2,128,128]{3,2,1,0:T(8,128)(2,1)}, bf16[4,2,128,128]{3,2,1,0:T(8,128)(2,1)}, u32[]{:S(2)}, u32[]{:S(2)}) collective-permute-start(bf16[4,2,128,128]{3,2,1,0:T(8,128)(2,1)} %pad_maximum_fusion.9), channel_id=1, source_target_pairs={{0,6},{2,4},{4,2},{6,0},{1,7},{3,5},{5,3},{7,1},{8,14},{10,12},{12... | collective-permute-start | bytes 786440 | tf_op jit(solution)/shard_map/ppermute | solution.py:148
  21.4 4.9 %copy-start.14 = (s32[9]{0:T(128)S(1)}, s32[9]{0:T(128)}, u32[]{:S(2)}) copy-start(s32[9]{0:T(128)} %constant.92.clone) | copy-start | bytes 112
  21.4 4.9 %copy-start.15 = (s32[9]{0:T(128)S(1)}, s32[9]{0:T(128)}, u32[]{:S(2)}) copy-start(s32[9]{0:T(128)} %constant.93.clone) | copy-start | bytes 112
  21.4 4.9 %copy-start.16 = (s32[9]{0:T(128)S(1)}, s32[9]{0:T(128)}, u32[]{:S(2)}) copy-start(s32[9]{0:T(128)} %constant.94.clone) | copy-start | bytes 112
  21.4 4.9 %copy-start.17 = (pred[9]{0:T(512)(128)(4,1)S(1)}, pred[9]{0:T(512)(128)(4,1)}, u32[]{:S(2)}) copy-start(pred[9]{0:T(512)(128)(4,1)} %constant.95.clone) | copy-start | bytes 31
  21.4 7.1 %copy-start.4 = (s32[24,32,32]{2,1,0:T(8,128)S(1)}, s32[24,32,32]{2,1,0:T(8,128)}, u32[]{:S(2)}) copy-start(s32[24,32,32]{2,1,0:T(8,128)} %mask_ref.2) | copy-start | bytes 294916
  21.5 7.1 %copy-start.6 = (s32[4,1]{1,0:T(4,128)S(1)}, s32[4,1]{1,0:T(4,128)}, u32[]{:S(2)}) copy-start(s32[4,1]{1,0:T(4,128)} %constant.98.clone.rows_ref) | copy-start | bytes 52
  21.5 7.1 %copy-start.7 = (s32[1,512]{1,0:T(1,128)S(1)}, s32[1,512]{1,0:T(1,128)}, u32[]{:S(2)}) copy-start(s32[1,512]{1,0:T(1,128)} %constant.99.clone.cols_ref) | copy-start | bytes 6148
  21.5 14.2 %all-to-all-start = ((bf16[4,6,128,128]{3,2,1,0:T(8,128)(2,1)}), bf16[4,6,128,128]{3,2,1,0:T(8,128)(2,1)S(1)}, u32[]{:S(2)}, u32[]{:S(2)}) async-start(bf16[4,6,128,128]{3,2,1,0:T(8,128)(2,1)} %pad_maximum_fusion.1), calls=%async_computation | async-start | bytes 1572864 | tf_op jit(solution)/shard_map/all_to_all | solution.py:151
  26.3 14.3 %collective-permute-start = (bf16[4,3,128,128]{3,2,1,0:T(8,128)(2,1)}, bf16[4,3,128,128]{3,2,1,0:T(8,128)(2,1)}, u32[]{:S(2)}, u32[]{:S(2)}) collective-permute-start(bf16[4,3,128,128]{3,2,1,0:T(8,128)(2,1)} %pad_maximum_fusion.5), channel_id=1, source_target_pairs={{0,2},{2,0},{1,3},{3,1},{4,6},{6,4},{5,7},{7,5},{8,10},{10,8},{9,1... | collective-permute-start | bytes 1179656 | tf_op jit(solution)/shard_map/ppermute | solution.py:148
  26.4 3.1 %copy-start.11 = (bf16[4,2,128,128]{3,2,1,0:T(8,128)(2,1)}, bf16[4,2,128,128]{3,2,1,0:T(8,128)(2,1)S(1)}, u32[]{:S(2)}) copy-start(bf16[4,2,128,128]{3,2,1,0:T(8,128)(2,1)S(1)} %collective-permute-done.2) | copy-start | bytes 786436
  35.7 4.9 %copy-start.10 = (bf16[2,1,2,128,128]{4,2,1,0,3:T(2,128)(2,1)S(1)}, bf16[2,1,2,128,128]{4,2,1,0,3:T(2,128)(2,1)}, u32[]{:S(2)}) copy-start(bf16[2,1,2,128,128]{4,2,1,0,3:T(2,128)(2,1)} %get-tuple-element.54) | copy-start | bytes 393220
  35.8 24.8 %collective-permute-start.4 = (bf16[4,4,128,128]{3,2,1,0:T(8,128)(2,1)S(1)}, bf16[4,4,128,128]{3,2,1,0:T(8,128)(2,1)}, u32[]{:S(2)}, u32[]{:S(2)}) collective-permute-start(bf16[4,4,128,128]{3,2,1,0:T(8,128)(2,1)S(1)} %pad_maximum_fusion.2.refs_0_), channel_id=1, source_target_pairs={{0,4},{4,0},{1,5},{5,1},{2,6},{6,2},{3,7},{7,3},{8,12},{12,8},{9,1... | collective-permute-start | bytes 1572872 | tf_op jit(solution)/shard_map/ppermute | solution.py:148
  38.0 25.5 %collective-permute-start.6 = (bf16[4,3,128,128]{3,2,1,0:T(8,128)(2,1)}, bf16[4,3,128,128]{3,2,1,0:T(8,128)(2,1)}, u32[]{:S(2)}, u32[]{:S(2)}) collective-permute-start(bf16[4,3,128,128]{3,2,1,0:T(8,128)(2,1)} %pad_maximum_fusion.7), channel_id=1, source_target_pairs={{0,2},{2,0},{1,3},{3,1},{4,6},{6,4},{5,7},{7,5},{8,10},{10,8},{9,1... | collective-permute-start | bytes 1179656 | tf_op jit(solution)/shard_map/ppermute | solution.py:148
  42.6 19.6 %all-to-all-start.1 = ((bf16[4,6,128,128]{3,2,1,0:T(8,128)(2,1)}), bf16[4,6,128,128]{3,2,1,0:T(8,128)(2,1)S(1)}, u32[]{:S(2)}, u32[]{:S(2)}) async-start(bf16[4,6,128,128]{3,2,1,0:T(8,128)(2,1)} %pad_maximum_fusion), calls=%async_computation.1 | async-start | bytes 1572864 | tf_op jit(solution)/shard_map/all_to_all | solution.py:151
  48.1 24.7 %collective-permute-start.9 = (bf16[4,4,128,128]{3,2,1,0:T(8,128)(2,1)S(1)}, bf16[4,4,128,128]{3,2,1,0:T(8,128)(2,1)}, u32[]{:S(2)}, u32[]{:S(2)}) collective-permute-start(bf16[4,4,128,128]{3,2,1,0:T(8,128)(2,1)S(1)} %pad_maximum_fusion.2.refs_0_), channel_id=1, source_target_pairs={{0,8},{8,0},{1,9},{9,1},{2,10},{10,2},{3,11},{11,3},{4,12},{12,4},... | collective-permute-start | bytes 1572872 | tf_op jit(solution)/shard_map/ppermute | solution.py:148
  62.1 3.2 %copy-start.12 = (bf16[4,2,128,128]{3,2,1,0:T(8,128)(2,1)S(1)}, bf16[4,2,128,128]{3,2,1,0:T(8,128)(2,1)}, u32[]{:S(2)}) copy-start(bf16[4,2,128,128]{3,2,1,0:T(8,128)(2,1)} %copy-done.11) | copy-start | bytes 786436
  62.1 15.2 %collective-permute-start.8 = (bf16[4,4,128,128]{3,2,1,0:T(8,128)(2,1)}, bf16[4,4,128,128]{3,2,1,0:T(8,128)(2,1)}, u32[]{:S(2)}, u32[]{:S(2)}) collective-permute-start(bf16[4,4,128,128]{3,2,1,0:T(8,128)(2,1)} %collective-permute-done.4.refs_0_), channel_id=1, source_target_pairs={{0,8},{8,0},{1,9},{9,1},{2,10},{10,2},{3,11},{11,3},{4,12},{12,4},... | collective-permute-start | bytes 1572872 | tf_op jit(solution)/shard_map/ppermute | solution.py:148
  63.0 19.2 %collective-permute-start.7 = (bf16[4,4,128,128]{3,2,1,0:T(8,128)(2,1)}, bf16[4,4,128,128]{3,2,1,0:T(8,128)(2,1)}, u32[]{:S(2)}, u32[]{:S(2)}) collective-permute-start(bf16[4,4,128,128]{3,2,1,0:T(8,128)(2,1)} %pad_maximum_fusion.3.refs_0_), channel_id=1, source_target_pairs={{0,8},{8,0},{1,9},{9,1},{2,10},{10,2},{3,11},{11,3},{4,12},{12,4},... | collective-permute-start | bytes 1572872 | tf_op jit(solution)/shard_map/ppermute | solution.py:148
  63.5 25.3 %collective-permute-start.5 = (bf16[4,4,128,128]{3,2,1,0:T(8,128)(2,1)}, bf16[4,4,128,128]{3,2,1,0:T(8,128)(2,1)}, u32[]{:S(2)}, u32[]{:S(2)}) collective-permute-start(bf16[4,4,128,128]{3,2,1,0:T(8,128)(2,1)} %pad_maximum_fusion.3.refs_0_), channel_id=1, source_target_pairs={{0,4},{4,0},{1,5},{5,1},{2,6},{6,2},{3,7},{7,3},{8,12},{12,8},{9,1... | collective-permute-start | bytes 1572872 | tf_op jit(solution)/shard_map/ppermute | solution.py:148
  66.1 5.5 %copy-start.13 = (s32[2,4]{1,0:T(2,128)S(1)}, s32[2,4]{1,0:T(2,128)}, u32[]{:S(2)}) copy-start(s32[2,4]{1,0:T(2,128)} %constant.96.clone) | copy-start | bytes 100
  67.8 21.9 %all-to-all-start.2 = ((bf16[4,10,128,128]{3,2,1,0:T(8,128)(2,1)}), bf16[4,10,128,128]{3,2,1,0:T(8,128)(2,1)S(1)}, u32[]{:S(2)}, u32[]{:S(2)}) async-start(bf16[4,10,128,128]{3,2,1,0:T(8,128)(2,1)} %constant_dynamic-update-slice_fusion), calls=%async_computation.2 | async-start | bytes 2621440 | tf_op jit(solution)/shard_map/all_to_all | solution.py:151
  77.4 4.9 %copy-start.3 = (f32[2,4,4096]{2,1,0:T(4,128)S(1)}, f32[2,4,4096]{2,1,0:T(4,128)}, u32[]{:S(2)}) copy-start(f32[2,4,4096]{2,1,0:T(4,128)} %copy-done.2) | copy-start | bytes 393220
  82.2 6.6 %copy-start.5 = (s32[24,32,32]{2,1,0:T(8,128)S(1)}, s32[24,32,32]{2,1,0:T(8,128)}, u32[]{:S(2)}) copy-start(s32[24,32,32]{2,1,0:T(8,128)} %mask_ref.2) | copy-start | bytes 294916
  89.8 3.1 %collective-permute-start.10 = (bf16[4,10,128,128]{3,2,1,0:T(8,128)(2,1)S(1)}, bf16[4,10,128,128]{3,2,1,0:T(8,128)(2,1)S(1)}, u32[]{:S(2)}, u32[]{:S(2)}) collective-permute-start(bf16[4,10,128,128]{3,2,1,0:T(8,128)(2,1)S(1)} %all-to-all-done.2.q_ref.refs_0_), channel_id=1, source_target_pairs={{0,8},{8,0},{1,9},{9,1},{2,10},{10,2},{3,11},{11,3},{4,12},{12,4},... | collective-permute-start | bytes 3932168 | tf_op jit(solution)/shard_map/ppermute | solution.py:148
  99.4 8.6 %copy-start.1 = (f32[1024,256]{1,0:T(8,128)S(1)}, f32[1024,256]{1,0:T(8,128)}, u32[]{:S(2)}) copy-start(f32[1024,256]{1,0:T(8,128)} %copy-done) | copy-start | bytes 3145732
  100.3 15.8 %all-to-all-start.3 = ((bf16[8,2,128,128]{3,2,1,0:T(8,128)(2,1)}), bf16[8,2,128,128]{3,2,1,0:T(8,128)(2,1)}, u32[]{:S(2)}, u32[]{:S(2)}) async-start(bf16[8,2,128,128]{3,2,1,0:T(8,128)(2,1)} %copy.75), calls=%async_computation.3 | async-start | bytes 1048576 | tf_op jit(solution)/shard_map/all_to_all | solution.py:151
  105.9 2.1 %collective-permute-start.11 = (bf16[4,4,128,128]{3,2,1,0:T(8,128)(2,1)}, bf16[4,4,128,128]{3,2,1,0:T(8,128)(2,1)S(1)}, u32[]{:S(2)}, u32[]{:S(2)}) collective-permute-start(bf16[4,4,128,128]{3,2,1,0:T(8,128)(2,1)} %collective-permute-done.5.refs_0_), channel_id=1, source_target_pairs={{0,8},{8,0},{1,9},{9,1},{2,10},{10,2},{3,11},{11,3},{4,12},{12,4},... | collective-permute-start | bytes 1572872 | tf_op jit(solution)/shard_map/ppermute | solution.py:148
  117.4 10.3 %all-to-all-start.4 = ((bf16[8,128,128]{2,1,0:T(8,128)(2,1)}), bf16[8,128,128]{2,1,0:T(8,128)(2,1)S(1)}, u32[]{:S(2)}, u32[]{:S(2)}) async-start(bf16[8,128,128]{2,1,0:T(8,128)(2,1)} %shard_map.170), calls=%async_computation.4 | async-start | bytes 524288 | tf_op jit(solution)/shard_map/all_to_all | solution.py:151
  (3 other events, 3.0 us)

commit v4 on v3

--- a/solution.py
+++ b/solution.py
@@ -50,7 +50,7 @@
             bias_ref[tile, :, n * span : (n + 1) * span] = jnp.where(seen > 0.5, 0.0, NEG)
 
 
-def attend_kernel(picks, count, scale, first, last, place_ref, bias_ref, q_ref, *refs):
+def attend_kernel(picks, count, qpart, scale, first, last, place_ref, bias_ref, q_ref, *refs):
     kv_refs, rest = refs[:count], refs[count:]
     if not first:
         m_in, acc_in = rest[:2]
@@ -60,7 +60,7 @@
     rows = qb * block
 
     def tile(index, carry):
-        q = q_ref[:, 3 * index].reshape(rows, hdim)
+        q = q_ref[:, qpart + 3 * index].reshape(rows, hdim)
         if first:
             m = jnp.full((rows, 1), NEG, jnp.float32)
             acc = jnp.zeros((rows, 2 * hdim), jnp.float32)
@@ -90,7 +90,7 @@
     lax.fori_loop(0, tiles, tile, 0)
 
 
-def attend(place, bias, q, arrays, picks, state, last):
+def attend(place, bias, q, qpart, arrays, picks, state, last):
     tiles, qb, _ = bias.shape
     block, hdim = q.shape[2:]
     groups = tiles * qb
@@ -108,13 +108,59 @@
     args = [place, bias, q, *arrays, *(() if first else state)]
     scale = hdim**-0.5 * math.log2(math.e)
     return pl.pallas_call(
-        functools.partial(attend_kernel, picks, len(arrays), scale, first, last),
+        functools.partial(attend_kernel, picks, len(arrays), qpart, scale, first, last),
         out_shape=out_shape,
         in_specs=[SMEM] + [VMEM] * (len(args) - 1),
         out_specs=out_specs,
         compiler_params=grant(*args),
         cost_estimate=pl.CostEstimate(flops=total, bytes_accessed=4 * total, transcendentals=0),
     )(*args)
+
+
+def pack_kernel(takes, *refs):
+    at = 0
+    for ref, parts in zip(refs, takes):
+        for part in parts:
+            refs[-1][:, at] = ref[:, part]
+            at += 1
+
+
+def pack(*takes):
+    arrays = [a for a, _ in takes]
+    first = arrays[0]
+    count = sum(len(parts) for _, parts in takes)
+    return pl.pallas_call(
+        functools.partial(pack_kernel, [tuple(parts) for _, parts in takes]),
+        out_shape=jax.ShapeDtypeStruct((first.shape[0], count) + first.shape[2:], first.dtype),
+        in_specs=[VMEM] * len(arrays),
+        out_specs=VMEM,
+        compiler_params=grant(*arrays),
+        cost_estimate=pl.CostEstimate(flops=10**6, bytes_accessed=10**4, transcendentals=0),
+    )(*arrays)
+
+
+def finish_kernel(part_ref, rows_ref, total_ref, out_ref):
+    pieces, tok, hdim = part_ref.shape
+    joined = jnp.concatenate([part_ref[i] for i in range(pieces)], axis=1)
+    step = math.gcd(out_ref.shape[1], 512)
+
+    def columns(index, carry):
+        at = pl.ds(pl.multiple_of(index * step, step), step)
+        product = jnp.dot(joined, rows_ref[:, at], preferred_element_type=jnp.float32)
+        out_ref[:, at] = (total_ref[:, at] + product).astype(out_ref.dtype)
+        return carry
+
+    lax.fori_loop(0, out_ref.shape[1] // step, columns, 0)
+
+
+def finish(part, rows, total):
+    return pl.pallas_call(
+        finish_kernel,
+        out_shape=jax.ShapeDtypeStruct(total.shape, jnp.bfloat16),
+        in_specs=[VMEM] * 3,
+        out_specs=VMEM,
+        compiler_params=grant(part, rows, total),
+    )(part, rows, total)
 
 
 def shards(split, gather, queries, keys, values, block_mask, out_weight):
@@ -174,55 +220,53 @@
             in_specs=[SMEM, VMEM, VMEM, VMEM],
             out_specs=VMEM,
             compiler_params=grant(out, block_mask),
-            cost_estimate=pl.CostEstimate(flops=3 * 10**9 if j else 8 * 10**9, bytes_accessed=0, transcendentals=0),
+            cost_estimate=pl.CostEstimate(flops={1: 3 * 10**9, 2: 2 * 10**10}.get(j, 10**6), bytes_accessed=0, transcendentals=0),
         )(place, after(block_mask, *before), local[:, None], np.repeat(local, BLOCK)[None, :])
 
     far0 = [across(pieces((keys, values), 0, b), ("zh", "zl"), 2 + b) for b in range(2)]
     trio = (queries, keys, values)
     own = []
-    for j in (1, 2, 0) if chunks == 3 else range(chunks):
+    for j in (1, 2, 0):
         own.append((j, pieces(trio, j, 0), across(pieces(trio, j, 1), "zl", 1)))
-    own = {j: jnp.concatenate([mine, got], axis=1) for j, mine, got in own}
+    own = {j: ((mine, range(3)), (got, range(3))) for j, mine, got in own}
+    assert chunks == 3
 
     near_pick = tuple((i, 2 * r, 2 * r + 1, 4 * i + r) for i in range(half) for r in range(2))
     far_pick = tuple((i, 2 * r, 2 * r + 1, 4 * i + 2 + r) for i in range(half) for r in range(2))
-    both_pick = tuple((i, 1 + 3 * r, 2 + 3 * r, 4 * i + r) for i in range(half) for r in range(2))
-    both_pick += tuple((i, 6 + 2 * r, 7 + 2 * r, 4 * i + 2 + r) for i in range(half) for r in range(2))
+    mine_pick = tuple((i, 1 + 3 * r, 2 + 3 * r, 4 * i + r) for i in range(half) for r in range(2))
+    both_pick = tuple((i, 7 + 3 * r, 8 + 3 * r, 4 * i + r) for i in range(half) for r in range(2))
+    both_pick += tuple((i, 12 + 2 * r, 13 + 2 * r, 4 * i + 2 + r) for i in range(half) for r in range(2))
     axes = gather + ("c",)
-    outs = [None] * chunks
-    waiting = []
-    far, gate = far0, ()
-    for j in range(1, chunks):
-        got = spread(after(own[j], *gate), flat)
-        bias = bias_of(j, far)
-        got = after(got, bias)
-        kv = jnp.concatenate([got[:, 1:3], got[:, 4:6]], axis=1)
-        gate = (kv,)
-        far = across(kv, "zh", 1)
-        near = gathered(kv, axes)
-        state = attend(home, bias, got, near, near_pick, None, False)
-        waiting.append((bias, got, far, state))
-    got = spread(after(jnp.concatenate([own[0], *far0], axis=1), kv), flat)
-    for j, (bias, mine, far, state) in enumerate(waiting[:-1], 1):
-        outs[j] = attend(home, bias, mine, gathered(far, axes), far_pick, state, True)
-    bias, mine, far, state = waiting[-1]
-    bias0 = bias_of(0, far)
-    got = after(got, bias0, state, outs[-2])
-    outs[0] = attend(home, bias0, got, gathered(got, axes), both_pick, None, True)
-    ready = jnp.stack(outs[:-1], axis=1)
+
+    def keyed(got):
+        return pack((got, (1, 2, 4, 5)))
+
+    got1 = spread(pack(*own[1]), flat)
+    bias1 = bias_of(1, *far0)
+    both = pack(*own[2], *own[0], *((f, range(2)) for f in far0))
+    got1 = after(got1, bias1, both)
+    kv1 = keyed(got1)
+    far1 = across(kv1, "zh", 1)
+    state1 = attend(home, bias1, got1, 0, gathered(kv1, axes), near_pick, None, False)
+    got = spread(after(both, kv1), flat)
+    bias2 = bias_of(2, far1)
+    got = after(got, bias2, state1)
+    kv2 = keyed(got)
+    far2 = across(kv2, "zh", 1)
+    shared = gathered(after(got, kv2), axes)
+    out1 = attend(home, bias1, got1, 0, gathered(far1, axes), far_pick, state1, True)
+    state2 = attend(home, bias2, got, 0, shared, mine_pick, None, False)
+    bias0 = bias_of(0, bias2)
+    out0 = attend(home, bias0, after(got, out1, state2[0]), 6, shared, both_pick, None, True)
+    ready = jnp.stack([out0, out1], axis=1)
     early = spread(ready, split)
-    far_all = gathered(far, axes)
-    outs[-1] = attend(home, bias, mine, far_all, far_pick, after(state, ready), True)
-    late = spread(after(outs[-1], early), split)
-
-    def project(part, j):
-        joined = jnp.transpose(part, (1, 0, 2)).reshape(tok, width)
-        rows = out_weight[j * width : (j + 1) * width]
-        return jnp.dot(joined, rows, preferred_element_type=jnp.float32)
-
-    early = after(early, outs[-1])
-    total = sum(project(early[:, j], j) for j in range(chunks - 1))
-    return (total + project(late, chunks - 1)).astype(jnp.bfloat16)
+    out2 = attend(home, bias2, got, 0, gathered(far2, axes), far_pick, after(state2, ready), True)
+    late = spread(after(out2, early), split)
+
+    rows = 2 * width
+    early = jnp.transpose(after(early, out2), (2, 1, 0, 3)).reshape(tok, rows)
+    total = jnp.dot(early, out_weight[:rows], preferred_element_type=jnp.float32)
+    return finish(late, out_weight[rows:], total)
 
 
 def solution(mesh):

time: 137 us -> 145 us (1.058)
  local copies, waits for them, and re-layouts: 15.6 us -> 29.3 us
  matrix products: 12.3 us -> 5.65 us
  starting transfers between devices: 30.8 us -> 26.9 us
  waiting for transfers between devices: 41.7 us -> 45.5 us
  Pallas kernels: 28.6 us -> 31.8 us
  other arithmetic: 6.83 us -> 4.7 us
    ppermute x12 -> x11, waiting for transfers between devices: 29.9 us -> 45 us  [across(): return lax.ppermute(a, axis, swap(n, bit))]
    all_to_all x5 -> x4, waiting for transfers between devices: 11.8 us -> 0.51 us  [spread(): return lax.all_to_all(a, axes, split_axis=0, concat_axis=0, tiled=True)]
    unnamed x59 -> x62, local copies, waits for them, and re-layouts: 6.89 us -> 14 us
    dot_general x3 -> x1, matrix products: 12.3 us -> 5.65 us  [shards(): jnp.dot(early, out_weight[:rows], preferred_element_type=jnp.float32)]
    slice x3 -> x1, local copies, waits for them, and re-layouts: 0.12 us -> 5.91 us  [shards(): return finish(late, out_weight[rows:], total)]
    all_to_all x5 -> x4, starting transfers between devices: 20.5 us -> 16.5 us  [spread(): return lax.all_to_all(a, axes, split_axis=0, concat_axis=0, tiled=True)]
    concatenate x4 -> x0, other arithmetic: 3.82 us -> none  [the longest x2 2.93 us: shards(): own = {j: jnp.concatenate([mine, got], axis=1) for j, mine, got in own}]
    pallas_call x5 -> x10, Pallas kernels: 25.8 us -> 29 us  [the longest x5 25 us: attend(): pl.pallas_call(functools.partial(attend_kernel, picks, len(arrays), qpart...]
  transfers between devices with their start and end apart: 17 -> 15, of which waited for: 9 -> 6; matrix products, arithmetic and copies ran while one was open for 14% -> 17% of each run, Pallas kernels for 16% -> 20%
where the time goes in v4:
time: 145 us; the launch traced here: 144 us
  waiting for transfers between devices  45.5 us (31%)
  Pallas kernels  31.8 us (22%)
  local copies, waits for them, and re-layouts  29.3 us (20%)
  starting transfers between devices  26.9 us (19%)
  matrix products  5.65 us (4%)
  other arithmetic  4.7 us (3%)
    ppermute x11, waiting for transfers between devices, across(): return lax.ppermute(a, axis, swap(n, bit))  45 us
    pallas_call x5, Pallas kernels, attend(): pl.pallas_call(functools.partial(attend_kernel, picks, len(arrays), qpart...  25 us
    all_to_all x4, starting transfers between devices, spread(): return lax.all_to_all(a, axes, split_axis=0, concat_axis=0, tiled=True)  16.5 us
    unnamed x62, local copies, waits for them, and re-layouts  14 us
    ppermute x11, starting transfers between devices, across(): return lax.ppermute(a, axis, swap(n, bit))  10.4 us
    slice x1, local copies, waits for them, and re-layouts, shards(): return finish(late, out_weight[rows:], total)  5.91 us
    dot_general x1, matrix products, shards(): jnp.dot(early, out_weight[:rows], preferred_element_type=jnp.float32)  5.65 us
    another operation x8, other arithmetic, pieces(): return jnp.stack(out, axis=1)  3.95 us
  transfers between devices with their start and end apart: 15, of which 6 were waited for; matrix products, arithmetic and copies ran while one was open for 17% of the time, Pallas kernels for 20%

profile of v4, /device:TPU:0, one launch (start us, length us, event | category | flops | bytes accessed | tf_op | source)
XLA Modules:
  0.0 144.4 jit_solution(11068067796398373915)
XLA Ops:
  0.0 1.2 fusion.3
  1.2 1.2 fusion.4
  3.5 4.0 %collective-permute-start.1 = (bf16[4,2,128,128]{3,2,1,0:T(8,128)(2,1)}, bf16[4,2,128,128]{3,2,1,0:T(8,128)(2,1)S(1)}, u32[]{:S(2)}, u32[]{:S(2)}) collective-permute-start(bf16[4,2,128,128]{3,2,1,0:T(8,128)(2,1)} %pad_maximum_fusion.7), channel_id=1, source_target_pairs={{0,4},{2,6},{4,0},{6,2},{1,5},{3,7},{5,1},{7,3},{8,12},{10,14},{12... | collective-permute-start | bytes 786440 | tf_op jit(solution)/shard_map/ppermute | solution.py:194
  8.3 1.3 collective-permute-start.2
  9.6 1.2 fusion.2
  11.7 1.1 constant_dynamic-slice_fusion.12
  13.9 1.1 constant_dynamic-slice_fusion
  15.8 1.8 %collective-permute-start.4 = (bf16[4,3,128,128]{3,2,1,0:T(8,128)(2,1)}, bf16[4,3,128,128]{3,2,1,0:T(8,128)(2,1)S(1)}, u32[]{:S(2)}, u32[]{:S(2)}) collective-permute-start(bf16[4,3,128,128]{3,2,1,0:T(8,128)(2,1)} %pad_maximum_fusion.6), channel_id=1, source_target_pairs={{0,2},{2,0},{1,3},{3,1},{4,6},{6,4},{5,7},{7,5},{8,10},{10,8},{9,1... | collective-permute-start | bytes 1179656 | tf_op jit(solution)/shard_map/ppermute | solution.py:194
  21.0 12.9 %collective-permute-done.refs_1_ = bf16[4,3,128,128]{3,2,1,0:T(8,128)(2,1)S(1)} collective-permute-done((bf16[4,3,128,128]{3,2,1,0:T(8,128)(2,1)}, bf16[4,3,128,128]{3,2,1,0:T(8,128)(2,1)S(1)}, u32[]{:S(2)}, u32[]{:S(2)}) %collective-permute-start) | collective-permute-done | bytes 393248 | tf_op jit(solution)/shard_map/ppermute | solution.py:194
  34.8 3.8 %all-to-all-start = ((bf16[4,6,128,128]{3,2,1,0:T(8,128)(2,1)}), bf16[4,6,128,128]{3,2,1,0:T(8,128)(2,1)S(1)}, u32[]{:S(2)}, u32[]{:S(2)}) async-start(bf16[4,6,128,128]{3,2,1,0:T(8,128)(2,1)} %shard_map.163), calls=%async_computation | async-start | bytes 1572864 | tf_op jit(solution)/shard_map/all_to_all | solution.py:197
  40.5 1.8 %collective-permute-done.4.refs_3_ = bf16[4,3,128,128]{3,2,1,0:T(8,128)(2,1)S(1)} collective-permute-done((bf16[4,3,128,128]{3,2,1,0:T(8,128)(2,1)}, bf16[4,3,128,128]{3,2,1,0:T(8,128)(2,1)S(1)}, u32[]{:S(2)}, u32[]{:S(2)}) %collective-permute-start.4) | collective-permute-done | bytes 393248 | tf_op jit(solution)/shard_map/ppermute | solution.py:194
  42.3 8.0 %collective-permute-done.3.refs_1_ = bf16[4,3,128,128]{3,2,1,0:T(8,128)(2,1)S(1)} collective-permute-done((bf16[4,3,128,128]{3,2,1,0:T(8,128)(2,1)}, bf16[4,3,128,128]{3,2,1,0:T(8,128)(2,1)S(1)}, u32[]{:S(2)}, u32[]{:S(2)}) %collective-permute-start.3) | collective-permute-done | bytes 393248 | tf_op jit(solution)/shard_map/ppermute | solution.py:194
  50.4 1.3 copy-done.1
  51.8 1.8 %collective-permute-start.5 = (bf16[4,4,128,128]{3,2,1,0:T(8,128)(2,1)S(1)}, bf16[4,4,128,128]{3,2,1,0:T(8,128)(2,1)}, u32[]{:S(2)}, u32[]{:S(2)}) collective-permute-start(bf16[4,4,128,128]{3,2,1,0:T(8,128)(2,1)S(1)} %shard_map.166.refs_0_), channel_id=1, source_target_pairs={{0,4},{4,0},{1,5},{5,1},{2,6},{6,2},{3,7},{7,3},{8,12},{12,8},{9,1... | collective-permute-start | bytes 1572872 | tf_op jit(solution)/shard_map/ppermute | solution.py:194
  53.7 3.8 %all-to-all-start.1 = ((bf16[4,16,128,128]{3,2,1,0:T(8,128)(2,1)}), bf16[4,16,128,128]{3,2,1,0:T(8,128)(2,1)S(1)}, u32[]{:S(2)}, u32[]{:S(2)}) async-start(bf16[4,16,128,128]{3,2,1,0:T(8,128)(2,1)} %copy-done.1), calls=%async_computation.1 | async-start | bytes 4194304 | tf_op jit(solution)/shard_map/all_to_all | solution.py:197
  57.5 20.1 %collective-permute-done.5.refs_0_ = bf16[4,4,128,128]{3,2,1,0:T(8,128)(2,1)} collective-permute-done((bf16[4,4,128,128]{3,2,1,0:T(8,128)(2,1)S(1)}, bf16[4,4,128,128]{3,2,1,0:T(8,128)(2,1)}, u32[]{:S(2)}, u32[]{:S(2)}) %collective-permute-start.5) | collective-permute-done | bytes 524320 | tf_op jit(solution)/shard_map/ppermute | solution.py:194
  77.6 4.5 %shard_map.168 = (f32[1024,128]{1,0:T(8,128)S(1)}, f32[1024,256]{1,0:T(8,128)S(1)}) custom-call(s32[8]{0:T(128)S(1)} %reshape.64.place_ref, f32[2,4,4096]{2,1,0:T(4,128)S(1)} %shard_map.164.bias_ref, bf16[4,6,128,128]{3,2,1,0:T(8,128)(2,1)S(1)} %all-to-all-done.refs_0_.q_ref, bf16[4,4,128,128]{3,2,1,0:T(8,128)(2,1)S(1)} %shard_map.166.refs_0_, ...), custom_call_target="tpu_custom_call" | custom-call | flops 1024 | bytes 4096 | tf_op jit(solution)/shard_map/pallas_call | solution.py:110
  87.1 1.0 copy-done.13
  89.0 2.3 %collective-permute-done.10.refs_1_ = bf16[4,4,128,128]{3,2,1,0:T(8,128)(2,1)S(1)} collective-permute-done((bf16[4,4,128,128]{3,2,1,0:T(8,128)(2,1)}, bf16[4,4,128,128]{3,2,1,0:T(8,128)(2,1)S(1)}, u32[]{:S(2)}, u32[]{:S(2)}) %collective-permute-start.10) | collective-permute-done | bytes 524320 | tf_op jit(solution)/shard_map/ppermute | solution.py:194
  91.3 1.2 copy-done.3
  92.5 1.0 copy-done.7
  93.6 4.6 %shard_map.172 = bf16[8,128,128]{2,1,0:T(8,128)(2,1)S(1)} custom-call(s32[8]{0:T(128)S(1)} %reshape.64.place_ref, f32[2,4,4096]{2,1,0:T(4,128)S(1)} %shard_map.164.bias_ref, bf16[4,6,128,128]{3,2,1,0:T(8,128)(2,1)S(1)} %all-to-all-done.refs_0_.q_ref, bf16[4,4,128,128]{3,2,1,0:T(8,128)(2,1)} %collective-permute-done.5.refs_0_, ...), custom_call_target="tpu_custom_call" | custom-call | flops 1024 | bytes 4096 | tf_op jit(solution)/shard_map/pallas_call | solution.py:110
  98.3 4.0 %shard_map.170 = (f32[1024,128]{1,0:T(8,128)S(1)}, f32[1024,256]{1,0:T(8,128)S(1)}) custom-call(s32[8]{0:T(128)S(1)} %reshape.64.place_ref, f32[2,4,4096]{2,1,0:T(4,128)S(1)} %copy-done.9, bf16[4,16,128,128]{3,2,1,0:T(8,128)(2,1)S(1)} %all-to-all-done.1.refs_0_.q_ref, bf16[4,16,128,128]{3,2,1,0:T(8,128)(2,1)S(1)} %all-to-all-done.1.refs_0_.q_ref, ...), custom_call_target="tpu_custom_call" | custom-call | flops 1024 | bytes 4096 | tf_op jit(solution)/shard_map/pallas_call | solution.py:110
  103.3 6.5 %shard_map.173 = bf16[8,128,128]{2,1,0:T(8,128)(2,1)S(1)} custom-call(s32[8]{0:T(128)S(1)} %reshape.64.place_ref, f32[2,4,4096]{2,1,0:T(4,128)S(1)} %shard_map.171.bias_ref, bf16[4,16,128,128]{3,2,1,0:T(8,128)(2,1)S(1)} %all-to-all-done.1.refs_0_.q_ref, bf16[4,16,128,128]{3,2,1,0:T(8,128)(2,1)S(1)} %all-to-all-done.1.refs_0_.q_ref, ...), custom_call_target="tpu_custom_call" | custom-call | flops 1024 | bytes 4096 | tf_op jit(solution)/shard_map/pallas_call | solution.py:110
  110.7 4.1 %all-to-all-start.2 = ((bf16[8,2,128,128]{3,2,1,0:T(8,128)(2,1)}), bf16[8,2,128,128]{3,2,1,0:T(8,128)(2,1)}, u32[]{:S(2)}, u32[]{:S(2)}) async-start(bf16[8,2,128,128]{3,2,1,0:T(8,128)(2,1)} %copy.73), calls=%async_computation.2 | async-start | bytes 1048576 | tf_op jit(solution)/shard_map/all_to_all | solution.py:197
  115.3 5.9 %slice.55.rows_ref = bf16[1024,3072]{1,0:T(8,128)(2,1)} slice(bf16[3072,3072]{1,0:T(8,128)(2,1)} %param.21), slice={[2048:3072], [0:3072]} | slice | bytes 12582912 | tf_op jit(solution)/shard_map/slice | solution.py:269
  121.2 5.4 %shard_map.174 = bf16[8,128,128]{2,1,0:T(8,128)(2,1)} custom-call(s32[8]{0:T(128)S(1)} %reshape.64.place_ref, f32[2,4,4096]{2,1,0:T(4,128)S(1)} %copy-done.10, bf16[4,16,128,128]{3,2,1,0:T(8,128)(2,1)S(1)} %all-to-all-done.1.refs_0_.q_ref, bf16[4,4,128,128]{3,2,1,0:T(8,128)(2,1)} %collective-permute-done.7.refs_0_, ...), custom_call_target="tpu_custom_call" | custom-call | flops 1024 | bytes 4096 | tf_op jit(solution)/shard_map/pallas_call | solution.py:110
  126.6 4.8 %all-to-all-start.3 = ((bf16[8,128,128]{2,1,0:T(8,128)(2,1)}), bf16[8,128,128]{2,1,0:T(8,128)(2,1)S(1)}, u32[]{:S(2)}, u32[]{:S(2)}) async-start(bf16[8,128,128]{2,1,0:T(8,128)(2,1)} %shard_map.174), calls=%async_computation.3 | async-start | bytes 524288 | tf_op jit(solution)/shard_map/all_to_all | solution.py:197
  131.4 1.3 copy.74
  132.7 5.7 %fusion.total_ref = f32[128,3072]{1,0:T(8,128)S(1)} fusion(bf16[128,2048]{0,1:T(8,128)(2,1)S(1)} %bitcast.70, bf16[3072,3072]{1,0:T(8,128)(2,1)} %param.21), kind=kOutput, calls=%fused_computation | convolution fusion | flops 1610612736 | bytes 14680064 | tf_op jit(solution)/shard_map/dot_general | solution.py:268
  138.9 2.8 %copy-done = bf16[1024,3072]{1,0:T(8,128)(2,1)S(1)} copy-done((bf16[1024,3072]{1,0:T(8,128)(2,1)S(1)}, bf16[1024,3072]{1,0:T(8,128)(2,1)}, u32[]{:S(2)}) %copy-start) | copy-done | bytes 6291480
  141.6 2.8 %shard_map.175 = bf16[128,3072]{1,0:T(8,128)(2,1)} custom-call(bf16[8,128,128]{2,1,0:T(8,128)(2,1)S(1)} %all-to-all-done.3.part_ref, bf16[1024,3072]{1,0:T(8,128)(2,1)S(1)} %copy-done, f32[128,3072]{1,0:T(8,128)S(1)} %fusion.total_ref), custom_call_target="tpu_custom_call" | custom-call | tf_op jit(solution)/shard_map/pallas_call | solution.py:157
  (97 shorter events, 19.7 us)
Async XLA Ops:
  3.5 36.0 %collective-permute-start.1 = (bf16[4,2,128,128]{3,2,1,0:T(8,128)(2,1)}, bf16[4,2,128,128]{3,2,1,0:T(8,128)(2,1)S(1)}, u32[]{:S(2)}, u32[]{:S(2)}) collective-permute-start(bf16[4,2,128,128]{3,2,1,0:T(8,128)(2,1)} %pad_maximum_fusion.7), channel_id=1, source_target_pairs={{0,4},{2,6},{4,0},{6,2},{1,5},{3,7},{5,1},{7,3},{8,12},{10,14},{12... | collective-permute-start | bytes 786440 | tf_op jit(solution)/shard_map/ppermute | solution.py:194
  8.3 31.2 %collective-permute-start.2 = (bf16[4,2,128,128]{3,2,1,0:T(8,128)(2,1)}, bf16[4,2,128,128]{3,2,1,0:T(8,128)(2,1)S(1)}, u32[]{:S(2)}, u32[]{:S(2)}) collective-permute-start(bf16[4,2,128,128]{3,2,1,0:T(8,128)(2,1)} %pad_maximum_fusion.8), channel_id=1, source_target_pairs={{0,6},{2,4},{4,2},{6,0},{1,7},{3,5},{5,3},{7,1},{8,14},{10,12},{12... | collective-permute-start | bytes 786440 | tf_op jit(solution)/shard_map/ppermute | solution.py:194
  10.8 27.8 %copy-start.21 = (pred[9]{0:T(512)(128)(4,1)S(1)}, pred[9]{0:T(512)(128)(4,1)}, u32[]{:S(2)}) copy-start(pred[9]{0:T(512)(128)(4,1)} %constant.95.clone) | copy-start | bytes 31
  12.8 8.1 %copy-start.18 = (bf16[2,1,2,128,128]{4,2,1,0,3:T(2,128)(2,1)S(1)}, bf16[2,1,2,128,128]{4,2,1,0,3:T(2,128)(2,1)}, u32[]{:S(2)}) copy-start(bf16[2,1,2,128,128]{4,2,1,0,3:T(2,128)(2,1)} %get-tuple-element.70) | copy-start | bytes 393220
  12.8 26.7 %copy-start.11 = (s32[24,32,32]{2,1,0:T(8,128)S(1)}, s32[24,32,32]{2,1,0:T(8,128)}, u32[]{:S(2)}) copy-start(s32[24,32,32]{2,1,0:T(8,128)} %mask_ref.2) | copy-start | bytes 294916
  12.8 26.7 %copy-start.14 = (s32[1,512]{1,0:T(1,128)S(1)}, s32[1,512]{1,0:T(1,128)}, u32[]{:S(2)}) copy-start(s32[1,512]{1,0:T(1,128)} %constant.99.clone.cols_ref) | copy-start | bytes 6148
  12.8 26.7 %copy-start.15 = (s32[4,1]{1,0:T(4,128)S(1)}, s32[4,1]{1,0:T(4,128)}, u32[]{:S(2)}) copy-start(s32[4,1]{1,0:T(4,128)} %constant.98.clone.rows_ref) | copy-start | bytes 52
  13.7 20.2 %collective-permute-start = (bf16[4,3,128,128]{3,2,1,0:T(8,128)(2,1)}, bf16[4,3,128,128]{3,2,1,0:T(8,128)(2,1)S(1)}, u32[]{:S(2)}, u32[]{:S(2)}) collective-permute-start(bf16[4,3,128,128]{3,2,1,0:T(8,128)(2,1)} %pad_maximum_fusion.2), channel_id=1, source_target_pairs={{0,2},{2,0},{1,3},{3,1},{4,6},{6,4},{5,7},{7,5},{8,10},{10,8},{9,1... | collective-permute-start | bytes 1179656 | tf_op jit(solution)/shard_map/ppermute | solution.py:194
  15.0 24.3 %copy-start.17 = (bf16[2,1,2,128,128]{4,2,1,0,3:T(2,128)(2,1)S(1)}, bf16[2,1,2,128,128]{4,2,1,0,3:T(2,128)(2,1)}, u32[]{:S(2)}) copy-start(bf16[2,1,2,128,128]{4,2,1,0,3:T(2,128)(2,1)} %get-tuple-element.47) | copy-start | bytes 393220
  15.0 24.4 %copy-start.16 = (bf16[2,1,2,128,128]{4,2,1,0,3:T(2,128)(2,1)S(1)}, bf16[2,1,2,128,128]{4,2,1,0,3:T(2,128)(2,1)}, u32[]{:S(2)}) copy-start(bf16[2,1,2,128,128]{4,2,1,0,3:T(2,128)(2,1)} %get-tuple-element.64) | copy-start | bytes 393220
  15.8 26.5 %collective-permute-start.4 = (bf16[4,3,128,128]{3,2,1,0:T(8,128)(2,1)}, bf16[4,3,128,128]{3,2,1,0:T(8,128)(2,1)S(1)}, u32[]{:S(2)}, u32[]{:S(2)}) collective-permute-start(bf16[4,3,128,128]{3,2,1,0:T(8,128)(2,1)} %pad_maximum_fusion.6), channel_id=1, source_target_pairs={{0,2},{2,0},{1,3},{3,1},{4,6},{6,4},{5,7},{7,5},{8,10},{10,8},{9,1... | collective-permute-start | bytes 1179656 | tf_op jit(solution)/shard_map/ppermute | solution.py:194
  18.8 31.4 %collective-permute-start.3 = (bf16[4,3,128,128]{3,2,1,0:T(8,128)(2,1)}, bf16[4,3,128,128]{3,2,1,0:T(8,128)(2,1)S(1)}, u32[]{:S(2)}, u32[]{:S(2)}) collective-permute-start(bf16[4,3,128,128]{3,2,1,0:T(8,128)(2,1)} %pad_maximum_fusion.4), channel_id=1, source_target_pairs={{0,2},{2,0},{1,3},{3,1},{4,6},{6,4},{5,7},{7,5},{8,10},{10,8},{9,1... | collective-permute-start | bytes 1179656 | tf_op jit(solution)/shard_map/ppermute | solution.py:194
  34.8 17.0 %all-to-all-start = ((bf16[4,6,128,128]{3,2,1,0:T(8,128)(2,1)}), bf16[4,6,128,128]{3,2,1,0:T(8,128)(2,1)S(1)}, u32[]{:S(2)}, u32[]{:S(2)}) async-start(bf16[4,6,128,128]{3,2,1,0:T(8,128)(2,1)} %shard_map.163), calls=%async_computation | async-start | bytes 1572864 | tf_op jit(solution)/shard_map/all_to_all | solution.py:197
  39.5 14.1 %copy-start.19 = (s32[2,4]{1,0:T(2,128)S(1)}, s32[2,4]{1,0:T(2,128)}, u32[]{:S(2)}) copy-start(s32[2,4]{1,0:T(2,128)} %constant.97.clone) | copy-start | bytes 100
  39.5 14.1 %copy-start.20 = (s32[2,4]{1,0:T(2,128)S(1)}, s32[2,4]{1,0:T(2,128)}, u32[]{:S(2)}) copy-start(s32[2,4]{1,0:T(2,128)} %constant.96.clone) | copy-start | bytes 100
  50.4 1.3 copy-start.1
  51.8 25.8 %collective-permute-start.5 = (bf16[4,4,128,128]{3,2,1,0:T(8,128)(2,1)S(1)}, bf16[4,4,128,128]{3,2,1,0:T(8,128)(2,1)}, u32[]{:S(2)}, u32[]{:S(2)}) collective-permute-start(bf16[4,4,128,128]{3,2,1,0:T(8,128)(2,1)S(1)} %shard_map.166.refs_0_), channel_id=1, source_target_pairs={{0,4},{4,0},{1,5},{5,1},{2,6},{6,2},{3,7},{7,3},{8,12},{12,8},{9,1... | collective-permute-start | bytes 1572872 | tf_op jit(solution)/shard_map/ppermute | solution.py:194
  53.6 24.0 %collective-permute-start.6 = (bf16[4,4,128,128]{3,2,1,0:T(8,128)(2,1)S(1)}, bf16[4,4,128,128]{3,2,1,0:T(8,128)(2,1)}, u32[]{:S(2)}, u32[]{:S(2)}) collective-permute-start(bf16[4,4,128,128]{3,2,1,0:T(8,128)(2,1)S(1)} %shard_map.166.refs_0_), channel_id=1, source_target_pairs={{0,8},{8,0},{1,9},{9,1},{2,10},{10,2},{3,11},{11,3},{4,12},{12,4},... | collective-permute-start | bytes 1572872 | tf_op jit(solution)/shard_map/ppermute | solution.py:194
  53.7 32.8 %all-to-all-start.1 = ((bf16[4,16,128,128]{3,2,1,0:T(8,128)(2,1)}), bf16[4,16,128,128]{3,2,1,0:T(8,128)(2,1)S(1)}, u32[]{:S(2)}, u32[]{:S(2)}) async-start(bf16[4,16,128,128]{3,2,1,0:T(8,128)(2,1)} %copy-done.1), calls=%async_computation.1 | async-start | bytes 4194304 | tf_op jit(solution)/shard_map/all_to_all | solution.py:197
  86.5 11.8 %copy-start.9 = (f32[2,4,4096]{2,1,0:T(4,128)S(1)}, f32[2,4,4096]{2,1,0:T(4,128)}, u32[]{:S(2)}) copy-start(f32[2,4,4096]{2,1,0:T(4,128)} %copy-done.8) | copy-start | bytes 393220
  86.5 11.7 %collective-permute-start.9 = (bf16[4,16,128,128]{3,2,1,0:T(8,128)(2,1)S(1)}, bf16[4,16,128,128]{3,2,1,0:T(8,128)(2,1)S(1)}, u32[]{:S(2)}, u32[]{:S(2)}) collective-permute-start(bf16[4,16,128,128]{3,2,1,0:T(8,128)(2,1)S(1)} %all-to-all-done.1.refs_0_.q_ref), channel_id=1, source_target_pairs={{0,8},{8,0},{1,9},{9,1},{2,10},{10,2},{3,11},{11,3},{4,12},{12,4},... | collective-permute-start | bytes 6291464 | tf_op jit(solution)/shard_map/ppermute | solution.py:194
  86.6 4.7 %collective-permute-start.10 = (bf16[4,4,128,128]{3,2,1,0:T(8,128)(2,1)}, bf16[4,4,128,128]{3,2,1,0:T(8,128)(2,1)S(1)}, u32[]{:S(2)}, u32[]{:S(2)}) collective-permute-start(bf16[4,4,128,128]{3,2,1,0:T(8,128)(2,1)} %collective-permute-done.5.refs_0_), channel_id=1, source_target_pairs={{0,8},{8,0},{1,9},{9,1},{2,10},{10,2},{3,11},{11,3},{4,12},{12,4},... | collective-permute-start | bytes 1572872 | tf_op jit(solution)/shard_map/ppermute | solution.py:194
  87.1 27.8 %collective-permute-start.7 = (bf16[4,4,128,128]{3,2,1,0:T(8,128)(2,1)S(1)}, bf16[4,4,128,128]{3,2,1,0:T(8,128)(2,1)}, u32[]{:S(2)}, u32[]{:S(2)}) collective-permute-start(bf16[4,4,128,128]{3,2,1,0:T(8,128)(2,1)S(1)} %shard_map.169), channel_id=1, source_target_pairs={{0,4},{4,0},{1,5},{5,1},{2,6},{6,2},{3,7},{7,3},{8,12},{12,8},{9,1... | collective-permute-start | bytes 1572872 | tf_op jit(solution)/shard_map/ppermute | solution.py:194
  87.1 1.0 copy-start.13
  91.3 1.2 copy-start.3
  92.5 1.0 copy-start.7
  110.7 15.9 %all-to-all-start.2 = ((bf16[8,2,128,128]{3,2,1,0:T(8,128)(2,1)}), bf16[8,2,128,128]{3,2,1,0:T(8,128)(2,1)}, u32[]{:S(2)}, u32[]{:S(2)}) async-start(bf16[8,2,128,128]{3,2,1,0:T(8,128)(2,1)} %copy.73), calls=%async_computation.2 | async-start | bytes 1048576 | tf_op jit(solution)/shard_map/all_to_all | solution.py:197
  114.8 6.4 %copy-start.5 = (f32[1024,256]{1,0:T(8,128)S(1)}, f32[1024,256]{1,0:T(8,128)}, u32[]{:S(2)}) copy-start(f32[1024,256]{1,0:T(8,128)} %copy-done.4) | copy-start | bytes 3145732
  114.8 6.4 %copy-start.10 = (f32[2,4,4096]{2,1,0:T(4,128)S(1)}, f32[2,4,4096]{2,1,0:T(4,128)}, u32[]{:S(2)}) copy-start(f32[2,4,4096]{2,1,0:T(4,128)} %copy-done.8) | copy-start | bytes 393220
  114.8 6.4 %collective-permute-start.8 = (bf16[4,4,128,128]{3,2,1,0:T(8,128)(2,1)}, bf16[4,4,128,128]{3,2,1,0:T(8,128)(2,1)S(1)}, u32[]{:S(2)}, u32[]{:S(2)}) collective-permute-start(bf16[4,4,128,128]{3,2,1,0:T(8,128)(2,1)} %collective-permute-done.7.refs_0_), channel_id=1, source_target_pairs={{0,8},{8,0},{1,9},{9,1},{2,10},{10,2},{3,11},{11,3},{4,12},{12,4},... | collective-permute-start | bytes 1572872 | tf_op jit(solution)/shard_map/ppermute | solution.py:194
  126.6 12.3 %all-to-all-start.3 = ((bf16[8,128,128]{2,1,0:T(8,128)(2,1)}), bf16[8,128,128]{2,1,0:T(8,128)(2,1)S(1)}, u32[]{:S(2)}, u32[]{:S(2)}) async-start(bf16[8,128,128]{2,1,0:T(8,128)(2,1)} %shard_map.174), calls=%async_computation.3 | async-start | bytes 524288 | tf_op jit(solution)/shard_map/all_to_all | solution.py:197
  138.9 2.8 %copy-start = (bf16[1024,3072]{1,0:T(8,128)(2,1)S(1)}, bf16[1024,3072]{1,0:T(8,128)(2,1)}, u32[]{:S(2)}) copy-start(bf16[1024,3072]{1,0:T(8,128)(2,1)} %slice.55.rows_ref) | copy-start | bytes 18874372
  (5 other events, 4.4 us)

commit v5 on v4

--- a/solution.py
+++ b/solution.py
@@ -50,7 +50,7 @@
             bias_ref[tile, :, n * span : (n + 1) * span] = jnp.where(seen > 0.5, 0.0, NEG)
 
 
-def attend_kernel(picks, count, qpart, scale, first, last, place_ref, bias_ref, q_ref, *refs):
+def attend_kernel(picks, count, scale, first, last, place_ref, bias_ref, q_ref, *refs):
     kv_refs, rest = refs[:count], refs[count:]
     if not first:
         m_in, acc_in = rest[:2]
@@ -60,7 +60,7 @@
     rows = qb * block
 
     def tile(index, carry):
-        q = q_ref[:, qpart + 3 * index].reshape(rows, hdim)
+        q = q_ref[:, 3 * index].reshape(rows, hdim)
         if first:
             m = jnp.full((rows, 1), NEG, jnp.float32)
             acc = jnp.zeros((rows, 2 * hdim), jnp.float32)
@@ -90,7 +90,7 @@
     lax.fori_loop(0, tiles, tile, 0)
 
 
-def attend(place, bias, q, qpart, arrays, picks, state, last):
+def attend(place, bias, q, arrays, picks, state, last):
     tiles, qb, _ = bias.shape
     block, hdim = q.shape[2:]
     groups = tiles * qb
@@ -108,7 +108,7 @@
     args = [place, bias, q, *arrays, *(() if first else state)]
     scale = hdim**-0.5 * math.log2(math.e)
     return pl.pallas_call(
-        functools.partial(attend_kernel, picks, len(arrays), qpart, scale, first, last),
+        functools.partial(attend_kernel, picks, len(arrays), scale, first, last),
         out_shape=out_shape,
         in_specs=[SMEM] + [VMEM] * (len(args) - 1),
         out_specs=out_specs,
@@ -140,27 +140,28 @@
 
 
 def finish_kernel(part_ref, rows_ref, total_ref, out_ref):
-    pieces, tok, hdim = part_ref.shape
-    joined = jnp.concatenate([part_ref[i] for i in range(pieces)], axis=1)
-    step = math.gcd(out_ref.shape[1], 512)
-
-    def columns(index, carry):
-        at = pl.ds(pl.multiple_of(index * step, step), step)
-        product = jnp.dot(joined, rows_ref[:, at], preferred_element_type=jnp.float32)
-        out_ref[:, at] = (total_ref[:, at] + product).astype(out_ref.dtype)
-        return carry
-
-    lax.fori_loop(0, out_ref.shape[1] // step, columns, 0)
-
-
-def finish(part, rows, total):
+    joined = jnp.concatenate([part_ref[i] for i in range(part_ref.shape[0])], axis=1)
+    product = jnp.dot(joined, rows_ref[...], preferred_element_type=jnp.float32)
+    out_ref[...] = (total_ref[...] + product).astype(out_ref.dtype)
+
+
+def finish(part, weight, total):
+    pieces, tok, hdim = part.shape
+    width = pieces * hdim
+    last = weight.shape[0] // width - 1
+    step = math.gcd(weight.shape[1], 768)
     return pl.pallas_call(
         finish_kernel,
         out_shape=jax.ShapeDtypeStruct(total.shape, jnp.bfloat16),
-        in_specs=[VMEM] * 3,
-        out_specs=VMEM,
-        compiler_params=grant(part, rows, total),
-    )(part, rows, total)
+        grid=(weight.shape[1] // step,),
+        in_specs=[
+            pl.BlockSpec((pieces, tok, hdim), lambda i: (0, 0, 0)),
+            pl.BlockSpec((width, step), lambda i: (last, i)),
+            pl.BlockSpec((tok, step), lambda i: (0, i)),
+        ],
+        out_specs=pl.BlockSpec((tok, step), lambda i: (0, i)),
+        compiler_params=grant(part, total),
+    )(part, weight, total)
 
 
 def shards(split, gather, queries, keys, values, block_mask, out_weight):
@@ -220,53 +221,59 @@
             in_specs=[SMEM, VMEM, VMEM, VMEM],
             out_specs=VMEM,
             compiler_params=grant(out, block_mask),
-            cost_estimate=pl.CostEstimate(flops={1: 3 * 10**9, 2: 2 * 10**10}.get(j, 10**6), bytes_accessed=0, transcendentals=0),
+            cost_estimate=pl.CostEstimate(flops={2: 3 * 10**9, 0: 8 * 10**9, 1: 8 * 10**9}[j], bytes_accessed=0, transcendentals=0),
         )(place, after(block_mask, *before), local[:, None], np.repeat(local, BLOCK)[None, :])
 
-    far0 = [across(pieces((keys, values), 0, b), ("zh", "zl"), 2 + b) for b in range(2)]
+    assert chunks == 3
     trio = (queries, keys, values)
-    own = []
-    for j in (1, 2, 0):
-        own.append((j, pieces(trio, j, 0), across(pieces(trio, j, 1), "zl", 1)))
-    own = {j: ((mine, range(3)), (got, range(3))) for j, mine, got in own}
-    assert chunks == 3
+
+    def cross(j, *before):
+        halves = [pieces((keys, values), j, b) for b in range(2)]
+        if before:
+            halves = after(halves, *before)
+        return [across(h, ("zh", "zl"), 2 + b) for b, h in enumerate(halves)]
+
+    def own(j, *before):
+        given = pieces(trio, j, 1)
+        if before:
+            given = after(given, *before)
+        return (pieces(trio, j, 0), range(3)), (across(given, "zl", 1), range(3))
 
     near_pick = tuple((i, 2 * r, 2 * r + 1, 4 * i + r) for i in range(half) for r in range(2))
     far_pick = tuple((i, 2 * r, 2 * r + 1, 4 * i + 2 + r) for i in range(half) for r in range(2))
-    mine_pick = tuple((i, 1 + 3 * r, 2 + 3 * r, 4 * i + r) for i in range(half) for r in range(2))
-    both_pick = tuple((i, 7 + 3 * r, 8 + 3 * r, 4 * i + r) for i in range(half) for r in range(2))
-    both_pick += tuple((i, 12 + 2 * r, 13 + 2 * r, 4 * i + 2 + r) for i in range(half) for r in range(2))
+    both_pick = tuple((i, 1 + 3 * r, 2 + 3 * r, 4 * i + r) for i in range(half) for r in range(2))
+    both_pick += tuple((i, 6 + 2 * r, 7 + 2 * r, 4 * i + 2 + r) for i in range(half) for r in range(2))
     axes = gather + ("c",)
 
-    def keyed(got):
-        return pack((got, (1, 2, 4, 5)))
-
-    got1 = spread(pack(*own[1]), flat)
-    bias1 = bias_of(1, *far0)
-    both = pack(*own[2], *own[0], *((f, range(2)) for f in far0))
-    got1 = after(got1, bias1, both)
-    kv1 = keyed(got1)
-    far1 = across(kv1, "zh", 1)
-    state1 = attend(home, bias1, got1, 0, gathered(kv1, axes), near_pick, None, False)
-    got = spread(after(both, kv1), flat)
-    bias2 = bias_of(2, far1)
-    got = after(got, bias2, state1)
-    kv2 = keyed(got)
-    far2 = across(kv2, "zh", 1)
-    shared = gathered(after(got, kv2), axes)
-    out1 = attend(home, bias1, got1, 0, gathered(far1, axes), far_pick, state1, True)
-    state2 = attend(home, bias2, got, 0, shared, mine_pick, None, False)
-    bias0 = bias_of(0, bias2)
-    out0 = attend(home, bias0, after(got, out1, state2[0]), 6, shared, both_pick, None, True)
+    far0 = cross(0)
+    own2 = own(2)
+    got2 = spread(pack(*own2), flat)
+    bias2 = bias_of(2, *far0)
+    own0 = pack(*own(0, own2[1][0]), *((f, range(2)) for f in far0))
+    got2 = after(got2, bias2, own0)
+    kv2 = pack((got2, (1, 2, 4, 5)))
+    far1 = cross(1, *far0)
+    got0 = spread(after(own0, kv2), flat)
+    bias0 = bias_of(0, *far1)
+    state2 = attend(home, bias2, got2, gathered(kv2, axes), near_pick, None, False)
+    own1 = pack(*own(1, *far0), *((f, range(2)) for f in far1))
+    got0 = after(got0, bias0, own1, state2)
+    far2 = across(after(kv2, *far1), "zh", 1)
+    got1 = spread(after(own1, got0), flat)
+    bias1 = bias_of(1, far2)
+    out0 = attend(home, bias0, got0, gathered(got0, axes), both_pick, None, True)
+    got1 = after(got1, bias1, out0)
+    far2 = gathered(far2, axes)
+    out1 = attend(home, bias1, got1, gathered(got1, axes), both_pick, None, True)
     ready = jnp.stack([out0, out1], axis=1)
     early = spread(ready, split)
-    out2 = attend(home, bias2, got, 0, gathered(far2, axes), far_pick, after(state2, ready), True)
+    out2 = attend(home, bias2, got2, far2, far_pick, after(state2, ready), True)
     late = spread(after(out2, early), split)
 
     rows = 2 * width
     early = jnp.transpose(after(early, out2), (2, 1, 0, 3)).reshape(tok, rows)
     total = jnp.dot(early, out_weight[:rows], preferred_element_type=jnp.float32)
-    return finish(late, out_weight[rows:], total)
+    return finish(late, out_weight, total)
 
 
 def solution(mesh):

time: 145 us -> 158 us (1.090)
  waiting for transfers between devices: 45.5 us -> 61.5 us
  local copies, waits for them, and re-layouts: 29.3 us -> 20.8 us
  starting transfers between devices: 26.9 us -> 29.7 us
  other arithmetic: 4.7 us -> 6.62 us
    ppermute x11 -> x12, waiting for transfers between devices: 45 us -> 57.6 us  [across(): return lax.ppermute(a, axis, swap(n, bit))]
    slice x1 -> x0, local copies, waits for them, and re-layouts: 5.91 us -> none  [shards(): return finish(late, out_weight[rows:], total)]
    all_to_all x4 -> x5, waiting for transfers between devices: 0.51 us -> 3.92 us  [spread(): return lax.all_to_all(a, axes, split_axis=0, concat_axis=0, tiled=True)]
    another operation x8 -> x10, other arithmetic: 3.95 us -> 6.56 us  [pieces(): return jnp.stack(out, axis=1)]
    all_to_all x4 -> x5, starting transfers between devices: 16.5 us -> 19 us  [spread(): return lax.all_to_all(a, axes, split_axis=0, concat_axis=0, tiled=True)]
    slice x3, local copies, waits for them, and re-layouts: 3.48 us -> 1.55 us  [pieces(): a = jnp.transpose(a[:, j * n_split:(j + 1) * n_split], (1, 0, 2))]
    pallas_call x4, Pallas kernels: 1.14 us -> 3.03 us  [pack(): pl.pallas_call(functools.partial(pack_kernel, [tuple(parts) for _, parts...]
    pallas_call x5 -> x4, Pallas kernels: 25 us -> 23.5 us  [attend(): pl.pallas_call(functools.partial(attend_kernel, picks, len(arrays), scale...]
  transfers between devices with their start and end apart: 15 -> 17, of which waited for: 6 -> 9; matrix products, arithmetic and copies ran while one was open for 17% -> 10% of each run, Pallas kernels for 20% -> 15%
where the time goes in v5:
time: 158 us; the launch traced here: 157 us
  waiting for transfers between devices  61.5 us (39%)
  Pallas kernels  32.2 us (20%)
  starting transfers between devices  29.7 us (19%)
  local copies, waits for them, and re-layouts  20.8 us (13%)
  other arithmetic  6.62 us (4%)
  matrix products  5.65 us (4%)
    ppermute x12, waiting for transfers between devices, across(): return lax.ppermute(a, axis, swap(n, bit))  57.6 us
    pallas_call x4, Pallas kernels, attend(): pl.pallas_call(functools.partial(attend_kernel, picks, len(arrays), scale...  23.5 us
    all_to_all x5, starting transfers between devices, spread(): return lax.all_to_all(a, axes, split_axis=0, concat_axis=0, tiled=True)  19 us
    unnamed x74, local copies, waits for them, and re-layouts  15 us
    ppermute x12, starting transfers between devices, across(): return lax.ppermute(a, axis, swap(n, bit))  10.7 us
    another operation x10, other arithmetic, pieces(): return jnp.stack(out, axis=1)  6.56 us
    dot_general x1, matrix products, shards(): jnp.dot(early, out_weight[:rows], preferred_element_type=jnp.float32)  5.65 us
    all_to_all x5, waiting for transfers between devices, spread(): return lax.all_to_all(a, axes, split_axis=0, concat_axis=0, tiled=True)  3.92 us
  transfers between devices with their start and end apart: 17, of which 9 were waited for; matrix products, arithmetic and copies ran while one was open for 10% of the time, Pallas kernels for 15%

profile of v5, /device:TPU:0, one launch (start us, length us, event | category | flops | bytes accessed | tf_op | source)
XLA Modules:
  0.0 156.9 jit_solution(8212200070379648422)
XLA Ops:
  0.0 1.3 fusion.2
  3.1 5.0 %collective-permute-start.1 = (bf16[4,2,128,128]{3,2,1,0:T(8,128)(2,1)}, bf16[4,2,128,128]{3,2,1,0:T(8,128)(2,1)S(1)}, u32[]{:S(2)}, u32[]{:S(2)}) collective-permute-start(bf16[4,2,128,128]{3,2,1,0:T(8,128)(2,1)} %pad_maximum_fusion.8), channel_id=1, source_target_pairs={{0,6},{2,4},{4,2},{6,0},{1,7},{3,5},{5,3},{7,1},{8,14},{10,12},{12... | collective-permute-start | bytes 786440 | tf_op jit(solution)/shard_map/ppermute | solution.py:195
  10.8 1.0 constant_dynamic-slice_fusion.3
  11.8 1.1 constant_dynamic-slice_fusion
  14.0 14.2 %collective-permute-done.2.refs_1_ = bf16[4,3,128,128]{3,2,1,0:T(8,128)(2,1)S(1)} collective-permute-done((bf16[4,3,128,128]{3,2,1,0:T(8,128)(2,1)}, bf16[4,3,128,128]{3,2,1,0:T(8,128)(2,1)S(1)}, u32[]{:S(2)}, u32[]{:S(2)}) %collective-permute-start.2) | collective-permute-done | bytes 393248 | tf_op jit(solution)/shard_map/ppermute | solution.py:195
  29.1 3.8 %all-to-all-start = ((bf16[4,6,128,128]{3,2,1,0:T(8,128)(2,1)}), bf16[4,6,128,128]{3,2,1,0:T(8,128)(2,1)S(1)}, u32[]{:S(2)}, u32[]{:S(2)}) async-start(bf16[4,6,128,128]{3,2,1,0:T(8,128)(2,1)} %shard_map.164), calls=%async_computation | async-start | bytes 1572864 | tf_op jit(solution)/shard_map/all_to_all | solution.py:198
  35.3 2.4 %collective-permute-start.3 = (bf16[4,3,128,128]{3,2,1,0:T(8,128)(2,1)}, bf16[4,3,128,128]{3,2,1,0:T(8,128)(2,1)S(1)}, u32[]{:S(2)}, u32[]{:S(2)}) collective-permute-start(bf16[4,3,128,128]{3,2,1,0:T(8,128)(2,1)} %pad_maximum_fusion.4), channel_id=1, source_target_pairs={{0,2},{2,0},{1,3},{3,1},{4,6},{6,4},{5,7},{7,5},{8,10},{10,8},{9,1... | collective-permute-start | bytes 1179656 | tf_op jit(solution)/shard_map/ppermute | solution.py:195
  38.5 2.4 %collective-permute-start.5 = (bf16[4,2,128,128]{3,2,1,0:T(8,128)(2,1)}, bf16[4,2,128,128]{3,2,1,0:T(8,128)(2,1)S(1)}, u32[]{:S(2)}, u32[]{:S(2)}) collective-permute-start(bf16[4,2,128,128]{3,2,1,0:T(8,128)(2,1)} %pad_maximum_fusion.10), channel_id=1, source_target_pairs={{0,6},{2,4},{4,2},{6,0},{1,7},{3,5},{5,3},{7,1},{8,14},{10,12},{12... | collective-permute-start | bytes 786440 | tf_op jit(solution)/shard_map/ppermute | solution.py:195
  41.8 9.0 %collective-permute-done.3.refs_1_ = bf16[4,3,128,128]{3,2,1,0:T(8,128)(2,1)S(1)} collective-permute-done((bf16[4,3,128,128]{3,2,1,0:T(8,128)(2,1)}, bf16[4,3,128,128]{3,2,1,0:T(8,128)(2,1)S(1)}, u32[]{:S(2)}, u32[]{:S(2)}) %collective-permute-start.3) | collective-permute-done | bytes 393248 | tf_op jit(solution)/shard_map/ppermute | solution.py:195
  50.8 1.2 shard_map.165
  52.8 3.9 %all-to-all-start.1 = ((bf16[4,10,128,128]{3,2,1,0:T(8,128)(2,1)}), bf16[4,10,128,128]{3,2,1,0:T(8,128)(2,1)S(1)}, u32[]{:S(2)}, u32[]{:S(2)}) async-start(bf16[4,10,128,128]{3,2,1,0:T(8,128)(2,1)} %shard_map.165), calls=%async_computation.1 | async-start | bytes 2621440 | tf_op jit(solution)/shard_map/all_to_all | solution.py:198
  57.6 1.0 pad_maximum_fusion.5.refs_0_
  58.7 1.3 collective-permute-done.4.refs_2_
  61.7 6.2 %collective-permute-done.9.refs_1_ = bf16[4,3,128,128]{3,2,1,0:T(8,128)(2,1)S(1)} collective-permute-done((bf16[4,3,128,128]{3,2,1,0:T(8,128)(2,1)S(1)}, bf16[4,3,128,128]{3,2,1,0:T(8,128)(2,1)S(1)}, u32[]{:S(2)}, u32[]{:S(2)}) %collective-permute-start.9) | collective-permute-done | bytes 393248 | tf_op jit(solution)/shard_map/ppermute | solution.py:195
  67.9 1.1 copy-done.1
  69.0 4.5 %shard_map.167 = (f32[1024,128]{1,0:T(8,128)S(1)}, f32[1024,256]{1,0:T(8,128)S(1)}) custom-call(s32[8]{0:T(128)S(1)} %reshape.68.place_ref, f32[2,4,4096]{2,1,0:T(4,128)S(1)} %shard_map.163.bias_ref, bf16[4,6,128,128]{3,2,1,0:T(8,128)(2,1)S(1)} %all-to-all-done.refs_0_.q_ref, bf16[4,4,128,128]{3,2,1,0:T(8,128)(2,1)} %shard_map.166.refs_0_, ...), custom_call_target="tpu_custom_call" | custom-call | flops 1024 | bytes 4096 | tf_op jit(solution)/shard_map/pallas_call | solution.py:110
  73.6 0.9 copy-done.4
  75.5 3.9 %all-to-all-start.2 = ((bf16[4,10,128,128]{3,2,1,0:T(8,128)(2,1)}), bf16[4,10,128,128]{3,2,1,0:T(8,128)(2,1)S(1)}, u32[]{:S(2)}, u32[]{:S(2)}) async-start(bf16[4,10,128,128]{3,2,1,0:T(8,128)(2,1)} %copy-done.1), calls=%async_computation.2 | async-start | bytes 2621440 | tf_op jit(solution)/shard_map/all_to_all | solution.py:198
  79.4 21.8 %collective-permute-done.6.refs_0_ = bf16[4,4,128,128]{3,2,1,0:T(8,128)(2,1)} collective-permute-done((bf16[4,4,128,128]{3,2,1,0:T(8,128)(2,1)}, bf16[4,4,128,128]{3,2,1,0:T(8,128)(2,1)}, u32[]{:S(2)}, u32[]{:S(2)}) %collective-permute-start.6) | collective-permute-done | bytes 524320 | tf_op jit(solution)/shard_map/ppermute | solution.py:195
  101.2 1.0 copy-done.13
  103.8 7.2 %shard_map.170 = bf16[8,128,128]{2,1,0:T(8,128)(2,1)S(1)} custom-call(s32[8]{0:T(128)S(1)} %reshape.68.place_ref, f32[2,4,4096]{2,1,0:T(4,128)S(1)} %copy-done.9, bf16[4,10,128,128]{3,2,1,0:T(8,128)(2,1)S(1)} %all-to-all-done.1.q_ref.refs_0_, bf16[4,10,128,128]{3,2,1,0:T(8,128)(2,1)S(1)} %all-to-all-done.1.q_ref.refs_0_, ...), custom_call_target="tpu_custom_call" | custom-call | flops 1024 | bytes 4096 | tf_op jit(solution)/shard_map/pallas_call | solution.py:110
  111.8 3.0 %collective-permute-done.11.refs_1_ = bf16[4,10,128,128]{3,2,1,0:T(8,128)(2,1)S(1)} collective-permute-done((bf16[4,10,128,128]{3,2,1,0:T(8,128)(2,1)S(1)}, bf16[4,10,128,128]{3,2,1,0:T(8,128)(2,1)S(1)}, u32[]{:S(2)}, u32[]{:S(2)}) %collective-permute-start.11) | collective-permute-done | bytes 1310752 | tf_op jit(solution)/shard_map/ppermute | solution.py:195
  115.7 6.5 %shard_map.172 = bf16[8,128,128]{2,1,0:T(8,128)(2,1)S(1)} custom-call(s32[8]{0:T(128)S(1)} %reshape.68.place_ref, f32[2,4,4096]{2,1,0:T(4,128)S(1)} %copy-done.11, bf16[4,10,128,128]{3,2,1,0:T(8,128)(2,1)S(1)} %all-to-all-done.2.q_ref.refs_0_, bf16[4,10,128,128]{3,2,1,0:T(8,128)(2,1)S(1)} %all-to-all-done.2.q_ref.refs_0_, ...), custom_call_target="tpu_custom_call" | custom-call | flops 1024 | bytes 4096 | tf_op jit(solution)/shard_map/pallas_call | solution.py:110
  123.0 3.9 %all-to-all-start.3 = ((bf16[8,2,128,128]{3,2,1,0:T(8,128)(2,1)}), bf16[8,2,128,128]{3,2,1,0:T(8,128)(2,1)S(1)}, u32[]{:S(2)}, u32[]{:S(2)}) async-start(bf16[8,2,128,128]{3,2,1,0:T(8,128)(2,1)} %copy.73), calls=%async_computation.3 | async-start | bytes 1048576 | tf_op jit(solution)/shard_map/all_to_all | solution.py:198
  127.0 2.1 %collective-permute-done.7.refs_1_ = bf16[4,4,128,128]{3,2,1,0:T(8,128)(2,1)S(1)} collective-permute-done((bf16[4,4,128,128]{3,2,1,0:T(8,128)(2,1)}, bf16[4,4,128,128]{3,2,1,0:T(8,128)(2,1)S(1)}, u32[]{:S(2)}, u32[]{:S(2)}) %collective-permute-start.7) | collective-permute-done | bytes 524320 | tf_op jit(solution)/shard_map/ppermute | solution.py:195
  129.1 5.3 %shard_map.173 = bf16[8,128,128]{2,1,0:T(8,128)(2,1)} custom-call(s32[8]{0:T(128)S(1)} %reshape.68.place_ref, f32[2,4,4096]{2,1,0:T(4,128)S(1)} %shard_map.163.bias_ref, bf16[4,6,128,128]{3,2,1,0:T(8,128)(2,1)S(1)} %all-to-all-done.refs_0_.q_ref, bf16[4,4,128,128]{3,2,1,0:T(8,128)(2,1)} %collective-permute-done.6.refs_0_, ...), custom_call_target="tpu_custom_call" | custom-call | flops 1024 | bytes 4096 | tf_op jit(solution)/shard_map/pallas_call | solution.py:110
  134.4 2.7 %all-to-all-done.3 = bf16[8,2,128,128]{3,2,1,0:T(8,128)(2,1)S(1)} async-done(((bf16[8,2,128,128]{3,2,1,0:T(8,128)(2,1)}), bf16[8,2,128,128]{3,2,1,0:T(8,128)(2,1)S(1)}, u32[]{:S(2)}, u32[]{:S(2)}) %all-to-all-start.3) | async-done | bytes 524320 | tf_op jit(solution)/shard_map/all_to_all | solution.py:198
  137.3 3.4 %all-to-all-start.4 = ((bf16[8,128,128]{2,1,0:T(8,128)(2,1)}), bf16[8,128,128]{2,1,0:T(8,128)(2,1)S(1)}, u32[]{:S(2)}, u32[]{:S(2)}) async-start(bf16[8,128,128]{2,1,0:T(8,128)(2,1)} %shard_map.173), calls=%async_computation.4 | async-start | bytes 524288 | tf_op jit(solution)/shard_map/all_to_all | solution.py:198
  140.8 5.7 %fusion.total_ref = f32[128,3072]{1,0:T(8,128)S(1)} fusion(bf16[128,2048]{0,1:T(8,128)(2,1)S(1)} %bitcast.78, bf16[3072,3072]{1,0:T(8,128)(2,1)} %rows_ref.4), kind=kOutput, calls=%fused_computation | convolution fusion | flops 1610612736 | bytes 14680064 | tf_op jit(solution)/shard_map/dot_general | solution.py:275
  146.4 1.2 all-to-all-done.4.part_ref
  147.7 6.4 %copy-done = bf16[3072,3072]{1,0:T(8,128)(2,1)S(1)} copy-done((bf16[3072,3072]{1,0:T(8,128)(2,1)S(1)}, bf16[3072,3072]{1,0:T(8,128)(2,1)}, u32[]{:S(2)}) %copy-start) | copy-done | bytes 18874392
  154.0 2.9 %shard_map.174 = bf16[128,3072]{1,0:T(8,128)(2,1)} custom-call(bf16[8,128,128]{2,1,0:T(8,128)(2,1)S(1)} %all-to-all-done.4.part_ref, bf16[3072,3072]{1,0:T(8,128)(2,1)S(1)} %copy-done, f32[128,3072]{1,0:T(8,128)S(1)} %fusion.total_ref), custom_call_target="tpu_custom_call" | custom-call | tf_op jit(solution)/shard_map/pallas_call | solution.py:153
  (113 shorter events, 19.2 us)
Async XLA Ops:
  3.1 35.3 %collective-permute-start.1 = (bf16[4,2,128,128]{3,2,1,0:T(8,128)(2,1)}, bf16[4,2,128,128]{3,2,1,0:T(8,128)(2,1)S(1)}, u32[]{:S(2)}, u32[]{:S(2)}) collective-permute-start(bf16[4,2,128,128]{3,2,1,0:T(8,128)(2,1)} %pad_maximum_fusion.8), channel_id=1, source_target_pairs={{0,6},{2,4},{4,2},{6,0},{1,7},{3,5},{5,3},{7,1},{8,14},{10,12},{12... | collective-permute-start | bytes 786440 | tf_op jit(solution)/shard_map/ppermute | solution.py:195
  8.9 29.5 %collective-permute-start = (bf16[4,2,128,128]{3,2,1,0:T(8,128)(2,1)}, bf16[4,2,128,128]{3,2,1,0:T(8,128)(2,1)S(1)}, u32[]{:S(2)}, u32[]{:S(2)}) collective-permute-start(bf16[4,2,128,128]{3,2,1,0:T(8,128)(2,1)} %pad_maximum_fusion.7), channel_id=1, source_target_pairs={{0,4},{2,6},{4,0},{6,2},{1,5},{3,7},{5,1},{7,3},{8,12},{10,14},{12... | collective-permute-start | bytes 786440 | tf_op jit(solution)/shard_map/ppermute | solution.py:195
  9.4 3.5 %copy-start.24 = (s32[9]{0:T(128)S(1)}, s32[9]{0:T(128)}, u32[]{:S(2)}) copy-start(s32[9]{0:T(128)} %constant.100.clone) | copy-start | bytes 112
  9.4 3.5 %copy-start.25 = (s32[9]{0:T(128)S(1)}, s32[9]{0:T(128)}, u32[]{:S(2)}) copy-start(s32[9]{0:T(128)} %constant.101.clone) | copy-start | bytes 112
  10.2 2.7 %copy-start.27 = (pred[9]{0:T(512)(128)(4,1)S(1)}, pred[9]{0:T(512)(128)(4,1)}, u32[]{:S(2)}) copy-start(pred[9]{0:T(512)(128)(4,1)} %constant.103.clone) | copy-start | bytes 31
  10.2 18.0 %collective-permute-start.2 = (bf16[4,3,128,128]{3,2,1,0:T(8,128)(2,1)}, bf16[4,3,128,128]{3,2,1,0:T(8,128)(2,1)S(1)}, u32[]{:S(2)}, u32[]{:S(2)}) collective-permute-start(bf16[4,3,128,128]{3,2,1,0:T(8,128)(2,1)} %pad_maximum_fusion.2), channel_id=1, source_target_pairs={{0,2},{2,0},{1,3},{3,1},{4,6},{6,4},{5,7},{7,5},{8,10},{10,8},{9,1... | collective-permute-start | bytes 1179656 | tf_op jit(solution)/shard_map/ppermute | solution.py:195
  14.0 19.7 %copy-start.19 = (bf16[2,1,2,128,128]{4,2,1,0,3:T(2,128)(2,1)S(1)}, bf16[2,1,2,128,128]{4,2,1,0,3:T(2,128)(2,1)}, u32[]{:S(2)}) copy-start(bf16[2,1,2,128,128]{4,2,1,0,3:T(2,128)(2,1)} %get-tuple-element.55) | copy-start | bytes 393220
  29.1 4.6 %copy-start.21 = (bf16[2,1,2,128,128]{4,2,1,0,3:T(2,128)(2,1)S(1)}, bf16[2,1,2,128,128]{4,2,1,0,3:T(2,128)(2,1)}, u32[]{:S(2)}) copy-start(bf16[2,1,2,128,128]{4,2,1,0,3:T(2,128)(2,1)} %get-tuple-element.70) | copy-start | bytes 393220
  29.1 4.7 %copy-start.20 = (bf16[2,1,2,128,128]{4,2,1,0,3:T(2,128)(2,1)S(1)}, bf16[2,1,2,128,128]{4,2,1,0,3:T(2,128)(2,1)}, u32[]{:S(2)}) copy-start(bf16[2,1,2,128,128]{4,2,1,0,3:T(2,128)(2,1)} %get-tuple-element.52) | copy-start | bytes 393220
  29.1 22.9 %all-to-all-start = ((bf16[4,6,128,128]{3,2,1,0:T(8,128)(2,1)}), bf16[4,6,128,128]{3,2,1,0:T(8,128)(2,1)S(1)}, u32[]{:S(2)}, u32[]{:S(2)}) async-start(bf16[4,6,128,128]{3,2,1,0:T(8,128)(2,1)} %shard_map.164), calls=%async_computation | async-start | bytes 1572864 | tf_op jit(solution)/shard_map/all_to_all | solution.py:198
  33.0 7.9 %copy-start.12 = (s32[24,32,32]{2,1,0:T(8,128)S(1)}, s32[24,32,32]{2,1,0:T(8,128)}, u32[]{:S(2)}) copy-start(s32[24,32,32]{2,1,0:T(8,128)} %mask_ref.2) | copy-start | bytes 294916
  33.0 7.9 %copy-start.14 = (s32[4,1]{1,0:T(4,128)S(1)}, s32[4,1]{1,0:T(4,128)}, u32[]{:S(2)}) copy-start(s32[4,1]{1,0:T(4,128)} %constant.106.clone.rows_ref) | copy-start | bytes 52
  33.0 7.9 %copy-start.15 = (s32[1,512]{1,0:T(1,128)S(1)}, s32[1,512]{1,0:T(1,128)}, u32[]{:S(2)}) copy-start(s32[1,512]{1,0:T(1,128)} %constant.107.clone.cols_ref) | copy-start | bytes 6148
  33.8 8.0 %copy-start.16 = (bf16[2,1,2,128,128]{4,3,2,0,1:T(8,128)(2,1)}, bf16[2,1,2,128,128]{4,3,2,0,1:T(8,128)(2,1)S(1)}, u32[]{:S(2)}) copy-start(bf16[2,1,2,128,128]{4,3,2,0,1:T(8,128)(2,1)S(1)} %copy.88) | copy-start | bytes 393220
  35.3 15.5 %collective-permute-start.3 = (bf16[4,3,128,128]{3,2,1,0:T(8,128)(2,1)}, bf16[4,3,128,128]{3,2,1,0:T(8,128)(2,1)S(1)}, u32[]{:S(2)}, u32[]{:S(2)}) collective-permute-start(bf16[4,3,128,128]{3,2,1,0:T(8,128)(2,1)} %pad_maximum_fusion.4), channel_id=1, source_target_pairs={{0,2},{2,0},{1,3},{3,1},{4,6},{6,4},{5,7},{7,5},{8,10},{10,8},{9,1... | collective-permute-start | bytes 1179656 | tf_op jit(solution)/shard_map/ppermute | solution.py:195
  38.5 21.6 %collective-permute-start.4 = (bf16[4,2,128,128]{3,2,1,0:T(8,128)(2,1)}, bf16[4,2,128,128]{3,2,1,0:T(8,128)(2,1)S(1)}, u32[]{:S(2)}, u32[]{:S(2)}) collective-permute-start(bf16[4,2,128,128]{3,2,1,0:T(8,128)(2,1)} %pad_maximum_fusion.9), channel_id=1, source_target_pairs={{0,4},{2,6},{4,0},{6,2},{1,5},{3,7},{5,1},{7,3},{8,12},{10,14},{12... | collective-permute-start | bytes 786440 | tf_op jit(solution)/shard_map/ppermute | solution.py:195
  38.5 21.6 %collective-permute-start.5 = (bf16[4,2,128,128]{3,2,1,0:T(8,128)(2,1)}, bf16[4,2,128,128]{3,2,1,0:T(8,128)(2,1)S(1)}, u32[]{:S(2)}, u32[]{:S(2)}) collective-permute-start(bf16[4,2,128,128]{3,2,1,0:T(8,128)(2,1)} %pad_maximum_fusion.10), channel_id=1, source_target_pairs={{0,6},{2,4},{4,2},{6,0},{1,7},{3,5},{5,3},{7,1},{8,14},{10,12},{12... | collective-permute-start | bytes 786440 | tf_op jit(solution)/shard_map/ppermute | solution.py:195
  52.8 22.5 %all-to-all-start.1 = ((bf16[4,10,128,128]{3,2,1,0:T(8,128)(2,1)}), bf16[4,10,128,128]{3,2,1,0:T(8,128)(2,1)S(1)}, u32[]{:S(2)}, u32[]{:S(2)}) async-start(bf16[4,10,128,128]{3,2,1,0:T(8,128)(2,1)} %shard_map.165), calls=%async_computation.1 | async-start | bytes 2621440 | tf_op jit(solution)/shard_map/all_to_all | solution.py:198
  58.6 9.2 %collective-permute-start.9 = (bf16[4,3,128,128]{3,2,1,0:T(8,128)(2,1)S(1)}, bf16[4,3,128,128]{3,2,1,0:T(8,128)(2,1)S(1)}, u32[]{:S(2)}, u32[]{:S(2)}) collective-permute-start(bf16[4,3,128,128]{3,2,1,0:T(8,128)(2,1)S(1)} %pad_maximum_fusion.6), channel_id=1, source_target_pairs={{0,2},{2,0},{1,3},{3,1},{4,6},{6,4},{5,7},{7,5},{8,10},{10,8},{9,1... | collective-permute-start | bytes 1179656 | tf_op jit(solution)/shard_map/ppermute | solution.py:195
  60.0 9.0 %collective-permute-start.8 = (bf16[4,4,128,128]{3,2,1,0:T(8,128)(2,1)}, bf16[4,4,128,128]{3,2,1,0:T(8,128)(2,1)S(1)}, u32[]{:S(2)}, u32[]{:S(2)}) collective-permute-start(bf16[4,4,128,128]{3,2,1,0:T(8,128)(2,1)} %shard_map.166.refs_0_), channel_id=1, source_target_pairs={{0,8},{8,0},{1,9},{9,1},{2,10},{10,2},{3,11},{11,3},{4,12},{12,4},... | collective-permute-start | bytes 1572872 | tf_op jit(solution)/shard_map/ppermute | solution.py:195
  75.3 28.5 %collective-permute-start.10 = (bf16[4,10,128,128]{3,2,1,0:T(8,128)(2,1)S(1)}, bf16[4,10,128,128]{3,2,1,0:T(8,128)(2,1)}, u32[]{:S(2)}, u32[]{:S(2)}) collective-permute-start(bf16[4,10,128,128]{3,2,1,0:T(8,128)(2,1)S(1)} %all-to-all-done.1.q_ref.refs_0_), channel_id=1, source_target_pairs={{0,8},{8,0},{1,9},{9,1},{2,10},{10,2},{3,11},{11,3},{4,12},{12,4},... | collective-permute-start | bytes 3932168 | tf_op jit(solution)/shard_map/ppermute | solution.py:195
  75.3 25.9 %collective-permute-start.6 = (bf16[4,4,128,128]{3,2,1,0:T(8,128)(2,1)}, bf16[4,4,128,128]{3,2,1,0:T(8,128)(2,1)}, u32[]{:S(2)}, u32[]{:S(2)}) collective-permute-start(bf16[4,4,128,128]{3,2,1,0:T(8,128)(2,1)} %shard_map.166.refs_0_), channel_id=1, source_target_pairs={{0,4},{4,0},{1,5},{5,1},{2,6},{6,2},{3,7},{7,3},{8,12},{12,8},{9,1... | collective-permute-start | bytes 1572872 | tf_op jit(solution)/shard_map/ppermute | solution.py:195
  75.5 36.3 %all-to-all-start.2 = ((bf16[4,10,128,128]{3,2,1,0:T(8,128)(2,1)}), bf16[4,10,128,128]{3,2,1,0:T(8,128)(2,1)S(1)}, u32[]{:S(2)}, u32[]{:S(2)}) async-start(bf16[4,10,128,128]{3,2,1,0:T(8,128)(2,1)} %copy-done.1), calls=%async_computation.2 | async-start | bytes 2621440 | tf_op jit(solution)/shard_map/all_to_all | solution.py:198
  79.4 24.4 %copy-start.9 = (f32[2,4,4096]{2,1,0:T(4,128)S(1)}, f32[2,4,4096]{2,1,0:T(4,128)}, u32[]{:S(2)}) copy-start(f32[2,4,4096]{2,1,0:T(4,128)} %copy-done.8) | copy-start | bytes 393220
  111.7 10.4 %copy-start.3 = (bf16[8,128,128]{2,1,0:T(8,128)(2,1)S(1)}, bf16[8,128,128]{2,1,0:T(8,128)(2,1)}, u32[]{:S(2)}) copy-start(bf16[8,128,128]{2,1,0:T(8,128)(2,1)} %copy-done.2) | copy-start | bytes 786436
  111.7 3.0 %collective-permute-start.11 = (bf16[4,10,128,128]{3,2,1,0:T(8,128)(2,1)S(1)}, bf16[4,10,128,128]{3,2,1,0:T(8,128)(2,1)S(1)}, u32[]{:S(2)}, u32[]{:S(2)}) collective-permute-start(bf16[4,10,128,128]{3,2,1,0:T(8,128)(2,1)S(1)} %all-to-all-done.2.q_ref.refs_0_), channel_id=1, source_target_pairs={{0,8},{8,0},{1,9},{9,1},{2,10},{10,2},{3,11},{11,3},{4,12},{12,4},... | collective-permute-start | bytes 3932168 | tf_op jit(solution)/shard_map/ppermute | solution.py:195
  122.1 7.0 %copy-start.5 = (f32[1024,256]{1,0:T(8,128)S(1)}, f32[1024,256]{1,0:T(8,128)}, u32[]{:S(2)}) copy-start(f32[1024,256]{1,0:T(8,128)} %copy-done.4) | copy-start | bytes 3145732
  122.1 7.0 %copy-start.7 = (f32[1024,128]{1,0:T(8,128)S(1)}, f32[1024,128]{1,0:T(8,128)}, u32[]{:S(2)}) copy-start(f32[1024,128]{1,0:T(8,128)} %copy-done.6) | copy-start | bytes 1572868
  123.0 14.0 %all-to-all-start.3 = ((bf16[8,2,128,128]{3,2,1,0:T(8,128)(2,1)}), bf16[8,2,128,128]{3,2,1,0:T(8,128)(2,1)S(1)}, u32[]{:S(2)}, u32[]{:S(2)}) async-start(bf16[8,2,128,128]{3,2,1,0:T(8,128)(2,1)} %copy.73), calls=%async_computation.3 | async-start | bytes 1048576 | tf_op jit(solution)/shard_map/all_to_all | solution.py:198
  127.0 2.1 %collective-permute-start.7 = (bf16[4,4,128,128]{3,2,1,0:T(8,128)(2,1)}, bf16[4,4,128,128]{3,2,1,0:T(8,128)(2,1)S(1)}, u32[]{:S(2)}, u32[]{:S(2)}) collective-permute-start(bf16[4,4,128,128]{3,2,1,0:T(8,128)(2,1)} %collective-permute-done.6.refs_0_), channel_id=1, source_target_pairs={{0,8},{8,0},{1,9},{9,1},{2,10},{10,2},{3,11},{11,3},{4,12},{12,4},... | collective-permute-start | bytes 1572872 | tf_op jit(solution)/shard_map/ppermute | solution.py:195
  137.3 10.3 %all-to-all-start.4 = ((bf16[8,128,128]{2,1,0:T(8,128)(2,1)}), bf16[8,128,128]{2,1,0:T(8,128)(2,1)S(1)}, u32[]{:S(2)}, u32[]{:S(2)}) async-start(bf16[8,128,128]{2,1,0:T(8,128)(2,1)} %shard_map.173), calls=%async_computation.4 | async-start | bytes 524288 | tf_op jit(solution)/shard_map/all_to_all | solution.py:198
  147.7 6.4 %copy-start = (bf16[3072,3072]{1,0:T(8,128)(2,1)S(1)}, bf16[3072,3072]{1,0:T(8,128)(2,1)}, u32[]{:S(2)}) copy-start(bf16[3072,3072]{1,0:T(8,128)(2,1)} %rows_ref.4) | copy-start | bytes 56623108
  (13 other events, 14.5 us)

commit v6 on v5

--- a/solution.py
+++ b/solution.py
@@ -139,28 +139,34 @@
     )(*arrays)
 
 
-def finish_kernel(part_ref, rows_ref, total_ref, out_ref):
+def finish_kernel(step, part_ref, weight_ref, total_ref, out_ref, rows_ref, sems):
+    width = rows_ref.shape[1]
+    first = weight_ref.shape[0] - width
+    copies = []
+    for i in range(rows_ref.shape[0]):
+        source = weight_ref.at[first:, i * step : (i + 1) * step]
+        copies.append(pltpu.make_async_copy(source, rows_ref.at[i], sems.at[i]))
+        copies[i].start()
     joined = jnp.concatenate([part_ref[i] for i in range(part_ref.shape[0])], axis=1)
-    product = jnp.dot(joined, rows_ref[...], preferred_element_type=jnp.float32)
-    out_ref[...] = (total_ref[...] + product).astype(out_ref.dtype)
+    for i, copy in enumerate(copies):
+        copy.wait()
+        at = slice(i * step, (i + 1) * step)
+        product = jnp.dot(joined, rows_ref[i], preferred_element_type=jnp.float32)
+        out_ref[:, at] = (total_ref[:, at] + product).astype(out_ref.dtype)
 
 
 def finish(part, weight, total):
-    pieces, tok, hdim = part.shape
-    width = pieces * hdim
-    last = weight.shape[0] // width - 1
-    step = math.gcd(weight.shape[1], 768)
+    pieces, _, hdim = part.shape
+    step = math.gcd(weight.shape[1], 512)
+    count = weight.shape[1] // step
+    rows = jax.ShapeDtypeStruct((count, pieces * hdim, step), weight.dtype)
     return pl.pallas_call(
-        finish_kernel,
+        functools.partial(finish_kernel, step),
         out_shape=jax.ShapeDtypeStruct(total.shape, jnp.bfloat16),
-        grid=(weight.shape[1] // step,),
-        in_specs=[
-            pl.BlockSpec((pieces, tok, hdim), lambda i: (0, 0, 0)),
-            pl.BlockSpec((width, step), lambda i: (last, i)),
-            pl.BlockSpec((tok, step), lambda i: (0, i)),
-        ],
-        out_specs=pl.BlockSpec((tok, step), lambda i: (0, i)),
-        compiler_params=grant(part, total),
+        in_specs=[VMEM, pl.BlockSpec(memory_space=pl.ANY), VMEM],
+        out_specs=VMEM,
+        scratch_shapes=[pltpu.VMEM(rows.shape, rows.dtype), pltpu.SemaphoreType.DMA((count,))],
+        compiler_params=grant(part, rows, total),
     )(part, weight, total)
 
 
@@ -245,24 +251,24 @@
     both_pick += tuple((i, 6 + 2 * r, 7 + 2 * r, 4 * i + 2 + r) for i in range(half) for r in range(2))
     axes = gather + ("c",)
 
-    far0 = cross(0)
     own2 = own(2)
+    far0 = cross(0, own2[0][0])
     got2 = spread(pack(*own2), flat)
     bias2 = bias_of(2, *far0)
     own0 = pack(*own(0, own2[1][0]), *((f, range(2)) for f in far0))
     got2 = after(got2, bias2, own0)
     kv2 = pack((got2, (1, 2, 4, 5)))
-    far1 = cross(1, *far0)
+    far1 = cross(1, own2[1][0])
     got0 = spread(after(own0, kv2), flat)
     bias0 = bias_of(0, *far1)
     state2 = attend(home, bias2, got2, gathered(kv2, axes), near_pick, None, False)
     own1 = pack(*own(1, *far0), *((f, range(2)) for f in far1))
     got0 = after(got0, bias0, own1, state2)
-    far2 = across(after(kv2, *far1), "zh", 1)
+    far2 = across(kv2, "zh", 1)
     got1 = spread(after(own1, got0), flat)
-    bias1 = bias_of(1, far2)
     out0 = attend(home, bias0, got0, gathered(got0, axes), both_pick, None, True)
-    got1 = after(got1, bias1, out0)
+    bias1 = bias_of(1, far2, out0)
+    got1 = after(got1, bias1)
     far2 = gathered(far2, axes)
     out1 = attend(home, bias1, got1, gathered(got1, axes), both_pick, None, True)
     ready = jnp.stack([out0, out1], axis=1)

time: 158 us -> 149 us (0.943)
  waiting for transfers between devices: 61.5 us -> 54.6 us
  local copies, waits for them, and re-layouts: 20.8 us -> 16.7 us
    ppermute x12, waiting for transfers between devices: 57.6 us -> 50.7 us  [across(): return lax.ppermute(a, axis, swap(n, bit))]
    unnamed x74 -> x72, local copies, waits for them, and re-layouts: 15 us -> 11.7 us
  transfers between devices with their start and end apart: 17 -> 17, of which waited for: 9 -> 9; matrix products, arithmetic and copies ran while one was open for 10% -> 9% of each run, Pallas kernels for 15% -> 15%
where the time goes in v6:
time: 149 us; the launch traced here: 148 us
  waiting for transfers between devices  54.6 us (37%)
  Pallas kernels  33 us (22%)
  starting transfers between devices  31.1 us (21%)
  local copies, waits for them, and re-layouts  16.7 us (11%)
  other arithmetic  6.62 us (4%)
  matrix products  5.66 us (4%)
    ppermute x12, waiting for transfers between devices, across(): return lax.ppermute(a, axis, swap(n, bit))  50.7 us
    pallas_call x4, Pallas kernels, attend(): pl.pallas_call(functools.partial(attend_kernel, picks, len(arrays), scale...  23.5 us
    all_to_all x5, starting transfers between devices, spread(): return lax.all_to_all(a, axes, split_axis=0, concat_axis=0, tiled=True)  19.3 us
    ppermute x12, starting transfers between devices, across(): return lax.ppermute(a, axis, swap(n, bit))  11.8 us
    unnamed x72, local copies, waits for them, and re-layouts  11.7 us
    another operation x10, other arithmetic, pieces(): return jnp.stack(out, axis=1)  6.56 us
    dot_general x1, matrix products, shards(): jnp.dot(early, out_weight[:rows], preferred_element_type=jnp.float32)  5.66 us
    all_to_all x5, waiting for transfers between devices, spread(): return lax.all_to_all(a, axes, split_axis=0, concat_axis=0, tiled=True)  3.92 us
  transfers between devices with their start and end apart: 17, of which 9 were waited for; matrix products, arithmetic and copies ran while one was open for 9% of the time, Pallas kernels for 15%

profile of v6, /device:TPU:0, one launch (start us, length us, event | category | flops | bytes accessed | tf_op | source)
XLA Modules:
  0.0 148.4 jit_solution(5867551473117851112)
XLA Ops:
  0.0 1.3 fusion.2
  4.4 4.1 %collective-permute-start = (bf16[4,2,128,128]{3,2,1,0:T(8,128)(2,1)}, bf16[4,2,128,128]{3,2,1,0:T(8,128)(2,1)S(1)}, u32[]{:S(2)}, u32[]{:S(2)}) collective-permute-start(bf16[4,2,128,128]{3,2,1,0:T(8,128)(2,1)} %pad_maximum_fusion.7), channel_id=1, source_target_pairs={{0,4},{2,6},{4,0},{6,2},{1,5},{3,7},{5,1},{7,3},{8,12},{10,14},{12... | collective-permute-start | bytes 786440 | tf_op jit(solution)/shard_map/ppermute | solution.py:201
  8.5 1.3 collective-permute-start.1
  11.4 1.0 constant_dynamic-slice_fusion
  14.1 17.2 %collective-permute-done.2.refs_1_ = bf16[4,3,128,128]{3,2,1,0:T(8,128)(2,1)S(1)} collective-permute-done((bf16[4,3,128,128]{3,2,1,0:T(8,128)(2,1)}, bf16[4,3,128,128]{3,2,1,0:T(8,128)(2,1)S(1)}, u32[]{:S(2)}, u32[]{:S(2)}) %collective-permute-start.2) | collective-permute-done | bytes 393248 | tf_op jit(solution)/shard_map/ppermute | solution.py:201
  32.3 3.9 %all-to-all-start = ((bf16[4,6,128,128]{3,2,1,0:T(8,128)(2,1)}), bf16[4,6,128,128]{3,2,1,0:T(8,128)(2,1)S(1)}, u32[]{:S(2)}, u32[]{:S(2)}) async-start(bf16[4,6,128,128]{3,2,1,0:T(8,128)(2,1)} %shard_map.164), calls=%async_computation | async-start | bytes 1572864 | tf_op jit(solution)/shard_map/all_to_all | solution.py:204
  37.9 2.1 %collective-permute-start.9 = (bf16[4,3,128,128]{3,2,1,0:T(8,128)(2,1)}, bf16[4,3,128,128]{3,2,1,0:T(8,128)(2,1)S(1)}, u32[]{:S(2)}, u32[]{:S(2)}) collective-permute-start(bf16[4,3,128,128]{3,2,1,0:T(8,128)(2,1)} %pad_maximum_fusion.6), channel_id=1, source_target_pairs={{0,2},{2,0},{1,3},{3,1},{4,6},{6,4},{5,7},{7,5},{8,10},{10,8},{9,1... | collective-permute-start | bytes 1179656 | tf_op jit(solution)/shard_map/ppermute | solution.py:201
  40.0 0.9 shard_map.163.bias_ref
  41.0 2.1 %collective-permute-start.7 = (bf16[4,2,128,128]{3,2,1,0:T(8,128)(2,1)}, bf16[4,2,128,128]{3,2,1,0:T(8,128)(2,1)S(1)}, u32[]{:S(2)}, u32[]{:S(2)}) collective-permute-start(bf16[4,2,128,128]{3,2,1,0:T(8,128)(2,1)} %pad_maximum_fusion.9), channel_id=1, source_target_pairs={{0,4},{2,6},{4,0},{6,2},{1,5},{3,7},{5,1},{7,3},{8,12},{10,14},{12... | collective-permute-start | bytes 786440 | tf_op jit(solution)/shard_map/ppermute | solution.py:201
  43.1 1.5 %collective-permute-start.8 = (bf16[4,2,128,128]{3,2,1,0:T(8,128)(2,1)}, bf16[4,2,128,128]{3,2,1,0:T(8,128)(2,1)S(1)}, u32[]{:S(2)}, u32[]{:S(2)}) collective-permute-start(bf16[4,2,128,128]{3,2,1,0:T(8,128)(2,1)} %pad_maximum_fusion.10), channel_id=1, source_target_pairs={{0,6},{2,4},{4,2},{6,0},{1,7},{3,5},{5,3},{7,1},{8,14},{10,12},{12... | collective-permute-start | bytes 786440 | tf_op jit(solution)/shard_map/ppermute | solution.py:201
  44.6 10.2 %collective-permute-done.3.refs_1_ = bf16[4,3,128,128]{3,2,1,0:T(8,128)(2,1)S(1)} collective-permute-done((bf16[4,3,128,128]{3,2,1,0:T(8,128)(2,1)S(1)}, bf16[4,3,128,128]{3,2,1,0:T(8,128)(2,1)S(1)}, u32[]{:S(2)}, u32[]{:S(2)}) %collective-permute-start.3) | collective-permute-done | bytes 393248 | tf_op jit(solution)/shard_map/ppermute | solution.py:201
  54.8 1.2 shard_map.165
  56.8 4.3 %all-to-all-start.1 = ((bf16[4,10,128,128]{3,2,1,0:T(8,128)(2,1)}), bf16[4,10,128,128]{3,2,1,0:T(8,128)(2,1)S(1)}, u32[]{:S(2)}, u32[]{:S(2)}) async-start(bf16[4,10,128,128]{3,2,1,0:T(8,128)(2,1)} %shard_map.165), calls=%async_computation.1 | async-start | bytes 2621440 | tf_op jit(solution)/shard_map/all_to_all | solution.py:204
  61.9 1.1 pad_maximum_fusion.5.refs_0_
  63.1 4.6 %collective-permute-done.8.refs_3_ = bf16[4,2,128,128]{3,2,1,0:T(8,128)(2,1)S(1)} collective-permute-done((bf16[4,2,128,128]{3,2,1,0:T(8,128)(2,1)}, bf16[4,2,128,128]{3,2,1,0:T(8,128)(2,1)S(1)}, u32[]{:S(2)}, u32[]{:S(2)}) %collective-permute-start.8) | collective-permute-done | bytes 262176 | tf_op jit(solution)/shard_map/ppermute | solution.py:201
  67.9 0.9 shard_map.168.bias_ref
  70.0 4.5 %shard_map.167 = (f32[1024,128]{1,0:T(8,128)S(1)}, f32[1024,256]{1,0:T(8,128)S(1)}) custom-call(s32[8]{0:T(128)S(1)} %reshape.68.place_ref, f32[2,4,4096]{2,1,0:T(4,128)S(1)} %shard_map.163.bias_ref, bf16[4,6,128,128]{3,2,1,0:T(8,128)(2,1)S(1)} %all-to-all-done.refs_0_.q_ref, bf16[4,4,128,128]{3,2,1,0:T(8,128)(2,1)} %shard_map.166.refs_0_, ...), custom_call_target="tpu_custom_call" | custom-call | flops 1024 | bytes 4096 | tf_op jit(solution)/shard_map/pallas_call | solution.py:110
  74.6 1.0 copy-done.4
  76.5 3.9 %all-to-all-start.2 = ((bf16[4,10,128,128]{3,2,1,0:T(8,128)(2,1)}), bf16[4,10,128,128]{3,2,1,0:T(8,128)(2,1)S(1)}, u32[]{:S(2)}, u32[]{:S(2)}) async-start(bf16[4,10,128,128]{3,2,1,0:T(8,128)(2,1)} %copy-done.1), calls=%async_computation.2 | async-start | bytes 2621440 | tf_op jit(solution)/shard_map/all_to_all | solution.py:204
  81.2 7.2 %shard_map.170 = bf16[8,128,128]{2,1,0:T(8,128)(2,1)S(1)} custom-call(s32[8]{0:T(128)S(1)} %reshape.68.place_ref, f32[2,4,4096]{2,1,0:T(4,128)S(1)} %copy-done.9, bf16[4,10,128,128]{3,2,1,0:T(8,128)(2,1)S(1)} %all-to-all-done.1.q_ref.refs_0_, bf16[4,10,128,128]{3,2,1,0:T(8,128)(2,1)S(1)} %all-to-all-done.1.q_ref.refs_0_, ...), custom_call_target="tpu_custom_call" | custom-call | flops 1024 | bytes 4096 | tf_op jit(solution)/shard_map/pallas_call | solution.py:110
  89.2 13.0 %collective-permute-done.4.refs_0_ = bf16[4,4,128,128]{3,2,1,0:T(8,128)(2,1)} collective-permute-done((bf16[4,4,128,128]{3,2,1,0:T(8,128)(2,1)}, bf16[4,4,128,128]{3,2,1,0:T(8,128)(2,1)}, u32[]{:S(2)}, u32[]{:S(2)}) %collective-permute-start.4) | collective-permute-done | bytes 524320 | tf_op jit(solution)/shard_map/ppermute | solution.py:201
  103.3 3.0 %collective-permute-done.11.refs_1_ = bf16[4,10,128,128]{3,2,1,0:T(8,128)(2,1)S(1)} collective-permute-done((bf16[4,10,128,128]{3,2,1,0:T(8,128)(2,1)S(1)}, bf16[4,10,128,128]{3,2,1,0:T(8,128)(2,1)S(1)}, u32[]{:S(2)}, u32[]{:S(2)}) %collective-permute-start.11) | collective-permute-done | bytes 1310752 | tf_op jit(solution)/shard_map/ppermute | solution.py:201
  106.3 6.4 %shard_map.172 = bf16[8,128,128]{2,1,0:T(8,128)(2,1)S(1)} custom-call(s32[8]{0:T(128)S(1)} %reshape.68.place_ref, f32[2,4,4096]{2,1,0:T(4,128)S(1)} %shard_map.171.bias_ref, bf16[4,10,128,128]{3,2,1,0:T(8,128)(2,1)S(1)} %all-to-all-done.2.q_ref.refs_0_, bf16[4,10,128,128]{3,2,1,0:T(8,128)(2,1)S(1)} %all-to-all-done.2.q_ref.refs_0_, ...), custom_call_target="tpu_custom_call" | custom-call | flops 1024 | bytes 4096 | tf_op jit(solution)/shard_map/pallas_call | solution.py:110
  113.6 3.8 %all-to-all-start.3 = ((bf16[8,2,128,128]{3,2,1,0:T(8,128)(2,1)}), bf16[8,2,128,128]{3,2,1,0:T(8,128)(2,1)S(1)}, u32[]{:S(2)}, u32[]{:S(2)}) async-start(bf16[8,2,128,128]{3,2,1,0:T(8,128)(2,1)} %copy.73), calls=%async_computation.3 | async-start | bytes 1048576 | tf_op jit(solution)/shard_map/all_to_all | solution.py:204
  117.5 2.1 %collective-permute-done.5.refs_1_ = bf16[4,4,128,128]{3,2,1,0:T(8,128)(2,1)S(1)} collective-permute-done((bf16[4,4,128,128]{3,2,1,0:T(8,128)(2,1)}, bf16[4,4,128,128]{3,2,1,0:T(8,128)(2,1)S(1)}, u32[]{:S(2)}, u32[]{:S(2)}) %collective-permute-start.5) | collective-permute-done | bytes 524320 | tf_op jit(solution)/shard_map/ppermute | solution.py:201
  119.6 5.3 %shard_map.173 = bf16[8,128,128]{2,1,0:T(8,128)(2,1)} custom-call(s32[8]{0:T(128)S(1)} %reshape.68.place_ref, f32[2,4,4096]{2,1,0:T(4,128)S(1)} %shard_map.163.bias_ref, bf16[4,6,128,128]{3,2,1,0:T(8,128)(2,1)S(1)} %all-to-all-done.refs_0_.q_ref, bf16[4,4,128,128]{3,2,1,0:T(8,128)(2,1)} %collective-permute-done.4.refs_0_, ...), custom_call_target="tpu_custom_call" | custom-call | flops 1024 | bytes 4096 | tf_op jit(solution)/shard_map/pallas_call | solution.py:110
  124.9 2.7 %all-to-all-done.3 = bf16[8,2,128,128]{3,2,1,0:T(8,128)(2,1)S(1)} async-done(((bf16[8,2,128,128]{3,2,1,0:T(8,128)(2,1)}), bf16[8,2,128,128]{3,2,1,0:T(8,128)(2,1)S(1)}, u32[]{:S(2)}, u32[]{:S(2)}) %all-to-all-start.3) | async-done | bytes 524320 | tf_op jit(solution)/shard_map/all_to_all | solution.py:204
  127.9 3.4 %all-to-all-start.4 = ((bf16[8,128,128]{2,1,0:T(8,128)(2,1)}), bf16[8,128,128]{2,1,0:T(8,128)(2,1)S(1)}, u32[]{:S(2)}, u32[]{:S(2)}) async-start(bf16[8,128,128]{2,1,0:T(8,128)(2,1)} %shard_map.173), calls=%async_computation.4 | async-start | bytes 524288 | tf_op jit(solution)/shard_map/all_to_all | solution.py:204
  131.3 5.7 %fusion.total_ref = f32[128,3072]{1,0:T(8,128)S(1)} fusion(bf16[128,2048]{0,1:T(8,128)(2,1)S(1)} %bitcast.78, bf16[3072,3072]{1,0:T(8,128)(2,1)} %weight_ref.1), kind=kOutput, calls=%fused_computation | convolution fusion | flops 1610612736 | bytes 14680064 | tf_op jit(solution)/shard_map/dot_general | solution.py:281
  136.9 1.2 all-to-all-done.4.part_ref
  138.2 6.4 %copy-done = bf16[3072,3072]{1,0:T(8,128)(2,1)S(1)} copy-done((bf16[3072,3072]{1,0:T(8,128)(2,1)S(1)}, bf16[3072,3072]{1,0:T(8,128)(2,1)}, u32[]{:S(2)}) %copy-start) | copy-done | bytes 18874392
  144.6 3.6 %shard_map.174 = bf16[128,3072]{1,0:T(8,128)(2,1)} custom-call(bf16[8,128,128]{2,1,0:T(8,128)(2,1)S(1)} %all-to-all-done.4.part_ref, bf16[3072,3072]{1,0:T(8,128)(2,1)S(1)} %copy-done, f32[128,3072]{1,0:T(8,128)S(1)} %fusion.total_ref), custom_call_target="tpu_custom_call" | custom-call | tf_op jit(solution)/shard_map/pallas_call | solution.py:163
  (111 shorter events, 16.5 us)
Async XLA Ops:
  4.4 33.5 %collective-permute-start = (bf16[4,2,128,128]{3,2,1,0:T(8,128)(2,1)}, bf16[4,2,128,128]{3,2,1,0:T(8,128)(2,1)S(1)}, u32[]{:S(2)}, u32[]{:S(2)}) collective-permute-start(bf16[4,2,128,128]{3,2,1,0:T(8,128)(2,1)} %pad_maximum_fusion.7), channel_id=1, source_target_pairs={{0,4},{2,6},{4,0},{6,2},{1,5},{3,7},{5,1},{7,3},{8,12},{10,14},{12... | collective-permute-start | bytes 786440 | tf_op jit(solution)/shard_map/ppermute | solution.py:201
  8.5 29.4 %collective-permute-start.1 = (bf16[4,2,128,128]{3,2,1,0:T(8,128)(2,1)}, bf16[4,2,128,128]{3,2,1,0:T(8,128)(2,1)S(1)}, u32[]{:S(2)}, u32[]{:S(2)}) collective-permute-start(bf16[4,2,128,128]{3,2,1,0:T(8,128)(2,1)} %pad_maximum_fusion.8), channel_id=1, source_target_pairs={{0,6},{2,4},{4,2},{6,0},{1,7},{3,5},{5,3},{7,1},{8,14},{10,12},{12... | collective-permute-start | bytes 786440 | tf_op jit(solution)/shard_map/ppermute | solution.py:201
  10.7 20.6 %collective-permute-start.2 = (bf16[4,3,128,128]{3,2,1,0:T(8,128)(2,1)}, bf16[4,3,128,128]{3,2,1,0:T(8,128)(2,1)S(1)}, u32[]{:S(2)}, u32[]{:S(2)}) collective-permute-start(bf16[4,3,128,128]{3,2,1,0:T(8,128)(2,1)} %pad_maximum_fusion.2), channel_id=1, source_target_pairs={{0,2},{2,0},{1,3},{3,1},{4,6},{6,4},{5,7},{7,5},{8,10},{10,8},{9,1... | collective-permute-start | bytes 1179656 | tf_op jit(solution)/shard_map/ppermute | solution.py:201
  11.4 2.8 %copy-start.23 = (s32[9]{0:T(128)S(1)}, s32[9]{0:T(128)}, u32[]{:S(2)}) copy-start(s32[9]{0:T(128)} %constant.100.clone) | copy-start | bytes 112
  11.4 2.7 %copy-start.24 = (s32[9]{0:T(128)S(1)}, s32[9]{0:T(128)}, u32[]{:S(2)}) copy-start(s32[9]{0:T(128)} %constant.101.clone) | copy-start | bytes 112
  32.3 4.8 %copy-start.20 = (bf16[4,3,128,128]{3,2,1,0:T(8,128)(2,1)S(1)}, bf16[4,3,128,128]{3,2,1,0:T(8,128)(2,1)}, u32[]{:S(2)}) copy-start(bf16[4,3,128,128]{3,2,1,0:T(8,128)(2,1)} %pad_maximum_fusion.4) | copy-start | bytes 1179652
  32.3 23.7 %all-to-all-start = ((bf16[4,6,128,128]{3,2,1,0:T(8,128)(2,1)}), bf16[4,6,128,128]{3,2,1,0:T(8,128)(2,1)S(1)}, u32[]{:S(2)}, u32[]{:S(2)}) async-start(bf16[4,6,128,128]{3,2,1,0:T(8,128)(2,1)} %shard_map.164), calls=%async_computation | async-start | bytes 1572864 | tf_op jit(solution)/shard_map/all_to_all | solution.py:204
  36.2 3.8 %copy-start.10 = (s32[24,32,32]{2,1,0:T(8,128)S(1)}, s32[24,32,32]{2,1,0:T(8,128)}, u32[]{:S(2)}) copy-start(s32[24,32,32]{2,1,0:T(8,128)} %mask_ref.2) | copy-start | bytes 294916
  36.2 3.8 %copy-start.13 = (s32[4,1]{1,0:T(4,128)S(1)}, s32[4,1]{1,0:T(4,128)}, u32[]{:S(2)}) copy-start(s32[4,1]{1,0:T(4,128)} %constant.106.clone.rows_ref) | copy-start | bytes 52
  36.2 3.8 %copy-start.14 = (s32[1,512]{1,0:T(1,128)S(1)}, s32[1,512]{1,0:T(1,128)}, u32[]{:S(2)}) copy-start(s32[1,512]{1,0:T(1,128)} %constant.107.clone.cols_ref) | copy-start | bytes 6148
  37.1 17.7 %collective-permute-start.3 = (bf16[4,3,128,128]{3,2,1,0:T(8,128)(2,1)S(1)}, bf16[4,3,128,128]{3,2,1,0:T(8,128)(2,1)S(1)}, u32[]{:S(2)}, u32[]{:S(2)}) collective-permute-start(bf16[4,3,128,128]{3,2,1,0:T(8,128)(2,1)S(1)} %copy-done.20), channel_id=1, source_target_pairs={{0,2},{2,0},{1,3},{3,1},{4,6},{6,4},{5,7},{7,5},{8,10},{10,8},{9,1... | collective-permute-start | bytes 1179656 | tf_op jit(solution)/shard_map/ppermute | solution.py:201
  37.9 29.8 %collective-permute-start.9 = (bf16[4,3,128,128]{3,2,1,0:T(8,128)(2,1)}, bf16[4,3,128,128]{3,2,1,0:T(8,128)(2,1)S(1)}, u32[]{:S(2)}, u32[]{:S(2)}) collective-permute-start(bf16[4,3,128,128]{3,2,1,0:T(8,128)(2,1)} %pad_maximum_fusion.6), channel_id=1, source_target_pairs={{0,2},{2,0},{1,3},{3,1},{4,6},{6,4},{5,7},{7,5},{8,10},{10,8},{9,1... | collective-permute-start | bytes 1179656 | tf_op jit(solution)/shard_map/ppermute | solution.py:201
  41.0 22.1 %collective-permute-start.7 = (bf16[4,2,128,128]{3,2,1,0:T(8,128)(2,1)}, bf16[4,2,128,128]{3,2,1,0:T(8,128)(2,1)S(1)}, u32[]{:S(2)}, u32[]{:S(2)}) collective-permute-start(bf16[4,2,128,128]{3,2,1,0:T(8,128)(2,1)} %pad_maximum_fusion.9), channel_id=1, source_target_pairs={{0,4},{2,6},{4,0},{6,2},{1,5},{3,7},{5,1},{7,3},{8,12},{10,14},{12... | collective-permute-start | bytes 786440 | tf_op jit(solution)/shard_map/ppermute | solution.py:201
  43.1 24.7 %collective-permute-start.8 = (bf16[4,2,128,128]{3,2,1,0:T(8,128)(2,1)}, bf16[4,2,128,128]{3,2,1,0:T(8,128)(2,1)S(1)}, u32[]{:S(2)}, u32[]{:S(2)}) collective-permute-start(bf16[4,2,128,128]{3,2,1,0:T(8,128)(2,1)} %pad_maximum_fusion.10), channel_id=1, source_target_pairs={{0,6},{2,4},{4,2},{6,0},{1,7},{3,5},{5,3},{7,1},{8,14},{10,12},{12... | collective-permute-start | bytes 786440 | tf_op jit(solution)/shard_map/ppermute | solution.py:201
  56.8 4.3 %copy-start.21 = (s32[2,4]{1,0:T(2,128)S(1)}, s32[2,4]{1,0:T(2,128)}, u32[]{:S(2)}) copy-start(s32[2,4]{1,0:T(2,128)} %constant.104.clone) | copy-start | bytes 100
  56.8 4.3 %copy-start.22 = (s32[2,4]{1,0:T(2,128)S(1)}, s32[2,4]{1,0:T(2,128)}, u32[]{:S(2)}) copy-start(s32[2,4]{1,0:T(2,128)} %constant.105.clone) | copy-start | bytes 100
  56.8 4.3 %copy-start.19 = (bf16[2,1,2,128,128]{4,2,1,0,3:T(2,128)(2,1)S(1)}, bf16[2,1,2,128,128]{4,2,1,0,3:T(2,128)(2,1)}, u32[]{:S(2)}) copy-start(bf16[2,1,2,128,128]{4,2,1,0,3:T(2,128)(2,1)} %get-tuple-element.55) | copy-start | bytes 393220
  56.8 19.5 %all-to-all-start.1 = ((bf16[4,10,128,128]{3,2,1,0:T(8,128)(2,1)}), bf16[4,10,128,128]{3,2,1,0:T(8,128)(2,1)S(1)}, u32[]{:S(2)}, u32[]{:S(2)}) async-start(bf16[4,10,128,128]{3,2,1,0:T(8,128)(2,1)} %shard_map.165), calls=%async_computation.1 | async-start | bytes 2621440 | tf_op jit(solution)/shard_map/all_to_all | solution.py:204
  61.9 6.0 %copy-start.11 = (s32[24,32,32]{2,1,0:T(8,128)S(1)}, s32[24,32,32]{2,1,0:T(8,128)}, u32[]{:S(2)}) copy-start(s32[24,32,32]{2,1,0:T(8,128)} %mask_ref.2) | copy-start | bytes 294916
  67.8 2.2 %collective-permute-start.6 = (bf16[4,4,128,128]{3,2,1,0:T(8,128)(2,1)}, bf16[4,4,128,128]{3,2,1,0:T(8,128)(2,1)S(1)}, u32[]{:S(2)}, u32[]{:S(2)}) collective-permute-start(bf16[4,4,128,128]{3,2,1,0:T(8,128)(2,1)} %shard_map.166.refs_0_), channel_id=1, source_target_pairs={{0,8},{8,0},{1,9},{9,1},{2,10},{10,2},{3,11},{11,3},{4,12},{12,4},... | collective-permute-start | bytes 1572872 | tf_op jit(solution)/shard_map/ppermute | solution.py:201
  76.3 4.0 %collective-permute-start.10 = (bf16[4,10,128,128]{3,2,1,0:T(8,128)(2,1)S(1)}, bf16[4,10,128,128]{3,2,1,0:T(8,128)(2,1)}, u32[]{:S(2)}, u32[]{:S(2)}) collective-permute-start(bf16[4,10,128,128]{3,2,1,0:T(8,128)(2,1)S(1)} %all-to-all-done.1.q_ref.refs_0_), channel_id=1, source_target_pairs={{0,8},{8,0},{1,9},{9,1},{2,10},{10,2},{3,11},{11,3},{4,12},{12,4},... | collective-permute-start | bytes 3932168 | tf_op jit(solution)/shard_map/ppermute | solution.py:201
  76.5 25.7 %collective-permute-start.4 = (bf16[4,4,128,128]{3,2,1,0:T(8,128)(2,1)}, bf16[4,4,128,128]{3,2,1,0:T(8,128)(2,1)}, u32[]{:S(2)}, u32[]{:S(2)}) collective-permute-start(bf16[4,4,128,128]{3,2,1,0:T(8,128)(2,1)} %shard_map.166.refs_0_), channel_id=1, source_target_pairs={{0,4},{4,0},{1,5},{5,1},{2,6},{6,2},{3,7},{7,3},{8,12},{12,8},{9,1... | collective-permute-start | bytes 1572872 | tf_op jit(solution)/shard_map/ppermute | solution.py:201
  76.5 26.7 %all-to-all-start.2 = ((bf16[4,10,128,128]{3,2,1,0:T(8,128)(2,1)}), bf16[4,10,128,128]{3,2,1,0:T(8,128)(2,1)S(1)}, u32[]{:S(2)}, u32[]{:S(2)}) async-start(bf16[4,10,128,128]{3,2,1,0:T(8,128)(2,1)} %copy-done.1), calls=%async_computation.2 | async-start | bytes 2621440 | tf_op jit(solution)/shard_map/all_to_all | solution.py:204
  81.2 21.0 %copy-start.12 = (s32[24,32,32]{2,1,0:T(8,128)S(1)}, s32[24,32,32]{2,1,0:T(8,128)}, u32[]{:S(2)}) copy-start(s32[24,32,32]{2,1,0:T(8,128)} %mask_ref.2) | copy-start | bytes 294916
  103.1 9.6 %copy-start.3 = (bf16[8,128,128]{2,1,0:T(8,128)(2,1)S(1)}, bf16[8,128,128]{2,1,0:T(8,128)(2,1)}, u32[]{:S(2)}) copy-start(bf16[8,128,128]{2,1,0:T(8,128)(2,1)} %copy-done.2) | copy-start | bytes 786436
  103.2 3.1 %collective-permute-start.11 = (bf16[4,10,128,128]{3,2,1,0:T(8,128)(2,1)S(1)}, bf16[4,10,128,128]{3,2,1,0:T(8,128)(2,1)S(1)}, u32[]{:S(2)}, u32[]{:S(2)}) collective-permute-start(bf16[4,10,128,128]{3,2,1,0:T(8,128)(2,1)S(1)} %all-to-all-done.2.q_ref.refs_0_), channel_id=1, source_target_pairs={{0,8},{8,0},{1,9},{9,1},{2,10},{10,2},{3,11},{11,3},{4,12},{12,4},... | collective-permute-start | bytes 3932168 | tf_op jit(solution)/shard_map/ppermute | solution.py:201
  112.7 6.9 %copy-start.5 = (f32[1024,256]{1,0:T(8,128)S(1)}, f32[1024,256]{1,0:T(8,128)}, u32[]{:S(2)}) copy-start(f32[1024,256]{1,0:T(8,128)} %copy-done.4) | copy-start | bytes 3145732
  112.7 6.9 %copy-start.7 = (f32[1024,128]{1,0:T(8,128)S(1)}, f32[1024,128]{1,0:T(8,128)}, u32[]{:S(2)}) copy-start(f32[1024,128]{1,0:T(8,128)} %copy-done.6) | copy-start | bytes 1572868
  113.6 13.9 %all-to-all-start.3 = ((bf16[8,2,128,128]{3,2,1,0:T(8,128)(2,1)}), bf16[8,2,128,128]{3,2,1,0:T(8,128)(2,1)S(1)}, u32[]{:S(2)}, u32[]{:S(2)}) async-start(bf16[8,2,128,128]{3,2,1,0:T(8,128)(2,1)} %copy.73), calls=%async_computation.3 | async-start | bytes 1048576 | tf_op jit(solution)/shard_map/all_to_all | solution.py:204
  117.5 2.1 %collective-permute-start.5 = (bf16[4,4,128,128]{3,2,1,0:T(8,128)(2,1)}, bf16[4,4,128,128]{3,2,1,0:T(8,128)(2,1)S(1)}, u32[]{:S(2)}, u32[]{:S(2)}) collective-permute-start(bf16[4,4,128,128]{3,2,1,0:T(8,128)(2,1)} %collective-permute-done.4.refs_0_), channel_id=1, source_target_pairs={{0,8},{8,0},{1,9},{9,1},{2,10},{10,2},{3,11},{11,3},{4,12},{12,4},... | collective-permute-start | bytes 1572872 | tf_op jit(solution)/shard_map/ppermute | solution.py:201
  127.9 10.3 %all-to-all-start.4 = ((bf16[8,128,128]{2,1,0:T(8,128)(2,1)}), bf16[8,128,128]{2,1,0:T(8,128)(2,1)S(1)}, u32[]{:S(2)}, u32[]{:S(2)}) async-start(bf16[8,128,128]{2,1,0:T(8,128)(2,1)} %shard_map.173), calls=%async_computation.4 | async-start | bytes 524288 | tf_op jit(solution)/shard_map/all_to_all | solution.py:204
  138.2 6.4 %copy-start = (bf16[3072,3072]{1,0:T(8,128)(2,1)S(1)}, bf16[3072,3072]{1,0:T(8,128)(2,1)}, u32[]{:S(2)}) copy-start(bf16[3072,3072]{1,0:T(8,128)(2,1)} %weight_ref.1) | copy-start | bytes 56623108
  (12 other events, 14.4 us)

commit v7 on v6

--- a/solution.py
+++ b/solution.py
@@ -125,7 +125,7 @@
             at += 1
 
 
-def pack(*takes):
+def pack(*takes, cost=10**6):
     arrays = [a for a, _ in takes]
     first = arrays[0]
     count = sum(len(parts) for _, parts in takes)
@@ -135,7 +135,7 @@
         in_specs=[VMEM] * len(arrays),
         out_specs=VMEM,
         compiler_params=grant(*arrays),
-        cost_estimate=pl.CostEstimate(flops=10**6, bytes_accessed=10**4, transcendentals=0),
+        cost_estimate=pl.CostEstimate(flops=cost, bytes_accessed=10**4, transcendentals=0),
     )(*arrays)
 
 
@@ -163,10 +163,10 @@
     return pl.pallas_call(
         functools.partial(finish_kernel, step),
         out_shape=jax.ShapeDtypeStruct(total.shape, jnp.bfloat16),
-        in_specs=[VMEM, pl.BlockSpec(memory_space=pl.ANY), VMEM],
+        in_specs=[VMEM, pl.BlockSpec(memory_space=pltpu.HBM), VMEM],
         out_specs=VMEM,
         scratch_shapes=[pltpu.VMEM(rows.shape, rows.dtype), pltpu.SemaphoreType.DMA((count,))],
-        compiler_params=grant(part, rows, total),
+        compiler_params=pltpu.CompilerParams(vmem_limit_bytes=50 * 2**20),
     )(part, weight, total)
 
 
@@ -235,8 +235,7 @@
 
     def cross(j, *before):
         halves = [pieces((keys, values), j, b) for b in range(2)]
-        if before:
-            halves = after(halves, *before)
+        halves = halves[:1] + after(halves[1:], *before) if j == 0 else after(halves, *before)
         return [across(h, ("zh", "zl"), 2 + b) for b, h in enumerate(halves)]
 
     def own(j, *before):
@@ -252,7 +251,7 @@
     axes = gather + ("c",)
 
     own2 = own(2)
-    far0 = cross(0, own2[0][0])
+    far0 = cross(0, own2[1][0])
     got2 = spread(pack(*own2), flat)
     bias2 = bias_of(2, *far0)
     own0 = pack(*own(0, own2[1][0]), *((f, range(2)) for f in far0))

time: 149 us -> 141 us (0.946)
  waiting for transfers between devices: 54.6 us -> 46.3 us
  local copies, waits for them, and re-layouts: 16.7 us -> 13.1 us
  starting transfers between devices: 31.1 us -> 33.9 us
    ppermute x12, waiting for transfers between devices: 50.7 us -> 42.2 us  [across(): return lax.ppermute(a, axis, swap(n, bit))]
    unnamed x72 -> x68, local copies, waits for them, and re-layouts: 11.7 us -> 6.99 us
    ppermute x12, starting transfers between devices: 11.8 us -> 14.3 us  [across(): return lax.ppermute(a, axis, swap(n, bit))]
  transfers between devices with their start and end apart: 17 -> 17, of which waited for: 9 -> 8; matrix products, arithmetic and copies ran while one was open for 9% -> 11% of each run, Pallas kernels for 15% -> 16%
where the time goes in v7:
time: 141 us; the launch traced here: 140 us
  waiting for transfers between devices  46.3 us (33%)
  starting transfers between devices  33.9 us (24%)
  Pallas kernels  33.4 us (24%)
  local copies, waits for them, and re-layouts  13.1 us (9%)
  other arithmetic  6.63 us (5%)
  matrix products  5.66 us (4%)
    ppermute x12, waiting for transfers between devices, across(): return lax.ppermute(a, axis, swap(n, bit))  42.2 us
    pallas_call x4, Pallas kernels, attend(): pl.pallas_call(functools.partial(attend_kernel, picks, len(arrays), scale...  23.5 us
    all_to_all x5, starting transfers between devices, spread(): return lax.all_to_all(a, axes, split_axis=0, concat_axis=0, tiled=True)  19.7 us
    ppermute x12, starting transfers between devices, across(): return lax.ppermute(a, axis, swap(n, bit))  14.3 us
    unnamed x68, local copies, waits for them, and re-layouts  6.99 us
    another operation x10, other arithmetic, pieces(): return jnp.stack(out, axis=1)  6.56 us
    dot_general x1, matrix products, shards(): jnp.dot(early, out_weight[:rows], preferred_element_type=jnp.float32)  5.66 us
    all_to_all x5, waiting for transfers between devices, spread(): return lax.all_to_all(a, axes, split_axis=0, concat_axis=0, tiled=True)  4.13 us
  transfers between devices with their start and end apart: 17, of which 8 were waited for; matrix products, arithmetic and copies ran while one was open for 11% of the time, Pallas kernels for 16%

profile of v7, /device:TPU:0, one launch (start us, length us, event | category | flops | bytes accessed | tf_op | source)
XLA Modules:
  0.0 139.8 jit_solution(7317792046220344241)
XLA Ops:
  0.0 1.3 fusion.2
  3.4 3.0 %collective-permute-start.1 = (bf16[4,3,128,128]{3,2,1,0:T(8,128)(2,1)}, bf16[4,3,128,128]{3,2,1,0:T(8,128)(2,1)S(1)}, u32[]{:S(2)}, u32[]{:S(2)}) collective-permute-start(bf16[4,3,128,128]{3,2,1,0:T(8,128)(2,1)} %pad_maximum_fusion.1), channel_id=1, source_target_pairs={{0,2},{2,0},{1,3},{3,1},{4,6},{6,4},{5,7},{7,5},{8,10},{10,8},{9,1... | collective-permute-start | bytes 1179656 | tf_op jit(solution)/shard_map/ppermute | solution.py:201
  7.4 2.6 %collective-permute-start = (bf16[4,2,128,128]{3,2,1,0:T(8,128)(2,1)}, bf16[4,2,128,128]{3,2,1,0:T(8,128)(2,1)S(1)}, u32[]{:S(2)}, u32[]{:S(2)}) collective-permute-start(bf16[4,2,128,128]{3,2,1,0:T(8,128)(2,1)} %pad_maximum_fusion.7), channel_id=1, source_target_pairs={{0,4},{2,6},{4,0},{6,2},{1,5},{3,7},{5,1},{7,3},{8,12},{10,14},{12... | collective-permute-start | bytes 786440 | tf_op jit(solution)/shard_map/ppermute | solution.py:201
  10.5 1.1 constant_dynamic-slice_fusion
  13.4 8.0 %collective-permute-done.1.refs_1_ = bf16[4,3,128,128]{3,2,1,0:T(8,128)(2,1)S(1)} collective-permute-done((bf16[4,3,128,128]{3,2,1,0:T(8,128)(2,1)}, bf16[4,3,128,128]{3,2,1,0:T(8,128)(2,1)S(1)}, u32[]{:S(2)}, u32[]{:S(2)}) %collective-permute-start.1) | collective-permute-done | bytes 393248 | tf_op jit(solution)/shard_map/ppermute | solution.py:201
  21.3 3.8 %collective-permute-start.2 = (bf16[4,2,128,128]{3,2,1,0:T(8,128)(2,1)}, bf16[4,2,128,128]{3,2,1,0:T(8,128)(2,1)S(1)}, u32[]{:S(2)}, u32[]{:S(2)}) collective-permute-start(bf16[4,2,128,128]{3,2,1,0:T(8,128)(2,1)} %pad_maximum_fusion.8), channel_id=1, source_target_pairs={{0,6},{2,4},{4,2},{6,0},{1,7},{3,5},{5,3},{7,1},{8,14},{10,12},{12... | collective-permute-start | bytes 786440 | tf_op jit(solution)/shard_map/ppermute | solution.py:201
  26.0 3.8 %all-to-all-start = ((bf16[4,6,128,128]{3,2,1,0:T(8,128)(2,1)}), bf16[4,6,128,128]{3,2,1,0:T(8,128)(2,1)S(1)}, u32[]{:S(2)}, u32[]{:S(2)}) async-start(bf16[4,6,128,128]{3,2,1,0:T(8,128)(2,1)} %shard_map.164), calls=%async_computation | async-start | bytes 1572864 | tf_op jit(solution)/shard_map/all_to_all | solution.py:204
  33.8 3.6 %collective-permute-start.8 = (bf16[4,2,128,128]{3,2,1,0:T(8,128)(2,1)}, bf16[4,2,128,128]{3,2,1,0:T(8,128)(2,1)S(1)}, u32[]{:S(2)}, u32[]{:S(2)}) collective-permute-start(bf16[4,2,128,128]{3,2,1,0:T(8,128)(2,1)} %pad_maximum_fusion.10), channel_id=1, source_target_pairs={{0,6},{2,4},{4,2},{6,0},{1,7},{3,5},{5,3},{7,1},{8,14},{10,12},{12... | collective-permute-start | bytes 786440 | tf_op jit(solution)/shard_map/ppermute | solution.py:201
  37.4 0.9 shard_map.163.bias_ref
  38.4 10.0 %collective-permute-done.3.refs_1_ = bf16[4,3,128,128]{3,2,1,0:T(8,128)(2,1)S(1)} collective-permute-done((bf16[4,3,128,128]{3,2,1,0:T(8,128)(2,1)}, bf16[4,3,128,128]{3,2,1,0:T(8,128)(2,1)S(1)}, u32[]{:S(2)}, u32[]{:S(2)}) %collective-permute-start.3) | collective-permute-done | bytes 393248 | tf_op jit(solution)/shard_map/ppermute | solution.py:201
  48.4 1.2 shard_map.165
  50.4 4.0 %all-to-all-start.1 = ((bf16[4,10,128,128]{3,2,1,0:T(8,128)(2,1)}), bf16[4,10,128,128]{3,2,1,0:T(8,128)(2,1)S(1)}, u32[]{:S(2)}, u32[]{:S(2)}) async-start(bf16[4,10,128,128]{3,2,1,0:T(8,128)(2,1)} %shard_map.165), calls=%async_computation.1 | async-start | bytes 2621440 | tf_op jit(solution)/shard_map/all_to_all | solution.py:204
  54.4 0.9 pad_maximum_fusion.6
  55.3 1.0 pad_maximum_fusion.5.refs_0_
  58.1 6.1 %collective-permute-done.9.refs_1_ = bf16[4,3,128,128]{3,2,1,0:T(8,128)(2,1)S(1)} collective-permute-done((bf16[4,3,128,128]{3,2,1,0:T(8,128)(2,1)S(1)}, bf16[4,3,128,128]{3,2,1,0:T(8,128)(2,1)S(1)}, u32[]{:S(2)}, u32[]{:S(2)}) %collective-permute-start.9) | collective-permute-done | bytes 393248 | tf_op jit(solution)/shard_map/ppermute | solution.py:201
  64.3 1.0 copy-done
  65.3 4.5 %shard_map.167 = (f32[1024,128]{1,0:T(8,128)S(1)}, f32[1024,256]{1,0:T(8,128)S(1)}) custom-call(s32[8]{0:T(128)S(1)} %reshape.68.place_ref, f32[2,4,4096]{2,1,0:T(4,128)S(1)} %shard_map.163.bias_ref, bf16[4,6,128,128]{3,2,1,0:T(8,128)(2,1)S(1)} %all-to-all-done.refs_0_.q_ref, bf16[4,4,128,128]{3,2,1,0:T(8,128)(2,1)} %shard_map.166.refs_0_, ...), custom_call_target="tpu_custom_call" | custom-call | flops 1024 | bytes 4096 | tf_op jit(solution)/shard_map/pallas_call | solution.py:110
  69.9 1.0 copy-done.3
  71.7 4.2 %all-to-all-start.2 = ((bf16[4,10,128,128]{3,2,1,0:T(8,128)(2,1)}), bf16[4,10,128,128]{3,2,1,0:T(8,128)(2,1)S(1)}, u32[]{:S(2)}, u32[]{:S(2)}) async-start(bf16[4,10,128,128]{3,2,1,0:T(8,128)(2,1)} %copy-done), calls=%async_computation.2 | async-start | bytes 2621440 | tf_op jit(solution)/shard_map/all_to_all | solution.py:204
  76.8 7.2 %shard_map.170 = bf16[8,128,128]{2,1,0:T(8,128)(2,1)S(1)} custom-call(s32[8]{0:T(128)S(1)} %reshape.68.place_ref, f32[2,4,4096]{2,1,0:T(4,128)S(1)} %copy-done.8, bf16[4,10,128,128]{3,2,1,0:T(8,128)(2,1)S(1)} %all-to-all-done.1.q_ref.refs_0_, bf16[4,10,128,128]{3,2,1,0:T(8,128)(2,1)S(1)} %all-to-all-done.1.q_ref.refs_0_, ...), custom_call_target="tpu_custom_call" | custom-call | flops 1024 | bytes 4096 | tf_op jit(solution)/shard_map/pallas_call | solution.py:110
  84.7 13.2 %collective-permute-done.4.refs_0_ = bf16[4,4,128,128]{3,2,1,0:T(8,128)(2,1)} collective-permute-done((bf16[4,4,128,128]{3,2,1,0:T(8,128)(2,1)}, bf16[4,4,128,128]{3,2,1,0:T(8,128)(2,1)}, u32[]{:S(2)}, u32[]{:S(2)}) %collective-permute-start.4) | collective-permute-done | bytes 524320 | tf_op jit(solution)/shard_map/ppermute | solution.py:201
  99.0 3.0 %collective-permute-done.11.refs_1_ = bf16[4,10,128,128]{3,2,1,0:T(8,128)(2,1)S(1)} collective-permute-done((bf16[4,10,128,128]{3,2,1,0:T(8,128)(2,1)S(1)}, bf16[4,10,128,128]{3,2,1,0:T(8,128)(2,1)S(1)}, u32[]{:S(2)}, u32[]{:S(2)}) %collective-permute-start.11) | collective-permute-done | bytes 1310752 | tf_op jit(solution)/shard_map/ppermute | solution.py:201
  102.0 6.4 %shard_map.172 = bf16[8,128,128]{2,1,0:T(8,128)(2,1)S(1)} custom-call(s32[8]{0:T(128)S(1)} %reshape.68.place_ref, f32[2,4,4096]{2,1,0:T(4,128)S(1)} %shard_map.171.bias_ref, bf16[4,10,128,128]{3,2,1,0:T(8,128)(2,1)S(1)} %all-to-all-done.2.q_ref.refs_0_, bf16[4,10,128,128]{3,2,1,0:T(8,128)(2,1)S(1)} %all-to-all-done.2.q_ref.refs_0_, ...), custom_call_target="tpu_custom_call" | custom-call | flops 1024 | bytes 4096 | tf_op jit(solution)/shard_map/pallas_call | solution.py:110
  109.3 4.2 %all-to-all-start.3 = ((bf16[8,2,128,128]{3,2,1,0:T(8,128)(2,1)}), bf16[8,2,128,128]{3,2,1,0:T(8,128)(2,1)}, u32[]{:S(2)}, u32[]{:S(2)}) async-start(bf16[8,2,128,128]{3,2,1,0:T(8,128)(2,1)} %copy.73), calls=%async_computation.3 | async-start | bytes 1048576 | tf_op jit(solution)/shard_map/all_to_all | solution.py:204
  113.7 2.0 %collective-permute-done.5.refs_1_ = bf16[4,4,128,128]{3,2,1,0:T(8,128)(2,1)S(1)} collective-permute-done((bf16[4,4,128,128]{3,2,1,0:T(8,128)(2,1)}, bf16[4,4,128,128]{3,2,1,0:T(8,128)(2,1)S(1)}, u32[]{:S(2)}, u32[]{:S(2)}) %collective-permute-start.5) | collective-permute-done | bytes 524320 | tf_op jit(solution)/shard_map/ppermute | solution.py:201
  115.7 5.3 %shard_map.173 = bf16[8,128,128]{2,1,0:T(8,128)(2,1)} custom-call(s32[8]{0:T(128)S(1)} %reshape.68.place_ref, f32[2,4,4096]{2,1,0:T(4,128)S(1)} %shard_map.163.bias_ref, bf16[4,6,128,128]{3,2,1,0:T(8,128)(2,1)S(1)} %all-to-all-done.refs_0_.q_ref, bf16[4,4,128,128]{3,2,1,0:T(8,128)(2,1)} %collective-permute-done.4.refs_0_, ...), custom_call_target="tpu_custom_call" | custom-call | flops 1024 | bytes 4096 | tf_op jit(solution)/shard_map/pallas_call | solution.py:110
  121.0 2.9 %all-to-all-done.3 = bf16[8,2,128,128]{3,2,1,0:T(8,128)(2,1)} async-done(((bf16[8,2,128,128]{3,2,1,0:T(8,128)(2,1)}), bf16[8,2,128,128]{3,2,1,0:T(8,128)(2,1)}, u32[]{:S(2)}, u32[]{:S(2)}) %all-to-all-start.3) | async-done | bytes 524320 | tf_op jit(solution)/shard_map/all_to_all | solution.py:204
  123.9 1.3 copy.74
  125.2 3.4 %all-to-all-start.4 = ((bf16[8,128,128]{2,1,0:T(8,128)(2,1)}), bf16[8,128,128]{2,1,0:T(8,128)(2,1)S(1)}, u32[]{:S(2)}, u32[]{:S(2)}) async-start(bf16[8,128,128]{2,1,0:T(8,128)(2,1)} %shard_map.173), calls=%async_computation.4 | async-start | bytes 524288 | tf_op jit(solution)/shard_map/all_to_all | solution.py:204
  128.6 5.7 %fusion.total_ref = f32[128,3072]{1,0:T(8,128)S(1)} fusion(bf16[128,2048]{0,1:T(8,128)(2,1)S(1)} %bitcast.78, bf16[3072,3072]{1,0:T(8,128)(2,1)} %weight_ref.1), kind=kOutput, calls=%fused_computation | convolution fusion | flops 1610612736 | bytes 14680064 | tf_op jit(solution)/shard_map/dot_general | solution.py:280
  134.3 1.2 all-to-all-done.4.part_ref
  135.5 4.1 %shard_map.174 = bf16[128,3072]{1,0:T(8,128)(2,1)} custom-call(bf16[8,128,128]{2,1,0:T(8,128)(2,1)S(1)} %all-to-all-done.4.part_ref, bf16[3072,3072]{1,0:T(8,128)(2,1)} %weight_ref.1, f32[128,3072]{1,0:T(8,128)S(1)} %fusion.total_ref), custom_call_target="tpu_custom_call" | custom-call | tf_op jit(solution)/shard_map/pallas_call | solution.py:163
  (107 shorter events, 17.2 us)
Async XLA Ops:
  3.4 18.0 %collective-permute-start.1 = (bf16[4,3,128,128]{3,2,1,0:T(8,128)(2,1)}, bf16[4,3,128,128]{3,2,1,0:T(8,128)(2,1)S(1)}, u32[]{:S(2)}, u32[]{:S(2)}) collective-permute-start(bf16[4,3,128,128]{3,2,1,0:T(8,128)(2,1)} %pad_maximum_fusion.1), channel_id=1, source_target_pairs={{0,2},{2,0},{1,3},{3,1},{4,6},{6,4},{5,7},{7,5},{8,10},{10,8},{9,1... | collective-permute-start | bytes 1179656 | tf_op jit(solution)/shard_map/ppermute | solution.py:201
  7.4 30.0 %collective-permute-start = (bf16[4,2,128,128]{3,2,1,0:T(8,128)(2,1)}, bf16[4,2,128,128]{3,2,1,0:T(8,128)(2,1)S(1)}, u32[]{:S(2)}, u32[]{:S(2)}) collective-permute-start(bf16[4,2,128,128]{3,2,1,0:T(8,128)(2,1)} %pad_maximum_fusion.7), channel_id=1, source_target_pairs={{0,4},{2,6},{4,0},{6,2},{1,5},{3,7},{5,1},{7,3},{8,12},{10,14},{12... | collective-permute-start | bytes 786440 | tf_op jit(solution)/shard_map/ppermute | solution.py:201
  10.0 2.4 %copy-start.21 = (s32[9]{0:T(128)S(1)}, s32[9]{0:T(128)}, u32[]{:S(2)}) copy-start(s32[9]{0:T(128)} %constant.100.clone) | copy-start | bytes 112
  10.0 2.3 %copy-start.22 = (s32[9]{0:T(128)S(1)}, s32[9]{0:T(128)}, u32[]{:S(2)}) copy-start(s32[9]{0:T(128)} %constant.101.clone) | copy-start | bytes 112
  10.1 2.3 %copy-start.23 = (s32[9]{0:T(128)S(1)}, s32[9]{0:T(128)}, u32[]{:S(2)}) copy-start(s32[9]{0:T(128)} %constant.102.clone) | copy-start | bytes 112
  10.1 2.3 %copy-start.24 = (pred[9]{0:T(512)(128)(4,1)S(1)}, pred[9]{0:T(512)(128)(4,1)}, u32[]{:S(2)}) copy-start(pred[9]{0:T(512)(128)(4,1)} %constant.103.clone) | copy-start | bytes 31
  21.3 16.1 %collective-permute-start.2 = (bf16[4,2,128,128]{3,2,1,0:T(8,128)(2,1)}, bf16[4,2,128,128]{3,2,1,0:T(8,128)(2,1)S(1)}, u32[]{:S(2)}, u32[]{:S(2)}) collective-permute-start(bf16[4,2,128,128]{3,2,1,0:T(8,128)(2,1)} %pad_maximum_fusion.8), channel_id=1, source_target_pairs={{0,6},{2,4},{4,2},{6,0},{1,7},{3,5},{5,3},{7,1},{8,14},{10,12},{12... | collective-permute-start | bytes 786440 | tf_op jit(solution)/shard_map/ppermute | solution.py:201
  26.0 5.3 %copy-start.18 = (bf16[2,1,2,128,128]{4,2,1,0,3:T(2,128)(2,1)S(1)}, bf16[2,1,2,128,128]{4,2,1,0,3:T(2,128)(2,1)}, u32[]{:S(2)}) copy-start(bf16[2,1,2,128,128]{4,2,1,0,3:T(2,128)(2,1)} %get-tuple-element.70) | copy-start | bytes 393220
  26.0 5.3 %copy-start.17 = (bf16[2,1,2,128,128]{4,2,1,0,3:T(2,128)(2,1)S(1)}, bf16[2,1,2,128,128]{4,2,1,0,3:T(2,128)(2,1)}, u32[]{:S(2)}) copy-start(bf16[2,1,2,128,128]{4,2,1,0,3:T(2,128)(2,1)} %get-tuple-element.53) | copy-start | bytes 393220
  26.0 23.5 %all-to-all-start = ((bf16[4,6,128,128]{3,2,1,0:T(8,128)(2,1)}), bf16[4,6,128,128]{3,2,1,0:T(8,128)(2,1)S(1)}, u32[]{:S(2)}, u32[]{:S(2)}) async-start(bf16[4,6,128,128]{3,2,1,0:T(8,128)(2,1)} %shard_map.164), calls=%async_computation | async-start | bytes 1572864 | tf_op jit(solution)/shard_map/all_to_all | solution.py:204
  29.9 7.5 %copy-start.9 = (s32[24,32,32]{2,1,0:T(8,128)S(1)}, s32[24,32,32]{2,1,0:T(8,128)}, u32[]{:S(2)}) copy-start(s32[24,32,32]{2,1,0:T(8,128)} %mask_ref.2) | copy-start | bytes 294916
  29.9 7.5 %copy-start.12 = (s32[4,1]{1,0:T(4,128)S(1)}, s32[4,1]{1,0:T(4,128)}, u32[]{:S(2)}) copy-start(s32[4,1]{1,0:T(4,128)} %constant.106.clone.rows_ref) | copy-start | bytes 52
  29.9 7.5 %copy-start.13 = (s32[1,512]{1,0:T(1,128)S(1)}, s32[1,512]{1,0:T(1,128)}, u32[]{:S(2)}) copy-start(s32[1,512]{1,0:T(1,128)} %constant.107.clone.cols_ref) | copy-start | bytes 6148
  31.4 7.0 %copy-start.14 = (bf16[2,1,2,128,128]{4,3,2,0,1:T(8,128)(2,1)}, bf16[2,1,2,128,128]{4,3,2,0,1:T(8,128)(2,1)S(1)}, u32[]{:S(2)}) copy-start(bf16[2,1,2,128,128]{4,3,2,0,1:T(8,128)(2,1)S(1)} %copy.88) | copy-start | bytes 393220
  32.2 16.1 %collective-permute-start.3 = (bf16[4,3,128,128]{3,2,1,0:T(8,128)(2,1)}, bf16[4,3,128,128]{3,2,1,0:T(8,128)(2,1)S(1)}, u32[]{:S(2)}, u32[]{:S(2)}) collective-permute-start(bf16[4,3,128,128]{3,2,1,0:T(8,128)(2,1)} %pad_maximum_fusion.4), channel_id=1, source_target_pairs={{0,2},{2,0},{1,3},{3,1},{4,6},{6,4},{5,7},{7,5},{8,10},{10,8},{9,1... | collective-permute-start | bytes 1179656 | tf_op jit(solution)/shard_map/ppermute | solution.py:201
  33.0 23.4 %collective-permute-start.7 = (bf16[4,2,128,128]{3,2,1,0:T(8,128)(2,1)}, bf16[4,2,128,128]{3,2,1,0:T(8,128)(2,1)S(1)}, u32[]{:S(2)}, u32[]{:S(2)}) collective-permute-start(bf16[4,2,128,128]{3,2,1,0:T(8,128)(2,1)} %pad_maximum_fusion.9), channel_id=1, source_target_pairs={{0,4},{2,6},{4,0},{6,2},{1,5},{3,7},{5,1},{7,3},{8,12},{10,14},{12... | collective-permute-start | bytes 786440 | tf_op jit(solution)/shard_map/ppermute | solution.py:201
  33.8 22.6 %collective-permute-start.8 = (bf16[4,2,128,128]{3,2,1,0:T(8,128)(2,1)}, bf16[4,2,128,128]{3,2,1,0:T(8,128)(2,1)S(1)}, u32[]{:S(2)}, u32[]{:S(2)}) collective-permute-start(bf16[4,2,128,128]{3,2,1,0:T(8,128)(2,1)} %pad_maximum_fusion.10), channel_id=1, source_target_pairs={{0,6},{2,4},{4,2},{6,0},{1,7},{3,5},{5,3},{7,1},{8,14},{10,12},{12... | collective-permute-start | bytes 786440 | tf_op jit(solution)/shard_map/ppermute | solution.py:201
  50.4 6.1 %copy-start.10 = (s32[24,32,32]{2,1,0:T(8,128)S(1)}, s32[24,32,32]{2,1,0:T(8,128)}, u32[]{:S(2)}) copy-start(s32[24,32,32]{2,1,0:T(8,128)} %mask_ref.2) | copy-start | bytes 294916
  50.4 21.3 %all-to-all-start.1 = ((bf16[4,10,128,128]{3,2,1,0:T(8,128)(2,1)}), bf16[4,10,128,128]{3,2,1,0:T(8,128)(2,1)S(1)}, u32[]{:S(2)}, u32[]{:S(2)}) async-start(bf16[4,10,128,128]{3,2,1,0:T(8,128)(2,1)} %shard_map.165), calls=%async_computation.1 | async-start | bytes 2621440 | tf_op jit(solution)/shard_map/all_to_all | solution.py:204
  56.4 7.8 %collective-permute-start.9 = (bf16[4,3,128,128]{3,2,1,0:T(8,128)(2,1)S(1)}, bf16[4,3,128,128]{3,2,1,0:T(8,128)(2,1)S(1)}, u32[]{:S(2)}, u32[]{:S(2)}) collective-permute-start(bf16[4,3,128,128]{3,2,1,0:T(8,128)(2,1)S(1)} %pad_maximum_fusion.6), channel_id=1, source_target_pairs={{0,2},{2,0},{1,3},{3,1},{4,6},{6,4},{5,7},{7,5},{8,10},{10,8},{9,1... | collective-permute-start | bytes 1179656 | tf_op jit(solution)/shard_map/ppermute | solution.py:201
  56.5 8.9 %collective-permute-start.6 = (bf16[4,4,128,128]{3,2,1,0:T(8,128)(2,1)}, bf16[4,4,128,128]{3,2,1,0:T(8,128)(2,1)S(1)}, u32[]{:S(2)}, u32[]{:S(2)}) collective-permute-start(bf16[4,4,128,128]{3,2,1,0:T(8,128)(2,1)} %shard_map.166.refs_0_), channel_id=1, source_target_pairs={{0,8},{8,0},{1,9},{9,1},{2,10},{10,2},{3,11},{11,3},{4,12},{12,4},... | collective-permute-start | bytes 1572872 | tf_op jit(solution)/shard_map/ppermute | solution.py:201
  71.7 4.2 %collective-permute-start.10 = (bf16[4,10,128,128]{3,2,1,0:T(8,128)(2,1)S(1)}, bf16[4,10,128,128]{3,2,1,0:T(8,128)(2,1)}, u32[]{:S(2)}, u32[]{:S(2)}) collective-permute-start(bf16[4,10,128,128]{3,2,1,0:T(8,128)(2,1)S(1)} %all-to-all-done.1.q_ref.refs_0_), channel_id=1, source_target_pairs={{0,8},{8,0},{1,9},{9,1},{2,10},{10,2},{3,11},{11,3},{4,12},{12,4},... | collective-permute-start | bytes 3932168 | tf_op jit(solution)/shard_map/ppermute | solution.py:201
  71.7 26.2 %collective-permute-start.4 = (bf16[4,4,128,128]{3,2,1,0:T(8,128)(2,1)}, bf16[4,4,128,128]{3,2,1,0:T(8,128)(2,1)}, u32[]{:S(2)}, u32[]{:S(2)}) collective-permute-start(bf16[4,4,128,128]{3,2,1,0:T(8,128)(2,1)} %shard_map.166.refs_0_), channel_id=1, source_target_pairs={{0,4},{4,0},{1,5},{5,1},{2,6},{6,2},{3,7},{7,3},{8,12},{12,8},{9,1... | collective-permute-start | bytes 1572872 | tf_op jit(solution)/shard_map/ppermute | solution.py:201
  71.7 27.2 %all-to-all-start.2 = ((bf16[4,10,128,128]{3,2,1,0:T(8,128)(2,1)}), bf16[4,10,128,128]{3,2,1,0:T(8,128)(2,1)S(1)}, u32[]{:S(2)}, u32[]{:S(2)}) async-start(bf16[4,10,128,128]{3,2,1,0:T(8,128)(2,1)} %copy-done), calls=%async_computation.2 | async-start | bytes 2621440 | tf_op jit(solution)/shard_map/all_to_all | solution.py:204
  76.8 21.1 %copy-start.11 = (s32[24,32,32]{2,1,0:T(8,128)S(1)}, s32[24,32,32]{2,1,0:T(8,128)}, u32[]{:S(2)}) copy-start(s32[24,32,32]{2,1,0:T(8,128)} %mask_ref.2) | copy-start | bytes 294916
  98.8 9.6 %copy-start.2 = (bf16[8,128,128]{2,1,0:T(8,128)(2,1)S(1)}, bf16[8,128,128]{2,1,0:T(8,128)(2,1)}, u32[]{:S(2)}) copy-start(bf16[8,128,128]{2,1,0:T(8,128)(2,1)} %copy-done.1) | copy-start | bytes 786436
  98.9 3.1 %collective-permute-start.11 = (bf16[4,10,128,128]{3,2,1,0:T(8,128)(2,1)S(1)}, bf16[4,10,128,128]{3,2,1,0:T(8,128)(2,1)S(1)}, u32[]{:S(2)}, u32[]{:S(2)}) collective-permute-start(bf16[4,10,128,128]{3,2,1,0:T(8,128)(2,1)S(1)} %all-to-all-done.2.q_ref.refs_0_), channel_id=1, source_target_pairs={{0,8},{8,0},{1,9},{9,1},{2,10},{10,2},{3,11},{11,3},{4,12},{12,4},... | collective-permute-start | bytes 3932168 | tf_op jit(solution)/shard_map/ppermute | solution.py:201
  108.4 7.3 %copy-start.4 = (f32[1024,256]{1,0:T(8,128)S(1)}, f32[1024,256]{1,0:T(8,128)}, u32[]{:S(2)}) copy-start(f32[1024,256]{1,0:T(8,128)} %copy-done.3) | copy-start | bytes 3145732
  108.4 7.3 %copy-start.6 = (f32[1024,128]{1,0:T(8,128)S(1)}, f32[1024,128]{1,0:T(8,128)}, u32[]{:S(2)}) copy-start(f32[1024,128]{1,0:T(8,128)} %copy-done.5) | copy-start | bytes 1572868
  109.3 14.5 %all-to-all-start.3 = ((bf16[8,2,128,128]{3,2,1,0:T(8,128)(2,1)}), bf16[8,2,128,128]{3,2,1,0:T(8,128)(2,1)}, u32[]{:S(2)}, u32[]{:S(2)}) async-start(bf16[8,2,128,128]{3,2,1,0:T(8,128)(2,1)} %copy.73), calls=%async_computation.3 | async-start | bytes 1048576 | tf_op jit(solution)/shard_map/all_to_all | solution.py:204
  113.5 2.2 %collective-permute-start.5 = (bf16[4,4,128,128]{3,2,1,0:T(8,128)(2,1)}, bf16[4,4,128,128]{3,2,1,0:T(8,128)(2,1)S(1)}, u32[]{:S(2)}, u32[]{:S(2)}) collective-permute-start(bf16[4,4,128,128]{3,2,1,0:T(8,128)(2,1)} %collective-permute-done.4.refs_0_), channel_id=1, source_target_pairs={{0,8},{8,0},{1,9},{9,1},{2,10},{10,2},{3,11},{11,3},{4,12},{12,4},... | collective-permute-start | bytes 1572872 | tf_op jit(solution)/shard_map/ppermute | solution.py:201
  125.2 10.3 %all-to-all-start.4 = ((bf16[8,128,128]{2,1,0:T(8,128)(2,1)}), bf16[8,128,128]{2,1,0:T(8,128)(2,1)S(1)}, u32[]{:S(2)}, u32[]{:S(2)}) async-start(bf16[8,128,128]{2,1,0:T(8,128)(2,1)} %shard_map.173), calls=%async_computation.4 | async-start | bytes 524288 | tf_op jit(solution)/shard_map/all_to_all | solution.py:204
  (10 other events, 11.6 us)

commit v8 on v7

--- a/solution.py
+++ b/solution.py
@@ -50,23 +50,16 @@
             bias_ref[tile, :, n * span : (n + 1) * span] = jnp.where(seen > 0.5, 0.0, NEG)
 
 
-def attend_kernel(picks, count, scale, first, last, place_ref, bias_ref, q_ref, *refs):
-    kv_refs, rest = refs[:count], refs[count:]
-    if not first:
-        m_in, acc_in = rest[:2]
-        rest = rest[2:]
+def attend_kernel(picks, count, scale, place_ref, bias_ref, q_ref, *refs):
+    kv_refs, out_ref = refs[:count], refs[count]
     tiles, qb, _ = bias_ref.shape
     block, hdim = q_ref.shape[2:]
     rows = qb * block
 
     def tile(index, carry):
         q = q_ref[:, 3 * index].reshape(rows, hdim)
-        if first:
-            m = jnp.full((rows, 1), NEG, jnp.float32)
-            acc = jnp.zeros((rows, 2 * hdim), jnp.float32)
-        else:
-            m = jnp.max(m_in[pl.ds(index * rows, rows), :], axis=1, keepdims=True)
-            acc = acc_in[pl.ds(index * rows, rows), :]
+        m = jnp.full((rows, 1), NEG, jnp.float32)
+        acc = jnp.zeros((rows, 2 * hdim), jnp.float32)
         for which, kpart, vpart, source in picks:
             k = kv_refs[which][:, kpart].reshape(rows, hdim)
             v = kv_refs[which][:, vpart].reshape(rows, hdim)
@@ -78,42 +71,27 @@
             p = jnp.exp2(s - m_next).astype(jnp.bfloat16)
             acc = acc * jnp.exp2(m - m_next) + jnp.dot(p, v, preferred_element_type=jnp.float32)
             m = m_next
-        if last:
-            out = (acc[:, :hdim] / acc[:, hdim:]).astype(jnp.bfloat16)
-            for row in range(qb):
-                rest[0][place_ref[index * qb + row]] = out[row * block : (row + 1) * block]
-        else:
-            rest[0][pl.ds(index * rows, rows), :] = jnp.broadcast_to(m, (rows, hdim))
-            rest[1][pl.ds(index * rows, rows), :] = acc
+        out = (acc[:, :hdim] / acc[:, hdim:]).astype(jnp.bfloat16)
+        for row in range(qb):
+            out_ref[place_ref[index * qb + row]] = out[row * block : (row + 1) * block]
         return carry
 
     lax.fori_loop(0, tiles, tile, 0)
 
 
-def attend(place, bias, q, arrays, picks, state, last):
+def attend(place, bias, got, arrays, picks):
     tiles, qb, _ = bias.shape
-    block, hdim = q.shape[2:]
+    block, hdim = got.shape[2:]
     groups = tiles * qb
-    total = groups * block
-    first = state is None
-    if last:
-        out_shape = jax.ShapeDtypeStruct((groups, block, hdim), jnp.bfloat16)
-        out_specs = VMEM
-    else:
-        out_shape = (
-            jax.ShapeDtypeStruct((total, hdim), jnp.float32),
-            jax.ShapeDtypeStruct((total, 2 * hdim), jnp.float32),
-        )
-        out_specs = (VMEM, VMEM)
-    args = [place, bias, q, *arrays, *(() if first else state)]
+    args = [place, bias, got, *arrays]
     scale = hdim**-0.5 * math.log2(math.e)
     return pl.pallas_call(
-        functools.partial(attend_kernel, picks, len(arrays), scale, first, last),
-        out_shape=out_shape,
+        functools.partial(attend_kernel, picks, len(arrays), scale),
+        out_shape=jax.ShapeDtypeStruct((groups, block, hdim), jnp.bfloat16),
         in_specs=[SMEM] + [VMEM] * (len(args) - 1),
-        out_specs=out_specs,
+        out_specs=VMEM,
         compiler_params=grant(*args),
-        cost_estimate=pl.CostEstimate(flops=total, bytes_accessed=4 * total, transcendentals=0),
+        cost_estimate=pl.CostEstimate(flops=groups * block, bytes_accessed=4 * groups * block, transcendentals=0),
     )(*args)
 
 
@@ -227,53 +205,47 @@
             in_specs=[SMEM, VMEM, VMEM, VMEM],
             out_specs=VMEM,
             compiler_params=grant(out, block_mask),
-            cost_estimate=pl.CostEstimate(flops={2: 3 * 10**9, 0: 8 * 10**9, 1: 8 * 10**9}[j], bytes_accessed=0, transcendentals=0),
+            cost_estimate=pl.CostEstimate(flops={2: 10**6, 0: 8 * 10**9, 1: 8 * 10**9}[j], bytes_accessed=0, transcendentals=0),
         )(place, after(block_mask, *before), local[:, None], np.repeat(local, BLOCK)[None, :])
 
     assert chunks == 3
-    trio = (queries, keys, values)
 
     def cross(j, *before):
         halves = [pieces((keys, values), j, b) for b in range(2)]
-        halves = halves[:1] + after(halves[1:], *before) if j == 0 else after(halves, *before)
+        if before:
+            halves = after(halves, *before)
         return [across(h, ("zh", "zl"), 2 + b) for b, h in enumerate(halves)]
 
-    def own(j, *before):
-        given = pieces(trio, j, 1)
-        if before:
-            given = after(given, *before)
-        return (pieces(trio, j, 0), range(3)), (across(given, "zl", 1), range(3))
-
-    near_pick = tuple((i, 2 * r, 2 * r + 1, 4 * i + r) for i in range(half) for r in range(2))
-    far_pick = tuple((i, 2 * r, 2 * r + 1, 4 * i + 2 + r) for i in range(half) for r in range(2))
-    both_pick = tuple((i, 1 + 3 * r, 2 + 3 * r, 4 * i + r) for i in range(half) for r in range(2))
-    both_pick += tuple((i, 6 + 2 * r, 7 + 2 * r, 4 * i + 2 + r) for i in range(half) for r in range(2))
+    def joined(j, far):
+        trio = (queries, keys, values)
+        swapped = across(pieces(trio, j, 1), "zl", 1)
+        return pack((pieces(trio, j, 0), range(3)), (swapped, range(3)), *((f, range(2)) for f in far))
+
+    picks = tuple((i, 1 + 3 * r, 2 + 3 * r, 4 * i + r) for i in range(half) for r in range(2))
+    picks += tuple((i, 6 + 2 * r, 7 + 2 * r, 4 * i + 2 + r) for i in range(half) for r in range(2))
     axes = gather + ("c",)
 
-    own2 = own(2)
-    far0 = cross(0, own2[1][0])
-    got2 = spread(pack(*own2), flat)
-    bias2 = bias_of(2, *far0)
-    own0 = pack(*own(0, own2[1][0]), *((f, range(2)) for f in far0))
-    got2 = after(got2, bias2, own0)
-    kv2 = pack((got2, (1, 2, 4, 5)))
-    far1 = cross(1, own2[1][0])
-    got0 = spread(after(own0, kv2), flat)
+    far0 = cross(0)
+    own0 = joined(0, far0)
+    far1 = cross(1, far0[0])
+    got0 = spread(own0, flat)
     bias0 = bias_of(0, *far1)
-    state2 = attend(home, bias2, got2, gathered(kv2, axes), near_pick, None, False)
-    own1 = pack(*own(1, *far0), *((f, range(2)) for f in far1))
-    got0 = after(got0, bias0, own1, state2)
-    far2 = across(kv2, "zh", 1)
+    own1 = joined(1, far1)
+    got0 = after(got0, bias0, own1)
+    far2 = cross(2, far1[0])
     got1 = spread(after(own1, got0), flat)
-    out0 = attend(home, bias0, got0, gathered(got0, axes), both_pick, None, True)
-    bias1 = bias_of(1, far2, out0)
-    got1 = after(got1, bias1)
-    far2 = gathered(far2, axes)
-    out1 = attend(home, bias1, got1, gathered(got1, axes), both_pick, None, True)
+    out0 = attend(home, bias0, got0, gathered(got0, axes), picks)
+    bias1 = bias_of(1, *far2, out0)
+    own2 = joined(2, far2)
+    got1 = after(got1, bias1, own2)
+    got2 = spread(after(own2, got1), flat)
+    bias2 = bias_of(2, bias1)
+    out1 = attend(home, bias1, got1, gathered(got1, axes), picks)
     ready = jnp.stack([out0, out1], axis=1)
+    got2 = after(got2, ready, bias2)
     early = spread(ready, split)
-    out2 = attend(home, bias2, got2, far2, far_pick, after(state2, ready), True)
-    late = spread(after(out2, early), split)
+    out2 = attend(home, bias2, got2, gathered(got2, axes), picks)
+    late = spread(out2, split)
 
     rows = 2 * width
     early = jnp.transpose(after(early, out2), (2, 1, 0, 3)).reshape(tok, rows)

time: 141 us -> 146 us (1.035)
  starting transfers between devices: 33.9 us -> 39.9 us
  waiting for transfers between devices: 46.3 us -> 49.2 us
  Pallas kernels: 33.4 us -> 30.7 us
    all_to_all x5, waiting for transfers between devices: 4.13 us -> 11.6 us  [spread(): return lax.all_to_all(a, axes, split_axis=0, concat_axis=0, tiled=True)]
    ppermute x12, waiting for transfers between devices: 42.2 us -> 37.6 us  [across(): return lax.ppermute(a, axis, swap(n, bit))]
    ppermute x12, starting transfers between devices: 14.3 us -> 18.5 us  [across(): return lax.ppermute(a, axis, swap(n, bit))]
    unnamed x68 -> x48, local copies, waits for them, and re-layouts: 6.99 us -> 3.6 us
    pallas_call x4 -> x3, Pallas kernels: 23.5 us -> 21.5 us  [attend(): pl.pallas_call(functools.partial(attend_kernel, picks, len(arrays), scale...]
    all_to_all x5, starting transfers between devices: 19.7 us -> 21.5 us  [spread(): return lax.all_to_all(a, axes, split_axis=0, concat_axis=0, tiled=True)]
    another operation x10 -> x12, other arithmetic: 6.56 us -> 5.7 us  [pieces(): return jnp.stack(out, axis=1)]
    pallas_call x4 -> x3, Pallas kernels: 3.04 us -> 2.36 us  [pack(): pl.pallas_call(functools.partial(pack_kernel, [tuple(parts) for _, parts...]
  transfers between devices with their start and end apart: 17 -> 17, of which waited for: 8 -> 9; matrix products, arithmetic and copies ran while one was open for 11% -> 14% of each run, Pallas kernels for 16% -> 18%
where the time goes in v8:
time: 146 us; the launch traced here: 145 us
  waiting for transfers between devices  49.2 us (34%)
  starting transfers between devices  39.9 us (27%)
  Pallas kernels  30.7 us (21%)
  local copies, waits for them, and re-layouts  12 us (8%)
  other arithmetic  7.1 us (5%)
  matrix products  5.65 us (4%)
    ppermute x12, waiting for transfers between devices, across(): return lax.ppermute(a, axis, swap(n, bit))  37.6 us
    pallas_call x3, Pallas kernels, attend(): pl.pallas_call(functools.partial(attend_kernel, picks, len(arrays), scale...  21.5 us
    all_to_all x5, starting transfers between devices, spread(): return lax.all_to_all(a, axes, split_axis=0, concat_axis=0, tiled=True)  21.5 us
    ppermute x12, starting transfers between devices, across(): return lax.ppermute(a, axis, swap(n, bit))  18.5 us
    all_to_all x5, waiting for transfers between devices, spread(): return lax.all_to_all(a, axes, split_axis=0, concat_axis=0, tiled=True)  11.6 us
    another operation x12, other arithmetic, pieces(): return jnp.stack(out, axis=1)  5.7 us
    dot_general x1, matrix products, shards(): jnp.dot(early, out_weight[:rows], preferred_element_type=jnp.float32)  5.65 us
    pallas_call x1, Pallas kernels, finish(): pl.pallas_call(functools.partial(finish_kernel, step), out_shape=jax.Shap...  4.09 us
  transfers between devices with their start and end apart: 17, of which 9 were waited for; matrix products, arithmetic and copies ran while one was open for 14% of the time, Pallas kernels for 18%

profile of v8, /device:TPU:0, one launch (start us, length us, event | category | flops | bytes accessed | tf_op | source)
XLA Modules:
  0.0 145.2 jit_solution(9815564743428859160)
XLA Ops:
  0.0 1.2 fusion.3
  2.0 4.1 %collective-permute-start = (bf16[4,2,128,128]{3,2,1,0:T(8,128)(2,1)S(1)}, bf16[4,2,128,128]{3,2,1,0:T(8,128)(2,1)S(1)}, u32[]{:S(2)}, u32[]{:S(2)}) collective-permute-start(bf16[4,2,128,128]{3,2,1,0:T(8,128)(2,1)S(1)} %pad_maximum_fusion.11), channel_id=1, source_target_pairs={{0,4},{2,6},{4,0},{6,2},{1,5},{3,7},{5,1},{7,3},{8,12},{10,14},{12... | collective-permute-start | bytes 786440 | tf_op jit(solution)/shard_map/ppermute | solution.py:179
  6.8 1.6 %collective-permute-start.5 = (bf16[4,3,128,128]{3,2,1,0:T(8,128)(2,1)S(1)}, bf16[4,3,128,128]{3,2,1,0:T(8,128)(2,1)S(1)}, u32[]{:S(2)}, u32[]{:S(2)}) collective-permute-start(bf16[4,3,128,128]{3,2,1,0:T(8,128)(2,1)S(1)} %pad_maximum_fusion.2), channel_id=1, source_target_pairs={{0,2},{2,0},{1,3},{3,1},{4,6},{6,4},{5,7},{7,5},{8,10},{10,8},{9,1... | collective-permute-start | bytes 1179656 | tf_op jit(solution)/shard_map/ppermute | solution.py:179
  10.0 1.0 constant_dynamic-slice_fusion
  14.1 4.8 %collective-permute-done.refs_2_ = bf16[4,2,128,128]{3,2,1,0:T(8,128)(2,1)S(1)} collective-permute-done((bf16[4,2,128,128]{3,2,1,0:T(8,128)(2,1)S(1)}, bf16[4,2,128,128]{3,2,1,0:T(8,128)(2,1)S(1)}, u32[]{:S(2)}, u32[]{:S(2)}) %collective-permute-start) | collective-permute-done | bytes 262176 | tf_op jit(solution)/shard_map/ppermute | solution.py:179
  18.9 2.8 %collective-permute-start.4 = (bf16[4,2,128,128]{3,2,1,0:T(8,128)(2,1)}, bf16[4,2,128,128]{3,2,1,0:T(8,128)(2,1)S(1)}, u32[]{:S(2)}, u32[]{:S(2)}) collective-permute-start(bf16[4,2,128,128]{3,2,1,0:T(8,128)(2,1)} %pad_maximum_fusion.10), channel_id=1, source_target_pairs={{0,6},{2,4},{4,2},{6,0},{1,7},{3,5},{5,3},{7,1},{8,14},{10,12},{12... | collective-permute-start | bytes 786440 | tf_op jit(solution)/shard_map/ppermute | solution.py:179
  21.7 7.0 %collective-permute-done.6.refs_3_ = bf16[4,2,128,128]{3,2,1,0:T(8,128)(2,1)S(1)} collective-permute-done((bf16[4,2,128,128]{3,2,1,0:T(8,128)(2,1)S(1)}, bf16[4,2,128,128]{3,2,1,0:T(8,128)(2,1)S(1)}, u32[]{:S(2)}, u32[]{:S(2)}) %collective-permute-start.6) | collective-permute-done | bytes 262176 | tf_op jit(solution)/shard_map/ppermute | solution.py:179
  29.4 1.2 shard_map.164
  30.6 4.2 %all-to-all-start = ((bf16[4,10,128,128]{3,2,1,0:T(8,128)(2,1)}), bf16[4,10,128,128]{3,2,1,0:T(8,128)(2,1)S(1)}, u32[]{:S(2)}, u32[]{:S(2)}) async-start(bf16[4,10,128,128]{3,2,1,0:T(8,128)(2,1)} %shard_map.164), calls=%async_computation | async-start | bytes 2621440 | tf_op jit(solution)/shard_map/all_to_all | solution.py:182
  34.9 6.2 %collective-permute-done.1.refs_2_ = bf16[4,2,128,128]{3,2,1,0:T(8,128)(2,1)S(1)} collective-permute-done((bf16[4,2,128,128]{3,2,1,0:T(8,128)(2,1)}, bf16[4,2,128,128]{3,2,1,0:T(8,128)(2,1)S(1)}, u32[]{:S(2)}, u32[]{:S(2)}) %collective-permute-start.1) | collective-permute-done | bytes 262176 | tf_op jit(solution)/shard_map/ppermute | solution.py:179
  41.1 6.2 %collective-permute-done.4.refs_3_ = bf16[4,2,128,128]{3,2,1,0:T(8,128)(2,1)S(1)} collective-permute-done((bf16[4,2,128,128]{3,2,1,0:T(8,128)(2,1)}, bf16[4,2,128,128]{3,2,1,0:T(8,128)(2,1)S(1)}, u32[]{:S(2)}, u32[]{:S(2)}) %collective-permute-start.4) | collective-permute-done | bytes 262176 | tf_op jit(solution)/shard_map/ppermute | solution.py:179
  47.5 1.1 copy-done
  50.7 5.3 %collective-permute-start.9 = (bf16[4,3,128,128]{3,2,1,0:T(8,128)(2,1)}, bf16[4,3,128,128]{3,2,1,0:T(8,128)(2,1)S(1)}, u32[]{:S(2)}, u32[]{:S(2)}) collective-permute-start(bf16[4,3,128,128]{3,2,1,0:T(8,128)(2,1)} %pad_maximum_fusion.6), channel_id=1, source_target_pairs={{0,2},{2,0},{1,3},{3,1},{4,6},{6,4},{5,7},{7,5},{8,10},{10,8},{9,1... | collective-permute-start | bytes 1179656 | tf_op jit(solution)/shard_map/ppermute | solution.py:179
  57.5 1.8 %collective-permute-start.2 = (bf16[4,2,128,128]{3,2,1,0:T(8,128)(2,1)}, bf16[4,2,128,128]{3,2,1,0:T(8,128)(2,1)}, u32[]{:S(2)}, u32[]{:S(2)}) collective-permute-start(bf16[4,2,128,128]{3,2,1,0:T(8,128)(2,1)} %pad_maximum_fusion.7), channel_id=1, source_target_pairs={{0,4},{2,6},{4,0},{6,2},{1,5},{3,7},{5,1},{7,3},{8,12},{10,14},{12... | collective-permute-start | bytes 786440 | tf_op jit(solution)/shard_map/ppermute | solution.py:179
  59.3 1.5 %collective-permute-start.3 = (bf16[4,2,128,128]{3,2,1,0:T(8,128)(2,1)}, bf16[4,2,128,128]{3,2,1,0:T(8,128)(2,1)}, u32[]{:S(2)}, u32[]{:S(2)}) collective-permute-start(bf16[4,2,128,128]{3,2,1,0:T(8,128)(2,1)} %pad_maximum_fusion.8), channel_id=1, source_target_pairs={{0,6},{2,4},{4,2},{6,0},{1,7},{3,5},{5,3},{7,1},{8,14},{10,12},{12... | collective-permute-start | bytes 786440 | tf_op jit(solution)/shard_map/ppermute | solution.py:179
  60.8 3.7 %all-to-all-start.1 = ((bf16[4,10,128,128]{3,2,1,0:T(8,128)(2,1)}), bf16[4,10,128,128]{3,2,1,0:T(8,128)(2,1)S(1)}, u32[]{:S(2)}, u32[]{:S(2)}) async-start(bf16[4,10,128,128]{3,2,1,0:T(8,128)(2,1)} %copy-done), calls=%async_computation.1 | async-start | bytes 2621440 | tf_op jit(solution)/shard_map/all_to_all | solution.py:182
  67.7 3.8 %collective-permute-done.9.refs_1_ = bf16[4,3,128,128]{3,2,1,0:T(8,128)(2,1)S(1)} collective-permute-done((bf16[4,3,128,128]{3,2,1,0:T(8,128)(2,1)}, bf16[4,3,128,128]{3,2,1,0:T(8,128)(2,1)S(1)}, u32[]{:S(2)}, u32[]{:S(2)}) %collective-permute-start.9) | collective-permute-done | bytes 393248 | tf_op jit(solution)/shard_map/ppermute | solution.py:179
  71.6 8.8 %collective-permute-done.3.refs_3_ = bf16[4,2,128,128]{3,2,1,0:T(8,128)(2,1)} collective-permute-done((bf16[4,2,128,128]{3,2,1,0:T(8,128)(2,1)}, bf16[4,2,128,128]{3,2,1,0:T(8,128)(2,1)}, u32[]{:S(2)}, u32[]{:S(2)}) %collective-permute-start.3) | collective-permute-done | bytes 262176 | tf_op jit(solution)/shard_map/ppermute | solution.py:179
  80.4 1.1 shard_map.169
  81.5 1.1 copy-done.1
  82.6 7.2 %shard_map.166 = bf16[8,128,128]{2,1,0:T(8,128)(2,1)S(1)} custom-call(s32[8]{0:T(128)S(1)} %reshape.72.place_ref, f32[2,4,4096]{2,1,0:T(4,128)S(1)} %shard_map.163.bias_ref, bf16[4,10,128,128]{3,2,1,0:T(8,128)(2,1)S(1)} %all-to-all-done.q_ref.refs_0_, bf16[4,10,128,128]{3,2,1,0:T(8,128)(2,1)S(1)} %all-to-all-done.q_ref.refs_0_, ...), custom_call_target="tpu_custom_call" | custom-call | flops 1024 | bytes 4096 | tf_op jit(solution)/shard_map/pallas_call | solution.py:88
  90.8 3.7 %all-to-all-start.2 = ((bf16[4,10,128,128]{3,2,1,0:T(8,128)(2,1)}), bf16[4,10,128,128]{3,2,1,0:T(8,128)(2,1)S(1)}, u32[]{:S(2)}, u32[]{:S(2)}) async-start(bf16[4,10,128,128]{3,2,1,0:T(8,128)(2,1)} %copy-done.1), calls=%async_computation.2 | async-start | bytes 2621440 | tf_op jit(solution)/shard_map/all_to_all | solution.py:182
  95.5 7.2 %shard_map.170 = bf16[8,128,128]{2,1,0:T(8,128)(2,1)S(1)} custom-call(s32[8]{0:T(128)S(1)} %reshape.72.place_ref, f32[2,4,4096]{2,1,0:T(4,128)S(1)} %shard_map.167.bias_ref, bf16[4,10,128,128]{3,2,1,0:T(8,128)(2,1)S(1)} %all-to-all-done.1.q_ref.refs_0_, bf16[4,10,128,128]{3,2,1,0:T(8,128)(2,1)S(1)} %all-to-all-done.1.q_ref.refs_0_, ...), custom_call_target="tpu_custom_call" | custom-call | flops 1024 | bytes 4096 | tf_op jit(solution)/shard_map/pallas_call | solution.py:88
  103.5 8.2 %all-to-all-done.2.q_ref.refs_0_ = bf16[4,10,128,128]{3,2,1,0:T(8,128)(2,1)S(1)} async-done(((bf16[4,10,128,128]{3,2,1,0:T(8,128)(2,1)}), bf16[4,10,128,128]{3,2,1,0:T(8,128)(2,1)S(1)}, u32[]{:S(2)}, u32[]{:S(2)}) %all-to-all-start.2) | async-done | bytes 1310752 | tf_op jit(solution)/shard_map/all_to_all | solution.py:182
  111.7 1.9 %copy.73 = bf16[8,2,128,128]{3,2,1,0:T(8,128)(2,1)} copy(bf16[8,2,128,128]{3,2,0,1:T(8,128)(2,1)} %pad_maximum_fusion) | data formatting | bytes 1048576 | tf_op jit(solution)/shard_map/stack | solution.py:244
  113.6 6.4 %all-to-all-start.4 = ((bf16[8,2,128,128]{3,2,1,0:T(8,128)(2,1)}), bf16[8,2,128,128]{3,2,1,0:T(8,128)(2,1)}, u32[]{:S(2)}, u32[]{:S(2)}) async-start(bf16[8,2,128,128]{3,2,1,0:T(8,128)(2,1)} %copy.73), calls=%async_computation.4 | async-start | bytes 1048576 | tf_op jit(solution)/shard_map/all_to_all | solution.py:182
  120.0 7.1 %shard_map.171 = bf16[8,128,128]{2,1,0:T(8,128)(2,1)} custom-call(s32[8]{0:T(128)S(1)} %reshape.72.place_ref, f32[2,4,4096]{2,1,0:T(4,128)S(1)} %shard_map.168.bias_ref, bf16[4,10,128,128]{3,2,1,0:T(8,128)(2,1)S(1)} %all-to-all-done.2.q_ref.refs_0_, bf16[4,10,128,128]{3,2,1,0:T(8,128)(2,1)S(1)} %all-to-all-done.2.q_ref.refs_0_, ...), custom_call_target="tpu_custom_call" | custom-call | flops 1024 | bytes 4096 | tf_op jit(solution)/shard_map/pallas_call | solution.py:88
  127.1 3.4 %all-to-all-done.4 = bf16[8,2,128,128]{3,2,1,0:T(8,128)(2,1)} async-done(((bf16[8,2,128,128]{3,2,1,0:T(8,128)(2,1)}), bf16[8,2,128,128]{3,2,1,0:T(8,128)(2,1)}, u32[]{:S(2)}, u32[]{:S(2)}) %all-to-all-start.4) | async-done | bytes 524320 | tf_op jit(solution)/shard_map/all_to_all | solution.py:182
  130.5 3.4 %all-to-all-start.3 = ((bf16[8,128,128]{2,1,0:T(8,128)(2,1)}), bf16[8,128,128]{2,1,0:T(8,128)(2,1)S(1)}, u32[]{:S(2)}, u32[]{:S(2)}) async-start(bf16[8,128,128]{2,1,0:T(8,128)(2,1)} %shard_map.171), calls=%async_computation.3 | async-start | bytes 524288 | tf_op jit(solution)/shard_map/all_to_all | solution.py:182
  134.0 1.3 copy.74
  135.3 5.7 %fusion.total_ref = f32[128,3072]{1,0:T(8,128)S(1)} fusion(bf16[128,2048]{0,1:T(8,128)(2,1)S(1)} %bitcast.86, bf16[3072,3072]{1,0:T(8,128)(2,1)} %weight_ref.1), kind=kOutput, calls=%fused_computation | convolution fusion | flops 1610612736 | bytes 14680064 | tf_op jit(solution)/shard_map/dot_general | solution.py:252
  141.0 4.1 %shard_map.172 = bf16[128,3072]{1,0:T(8,128)(2,1)} custom-call(bf16[8,128,128]{2,1,0:T(8,128)(2,1)S(1)} %all-to-all-done.3.part_ref, bf16[3072,3072]{1,0:T(8,128)(2,1)} %weight_ref.1, f32[128,3072]{1,0:T(8,128)S(1)} %fusion.total_ref), custom_call_target="tpu_custom_call" | custom-call | tf_op jit(solution)/shard_map/pallas_call | solution.py:141
  (87 shorter events, 16.4 us)
Async XLA Ops:
  0.0 1.4 copy-start.7
  1.5 4.6 %copy-start.8 = (bf16[128,24,128]{2,1,0:T(8,128)(2,1)S(1)}, bf16[128,24,128]{2,1,0:T(8,128)(2,1)}, u32[]{:S(2)}) copy-start(bf16[128,24,128]{2,1,0:T(8,128)(2,1)} %param.17) | copy-start | bytes 2359300
  2.0 16.9 %collective-permute-start = (bf16[4,2,128,128]{3,2,1,0:T(8,128)(2,1)S(1)}, bf16[4,2,128,128]{3,2,1,0:T(8,128)(2,1)S(1)}, u32[]{:S(2)}, u32[]{:S(2)}) collective-permute-start(bf16[4,2,128,128]{3,2,1,0:T(8,128)(2,1)S(1)} %pad_maximum_fusion.11), channel_id=1, source_target_pairs={{0,4},{2,6},{4,0},{6,2},{1,5},{3,7},{5,1},{7,3},{8,12},{10,14},{12... | collective-permute-start | bytes 786440 | tf_op jit(solution)/shard_map/ppermute | solution.py:179
  6.8 22.6 %collective-permute-start.5 = (bf16[4,3,128,128]{3,2,1,0:T(8,128)(2,1)S(1)}, bf16[4,3,128,128]{3,2,1,0:T(8,128)(2,1)S(1)}, u32[]{:S(2)}, u32[]{:S(2)}) collective-permute-start(bf16[4,3,128,128]{3,2,1,0:T(8,128)(2,1)S(1)} %pad_maximum_fusion.2), channel_id=1, source_target_pairs={{0,2},{2,0},{1,3},{3,1},{4,6},{6,4},{5,7},{7,5},{8,10},{10,8},{9,1... | collective-permute-start | bytes 1179656 | tf_op jit(solution)/shard_map/ppermute | solution.py:179
  8.4 20.3 %collective-permute-start.6 = (bf16[4,2,128,128]{3,2,1,0:T(8,128)(2,1)S(1)}, bf16[4,2,128,128]{3,2,1,0:T(8,128)(2,1)S(1)}, u32[]{:S(2)}, u32[]{:S(2)}) collective-permute-start(bf16[4,2,128,128]{3,2,1,0:T(8,128)(2,1)S(1)} %pad_maximum_fusion.12), channel_id=1, source_target_pairs={{0,6},{2,4},{4,2},{6,0},{1,7},{3,5},{5,3},{7,1},{8,14},{10,12},{12... | collective-permute-start | bytes 786440 | tf_op jit(solution)/shard_map/ppermute | solution.py:179
  11.9 35.5 %collective-permute-start.7 = (bf16[4,3,128,128]{3,2,1,0:T(8,128)(2,1)}, bf16[4,3,128,128]{3,2,1,0:T(8,128)(2,1)S(1)}, u32[]{:S(2)}, u32[]{:S(2)}) collective-permute-start(bf16[4,3,128,128]{3,2,1,0:T(8,128)(2,1)} %pad_maximum_fusion.4), channel_id=1, source_target_pairs={{0,2},{2,0},{1,3},{3,1},{4,6},{6,4},{5,7},{7,5},{8,10},{10,8},{9,1... | collective-permute-start | bytes 1179656 | tf_op jit(solution)/shard_map/ppermute | solution.py:179
  18.9 22.2 %collective-permute-start.1 = (bf16[4,2,128,128]{3,2,1,0:T(8,128)(2,1)}, bf16[4,2,128,128]{3,2,1,0:T(8,128)(2,1)S(1)}, u32[]{:S(2)}, u32[]{:S(2)}) collective-permute-start(bf16[4,2,128,128]{3,2,1,0:T(8,128)(2,1)} %pad_maximum_fusion.9), channel_id=1, source_target_pairs={{0,4},{2,6},{4,0},{6,2},{1,5},{3,7},{5,1},{7,3},{8,12},{10,14},{12... | collective-permute-start | bytes 786440 | tf_op jit(solution)/shard_map/ppermute | solution.py:179
  18.9 28.5 %collective-permute-start.4 = (bf16[4,2,128,128]{3,2,1,0:T(8,128)(2,1)}, bf16[4,2,128,128]{3,2,1,0:T(8,128)(2,1)S(1)}, u32[]{:S(2)}, u32[]{:S(2)}) collective-permute-start(bf16[4,2,128,128]{3,2,1,0:T(8,128)(2,1)} %pad_maximum_fusion.10), channel_id=1, source_target_pairs={{0,6},{2,4},{4,2},{6,0},{1,7},{3,5},{5,3},{7,1},{8,14},{10,12},{12... | collective-permute-start | bytes 786440 | tf_op jit(solution)/shard_map/ppermute | solution.py:179
  30.5 4.3 %copy-start.11 = (pred[9]{0:T(512)(128)(4,1)S(1)}, pred[9]{0:T(512)(128)(4,1)}, u32[]{:S(2)}) copy-start(pred[9]{0:T(512)(128)(4,1)} %constant.111.clone) | copy-start | bytes 31
  30.5 4.3 %copy-start.12 = (s32[9]{0:T(128)S(1)}, s32[9]{0:T(128)}, u32[]{:S(2)}) copy-start(s32[9]{0:T(128)} %constant.110.clone) | copy-start | bytes 112
  30.5 4.3 %copy-start.13 = (s32[9]{0:T(128)S(1)}, s32[9]{0:T(128)}, u32[]{:S(2)}) copy-start(s32[9]{0:T(128)} %constant.109.clone) | copy-start | bytes 112
  30.5 4.3 %copy-start.14 = (s32[9]{0:T(128)S(1)}, s32[9]{0:T(128)}, u32[]{:S(2)}) copy-start(s32[9]{0:T(128)} %constant.108.clone) | copy-start | bytes 112
  30.6 19.0 %all-to-all-start = ((bf16[4,10,128,128]{3,2,1,0:T(8,128)(2,1)}), bf16[4,10,128,128]{3,2,1,0:T(8,128)(2,1)S(1)}, u32[]{:S(2)}, u32[]{:S(2)}) async-start(bf16[4,10,128,128]{3,2,1,0:T(8,128)(2,1)} %shard_map.164), calls=%async_computation | async-start | bytes 2621440 | tf_op jit(solution)/shard_map/all_to_all | solution.py:182
  34.9 13.7 %copy-start.2 = (s32[24,32,32]{2,1,0:T(8,128)S(1)}, s32[24,32,32]{2,1,0:T(8,128)}, u32[]{:S(2)}) copy-start(s32[24,32,32]{2,1,0:T(8,128)} %mask_ref.2) | copy-start | bytes 294916
  34.9 13.7 %copy-start.3 = (s32[4,1]{1,0:T(4,128)S(1)}, s32[4,1]{1,0:T(4,128)}, u32[]{:S(2)}) copy-start(s32[4,1]{1,0:T(4,128)} %constant.114.clone.rows_ref) | copy-start | bytes 52
  34.9 13.7 %copy-start.4 = (s32[1,512]{1,0:T(1,128)S(1)}, s32[1,512]{1,0:T(1,128)}, u32[]{:S(2)}) copy-start(s32[1,512]{1,0:T(1,128)} %constant.115.clone.cols_ref) | copy-start | bytes 6148
  47.5 1.1 copy-start
  48.6 1.0 copy-start.9
  49.5 33.0 %collective-permute-start.8 = (bf16[4,10,128,128]{3,2,1,0:T(8,128)(2,1)S(1)}, bf16[4,10,128,128]{3,2,1,0:T(8,128)(2,1)}, u32[]{:S(2)}, u32[]{:S(2)}) collective-permute-start(bf16[4,10,128,128]{3,2,1,0:T(8,128)(2,1)S(1)} %all-to-all-done.q_ref.refs_0_), channel_id=1, source_target_pairs={{0,8},{8,0},{1,9},{9,1},{2,10},{10,2},{3,11},{11,3},{4,12},{12,4},... | collective-permute-start | bytes 3932168 | tf_op jit(solution)/shard_map/ppermute | solution.py:179
  50.7 20.9 %collective-permute-start.9 = (bf16[4,3,128,128]{3,2,1,0:T(8,128)(2,1)}, bf16[4,3,128,128]{3,2,1,0:T(8,128)(2,1)S(1)}, u32[]{:S(2)}, u32[]{:S(2)}) collective-permute-start(bf16[4,3,128,128]{3,2,1,0:T(8,128)(2,1)} %pad_maximum_fusion.6), channel_id=1, source_target_pairs={{0,2},{2,0},{1,3},{3,1},{4,6},{6,4},{5,7},{7,5},{8,10},{10,8},{9,1... | collective-permute-start | bytes 1179656 | tf_op jit(solution)/shard_map/ppermute | solution.py:179
  56.0 0.8 copy-start.5
  56.0 0.8 copy-start.6
  57.5 7.0 %copy-start.10 = (s32[2,4]{1,0:T(2,128)S(1)}, s32[2,4]{1,0:T(2,128)}, u32[]{:S(2)}) copy-start(s32[2,4]{1,0:T(2,128)} %constant.112.clone) | copy-start | bytes 100
  57.5 14.1 %collective-permute-start.2 = (bf16[4,2,128,128]{3,2,1,0:T(8,128)(2,1)}, bf16[4,2,128,128]{3,2,1,0:T(8,128)(2,1)}, u32[]{:S(2)}, u32[]{:S(2)}) collective-permute-start(bf16[4,2,128,128]{3,2,1,0:T(8,128)(2,1)} %pad_maximum_fusion.7), channel_id=1, source_target_pairs={{0,4},{2,6},{4,0},{6,2},{1,5},{3,7},{5,1},{7,3},{8,12},{10,14},{12... | collective-permute-start | bytes 786440 | tf_op jit(solution)/shard_map/ppermute | solution.py:179
  59.3 21.1 %collective-permute-start.3 = (bf16[4,2,128,128]{3,2,1,0:T(8,128)(2,1)}, bf16[4,2,128,128]{3,2,1,0:T(8,128)(2,1)}, u32[]{:S(2)}, u32[]{:S(2)}) collective-permute-start(bf16[4,2,128,128]{3,2,1,0:T(8,128)(2,1)} %pad_maximum_fusion.8), channel_id=1, source_target_pairs={{0,6},{2,4},{4,2},{6,0},{1,7},{3,5},{5,3},{7,1},{8,14},{10,12},{12... | collective-permute-start | bytes 786440 | tf_op jit(solution)/shard_map/ppermute | solution.py:179
  60.8 29.9 %all-to-all-start.1 = ((bf16[4,10,128,128]{3,2,1,0:T(8,128)(2,1)}), bf16[4,10,128,128]{3,2,1,0:T(8,128)(2,1)S(1)}, u32[]{:S(2)}, u32[]{:S(2)}) async-start(bf16[4,10,128,128]{3,2,1,0:T(8,128)(2,1)} %copy-done), calls=%async_computation.1 | async-start | bytes 2621440 | tf_op jit(solution)/shard_map/all_to_all | solution.py:182
  81.5 1.1 copy-start.1
  90.7 4.8 %collective-permute-start.10 = (bf16[4,10,128,128]{3,2,1,0:T(8,128)(2,1)S(1)}, bf16[4,10,128,128]{3,2,1,0:T(8,128)(2,1)}, u32[]{:S(2)}, u32[]{:S(2)}) collective-permute-start(bf16[4,10,128,128]{3,2,1,0:T(8,128)(2,1)S(1)} %all-to-all-done.1.q_ref.refs_0_), channel_id=1, source_target_pairs={{0,8},{8,0},{1,9},{9,1},{2,10},{10,2},{3,11},{11,3},{4,12},{12,4},... | collective-permute-start | bytes 3932168 | tf_op jit(solution)/shard_map/ppermute | solution.py:179
  90.8 20.9 %all-to-all-start.2 = ((bf16[4,10,128,128]{3,2,1,0:T(8,128)(2,1)}), bf16[4,10,128,128]{3,2,1,0:T(8,128)(2,1)S(1)}, u32[]{:S(2)}, u32[]{:S(2)}) async-start(bf16[4,10,128,128]{3,2,1,0:T(8,128)(2,1)} %copy-done.1), calls=%async_computation.2 | async-start | bytes 2621440 | tf_op jit(solution)/shard_map/all_to_all | solution.py:182
  111.7 8.3 %collective-permute-start.11 = (bf16[4,10,128,128]{3,2,1,0:T(8,128)(2,1)S(1)}, bf16[4,10,128,128]{3,2,1,0:T(8,128)(2,1)S(1)}, u32[]{:S(2)}, u32[]{:S(2)}) collective-permute-start(bf16[4,10,128,128]{3,2,1,0:T(8,128)(2,1)S(1)} %all-to-all-done.2.q_ref.refs_0_), channel_id=1, source_target_pairs={{0,8},{8,0},{1,9},{9,1},{2,10},{10,2},{3,11},{11,3},{4,12},{12,4},... | collective-permute-start | bytes 3932168 | tf_op jit(solution)/shard_map/ppermute | solution.py:179
  113.6 16.9 %all-to-all-start.4 = ((bf16[8,2,128,128]{3,2,1,0:T(8,128)(2,1)}), bf16[8,2,128,128]{3,2,1,0:T(8,128)(2,1)}, u32[]{:S(2)}, u32[]{:S(2)}) async-start(bf16[8,2,128,128]{3,2,1,0:T(8,128)(2,1)} %copy.73), calls=%async_computation.4 | async-start | bytes 1048576 | tf_op jit(solution)/shard_map/all_to_all | solution.py:182
  130.5 10.4 %all-to-all-start.3 = ((bf16[8,128,128]{2,1,0:T(8,128)(2,1)}), bf16[8,128,128]{2,1,0:T(8,128)(2,1)S(1)}, u32[]{:S(2)}, u32[]{:S(2)}) async-start(bf16[8,128,128]{2,1,0:T(8,128)(2,1)} %shard_map.171), calls=%async_computation.3 | async-start | bytes 524288 | tf_op jit(solution)/shard_map/all_to_all | solution.py:182

commit v9 on v8

--- a/solution.py
+++ b/solution.py
@@ -210,33 +210,40 @@
 
     assert chunks == 3
 
-    def cross(j, *before):
-        halves = [pieces((keys, values), j, b) for b in range(2)]
-        if before:
-            halves = after(halves, *before)
-        return [across(h, ("zh", "zl"), 2 + b) for b, h in enumerate(halves)]
-
-    def joined(j, far):
-        trio = (queries, keys, values)
-        swapped = across(pieces(trio, j, 1), "zl", 1)
-        return pack((pieces(trio, j, 0), range(3)), (swapped, range(3)), *((f, range(2)) for f in far))
+    trio = (queries, keys, values)
+
+    def halves(j):
+        return [pieces((keys, values), j, b) for b in range(2)]
+
+    def cross(held):
+        return [across(h, ("zh", "zl"), 2 + b) for b, h in enumerate(held)]
+
+    def plane(j, *before):
+        given = pieces(trio, j, 1)
+        return pieces(trio, j, 0), across(after(given, *before) if before else given, "zl", 1)
+
+    def joined(own, far):
+        return pack(*((a, range(3)) for a in own), *((a, range(2)) for a in far))
 
     picks = tuple((i, 1 + 3 * r, 2 + 3 * r, 4 * i + r) for i in range(half) for r in range(2))
     picks += tuple((i, 6 + 2 * r, 7 + 2 * r, 4 * i + 2 + r) for i in range(half) for r in range(2))
     axes = gather + ("c",)
 
-    far0 = cross(0)
-    own0 = joined(0, far0)
-    far1 = cross(1, far0[0])
+    far0 = cross(halves(0))
+    plane0 = plane(0)
+    own0 = joined(plane0, far0)
+    far1 = cross(after(halves(1), far0[0]))
     got0 = spread(own0, flat)
-    bias0 = bias_of(0, *far1)
-    own1 = joined(1, far1)
+    next2, plane1, plane2 = halves(2), plane(1), plane(2, far0[0])
+    bias0 = bias_of(0, *far1, *next2, *plane2)
+    own1 = joined(plane1, far1)
     got0 = after(got0, bias0, own1)
-    far2 = cross(2, far1[0])
+    far2 = cross(after(next2, bias0))
     got1 = spread(after(own1, got0), flat)
     out0 = attend(home, bias0, got0, gathered(got0, axes), picks)
-    bias1 = bias_of(1, *far2, out0)
-    own2 = joined(2, far2)
+    far2 = after(far2, out0)
+    bias1 = bias_of(1, *far2)
+    own2 = joined(plane2, far2)
     got1 = after(got1, bias1, own2)
     got2 = spread(after(own2, got1), flat)
     bias2 = bias_of(2, bias1)

time: 146 us -> 141 us (0.966)
  waiting for transfers between devices: 49.2 us -> 46.8 us
  starting transfers between devices: 39.9 us -> 38 us
    ppermute x12, starting transfers between devices: 18.5 us -> 15 us  [across(): return lax.ppermute(a, axis, swap(n, bit))]
    unnamed x48 -> x60, local copies, waits for them, and re-layouts: 3.6 us -> 5.87 us
    ppermute x12, waiting for transfers between devices: 37.6 us -> 35.3 us  [across(): return lax.ppermute(a, axis, swap(n, bit))]
    all_to_all x5, starting transfers between devices: 21.5 us -> 23.1 us  [spread(): return lax.all_to_all(a, axes, split_axis=0, concat_axis=0, tiled=True)]
  transfers between devices with their start and end apart: 17 -> 17, of which waited for: 9 -> 9; matrix products, arithmetic and copies ran while one was open for 14% -> 12% of each run, Pallas kernels for 18% -> 19%
where the time goes in v9:
time: 141 us; the launch traced here: 140 us
  waiting for transfers between devices  46.8 us (33%)
  starting transfers between devices  38 us (27%)
  Pallas kernels  30.6 us (22%)
  local copies, waits for them, and re-layouts  11.3 us (8%)
  other arithmetic  7.16 us (5%)
  matrix products  5.66 us (4%)
    ppermute x12, waiting for transfers between devices, across(): return lax.ppermute(a, axis, swap(n, bit))  35.3 us
    all_to_all x5, starting transfers between devices, spread(): return lax.all_to_all(a, axes, split_axis=0, concat_axis=0, tiled=True)  23.1 us
    pallas_call x3, Pallas kernels, attend(): pl.pallas_call(functools.partial(attend_kernel, picks, len(arrays), scale...  21.5 us
    ppermute x12, starting transfers between devices, across(): return lax.ppermute(a, axis, swap(n, bit))  15 us
    all_to_all x5, waiting for transfers between devices, spread(): return lax.all_to_all(a, axes, split_axis=0, concat_axis=0, tiled=True)  11.5 us
    unnamed x60, local copies, waits for them, and re-layouts  5.87 us
    dot_general x1, matrix products, shards(): jnp.dot(early, out_weight[:rows], preferred_element_type=jnp.float32)  5.66 us
    another operation x12, other arithmetic, pieces(): return jnp.stack(out, axis=1)  5.64 us
  transfers between devices with their start and end apart: 17, of which 9 were waited for; matrix products, arithmetic and copies ran while one was open for 12% of the time, Pallas kernels for 19%

profile of v9, /device:TPU:0, one launch (start us, length us, event | category | flops | bytes accessed | tf_op | source)
XLA Modules:
  0.0 140.2 jit_solution(4413676798080122553)
XLA Ops:
  0.0 1.2 fusion.2
  3.1 4.1 %collective-permute-start = (bf16[4,2,128,128]{3,2,1,0:T(8,128)(2,1)S(1)}, bf16[4,2,128,128]{3,2,1,0:T(8,128)(2,1)S(1)}, u32[]{:S(2)}, u32[]{:S(2)}) collective-permute-start(bf16[4,2,128,128]{3,2,1,0:T(8,128)(2,1)S(1)} %pad_maximum_fusion.11), channel_id=1, source_target_pairs={{0,4},{2,6},{4,0},{6,2},{1,5},{3,7},{5,1},{7,3},{8,12},{10,14},{12... | collective-permute-start | bytes 786440 | tf_op jit(solution)/shard_map/ppermute | solution.py:179
  7.3 1.4 %collective-permute-start.7 = (bf16[4,2,128,128]{3,2,1,0:T(8,128)(2,1)S(1)}, bf16[4,2,128,128]{3,2,1,0:T(8,128)(2,1)S(1)}, u32[]{:S(2)}, u32[]{:S(2)}) collective-permute-start(bf16[4,2,128,128]{3,2,1,0:T(8,128)(2,1)S(1)} %pad_maximum_fusion.12), channel_id=1, source_target_pairs={{0,6},{2,4},{4,2},{6,0},{1,7},{3,5},{5,3},{7,1},{8,14},{10,12},{12... | collective-permute-start | bytes 786440 | tf_op jit(solution)/shard_map/ppermute | solution.py:179
  10.7 1.8 %collective-permute-start.8 = (bf16[4,3,128,128]{3,2,1,0:T(8,128)(2,1)}, bf16[4,3,128,128]{3,2,1,0:T(8,128)(2,1)S(1)}, u32[]{:S(2)}, u32[]{:S(2)}) collective-permute-start(bf16[4,3,128,128]{3,2,1,0:T(8,128)(2,1)} %pad_maximum_fusion.6), channel_id=1, source_target_pairs={{0,2},{2,0},{1,3},{3,1},{4,6},{6,4},{5,7},{7,5},{8,10},{10,8},{9,1... | collective-permute-start | bytes 1179656 | tf_op jit(solution)/shard_map/ppermute | solution.py:179
  15.4 10.2 %collective-permute-done.refs_2_ = bf16[4,2,128,128]{3,2,1,0:T(8,128)(2,1)S(1)} collective-permute-done((bf16[4,2,128,128]{3,2,1,0:T(8,128)(2,1)S(1)}, bf16[4,2,128,128]{3,2,1,0:T(8,128)(2,1)S(1)}, u32[]{:S(2)}, u32[]{:S(2)}) %collective-permute-start) | collective-permute-done | bytes 262176 | tf_op jit(solution)/shard_map/ppermute | solution.py:179
  26.3 3.4 %collective-permute-start.1 = (bf16[4,2,128,128]{3,2,1,0:T(8,128)(2,1)}, bf16[4,2,128,128]{3,2,1,0:T(8,128)(2,1)S(1)}, u32[]{:S(2)}, u32[]{:S(2)}) collective-permute-start(bf16[4,2,128,128]{3,2,1,0:T(8,128)(2,1)} %pad_maximum_fusion.9), channel_id=1, source_target_pairs={{0,4},{2,6},{4,0},{6,2},{1,5},{3,7},{5,1},{7,3},{8,12},{10,14},{12... | collective-permute-start | bytes 786440 | tf_op jit(solution)/shard_map/ppermute | solution.py:179
  29.7 1.0 collective-permute-start.2
  30.7 5.3 %collective-permute-done.6.refs_1_ = bf16[4,3,128,128]{3,2,1,0:T(8,128)(2,1)S(1)} collective-permute-done((bf16[4,3,128,128]{3,2,1,0:T(8,128)(2,1)S(1)}, bf16[4,3,128,128]{3,2,1,0:T(8,128)(2,1)S(1)}, u32[]{:S(2)}, u32[]{:S(2)}) %collective-permute-start.6) | collective-permute-done | bytes 393248 | tf_op jit(solution)/shard_map/ppermute | solution.py:179
  36.1 1.1 shard_map.164
  37.2 4.0 %all-to-all-start = ((bf16[4,10,128,128]{3,2,1,0:T(8,128)(2,1)}), bf16[4,10,128,128]{3,2,1,0:T(8,128)(2,1)S(1)}, u32[]{:S(2)}, u32[]{:S(2)}) async-start(bf16[4,10,128,128]{3,2,1,0:T(8,128)(2,1)} %shard_map.164), calls=%async_computation | async-start | bytes 2621440 | tf_op jit(solution)/shard_map/all_to_all | solution.py:182
  41.2 1.6 %pad_maximum_fusion.7 = bf16[4,2,128,128]{3,2,1,0:T(8,128)(2,1)} fusion(bf16[4,1,128,128]{3,2,1,0:T(8,128)(2,1)} %bitcast.64, bf16[4,1,128,128]{3,2,1,0:T(8,128)(2,1)S(1)} %bitcast.62), kind=kLoop, calls=%fused_computation.9 | loop fusion | flops 131072 | bytes 524288 | tf_op jit(solution)/shard_map/stack | solution.py:191
  43.5 1.5 %collective-permute-done.8.refs_1_ = bf16[4,3,128,128]{3,2,1,0:T(8,128)(2,1)S(1)} collective-permute-done((bf16[4,3,128,128]{3,2,1,0:T(8,128)(2,1)}, bf16[4,3,128,128]{3,2,1,0:T(8,128)(2,1)S(1)}, u32[]{:S(2)}, u32[]{:S(2)}) %collective-permute-start.8) | collective-permute-done | bytes 393248 | tf_op jit(solution)/shard_map/ppermute | solution.py:179
  45.0 5.6 %collective-permute-done.1.refs_2_ = bf16[4,2,128,128]{3,2,1,0:T(8,128)(2,1)S(1)} collective-permute-done((bf16[4,2,128,128]{3,2,1,0:T(8,128)(2,1)}, bf16[4,2,128,128]{3,2,1,0:T(8,128)(2,1)S(1)}, u32[]{:S(2)}, u32[]{:S(2)}) %collective-permute-start.1) | collective-permute-done | bytes 262176 | tf_op jit(solution)/shard_map/ppermute | solution.py:179
  50.6 6.3 %collective-permute-done.2.refs_3_ = bf16[4,2,128,128]{3,2,1,0:T(8,128)(2,1)S(1)} collective-permute-done((bf16[4,2,128,128]{3,2,1,0:T(8,128)(2,1)}, bf16[4,2,128,128]{3,2,1,0:T(8,128)(2,1)S(1)}, u32[]{:S(2)}, u32[]{:S(2)}) %collective-permute-start.2) | collective-permute-done | bytes 262176 | tf_op jit(solution)/shard_map/ppermute | solution.py:179
  57.0 1.1 copy-done
  60.7 1.9 %collective-permute-start.5 = (bf16[4,2,128,128]{3,2,1,0:T(8,128)(2,1)}, bf16[4,2,128,128]{3,2,1,0:T(8,128)(2,1)}, u32[]{:S(2)}, u32[]{:S(2)}) collective-permute-start(bf16[4,2,128,128]{3,2,1,0:T(8,128)(2,1)} %pad_maximum_fusion.8), channel_id=1, source_target_pairs={{0,6},{2,4},{4,2},{6,0},{1,7},{3,5},{5,3},{7,1},{8,14},{10,12},{12... | collective-permute-start | bytes 786440 | tf_op jit(solution)/shard_map/ppermute | solution.py:179
  62.6 3.7 %all-to-all-start.1 = ((bf16[4,10,128,128]{3,2,1,0:T(8,128)(2,1)}), bf16[4,10,128,128]{3,2,1,0:T(8,128)(2,1)S(1)}, u32[]{:S(2)}, u32[]{:S(2)}) async-start(bf16[4,10,128,128]{3,2,1,0:T(8,128)(2,1)} %copy-done), calls=%async_computation.1 | async-start | bytes 2621440 | tf_op jit(solution)/shard_map/all_to_all | solution.py:182
  67.4 7.2 %shard_map.166 = bf16[8,128,128]{2,1,0:T(8,128)(2,1)S(1)} custom-call(s32[8]{0:T(128)S(1)} %reshape.72.place_ref, f32[2,4,4096]{2,1,0:T(4,128)S(1)} %copy-done.8, bf16[4,10,128,128]{3,2,1,0:T(8,128)(2,1)S(1)} %all-to-all-done.q_ref.refs_0_, bf16[4,10,128,128]{3,2,1,0:T(8,128)(2,1)S(1)} %all-to-all-done.q_ref.refs_0_, ...), custom_call_target="tpu_custom_call" | custom-call | flops 1024 | bytes 4096 | tf_op jit(solution)/shard_map/pallas_call | solution.py:88
  74.6 6.4 %collective-permute-done.4.refs_2_ = bf16[4,2,128,128]{3,2,1,0:T(8,128)(2,1)S(1)} collective-permute-done((bf16[4,2,128,128]{3,2,1,0:T(8,128)(2,1)}, bf16[4,2,128,128]{3,2,1,0:T(8,128)(2,1)S(1)}, u32[]{:S(2)}, u32[]{:S(2)}) %collective-permute-start.4) | collective-permute-done | bytes 262176 | tf_op jit(solution)/shard_map/ppermute | solution.py:179
  81.0 1.0 shard_map.169
  82.0 1.0 copy-done.1
  84.1 3.7 %all-to-all-start.2 = ((bf16[4,10,128,128]{3,2,1,0:T(8,128)(2,1)}), bf16[4,10,128,128]{3,2,1,0:T(8,128)(2,1)S(1)}, u32[]{:S(2)}, u32[]{:S(2)}) async-start(bf16[4,10,128,128]{3,2,1,0:T(8,128)(2,1)} %copy-done.1), calls=%async_computation.2 | async-start | bytes 2621440 | tf_op jit(solution)/shard_map/all_to_all | solution.py:182
  87.8 1.0 copy-done.6
  89.8 7.2 %shard_map.170 = bf16[8,128,128]{2,1,0:T(8,128)(2,1)S(1)} custom-call(s32[8]{0:T(128)S(1)} %reshape.72.place_ref, f32[2,4,4096]{2,1,0:T(4,128)S(1)} %shard_map.167.bias_ref, bf16[4,10,128,128]{3,2,1,0:T(8,128)(2,1)S(1)} %all-to-all-done.1.q_ref.refs_0_, bf16[4,10,128,128]{3,2,1,0:T(8,128)(2,1)S(1)} %all-to-all-done.1.q_ref.refs_0_, ...), custom_call_target="tpu_custom_call" | custom-call | flops 1024 | bytes 4096 | tf_op jit(solution)/shard_map/pallas_call | solution.py:88
  97.8 7.2 %all-to-all-done.2.q_ref.refs_0_ = bf16[4,10,128,128]{3,2,1,0:T(8,128)(2,1)S(1)} async-done(((bf16[4,10,128,128]{3,2,1,0:T(8,128)(2,1)}), bf16[4,10,128,128]{3,2,1,0:T(8,128)(2,1)S(1)}, u32[]{:S(2)}, u32[]{:S(2)}) %all-to-all-start.2) | async-done | bytes 1310752 | tf_op jit(solution)/shard_map/all_to_all | solution.py:182
  105.0 1.9 %copy.73 = bf16[8,2,128,128]{3,2,1,0:T(8,128)(2,1)} copy(bf16[8,2,128,128]{3,2,0,1:T(8,128)(2,1)} %pad_maximum_fusion) | data formatting | bytes 1048576 | tf_op jit(solution)/shard_map/stack | solution.py:251
  106.9 8.3 %all-to-all-start.4 = ((bf16[8,2,128,128]{3,2,1,0:T(8,128)(2,1)}), bf16[8,2,128,128]{3,2,1,0:T(8,128)(2,1)S(1)}, u32[]{:S(2)}, u32[]{:S(2)}) async-start(bf16[8,2,128,128]{3,2,1,0:T(8,128)(2,1)} %copy.73), calls=%async_computation.4 | async-start | bytes 1048576 | tf_op jit(solution)/shard_map/all_to_all | solution.py:182
  115.2 7.1 %shard_map.171 = bf16[8,128,128]{2,1,0:T(8,128)(2,1)} custom-call(s32[8]{0:T(128)S(1)} %reshape.72.place_ref, f32[2,4,4096]{2,1,0:T(4,128)S(1)} %shard_map.168.bias_ref, bf16[4,10,128,128]{3,2,1,0:T(8,128)(2,1)S(1)} %all-to-all-done.2.q_ref.refs_0_, bf16[4,10,128,128]{3,2,1,0:T(8,128)(2,1)S(1)} %all-to-all-done.2.q_ref.refs_0_, ...), custom_call_target="tpu_custom_call" | custom-call | flops 1024 | bytes 4096 | tf_op jit(solution)/shard_map/pallas_call | solution.py:88
  122.3 3.3 %all-to-all-done.4 = bf16[8,2,128,128]{3,2,1,0:T(8,128)(2,1)S(1)} async-done(((bf16[8,2,128,128]{3,2,1,0:T(8,128)(2,1)}), bf16[8,2,128,128]{3,2,1,0:T(8,128)(2,1)S(1)}, u32[]{:S(2)}, u32[]{:S(2)}) %all-to-all-start.4) | async-done | bytes 524320 | tf_op jit(solution)/shard_map/all_to_all | solution.py:182
  125.6 3.4 %all-to-all-start.3 = ((bf16[8,128,128]{2,1,0:T(8,128)(2,1)}), bf16[8,128,128]{2,1,0:T(8,128)(2,1)S(1)}, u32[]{:S(2)}, u32[]{:S(2)}) async-start(bf16[8,128,128]{2,1,0:T(8,128)(2,1)} %shard_map.171), calls=%async_computation.3 | async-start | bytes 524288 | tf_op jit(solution)/shard_map/all_to_all | solution.py:182
  129.3 5.7 %fusion.total_ref = f32[128,3072]{1,0:T(8,128)S(1)} fusion(bf16[128,2048]{0,1:T(8,128)(2,1)S(1)} %bitcast.86, bf16[3072,3072]{1,0:T(8,128)(2,1)} %weight_ref.1), kind=kOutput, calls=%fused_computation | convolution fusion | flops 1610612736 | bytes 14680064 | tf_op jit(solution)/shard_map/dot_general | solution.py:259
  135.9 4.1 %shard_map.172 = bf16[128,3072]{1,0:T(8,128)(2,1)} custom-call(bf16[8,128,128]{2,1,0:T(8,128)(2,1)S(1)} %all-to-all-done.3.part_ref, bf16[3072,3072]{1,0:T(8,128)(2,1)} %weight_ref.1, f32[128,3072]{1,0:T(8,128)S(1)} %fusion.total_ref), custom_call_target="tpu_custom_call" | custom-call | tf_op jit(solution)/shard_map/pallas_call | solution.py:141
  (99 shorter events, 15.8 us)
Async XLA Ops:
  0.0 1.4 copy-start.14
  1.4 1.1 copy-start.15
  3.1 22.5 %collective-permute-start = (bf16[4,2,128,128]{3,2,1,0:T(8,128)(2,1)S(1)}, bf16[4,2,128,128]{3,2,1,0:T(8,128)(2,1)S(1)}, u32[]{:S(2)}, u32[]{:S(2)}) collective-permute-start(bf16[4,2,128,128]{3,2,1,0:T(8,128)(2,1)S(1)} %pad_maximum_fusion.11), channel_id=1, source_target_pairs={{0,4},{2,6},{4,0},{6,2},{1,5},{3,7},{5,1},{7,3},{8,12},{10,14},{12... | collective-permute-start | bytes 786440 | tf_op jit(solution)/shard_map/ppermute | solution.py:179
  7.3 22.4 %collective-permute-start.7 = (bf16[4,2,128,128]{3,2,1,0:T(8,128)(2,1)S(1)}, bf16[4,2,128,128]{3,2,1,0:T(8,128)(2,1)S(1)}, u32[]{:S(2)}, u32[]{:S(2)}) collective-permute-start(bf16[4,2,128,128]{3,2,1,0:T(8,128)(2,1)S(1)} %pad_maximum_fusion.12), channel_id=1, source_target_pairs={{0,6},{2,4},{4,2},{6,0},{1,7},{3,5},{5,3},{7,1},{8,14},{10,12},{12... | collective-permute-start | bytes 786440 | tf_op jit(solution)/shard_map/ppermute | solution.py:179
  8.8 27.3 %collective-permute-start.6 = (bf16[4,3,128,128]{3,2,1,0:T(8,128)(2,1)S(1)}, bf16[4,3,128,128]{3,2,1,0:T(8,128)(2,1)S(1)}, u32[]{:S(2)}, u32[]{:S(2)}) collective-permute-start(bf16[4,3,128,128]{3,2,1,0:T(8,128)(2,1)S(1)} %pad_maximum_fusion.4), channel_id=1, source_target_pairs={{0,2},{2,0},{1,3},{3,1},{4,6},{6,4},{5,7},{7,5},{8,10},{10,8},{9,1... | collective-permute-start | bytes 1179656 | tf_op jit(solution)/shard_map/ppermute | solution.py:179
  10.7 34.3 %collective-permute-start.8 = (bf16[4,3,128,128]{3,2,1,0:T(8,128)(2,1)}, bf16[4,3,128,128]{3,2,1,0:T(8,128)(2,1)S(1)}, u32[]{:S(2)}, u32[]{:S(2)}) collective-permute-start(bf16[4,3,128,128]{3,2,1,0:T(8,128)(2,1)} %pad_maximum_fusion.6), channel_id=1, source_target_pairs={{0,2},{2,0},{1,3},{3,1},{4,6},{6,4},{5,7},{7,5},{8,10},{10,8},{9,1... | collective-permute-start | bytes 1179656 | tf_op jit(solution)/shard_map/ppermute | solution.py:179
  15.2 20.8 %copy-start.11 = (bf16[2,1,2,128,128]{4,3,2,0,1:T(8,128)(2,1)}, bf16[2,1,2,128,128]{4,3,2,0,1:T(8,128)(2,1)S(1)}, u32[]{:S(2)}) copy-start(bf16[2,1,2,128,128]{4,3,2,0,1:T(8,128)(2,1)S(1)} %copy.75) | copy-start | bytes 393220
  15.3 20.8 %copy-start.13 = (bf16[2,1,2,128,128]{4,3,2,0,1:T(8,128)(2,1)}, bf16[2,1,2,128,128]{4,3,2,0,1:T(8,128)(2,1)S(1)}, u32[]{:S(2)}) copy-start(bf16[2,1,2,128,128]{4,3,2,0,1:T(8,128)(2,1)S(1)} %copy.76) | copy-start | bytes 393220
  25.6 32.5 %collective-permute-start.3 = (bf16[4,3,128,128]{3,2,1,0:T(8,128)(2,1)}, bf16[4,3,128,128]{3,2,1,0:T(8,128)(2,1)S(1)}, u32[]{:S(2)}, u32[]{:S(2)}) collective-permute-start(bf16[4,3,128,128]{3,2,1,0:T(8,128)(2,1)} %pad_maximum_fusion.2), channel_id=1, source_target_pairs={{0,2},{2,0},{1,3},{3,1},{4,6},{6,4},{5,7},{7,5},{8,10},{10,8},{9,1... | collective-permute-start | bytes 1179656 | tf_op jit(solution)/shard_map/ppermute | solution.py:179
  26.3 24.3 %collective-permute-start.1 = (bf16[4,2,128,128]{3,2,1,0:T(8,128)(2,1)}, bf16[4,2,128,128]{3,2,1,0:T(8,128)(2,1)S(1)}, u32[]{:S(2)}, u32[]{:S(2)}) collective-permute-start(bf16[4,2,128,128]{3,2,1,0:T(8,128)(2,1)} %pad_maximum_fusion.9), channel_id=1, source_target_pairs={{0,4},{2,6},{4,0},{6,2},{1,5},{3,7},{5,1},{7,3},{8,12},{10,14},{12... | collective-permute-start | bytes 786440 | tf_op jit(solution)/shard_map/ppermute | solution.py:179
  29.7 27.2 %collective-permute-start.2 = (bf16[4,2,128,128]{3,2,1,0:T(8,128)(2,1)}, bf16[4,2,128,128]{3,2,1,0:T(8,128)(2,1)S(1)}, u32[]{:S(2)}, u32[]{:S(2)}) collective-permute-start(bf16[4,2,128,128]{3,2,1,0:T(8,128)(2,1)} %pad_maximum_fusion.10), channel_id=1, source_target_pairs={{0,6},{2,4},{4,2},{6,0},{1,7},{3,5},{5,3},{7,1},{8,14},{10,12},{12... | collective-permute-start | bytes 786440 | tf_op jit(solution)/shard_map/ppermute | solution.py:179
  37.2 4.0 %copy-start.12 = (bf16[2,1,2,128,128]{4,3,2,0,1:T(8,128)(2,1)S(1)}, bf16[2,1,2,128,128]{4,3,2,0,1:T(8,128)(2,1)}, u32[]{:S(2)}) copy-start(bf16[2,1,2,128,128]{4,3,2,0,1:T(8,128)(2,1)} %copy-done.11) | copy-start | bytes 393220
  37.2 5.6 %copy-start.18 = (pred[9]{0:T(512)(128)(4,1)S(1)}, pred[9]{0:T(512)(128)(4,1)}, u32[]{:S(2)}) copy-start(pred[9]{0:T(512)(128)(4,1)} %constant.111.clone) | copy-start | bytes 31
  37.2 5.6 %copy-start.19 = (s32[9]{0:T(128)S(1)}, s32[9]{0:T(128)}, u32[]{:S(2)}) copy-start(s32[9]{0:T(128)} %constant.110.clone) | copy-start | bytes 112
  37.2 5.6 %copy-start.20 = (s32[9]{0:T(128)S(1)}, s32[9]{0:T(128)}, u32[]{:S(2)}) copy-start(s32[9]{0:T(128)} %constant.109.clone) | copy-start | bytes 112
  37.2 22.5 %all-to-all-start = ((bf16[4,10,128,128]{3,2,1,0:T(8,128)(2,1)}), bf16[4,10,128,128]{3,2,1,0:T(8,128)(2,1)S(1)}, u32[]{:S(2)}, u32[]{:S(2)}) async-start(bf16[4,10,128,128]{3,2,1,0:T(8,128)(2,1)} %shard_map.164), calls=%async_computation | async-start | bytes 2621440 | tf_op jit(solution)/shard_map/all_to_all | solution.py:182
  43.5 14.6 %copy-start.4 = (s32[24,32,32]{2,1,0:T(8,128)S(1)}, s32[24,32,32]{2,1,0:T(8,128)}, u32[]{:S(2)}) copy-start(s32[24,32,32]{2,1,0:T(8,128)} %mask_ref.2) | copy-start | bytes 294916
  43.5 14.6 %copy-start.9 = (s32[1,512]{1,0:T(1,128)S(1)}, s32[1,512]{1,0:T(1,128)}, u32[]{:S(2)}) copy-start(s32[1,512]{1,0:T(1,128)} %constant.115.clone.cols_ref) | copy-start | bytes 6148
  43.5 14.6 %copy-start.10 = (s32[4,1]{1,0:T(4,128)S(1)}, s32[4,1]{1,0:T(4,128)}, u32[]{:S(2)}) copy-start(s32[4,1]{1,0:T(4,128)} %constant.114.clone.rows_ref) | copy-start | bytes 52
  59.7 6.6 %copy-start.16 = (s32[2,4]{1,0:T(2,128)S(1)}, s32[2,4]{1,0:T(2,128)}, u32[]{:S(2)}) copy-start(s32[2,4]{1,0:T(2,128)} %constant.113.clone) | copy-start | bytes 100
  59.7 6.6 %copy-start.17 = (s32[2,4]{1,0:T(2,128)S(1)}, s32[2,4]{1,0:T(2,128)}, u32[]{:S(2)}) copy-start(s32[2,4]{1,0:T(2,128)} %constant.112.clone) | copy-start | bytes 100
  59.7 6.7 %collective-permute-start.9 = (bf16[4,10,128,128]{3,2,1,0:T(8,128)(2,1)S(1)}, bf16[4,10,128,128]{3,2,1,0:T(8,128)(2,1)}, u32[]{:S(2)}, u32[]{:S(2)}) collective-permute-start(bf16[4,10,128,128]{3,2,1,0:T(8,128)(2,1)S(1)} %all-to-all-done.q_ref.refs_0_), channel_id=1, source_target_pairs={{0,8},{8,0},{1,9},{9,1},{2,10},{10,2},{3,11},{11,3},{4,12},{12,4},... | collective-permute-start | bytes 3932168 | tf_op jit(solution)/shard_map/ppermute | solution.py:179
  59.7 21.2 %collective-permute-start.4 = (bf16[4,2,128,128]{3,2,1,0:T(8,128)(2,1)}, bf16[4,2,128,128]{3,2,1,0:T(8,128)(2,1)S(1)}, u32[]{:S(2)}, u32[]{:S(2)}) collective-permute-start(bf16[4,2,128,128]{3,2,1,0:T(8,128)(2,1)} %pad_maximum_fusion.7), channel_id=1, source_target_pairs={{0,4},{2,6},{4,0},{6,2},{1,5},{3,7},{5,1},{7,3},{8,12},{10,14},{12... | collective-permute-start | bytes 786440 | tf_op jit(solution)/shard_map/ppermute | solution.py:179
  60.7 20.3 %collective-permute-start.5 = (bf16[4,2,128,128]{3,2,1,0:T(8,128)(2,1)}, bf16[4,2,128,128]{3,2,1,0:T(8,128)(2,1)}, u32[]{:S(2)}, u32[]{:S(2)}) collective-permute-start(bf16[4,2,128,128]{3,2,1,0:T(8,128)(2,1)} %pad_maximum_fusion.8), channel_id=1, source_target_pairs={{0,6},{2,4},{4,2},{6,0},{1,7},{3,5},{5,3},{7,1},{8,14},{10,12},{12... | collective-permute-start | bytes 786440 | tf_op jit(solution)/shard_map/ppermute | solution.py:179
  62.6 21.4 %all-to-all-start.1 = ((bf16[4,10,128,128]{3,2,1,0:T(8,128)(2,1)}), bf16[4,10,128,128]{3,2,1,0:T(8,128)(2,1)S(1)}, u32[]{:S(2)}, u32[]{:S(2)}) async-start(bf16[4,10,128,128]{3,2,1,0:T(8,128)(2,1)} %copy-done), calls=%async_computation.1 | async-start | bytes 2621440 | tf_op jit(solution)/shard_map/all_to_all | solution.py:182
  66.4 14.5 %copy-start.3 = (bf16[4,3,128,128]{3,2,1,0:T(8,128)(2,1)S(1)}, bf16[4,3,128,128]{3,2,1,0:T(8,128)(2,1)}, u32[]{:S(2)}) copy-start(bf16[4,3,128,128]{3,2,1,0:T(8,128)(2,1)} %copy-done.2) | copy-start | bytes 1179652
  74.6 8.5 %copy-start.5 = (s32[24,32,32]{2,1,0:T(8,128)S(1)}, s32[24,32,32]{2,1,0:T(8,128)}, u32[]{:S(2)}) copy-start(s32[24,32,32]{2,1,0:T(8,128)} %mask_ref.2) | copy-start | bytes 294916
  84.0 5.8 %collective-permute-start.10 = (bf16[4,10,128,128]{3,2,1,0:T(8,128)(2,1)S(1)}, bf16[4,10,128,128]{3,2,1,0:T(8,128)(2,1)}, u32[]{:S(2)}, u32[]{:S(2)}) collective-permute-start(bf16[4,10,128,128]{3,2,1,0:T(8,128)(2,1)S(1)} %all-to-all-done.1.q_ref.refs_0_), channel_id=1, source_target_pairs={{0,8},{8,0},{1,9},{9,1},{2,10},{10,2},{3,11},{11,3},{4,12},{12,4},... | collective-permute-start | bytes 3932168 | tf_op jit(solution)/shard_map/ppermute | solution.py:179
  84.1 20.9 %all-to-all-start.2 = ((bf16[4,10,128,128]{3,2,1,0:T(8,128)(2,1)}), bf16[4,10,128,128]{3,2,1,0:T(8,128)(2,1)S(1)}, u32[]{:S(2)}, u32[]{:S(2)}) async-start(bf16[4,10,128,128]{3,2,1,0:T(8,128)(2,1)} %copy-done.1), calls=%async_computation.2 | async-start | bytes 2621440 | tf_op jit(solution)/shard_map/all_to_all | solution.py:182
  105.0 10.2 %collective-permute-start.11 = (bf16[4,10,128,128]{3,2,1,0:T(8,128)(2,1)S(1)}, bf16[4,10,128,128]{3,2,1,0:T(8,128)(2,1)S(1)}, u32[]{:S(2)}, u32[]{:S(2)}) collective-permute-start(bf16[4,10,128,128]{3,2,1,0:T(8,128)(2,1)S(1)} %all-to-all-done.2.q_ref.refs_0_), channel_id=1, source_target_pairs={{0,8},{8,0},{1,9},{9,1},{2,10},{10,2},{3,11},{11,3},{4,12},{12,4},... | collective-permute-start | bytes 3932168 | tf_op jit(solution)/shard_map/ppermute | solution.py:179
  106.9 18.7 %all-to-all-start.4 = ((bf16[8,2,128,128]{3,2,1,0:T(8,128)(2,1)}), bf16[8,2,128,128]{3,2,1,0:T(8,128)(2,1)S(1)}, u32[]{:S(2)}, u32[]{:S(2)}) async-start(bf16[8,2,128,128]{3,2,1,0:T(8,128)(2,1)} %copy.73), calls=%async_computation.4 | async-start | bytes 1048576 | tf_op jit(solution)/shard_map/all_to_all | solution.py:182
  125.6 10.3 %all-to-all-start.3 = ((bf16[8,128,128]{2,1,0:T(8,128)(2,1)}), bf16[8,128,128]{2,1,0:T(8,128)(2,1)S(1)}, u32[]{:S(2)}, u32[]{:S(2)}) async-start(bf16[8,128,128]{2,1,0:T(8,128)(2,1)} %shard_map.171), calls=%async_computation.3 | async-start | bytes 524288 | tf_op jit(solution)/shard_map/all_to_all | solution.py:182
  (6 other events, 5.7 us)

commit v10 on v3

--- a/solution.py
+++ b/solution.py
@@ -117,6 +117,59 @@
     )(*args)
 
 
+def pack_kernel(takes, *refs):
+    at = 0
+    for ref, parts in zip(refs, takes):
+        for part in parts:
+            refs[-1][:, at] = ref[:, part]
+            at += 1
+
+
+def pack(*takes, cost=10**6):
+    arrays = [a for a, _ in takes]
+    first = arrays[0]
+    count = sum(len(parts) for _, parts in takes)
+    return pl.pallas_call(
+        functools.partial(pack_kernel, [tuple(parts) for _, parts in takes]),
+        out_shape=jax.ShapeDtypeStruct((first.shape[0], count) + first.shape[2:], first.dtype),
+        in_specs=[VMEM] * len(arrays),
+        out_specs=VMEM,
+        compiler_params=grant(*arrays),
+        cost_estimate=pl.CostEstimate(flops=cost, bytes_accessed=10**4, transcendentals=0),
+    )(*arrays)
+
+
+def finish_kernel(step, part_ref, weight_ref, total_ref, out_ref, rows_ref, sems):
+    width = rows_ref.shape[1]
+    first = weight_ref.shape[0] - width
+    copies = []
+    for i in range(rows_ref.shape[0]):
+        source = weight_ref.at[first:, i * step : (i + 1) * step]
+        copies.append(pltpu.make_async_copy(source, rows_ref.at[i], sems.at[i]))
+        copies[i].start()
+    joined = jnp.concatenate([part_ref[i] for i in range(part_ref.shape[0])], axis=1)
+    for i, copy in enumerate(copies):
+        copy.wait()
+        at = slice(i * step, (i + 1) * step)
+        product = jnp.dot(joined, rows_ref[i], preferred_element_type=jnp.float32)
+        out_ref[:, at] = (total_ref[:, at] + product).astype(out_ref.dtype)
+
+
+def finish(part, weight, total):
+    pieces, _, hdim = part.shape
+    step = math.gcd(weight.shape[1], 512)
+    count = weight.shape[1] // step
+    rows = jax.ShapeDtypeStruct((count, pieces * hdim, step), weight.dtype)
+    return pl.pallas_call(
+        functools.partial(finish_kernel, step),
+        out_shape=jax.ShapeDtypeStruct(total.shape, jnp.bfloat16),
+        in_specs=[VMEM, pl.BlockSpec(memory_space=pltpu.HBM), VMEM],
+        out_specs=VMEM,
+        scratch_shapes=[pltpu.VMEM(rows.shape, rows.dtype), pltpu.SemaphoreType.DMA((count,))],
+        compiler_params=pltpu.CompilerParams(vmem_limit_bytes=50 * 2**20),
+    )(part, weight, total)
+
+
 def shards(split, gather, queries, keys, values, block_mask, out_weight):
     sizes = {a: lax.axis_size(a) for a in AXES}
     stride = {a: math.prod(list(sizes.values())[i + 1 :]) for i, a in enumerate(AXES)}
@@ -182,7 +235,8 @@
     own = []
     for j in (1, 2, 0) if chunks == 3 else range(chunks):
         own.append((j, pieces(trio, j, 0), across(pieces(trio, j, 1), "zl", 1)))
-    own = {j: jnp.concatenate([mine, got], axis=1) for j, mine, got in own}
+    last = own[-1]
+    own = {j: jnp.concatenate([mine, got], axis=1) for j, mine, got in own[:-1]}
 
     near_pick = tuple((i, 2 * r, 2 * r + 1, 4 * i + r) for i in range(half) for r in range(2))
     far_pick = tuple((i, 2 * r, 2 * r + 1, 4 * i + 2 + r) for i in range(half) for r in range(2))
@@ -202,27 +256,25 @@
         near = gathered(kv, axes)
         state = attend(home, bias, got, near, near_pick, None, False)
         waiting.append((bias, got, far, state))
-    got = spread(after(jnp.concatenate([own[0], *far0], axis=1), kv), flat)
+    parts = [(a, range(a.shape[1])) for a in (*last[1:], *far0)]
+    got = spread(after(pack(*parts), kv), flat)
     for j, (bias, mine, far, state) in enumerate(waiting[:-1], 1):
         outs[j] = attend(home, bias, mine, gathered(far, axes), far_pick, state, True)
     bias, mine, far, state = waiting[-1]
     bias0 = bias_of(0, far)
     got = after(got, bias0, state, outs[-2])
-    outs[0] = attend(home, bias0, got, gathered(got, axes), both_pick, None, True)
+    all0 = gathered(got, axes)
+    far_all = gathered(far, axes)
+    outs[0] = attend(home, bias0, after(got, *far_all), all0, both_pick, None, True)
     ready = jnp.stack(outs[:-1], axis=1)
     early = spread(ready, split)
-    far_all = gathered(far, axes)
     outs[-1] = attend(home, bias, mine, far_all, far_pick, after(state, ready), True)
-    late = spread(after(outs[-1], early), split)
-
-    def project(part, j):
-        joined = jnp.transpose(part, (1, 0, 2)).reshape(tok, width)
-        rows = out_weight[j * width : (j + 1) * width]
-        return jnp.dot(joined, rows, preferred_element_type=jnp.float32)
-
-    early = after(early, outs[-1])
-    total = sum(project(early[:, j], j) for j in range(chunks - 1))
-    return (total + project(late, chunks - 1)).astype(jnp.bfloat16)
+    late = spread(outs[-1], split)
+
+    rows = (chunks - 1) * width
+    early = jnp.transpose(after(early, outs[-1]), (2, 1, 0, 3)).reshape(tok, rows)
+    total = jnp.dot(early, out_weight[:rows], preferred_element_type=jnp.float32)
+    return finish(late, out_weight, total)
 
 
 def solution(mesh):

time: 137 us -> 135 us (0.985)
  matrix products: 12.3 us -> 5.66 us
  Pallas kernels: 28.6 us -> 32.7 us
  waiting for transfers between devices: 41.7 us -> 38.3 us
  other arithmetic: 6.83 us -> 9.25 us
  local copies, waits for them, and re-layouts: 15.6 us -> 17.7 us
    dot_general x3 -> x1, matrix products: 12.3 us -> 5.66 us  [shards(): jnp.dot(early, out_weight[:rows], preferred_element_type=jnp.float32)]
    pallas_call x0 -> x2, Pallas kernels: none -> 4.17 us  [the longest x1 4.08 us: finish(): pl.pallas_call(functools.partial(finish_kernel, step), out_shape=jax.Shap...]
    unnamed x59 -> x50, local copies, waits for them, and re-layouts: 6.89 us -> 9.87 us
    all_to_all x5, waiting for transfers between devices: 11.8 us -> 9.52 us  [spread(): return lax.all_to_all(a, axes, split_axis=0, concat_axis=0, tiled=True)]
    slice x3, local copies, waits for them, and re-layouts: 1.55 us -> 3.54 us  [pieces(): a = jnp.transpose(a[:, j * n_split:(j + 1) * n_split], (1, 0, 2))]
    concatenate x1 -> x0, local copies, waits for them, and re-layouts: 1.72 us -> none  [shards(): got = spread(after(jnp.concatenate([own[0], *far0], axis=1), kv), flat)]
    another operation x5 -> x6, other arithmetic: 2.4 us -> 4.1 us  [pieces(): return jnp.stack(out, axis=1)]
  transfers between devices with their start and end apart: 17 -> 17, of which waited for: 9 -> 8; matrix products, arithmetic and copies ran while one was open for 14% -> 15% of each run, Pallas kernels for 16% -> 17%
where the time goes in v10:
time: 135 us; the launch traced here: 134 us
  waiting for transfers between devices  38.3 us (28%)
  Pallas kernels  32.7 us (24%)
  starting transfers between devices  30.2 us (22%)
  local copies, waits for them, and re-layouts  17.7 us (13%)
  other arithmetic  9.25 us (7%)
  matrix products  5.66 us (4%)
    ppermute x12, waiting for transfers between devices, across(): return lax.ppermute(a, axis, swap(n, bit))  28.7 us
    pallas_call x5, Pallas kernels, attend(): pl.pallas_call(functools.partial(attend_kernel, picks, len(arrays), scale...  25.7 us
    all_to_all x5, starting transfers between devices, spread(): return lax.all_to_all(a, axes, split_axis=0, concat_axis=0, tiled=True)  19.9 us
    ppermute x12, starting transfers between devices, across(): return lax.ppermute(a, axis, swap(n, bit))  10.3 us
    unnamed x50, local copies, waits for them, and re-layouts  9.87 us
    all_to_all x5, waiting for transfers between devices, spread(): return lax.all_to_all(a, axes, split_axis=0, concat_axis=0, tiled=True)  9.52 us
    dot_general x1, matrix products, shards(): jnp.dot(early, out_weight[:rows], preferred_element_type=jnp.float32)  5.66 us
    another operation x6, other arithmetic, pieces(): return jnp.stack(out, axis=1)  4.1 us
  transfers between devices with their start and end apart: 17, of which 8 were waited for; matrix products, arithmetic and copies ran while one was open for 15% of the time, Pallas kernels for 17%

profile of v10, /device:TPU:0, one launch (start us, length us, event | category | flops | bytes accessed | tf_op | source)
XLA Modules:
  0.0 134.4 jit_solution(13307434498891078749)
XLA Ops:
  0.0 1.2 fusion.4
  1.2 1.2 fusion.5
  2.4 1.2 fusion.2
  4.3 3.1 %collective-permute-start = (bf16[4,3,128,128]{3,2,1,0:T(8,128)(2,1)S(1)}, bf16[4,3,128,128]{3,2,1,0:T(8,128)(2,1)S(1)}, u32[]{:S(2)}, u32[]{:S(2)}) collective-permute-start(bf16[4,3,128,128]{3,2,1,0:T(8,128)(2,1)S(1)} %pad_maximum_fusion.5), channel_id=1, source_target_pairs={{0,2},{2,0},{1,3},{3,1},{4,6},{6,4},{5,7},{7,5},{8,10},{10,8},{9,1... | collective-permute-start | bytes 1179656 | tf_op jit(solution)/shard_map/ppermute | solution.py:201
  8.6 2.6 %collective-permute-start.1 = (bf16[4,2,128,128]{3,2,1,0:T(8,128)(2,1)}, bf16[4,2,128,128]{3,2,1,0:T(8,128)(2,1)S(1)}, u32[]{:S(2)}, u32[]{:S(2)}) collective-permute-start(bf16[4,2,128,128]{3,2,1,0:T(8,128)(2,1)} %pad_maximum_fusion.9), channel_id=1, source_target_pairs={{0,4},{2,6},{4,0},{6,2},{1,5},{3,7},{5,1},{7,3},{8,12},{10,14},{12... | collective-permute-start | bytes 786440 | tf_op jit(solution)/shard_map/ppermute | solution.py:201
  12.4 1.1 constant_dynamic-slice_fusion
  13.6 8.5 %collective-permute-done = bf16[4,3,128,128]{3,2,1,0:T(8,128)(2,1)S(1)} collective-permute-done((bf16[4,3,128,128]{3,2,1,0:T(8,128)(2,1)S(1)}, bf16[4,3,128,128]{3,2,1,0:T(8,128)(2,1)S(1)}, u32[]{:S(2)}, u32[]{:S(2)}) %collective-permute-start) | collective-permute-done | bytes 393248 | tf_op jit(solution)/shard_map/ppermute | solution.py:201
  23.0 3.9 %all-to-all-start = ((bf16[4,6,128,128]{3,2,1,0:T(8,128)(2,1)}), bf16[4,6,128,128]{3,2,1,0:T(8,128)(2,1)S(1)}, u32[]{:S(2)}, u32[]{:S(2)}) async-start(bf16[4,6,128,128]{3,2,1,0:T(8,128)(2,1)} %pad_maximum_fusion), calls=%async_computation | async-start | bytes 1572864 | tf_op jit(solution)/shard_map/all_to_all | solution.py:204
  28.4 1.8 %collective-permute-done.1.refs_2_ = bf16[4,2,128,128]{3,2,1,0:T(8,128)(2,1)S(1)} collective-permute-done((bf16[4,2,128,128]{3,2,1,0:T(8,128)(2,1)}, bf16[4,2,128,128]{3,2,1,0:T(8,128)(2,1)S(1)}, u32[]{:S(2)}, u32[]{:S(2)}) %collective-permute-start.1) | collective-permute-done | bytes 262176 | tf_op jit(solution)/shard_map/ppermute | solution.py:201
  31.1 5.9 %all-to-all-done.q_ref = bf16[4,6,128,128]{3,2,1,0:T(8,128)(2,1)S(1)} async-done(((bf16[4,6,128,128]{3,2,1,0:T(8,128)(2,1)}), bf16[4,6,128,128]{3,2,1,0:T(8,128)(2,1)S(1)}, u32[]{:S(2)}, u32[]{:S(2)}) %all-to-all-start) | async-done | bytes 786464 | tf_op jit(solution)/shard_map/all_to_all | solution.py:204
  37.2 1.0 collective-permute-start.3
  39.2 2.0 %pad_maximum_fusion.1 = bf16[4,6,128,128]{3,2,1,0:T(8,128)(2,1)} fusion(bf16[4,3,128,128]{3,2,1,0:T(8,128)(2,1)} %collective-permute-done.4, bf16[4,1,128,128]{3,2,1,0:T(8,128)(2,1)S(1)} %bitcast.75, bf16[4,1,128,128]{3,2,1,0:T(8,128)(2,1)S(1)} %bitcast.73, bf16[4,1,128,128]{3,2,1,0:T(8,128)(2,1)S(1)} %bitcast.71), kind=kLoop, calls=%fused_computation.3 | loop fusion | flops 1179648 | bytes 1572864 | tf_op jit(solution)/shard_map/concatenate | solution.py:239
  41.2 3.5 %all-to-all-start.1 = ((bf16[4,6,128,128]{3,2,1,0:T(8,128)(2,1)}), bf16[4,6,128,128]{3,2,1,0:T(8,128)(2,1)S(1)}, u32[]{:S(2)}, u32[]{:S(2)}) async-start(bf16[4,6,128,128]{3,2,1,0:T(8,128)(2,1)} %pad_maximum_fusion.1), calls=%async_computation.1 | async-start | bytes 1572864 | tf_op jit(solution)/shard_map/all_to_all | solution.py:204
  45.5 2.5 %collective-permute-start.8 = (bf16[4,3,128,128]{3,2,1,0:T(8,128)(2,1)}, bf16[4,3,128,128]{3,2,1,0:T(8,128)(2,1)S(1)}, u32[]{:S(2)}, u32[]{:S(2)}) collective-permute-start(bf16[4,3,128,128]{3,2,1,0:T(8,128)(2,1)} %pad_maximum_fusion.8), channel_id=1, source_target_pairs={{0,2},{2,0},{1,3},{3,1},{4,6},{6,4},{5,7},{7,5},{8,10},{10,8},{9,1... | collective-permute-start | bytes 1179656 | tf_op jit(solution)/shard_map/ppermute | solution.py:201
  48.0 14.0 %collective-permute-done.3.refs_0_ = bf16[4,4,128,128]{3,2,1,0:T(8,128)(2,1)} collective-permute-done((bf16[4,4,128,128]{3,2,1,0:T(8,128)(2,1)S(1)}, bf16[4,4,128,128]{3,2,1,0:T(8,128)(2,1)}, u32[]{:S(2)}, u32[]{:S(2)}) %collective-permute-start.3) | collective-permute-done | bytes 524320 | tf_op jit(solution)/shard_map/ppermute | solution.py:201
  65.9 1.0 pad_maximum_fusion.7.refs_0_
  67.0 1.1 copy-done
  68.1 3.7 %all-to-all-start.2 = ((bf16[4,10,128,128]{3,2,1,0:T(8,128)(2,1)}), bf16[4,10,128,128]{3,2,1,0:T(8,128)(2,1)S(1)}, u32[]{:S(2)}, u32[]{:S(2)}) async-start(bf16[4,10,128,128]{3,2,1,0:T(8,128)(2,1)} %copy-done), calls=%async_computation.2 | async-start | bytes 2621440 | tf_op jit(solution)/shard_map/all_to_all | solution.py:204
  73.2 4.5 %shard_map.168 = (f32[1024,128]{1,0:T(8,128)S(1)}, f32[1024,256]{1,0:T(8,128)S(1)}) custom-call(s32[8]{0:T(128)S(1)} %reshape.64.place_ref, f32[2,4,4096]{2,1,0:T(4,128)S(1)} %shard_map.163.bias_ref, bf16[4,6,128,128]{3,2,1,0:T(8,128)(2,1)S(1)} %all-to-all-done.q_ref, bf16[4,4,128,128]{3,2,1,0:T(8,128)(2,1)S(1)} %pad_maximum_fusion.2.refs_0_, ...), custom_call_target="tpu_custom_call" | custom-call | flops 1024 | bytes 4096 | tf_op jit(solution)/shard_map/pallas_call | solution.py:110
  77.7 4.8 %shard_map.169 = bf16[8,128,128]{2,1,0:T(8,128)(2,1)S(1)} custom-call(s32[8]{0:T(128)S(1)} %reshape.64.place_ref, f32[2,4,4096]{2,1,0:T(4,128)S(1)} %shard_map.163.bias_ref, bf16[4,6,128,128]{3,2,1,0:T(8,128)(2,1)S(1)} %all-to-all-done.q_ref, bf16[4,4,128,128]{3,2,1,0:T(8,128)(2,1)} %collective-permute-done.3.refs_0_, ...), custom_call_target="tpu_custom_call" | custom-call | flops 1024 | bytes 4096 | tf_op jit(solution)/shard_map/pallas_call | solution.py:110
  83.4 4.7 %shard_map.165 = (f32[1024,128]{1,0:T(8,128)S(1)}, f32[1024,256]{1,0:T(8,128)S(1)}) custom-call(s32[8]{0:T(128)S(1)} %reshape.64.place_ref, f32[2,4,4096]{2,1,0:T(4,128)S(1)} %copy-done.4, bf16[4,6,128,128]{3,2,1,0:T(8,128)(2,1)S(1)} %all-to-all-done.1.q_ref, bf16[4,4,128,128]{3,2,1,0:T(8,128)(2,1)} %pad_maximum_fusion.3.refs_0_, ...), custom_call_target="tpu_custom_call" | custom-call | flops 1024 | bytes 4096 | tf_op jit(solution)/shard_map/pallas_call | solution.py:110
  89.1 1.3 collective-permute-done.5.refs_0_
  92.9 3.1 %collective-permute-done.6.refs_1_ = bf16[4,4,128,128]{3,2,1,0:T(8,128)(2,1)S(1)} collective-permute-done((bf16[4,4,128,128]{3,2,1,0:T(8,128)(2,1)}, bf16[4,4,128,128]{3,2,1,0:T(8,128)(2,1)S(1)}, u32[]{:S(2)}, u32[]{:S(2)}) %collective-permute-start.6) | collective-permute-done | bytes 524320 | tf_op jit(solution)/shard_map/ppermute | solution.py:201
  96.8 6.4 %shard_map.170 = bf16[8,128,128]{2,1,0:T(8,128)(2,1)S(1)} custom-call(s32[8]{0:T(128)S(1)} %reshape.64.place_ref, f32[2,4,4096]{2,1,0:T(4,128)S(1)} %shard_map.166.bias_ref, bf16[4,10,128,128]{3,2,1,0:T(8,128)(2,1)S(1)} %all-to-all-done.2.q_ref.refs_0_, bf16[4,10,128,128]{3,2,1,0:T(8,128)(2,1)S(1)} %all-to-all-done.2.q_ref.refs_0_, ...), custom_call_target="tpu_custom_call" | custom-call | flops 1024 | bytes 4096 | tf_op jit(solution)/shard_map/pallas_call | solution.py:110
  104.2 5.4 %all-to-all-start.4 = ((bf16[8,2,128,128]{3,2,1,0:T(8,128)(2,1)}), bf16[8,2,128,128]{3,2,1,0:T(8,128)(2,1)S(1)}, u32[]{:S(2)}, u32[]{:S(2)}) async-start(bf16[8,2,128,128]{3,2,1,0:T(8,128)(2,1)} %copy.73), calls=%async_computation.4 | async-start | bytes 1048576 | tf_op jit(solution)/shard_map/all_to_all | solution.py:204
  109.6 1.2 copy-done.2
  110.8 1.0 copy-done.7
  111.9 5.3 %shard_map.171 = bf16[8,128,128]{2,1,0:T(8,128)(2,1)} custom-call(s32[8]{0:T(128)S(1)} %reshape.64.place_ref, f32[2,4,4096]{2,1,0:T(4,128)S(1)} %copy-done.5, bf16[4,6,128,128]{3,2,1,0:T(8,128)(2,1)S(1)} %all-to-all-done.1.q_ref, bf16[4,4,128,128]{3,2,1,0:T(8,128)(2,1)} %collective-permute-done.5.refs_0_, bf16[4,4,128,128]{3,2,1,0:T(8,128)(2,1)S(1)} %copy-done.7, ...), custom_call_target="tpu_custom_call" | custom-call | flops 1024 | bytes 4096 | tf_op jit(solution)/shard_map/pallas_call | solution.py:110
  117.2 2.7 %all-to-all-done.4 = bf16[8,2,128,128]{3,2,1,0:T(8,128)(2,1)S(1)} async-done(((bf16[8,2,128,128]{3,2,1,0:T(8,128)(2,1)}), bf16[8,2,128,128]{3,2,1,0:T(8,128)(2,1)S(1)}, u32[]{:S(2)}, u32[]{:S(2)}) %all-to-all-start.4) | async-done | bytes 524320 | tf_op jit(solution)/shard_map/all_to_all | solution.py:204
  119.9 3.4 %all-to-all-start.3 = ((bf16[8,128,128]{2,1,0:T(8,128)(2,1)}), bf16[8,128,128]{2,1,0:T(8,128)(2,1)S(1)}, u32[]{:S(2)}, u32[]{:S(2)}) async-start(bf16[8,128,128]{2,1,0:T(8,128)(2,1)} %shard_map.171), calls=%async_computation.3 | async-start | bytes 524288 | tf_op jit(solution)/shard_map/all_to_all | solution.py:204
  123.6 5.7 %fusion.total_ref = f32[128,3072]{1,0:T(8,128)S(1)} fusion(bf16[128,2048]{0,1:T(8,128)(2,1)S(1)} %bitcast.76, bf16[3072,3072]{1,0:T(8,128)(2,1)} %weight_ref.1), kind=kOutput, calls=%fused_computation | convolution fusion | flops 1610612736 | bytes 14680064 | tf_op jit(solution)/shard_map/dot_general | solution.py:276
  130.2 4.1 %shard_map.172 = bf16[128,3072]{1,0:T(8,128)(2,1)} custom-call(bf16[8,128,128]{2,1,0:T(8,128)(2,1)S(1)} %all-to-all-done.3.part_ref, bf16[3072,3072]{1,0:T(8,128)(2,1)} %weight_ref.1, f32[128,3072]{1,0:T(8,128)S(1)} %fusion.total_ref), custom_call_target="tpu_custom_call" | custom-call | tf_op jit(solution)/shard_map/pallas_call | solution.py:163
  (89 shorter events, 21.0 us)
Async XLA Ops:
  0.0 27.7 %copy-start.15 = (s32[9]{0:T(128)S(1)}, s32[9]{0:T(128)}, u32[]{:S(2)}) copy-start(s32[9]{0:T(128)} %constant.92.clone) | copy-start | bytes 112
  0.0 30.2 %copy-start.10 = (s32[4,1]{1,0:T(4,128)S(1)}, s32[4,1]{1,0:T(4,128)}, u32[]{:S(2)}) copy-start(s32[4,1]{1,0:T(4,128)} %constant.98.clone.rows_ref) | copy-start | bytes 52
  0.0 30.2 %copy-start.11 = (s32[1,512]{1,0:T(1,128)S(1)}, s32[1,512]{1,0:T(1,128)}, u32[]{:S(2)}) copy-start(s32[1,512]{1,0:T(1,128)} %constant.99.clone.cols_ref) | copy-start | bytes 6148
  0.0 30.2 %copy-start.8 = (s32[24,32,32]{2,1,0:T(8,128)S(1)}, s32[24,32,32]{2,1,0:T(8,128)}, u32[]{:S(2)}) copy-start(s32[24,32,32]{2,1,0:T(8,128)} %mask_ref.2) | copy-start | bytes 294916
  4.3 17.8 %collective-permute-start = (bf16[4,3,128,128]{3,2,1,0:T(8,128)(2,1)S(1)}, bf16[4,3,128,128]{3,2,1,0:T(8,128)(2,1)S(1)}, u32[]{:S(2)}, u32[]{:S(2)}) collective-permute-start(bf16[4,3,128,128]{3,2,1,0:T(8,128)(2,1)S(1)} %pad_maximum_fusion.5), channel_id=1, source_target_pairs={{0,2},{2,0},{1,3},{3,1},{4,6},{6,4},{5,7},{7,5},{8,10},{10,8},{9,1... | collective-permute-start | bytes 1179656 | tf_op jit(solution)/shard_map/ppermute | solution.py:201
  7.8 29.3 %copy-start.12 = (bf16[2,1,2,128,128]{4,3,2,0,1:T(8,128)(2,1)}, bf16[2,1,2,128,128]{4,3,2,0,1:T(8,128)(2,1)S(1)}, u32[]{:S(2)}) copy-start(bf16[2,1,2,128,128]{4,3,2,0,1:T(8,128)(2,1)S(1)} %copy.81) | copy-start | bytes 393220
  7.8 29.3 %copy-start.13 = (bf16[2,1,2,128,128]{4,3,2,0,1:T(8,128)(2,1)}, bf16[2,1,2,128,128]{4,3,2,0,1:T(8,128)(2,1)S(1)}, u32[]{:S(2)}) copy-start(bf16[2,1,2,128,128]{4,3,2,0,1:T(8,128)(2,1)S(1)} %copy.82) | copy-start | bytes 393220
  8.6 21.6 %collective-permute-start.1 = (bf16[4,2,128,128]{3,2,1,0:T(8,128)(2,1)}, bf16[4,2,128,128]{3,2,1,0:T(8,128)(2,1)S(1)}, u32[]{:S(2)}, u32[]{:S(2)}) collective-permute-start(bf16[4,2,128,128]{3,2,1,0:T(8,128)(2,1)} %pad_maximum_fusion.9), channel_id=1, source_target_pairs={{0,4},{2,6},{4,0},{6,2},{1,5},{3,7},{5,1},{7,3},{8,12},{10,14},{12... | collective-permute-start | bytes 786440 | tf_op jit(solution)/shard_map/ppermute | solution.py:201
  12.0 18.2 %collective-permute-start.2 = (bf16[4,2,128,128]{3,2,1,0:T(8,128)(2,1)}, bf16[4,2,128,128]{3,2,1,0:T(8,128)(2,1)S(1)}, u32[]{:S(2)}, u32[]{:S(2)}) collective-permute-start(bf16[4,2,128,128]{3,2,1,0:T(8,128)(2,1)} %pad_maximum_fusion.10), channel_id=1, source_target_pairs={{0,6},{2,4},{4,2},{6,0},{1,7},{3,5},{5,3},{7,1},{8,14},{10,12},{12... | collective-permute-start | bytes 786440 | tf_op jit(solution)/shard_map/ppermute | solution.py:201
  23.0 14.0 %all-to-all-start = ((bf16[4,6,128,128]{3,2,1,0:T(8,128)(2,1)}), bf16[4,6,128,128]{3,2,1,0:T(8,128)(2,1)S(1)}, u32[]{:S(2)}, u32[]{:S(2)}) async-start(bf16[4,6,128,128]{3,2,1,0:T(8,128)(2,1)} %pad_maximum_fusion), calls=%async_computation | async-start | bytes 1572864 | tf_op jit(solution)/shard_map/all_to_all | solution.py:204
  27.7 11.5 %collective-permute-start.4 = (bf16[4,3,128,128]{3,2,1,0:T(8,128)(2,1)}, bf16[4,3,128,128]{3,2,1,0:T(8,128)(2,1)}, u32[]{:S(2)}, u32[]{:S(2)}) collective-permute-start(bf16[4,3,128,128]{3,2,1,0:T(8,128)(2,1)} %pad_maximum_fusion.6), channel_id=1, source_target_pairs={{0,2},{2,0},{1,3},{3,1},{4,6},{6,4},{5,7},{7,5},{8,10},{10,8},{9,1... | collective-permute-start | bytes 1179656 | tf_op jit(solution)/shard_map/ppermute | solution.py:201
  37.1 34.8 %copy-start.14 = (s32[2,4]{1,0:T(2,128)S(1)}, s32[2,4]{1,0:T(2,128)}, u32[]{:S(2)}) copy-start(s32[2,4]{1,0:T(2,128)} %constant.96.clone) | copy-start | bytes 100
  37.2 24.8 %collective-permute-start.3 = (bf16[4,4,128,128]{3,2,1,0:T(8,128)(2,1)S(1)}, bf16[4,4,128,128]{3,2,1,0:T(8,128)(2,1)}, u32[]{:S(2)}, u32[]{:S(2)}) collective-permute-start(bf16[4,4,128,128]{3,2,1,0:T(8,128)(2,1)S(1)} %pad_maximum_fusion.2.refs_0_), channel_id=1, source_target_pairs={{0,4},{4,0},{1,5},{5,1},{2,6},{6,2},{3,7},{7,3},{8,12},{12,8},{9,1... | collective-permute-start | bytes 1572872 | tf_op jit(solution)/shard_map/ppermute | solution.py:201
  41.2 22.4 %all-to-all-start.1 = ((bf16[4,6,128,128]{3,2,1,0:T(8,128)(2,1)}), bf16[4,6,128,128]{3,2,1,0:T(8,128)(2,1)S(1)}, u32[]{:S(2)}, u32[]{:S(2)}) async-start(bf16[4,6,128,128]{3,2,1,0:T(8,128)(2,1)} %pad_maximum_fusion.1), calls=%async_computation.1 | async-start | bytes 1572864 | tf_op jit(solution)/shard_map/all_to_all | solution.py:204
  45.5 21.4 %collective-permute-start.8 = (bf16[4,3,128,128]{3,2,1,0:T(8,128)(2,1)}, bf16[4,3,128,128]{3,2,1,0:T(8,128)(2,1)S(1)}, u32[]{:S(2)}, u32[]{:S(2)}) collective-permute-start(bf16[4,3,128,128]{3,2,1,0:T(8,128)(2,1)} %pad_maximum_fusion.8), channel_id=1, source_target_pairs={{0,2},{2,0},{1,3},{3,1},{4,6},{6,4},{5,7},{7,5},{8,10},{10,8},{9,1... | collective-permute-start | bytes 1179656 | tf_op jit(solution)/shard_map/ppermute | solution.py:201
  48.0 25.2 %collective-permute-start.10 = (bf16[4,4,128,128]{3,2,1,0:T(8,128)(2,1)S(1)}, bf16[4,4,128,128]{3,2,1,0:T(8,128)(2,1)}, u32[]{:S(2)}, u32[]{:S(2)}) collective-permute-start(bf16[4,4,128,128]{3,2,1,0:T(8,128)(2,1)S(1)} %pad_maximum_fusion.2.refs_0_), channel_id=1, source_target_pairs={{0,8},{8,0},{1,9},{9,1},{2,10},{10,2},{3,11},{11,3},{4,12},{12,4},... | collective-permute-start | bytes 1572872 | tf_op jit(solution)/shard_map/ppermute | solution.py:201
  62.0 15.7 %collective-permute-start.9 = (bf16[4,4,128,128]{3,2,1,0:T(8,128)(2,1)}, bf16[4,4,128,128]{3,2,1,0:T(8,128)(2,1)}, u32[]{:S(2)}, u32[]{:S(2)}) collective-permute-start(bf16[4,4,128,128]{3,2,1,0:T(8,128)(2,1)} %collective-permute-done.3.refs_0_), channel_id=1, source_target_pairs={{0,8},{8,0},{1,9},{9,1},{2,10},{10,2},{3,11},{11,3},{4,12},{12,4},... | collective-permute-start | bytes 1572872 | tf_op jit(solution)/shard_map/ppermute | solution.py:201
  64.5 18.1 %collective-permute-start.7 = (bf16[4,4,128,128]{3,2,1,0:T(8,128)(2,1)}, bf16[4,4,128,128]{3,2,1,0:T(8,128)(2,1)}, u32[]{:S(2)}, u32[]{:S(2)}) collective-permute-start(bf16[4,4,128,128]{3,2,1,0:T(8,128)(2,1)} %pad_maximum_fusion.3.refs_0_), channel_id=1, source_target_pairs={{0,8},{8,0},{1,9},{9,1},{2,10},{10,2},{3,11},{11,3},{4,12},{12,4},... | collective-permute-start | bytes 1572872 | tf_op jit(solution)/shard_map/ppermute | solution.py:201
  65.0 25.4 %collective-permute-start.5 = (bf16[4,4,128,128]{3,2,1,0:T(8,128)(2,1)}, bf16[4,4,128,128]{3,2,1,0:T(8,128)(2,1)}, u32[]{:S(2)}, u32[]{:S(2)}) collective-permute-start(bf16[4,4,128,128]{3,2,1,0:T(8,128)(2,1)} %pad_maximum_fusion.3.refs_0_), channel_id=1, source_target_pairs={{0,4},{4,0},{1,5},{5,1},{2,6},{6,2},{3,7},{7,3},{8,12},{12,8},{9,1... | collective-permute-start | bytes 1572872 | tf_op jit(solution)/shard_map/ppermute | solution.py:201
  67.0 1.1 copy-start
  68.1 24.2 %all-to-all-start.2 = ((bf16[4,10,128,128]{3,2,1,0:T(8,128)(2,1)}), bf16[4,10,128,128]{3,2,1,0:T(8,128)(2,1)S(1)}, u32[]{:S(2)}, u32[]{:S(2)}) async-start(bf16[4,10,128,128]{3,2,1,0:T(8,128)(2,1)} %copy-done), calls=%async_computation.2 | async-start | bytes 2621440 | tf_op jit(solution)/shard_map/all_to_all | solution.py:204
  82.5 0.9 copy-start.4
  88.1 1.0 copy-start.1
  89.1 20.5 %copy-start.5 = (f32[2,4,4096]{2,1,0:T(4,128)S(1)}, f32[2,4,4096]{2,1,0:T(4,128)}, u32[]{:S(2)}) copy-start(f32[2,4,4096]{2,1,0:T(4,128)} %copy-done.3) | copy-start | bytes 393220
  90.4 1.0 copy-start.9
  92.3 4.5 %collective-permute-start.11 = (bf16[4,10,128,128]{3,2,1,0:T(8,128)(2,1)S(1)}, bf16[4,10,128,128]{3,2,1,0:T(8,128)(2,1)S(1)}, u32[]{:S(2)}, u32[]{:S(2)}) collective-permute-start(bf16[4,10,128,128]{3,2,1,0:T(8,128)(2,1)S(1)} %all-to-all-done.2.q_ref.refs_0_), channel_id=1, source_target_pairs={{0,8},{8,0},{1,9},{9,1},{2,10},{10,2},{3,11},{11,3},{4,12},{12,4},... | collective-permute-start | bytes 3932168 | tf_op jit(solution)/shard_map/ppermute | solution.py:201
  92.4 3.6 %collective-permute-start.6 = (bf16[4,4,128,128]{3,2,1,0:T(8,128)(2,1)}, bf16[4,4,128,128]{3,2,1,0:T(8,128)(2,1)S(1)}, u32[]{:S(2)}, u32[]{:S(2)}) collective-permute-start(bf16[4,4,128,128]{3,2,1,0:T(8,128)(2,1)} %collective-permute-done.5.refs_0_), channel_id=1, source_target_pairs={{0,8},{8,0},{1,9},{9,1},{2,10},{10,2},{3,11},{11,3},{4,12},{12,4},... | collective-permute-start | bytes 1572872 | tf_op jit(solution)/shard_map/ppermute | solution.py:201
  96.0 0.8 copy-start.6
  104.2 15.7 %all-to-all-start.4 = ((bf16[8,2,128,128]{3,2,1,0:T(8,128)(2,1)}), bf16[8,2,128,128]{3,2,1,0:T(8,128)(2,1)S(1)}, u32[]{:S(2)}, u32[]{:S(2)}) async-start(bf16[8,2,128,128]{3,2,1,0:T(8,128)(2,1)} %copy.73), calls=%async_computation.4 | async-start | bytes 1048576 | tf_op jit(solution)/shard_map/all_to_all | solution.py:204
  109.6 1.2 copy-start.2
  110.8 1.0 copy-start.7
  119.9 10.3 %all-to-all-start.3 = ((bf16[8,128,128]{2,1,0:T(8,128)(2,1)}), bf16[8,128,128]{2,1,0:T(8,128)(2,1)S(1)}, u32[]{:S(2)}, u32[]{:S(2)}) async-start(bf16[8,128,128]{2,1,0:T(8,128)(2,1)} %shard_map.171), calls=%async_computation.3 | async-start | bytes 524288 | tf_op jit(solution)/shard_map/all_to_all | solution.py:204
  (1 other events, 0.7 us)

commit v11 on v10

--- a/solution.py
+++ b/solution.py
@@ -50,11 +50,14 @@
             bias_ref[tile, :, n * span : (n + 1) * span] = jnp.where(seen > 0.5, 0.0, NEG)
 
 
-def attend_kernel(picks, count, scale, first, last, place_ref, bias_ref, q_ref, *refs):
+def attend_kernel(picks, count, extra, scale, first, last, place_ref, bias_ref, q_ref, *refs):
     kv_refs, rest = refs[:count], refs[count:]
     if not first:
         m_in, acc_in = rest[:2]
         rest = rest[2:]
+    others, rest = rest[:extra], rest[extra:]
+    for i, other in enumerate(others):
+        rest[0][:, 1 + i] = other[...]
     tiles, qb, _ = bias_ref.shape
     block, hdim = q_ref.shape[2:]
     rows = qb * block
@@ -81,7 +84,8 @@
         if last:
             out = (acc[:, :hdim] / acc[:, hdim:]).astype(jnp.bfloat16)
             for row in range(qb):
-                rest[0][place_ref[index * qb + row]] = out[row * block : (row + 1) * block]
+                at = place_ref[index * qb + row]
+                rest[0][(at, 0) if extra else at] = out[row * block : (row + 1) * block]
         else:
             rest[0][pl.ds(index * rows, rows), :] = jnp.broadcast_to(m, (rows, hdim))
             rest[1][pl.ds(index * rows, rows), :] = acc
@@ -90,14 +94,15 @@
     lax.fori_loop(0, tiles, tile, 0)
 
 
-def attend(place, bias, q, arrays, picks, state, last):
+def attend(place, bias, q, arrays, picks, state, last, beside=()):
     tiles, qb, _ = bias.shape
     block, hdim = q.shape[2:]
     groups = tiles * qb
     total = groups * block
     first = state is None
     if last:
-        out_shape = jax.ShapeDtypeStruct((groups, block, hdim), jnp.bfloat16)
+        held = (groups, 1 + len(beside), block, hdim) if beside else (groups, block, hdim)
+        out_shape = jax.ShapeDtypeStruct(held, jnp.bfloat16)
         out_specs = VMEM
     else:
         out_shape = (
@@ -105,10 +110,10 @@
             jax.ShapeDtypeStruct((total, 2 * hdim), jnp.float32),
         )
         out_specs = (VMEM, VMEM)
-    args = [place, bias, q, *arrays, *(() if first else state)]
+    args = [place, bias, q, *arrays, *(() if first else state), *beside]
     scale = hdim**-0.5 * math.log2(math.e)
     return pl.pallas_call(
-        functools.partial(attend_kernel, picks, len(arrays), scale, first, last),
+        functools.partial(attend_kernel, picks, len(arrays), len(beside), scale, first, last),
         out_shape=out_shape,
         in_specs=[SMEM] + [VMEM] * (len(args) - 1),
         out_specs=out_specs,
@@ -249,6 +254,9 @@
     for j in range(1, chunks):
         got = spread(after(own[j], *gate), flat)
         bias = bias_of(j, far)
+        if j == chunks - 1:
+            packed = pack(*((a, range(a.shape[1])) for a in (*last[1:], *far0)))
+            got = after(got, packed)
         got = after(got, bias)
         kv = jnp.concatenate([got[:, 1:3], got[:, 4:6]], axis=1)
         gate = (kv,)
@@ -256,8 +264,7 @@
         near = gathered(kv, axes)
         state = attend(home, bias, got, near, near_pick, None, False)
         waiting.append((bias, got, far, state))
-    parts = [(a, range(a.shape[1])) for a in (*last[1:], *far0)]
-    got = spread(after(pack(*parts), kv), flat)
+    got = spread(after(packed, kv), flat)
     for j, (bias, mine, far, state) in enumerate(waiting[:-1], 1):
         outs[j] = attend(home, bias, mine, gathered(far, axes), far_pick, state, True)
     bias, mine, far, state = waiting[-1]
@@ -265,8 +272,7 @@
     got = after(got, bias0, state, outs[-2])
     all0 = gathered(got, axes)
     far_all = gathered(far, axes)
-    outs[0] = attend(home, bias0, after(got, *far_all), all0, both_pick, None, True)
-    ready = jnp.stack(outs[:-1], axis=1)
+    ready = attend(home, bias0, after(got, *far_all), all0, both_pick, None, True, outs[1:-1])
     early = spread(ready, split)
     outs[-1] = attend(home, bias, mine, far_all, far_pick, after(state, ready), True)
     late = spread(outs[-1], split)

time: 135 us -> 134 us (level)
  waiting for transfers between devices: 38.3 us -> 35.6 us
  local copies, waits for them, and re-layouts: 17.7 us -> 19.4 us
  starting transfers between devices: 30.2 us -> 28.6 us
    ppermute x12, waiting for transfers between devices: 28.7 us -> 26.1 us  [across(): return lax.ppermute(a, axis, swap(n, bit))]
    unnamed x50, local copies, waits for them, and re-layouts: 9.87 us -> 11.7 us
    all_to_all x5, starting transfers between devices: 19.9 us -> 18.3 us  [spread(): return lax.all_to_all(a, axes, split_axis=0, concat_axis=0, tiled=True)]
  transfers between devices with their start and end apart: 17 -> 17, of which waited for: 8 -> 9; matrix products, arithmetic and copies ran while one was open for 15% -> 17% of each run, Pallas kernels for 17% -> 17%
where the time goes in v11:
time: 134 us; the launch traced here: 133 us
  waiting for transfers between devices  35.6 us (27%)
  Pallas kernels  33.5 us (25%)
  starting transfers between devices  28.6 us (21%)
  local copies, waits for them, and re-layouts  19.4 us (14%)
  other arithmetic  9.21 us (7%)
  matrix products  5.66 us (4%)
    pallas_call x5, Pallas kernels, attend(): pl.pallas_call(functools.partial(attend_kernel, picks, len(arrays), len(b...  26.6 us
    ppermute x12, waiting for transfers between devices, across(): return lax.ppermute(a, axis, swap(n, bit))  26.1 us
    all_to_all x5, starting transfers between devices, spread(): return lax.all_to_all(a, axes, split_axis=0, concat_axis=0, tiled=True)  18.3 us
    unnamed x50, local copies, waits for them, and re-layouts  11.7 us
    ppermute x12, starting transfers between devices, across(): return lax.ppermute(a, axis, swap(n, bit))  10.3 us
    all_to_all x5, waiting for transfers between devices, spread(): return lax.all_to_all(a, axes, split_axis=0, concat_axis=0, tiled=True)  9.54 us
    dot_general x1, matrix products, shards(): jnp.dot(early, out_weight[:rows], preferred_element_type=jnp.float32)  5.66 us
    another operation x6, other arithmetic, pieces(): return jnp.stack(out, axis=1)  4.1 us
  transfers between devices with their start and end apart: 17, of which 9 were waited for; matrix products, arithmetic and copies ran while one was open for 17% of the time, Pallas kernels for 17%

profile of v11, /device:TPU:0, one launch (start us, length us, event | category | flops | bytes accessed | tf_op | source)
XLA Modules:
  0.0 132.6 jit_solution(11259835702059759784)
XLA Ops:
  0.0 1.2 fusion.4
  1.2 1.2 fusion.5
  2.8 1.2 fusion.3
  4.3 3.1 %collective-permute-start = (bf16[4,3,128,128]{3,2,1,0:T(8,128)(2,1)S(1)}, bf16[4,3,128,128]{3,2,1,0:T(8,128)(2,1)S(1)}, u32[]{:S(2)}, u32[]{:S(2)}) collective-permute-start(bf16[4,3,128,128]{3,2,1,0:T(8,128)(2,1)S(1)} %pad_maximum_fusion.4), channel_id=1, source_target_pairs={{0,2},{2,0},{1,3},{3,1},{4,6},{6,4},{5,7},{7,5},{8,10},{10,8},{9,1... | collective-permute-start | bytes 1179656 | tf_op jit(solution)/shard_map/ppermute | solution.py:206
  8.6 2.6 %collective-permute-start.1 = (bf16[4,2,128,128]{3,2,1,0:T(8,128)(2,1)}, bf16[4,2,128,128]{3,2,1,0:T(8,128)(2,1)S(1)}, u32[]{:S(2)}, u32[]{:S(2)}) collective-permute-start(bf16[4,2,128,128]{3,2,1,0:T(8,128)(2,1)} %pad_maximum_fusion.8), channel_id=1, source_target_pairs={{0,4},{2,6},{4,0},{6,2},{1,5},{3,7},{5,1},{7,3},{8,12},{10,14},{12... | collective-permute-start | bytes 786440 | tf_op jit(solution)/shard_map/ppermute | solution.py:206
  12.0 1.1 constant_dynamic-slice_fusion.6
  13.1 1.1 constant_dynamic-slice_fusion
  14.3 7.8 %collective-permute-done = bf16[4,3,128,128]{3,2,1,0:T(8,128)(2,1)S(1)} collective-permute-done((bf16[4,3,128,128]{3,2,1,0:T(8,128)(2,1)S(1)}, bf16[4,3,128,128]{3,2,1,0:T(8,128)(2,1)S(1)}, u32[]{:S(2)}, u32[]{:S(2)}) %collective-permute-start) | collective-permute-done | bytes 393248 | tf_op jit(solution)/shard_map/ppermute | solution.py:206
  23.0 3.9 %all-to-all-start = ((bf16[4,6,128,128]{3,2,1,0:T(8,128)(2,1)}), bf16[4,6,128,128]{3,2,1,0:T(8,128)(2,1)S(1)}, u32[]{:S(2)}, u32[]{:S(2)}) async-start(bf16[4,6,128,128]{3,2,1,0:T(8,128)(2,1)} %pad_maximum_fusion), calls=%async_computation | async-start | bytes 1572864 | tf_op jit(solution)/shard_map/all_to_all | solution.py:209
  28.4 1.7 %collective-permute-done.1.refs_2_ = bf16[4,2,128,128]{3,2,1,0:T(8,128)(2,1)S(1)} collective-permute-done((bf16[4,2,128,128]{3,2,1,0:T(8,128)(2,1)}, bf16[4,2,128,128]{3,2,1,0:T(8,128)(2,1)S(1)}, u32[]{:S(2)}, u32[]{:S(2)}) %collective-permute-start.1) | collective-permute-done | bytes 262176 | tf_op jit(solution)/shard_map/ppermute | solution.py:206
  31.1 5.9 %all-to-all-done.q_ref = bf16[4,6,128,128]{3,2,1,0:T(8,128)(2,1)S(1)} async-done(((bf16[4,6,128,128]{3,2,1,0:T(8,128)(2,1)}), bf16[4,6,128,128]{3,2,1,0:T(8,128)(2,1)S(1)}, u32[]{:S(2)}, u32[]{:S(2)}) %all-to-all-start) | async-done | bytes 786464 | tf_op jit(solution)/shard_map/all_to_all | solution.py:209
  39.0 2.5 %collective-permute-start.5 = (bf16[4,3,128,128]{3,2,1,0:T(8,128)(2,1)}, bf16[4,3,128,128]{3,2,1,0:T(8,128)(2,1)S(1)}, u32[]{:S(2)}, u32[]{:S(2)}) collective-permute-start(bf16[4,3,128,128]{3,2,1,0:T(8,128)(2,1)} %pad_maximum_fusion.7), channel_id=1, source_target_pairs={{0,2},{2,0},{1,3},{3,1},{4,6},{6,4},{5,7},{7,5},{8,10},{10,8},{9,1... | collective-permute-start | bytes 1179656 | tf_op jit(solution)/shard_map/ppermute | solution.py:206
  44.3 2.0 %pad_maximum_fusion.1 = bf16[4,6,128,128]{3,2,1,0:T(8,128)(2,1)} fusion(bf16[4,3,128,128]{3,2,1,0:T(8,128)(2,1)} %collective-permute-done.4, bf16[4,1,128,128]{3,2,1,0:T(8,128)(2,1)S(1)} %bitcast.71, bf16[4,1,128,128]{3,2,1,0:T(8,128)(2,1)S(1)} %bitcast.70, bf16[4,1,128,128]{3,2,1,0:T(8,128)(2,1)S(1)} %bitcast.69), kind=kLoop, calls=%fused_computation.3 | loop fusion | flops 1179648 | bytes 1572864 | tf_op jit(solution)/shard_map/concatenate | solution.py:244
  46.2 3.5 %all-to-all-start.1 = ((bf16[4,6,128,128]{3,2,1,0:T(8,128)(2,1)}), bf16[4,6,128,128]{3,2,1,0:T(8,128)(2,1)S(1)}, u32[]{:S(2)}, u32[]{:S(2)}) async-start(bf16[4,6,128,128]{3,2,1,0:T(8,128)(2,1)} %pad_maximum_fusion.1), calls=%async_computation.1 | async-start | bytes 1572864 | tf_op jit(solution)/shard_map/all_to_all | solution.py:209
  51.7 4.9 %collective-permute-done.5.refs_1_ = bf16[4,3,128,128]{3,2,1,0:T(8,128)(2,1)S(1)} collective-permute-done((bf16[4,3,128,128]{3,2,1,0:T(8,128)(2,1)}, bf16[4,3,128,128]{3,2,1,0:T(8,128)(2,1)S(1)}, u32[]{:S(2)}, u32[]{:S(2)}) %collective-permute-start.5) | collective-permute-done | bytes 393248 | tf_op jit(solution)/shard_map/ppermute | solution.py:206
  56.7 1.1 copy-done
  57.8 4.1 %collective-permute-done.3.refs_0_ = bf16[4,4,128,128]{3,2,1,0:T(8,128)(2,1)} collective-permute-done((bf16[4,4,128,128]{3,2,1,0:T(8,128)(2,1)S(1)}, bf16[4,4,128,128]{3,2,1,0:T(8,128)(2,1)}, u32[]{:S(2)}, u32[]{:S(2)}) %collective-permute-start.3) | collective-permute-done | bytes 524320 | tf_op jit(solution)/shard_map/ppermute | solution.py:206
  64.9 3.7 %all-to-all-start.2 = ((bf16[4,10,128,128]{3,2,1,0:T(8,128)(2,1)}), bf16[4,10,128,128]{3,2,1,0:T(8,128)(2,1)S(1)}, u32[]{:S(2)}, u32[]{:S(2)}) async-start(bf16[4,10,128,128]{3,2,1,0:T(8,128)(2,1)} %copy-done), calls=%async_computation.2 | async-start | bytes 2621440 | tf_op jit(solution)/shard_map/all_to_all | solution.py:209
  69.9 4.5 %shard_map.168 = (f32[1024,128]{1,0:T(8,128)S(1)}, f32[1024,256]{1,0:T(8,128)S(1)}) custom-call(s32[8]{0:T(128)S(1)} %reshape.64.place_ref, f32[2,4,4096]{2,1,0:T(4,128)S(1)} %shard_map.163.bias_ref, bf16[4,6,128,128]{3,2,1,0:T(8,128)(2,1)S(1)} %all-to-all-done.q_ref, bf16[4,4,128,128]{3,2,1,0:T(8,128)(2,1)S(1)} %pad_maximum_fusion.2.refs_0_, ...), custom_call_target="tpu_custom_call" | custom-call | flops 1024 | bytes 4096 | tf_op jit(solution)/shard_map/pallas_call | solution.py:115
  74.5 4.8 %shard_map.169.refs_2_ = bf16[8,128,128]{2,1,0:T(8,128)(2,1)S(1)} custom-call(s32[8]{0:T(128)S(1)} %reshape.64.place_ref, f32[2,4,4096]{2,1,0:T(4,128)S(1)} %shard_map.163.bias_ref, bf16[4,6,128,128]{3,2,1,0:T(8,128)(2,1)S(1)} %all-to-all-done.q_ref, bf16[4,4,128,128]{3,2,1,0:T(8,128)(2,1)} %collective-permute-done.3.refs_0_, ...), custom_call_target="tpu_custom_call" | custom-call | flops 1024 | bytes 4096 | tf_op jit(solution)/shard_map/pallas_call | solution.py:115
  80.2 4.7 %shard_map.166 = (f32[1024,128]{1,0:T(8,128)S(1)}, f32[1024,256]{1,0:T(8,128)S(1)}) custom-call(s32[8]{0:T(128)S(1)} %reshape.64.place_ref, f32[2,4,4096]{2,1,0:T(4,128)S(1)} %copy-done.4, bf16[4,6,128,128]{3,2,1,0:T(8,128)(2,1)S(1)} %all-to-all-done.1.q_ref, bf16[4,4,128,128]{3,2,1,0:T(8,128)(2,1)} %pad_maximum_fusion.3.refs_0_, ...), custom_call_target="tpu_custom_call" | custom-call | flops 1024 | bytes 4096 | tf_op jit(solution)/shard_map/pallas_call | solution.py:115
  85.8 4.4 %collective-permute-done.6.refs_0_ = bf16[4,4,128,128]{3,2,1,0:T(8,128)(2,1)} collective-permute-done((bf16[4,4,128,128]{3,2,1,0:T(8,128)(2,1)}, bf16[4,4,128,128]{3,2,1,0:T(8,128)(2,1)}, u32[]{:S(2)}, u32[]{:S(2)}) %collective-permute-start.6) | collective-permute-done | bytes 524320 | tf_op jit(solution)/shard_map/ppermute | solution.py:206
  92.8 3.1 %collective-permute-done.7.refs_1_ = bf16[4,4,128,128]{3,2,1,0:T(8,128)(2,1)S(1)} collective-permute-done((bf16[4,4,128,128]{3,2,1,0:T(8,128)(2,1)}, bf16[4,4,128,128]{3,2,1,0:T(8,128)(2,1)S(1)}, u32[]{:S(2)}, u32[]{:S(2)}) %collective-permute-start.7) | collective-permute-done | bytes 524320 | tf_op jit(solution)/shard_map/ppermute | solution.py:206
  96.7 7.3 %shard_map.170 = bf16[8,2,128,128]{3,2,1,0:T(8,128)(2,1)} custom-call(s32[8]{0:T(128)S(1)} %reshape.64.place_ref, f32[2,4,4096]{2,1,0:T(4,128)S(1)} %shard_map.167.bias_ref, bf16[4,10,128,128]{3,2,1,0:T(8,128)(2,1)S(1)} %all-to-all-done.2.q_ref.refs_0_, bf16[4,10,128,128]{3,2,1,0:T(8,128)(2,1)S(1)} %all-to-all-done.2.q_ref.refs_0_, ...), custom_call_target="tpu_custom_call" | custom-call | flops 1024 | bytes 4096 | tf_op jit(solution)/shard_map/pallas_call | solution.py:115
  104.0 3.8 %all-to-all-start.4 = ((bf16[8,2,128,128]{3,2,1,0:T(8,128)(2,1)}), bf16[8,2,128,128]{3,2,1,0:T(8,128)(2,1)S(1)}, u32[]{:S(2)}, u32[]{:S(2)}) async-start(bf16[8,2,128,128]{3,2,1,0:T(8,128)(2,1)} %shard_map.170), calls=%async_computation.4 | async-start | bytes 1048576 | tf_op jit(solution)/shard_map/all_to_all | solution.py:209
  107.8 1.2 copy-done.2
  109.0 1.0 copy-done.7
  110.1 5.3 %shard_map.171 = bf16[8,128,128]{2,1,0:T(8,128)(2,1)} custom-call(s32[8]{0:T(128)S(1)} %reshape.64.place_ref, f32[2,4,4096]{2,1,0:T(4,128)S(1)} %copy-done.5, bf16[4,6,128,128]{3,2,1,0:T(8,128)(2,1)S(1)} %all-to-all-done.1.q_ref, bf16[4,4,128,128]{3,2,1,0:T(8,128)(2,1)} %collective-permute-done.6.refs_0_, bf16[4,4,128,128]{3,2,1,0:T(8,128)(2,1)S(1)} %copy-done.7, ...), custom_call_target="tpu_custom_call" | custom-call | flops 1024 | bytes 4096 | tf_op jit(solution)/shard_map/pallas_call | solution.py:115
  115.4 2.7 %all-to-all-done.4 = bf16[8,2,128,128]{3,2,1,0:T(8,128)(2,1)S(1)} async-done(((bf16[8,2,128,128]{3,2,1,0:T(8,128)(2,1)}), bf16[8,2,128,128]{3,2,1,0:T(8,128)(2,1)S(1)}, u32[]{:S(2)}, u32[]{:S(2)}) %all-to-all-start.4) | async-done | bytes 524320 | tf_op jit(solution)/shard_map/all_to_all | solution.py:209
  118.1 3.4 %all-to-all-start.3 = ((bf16[8,128,128]{2,1,0:T(8,128)(2,1)}), bf16[8,128,128]{2,1,0:T(8,128)(2,1)S(1)}, u32[]{:S(2)}, u32[]{:S(2)}) async-start(bf16[8,128,128]{2,1,0:T(8,128)(2,1)} %shard_map.171), calls=%async_computation.3 | async-start | bytes 524288 | tf_op jit(solution)/shard_map/all_to_all | solution.py:209
  121.8 5.7 %fusion.total_ref = f32[128,3072]{1,0:T(8,128)S(1)} fusion(bf16[128,2048]{0,1:T(8,128)(2,1)S(1)} %bitcast.72, bf16[3072,3072]{1,0:T(8,128)(2,1)} %weight_ref.1), kind=kOutput, calls=%fused_computation | convolution fusion | flops 1610612736 | bytes 14680064 | tf_op jit(solution)/shard_map/dot_general | solution.py:282
  128.4 4.1 %shard_map.172 = bf16[128,3072]{1,0:T(8,128)(2,1)} custom-call(bf16[8,128,128]{2,1,0:T(8,128)(2,1)S(1)} %all-to-all-done.3.part_ref, bf16[3072,3072]{1,0:T(8,128)(2,1)} %weight_ref.1, f32[128,3072]{1,0:T(8,128)S(1)} %fusion.total_ref), custom_call_target="tpu_custom_call" | custom-call | tf_op jit(solution)/shard_map/pallas_call | solution.py:168
  (87 shorter events, 23.6 us)
Async XLA Ops:
  0.0 27.7 %copy-start.15 = (s32[9]{0:T(128)S(1)}, s32[9]{0:T(128)}, u32[]{:S(2)}) copy-start(s32[9]{0:T(128)} %constant.92.clone) | copy-start | bytes 112
  0.0 30.2 %copy-start.10 = (s32[4,1]{1,0:T(4,128)S(1)}, s32[4,1]{1,0:T(4,128)}, u32[]{:S(2)}) copy-start(s32[4,1]{1,0:T(4,128)} %constant.98.clone.rows_ref) | copy-start | bytes 52
  0.0 30.2 %copy-start.11 = (s32[1,512]{1,0:T(1,128)S(1)}, s32[1,512]{1,0:T(1,128)}, u32[]{:S(2)}) copy-start(s32[1,512]{1,0:T(1,128)} %constant.99.clone.cols_ref) | copy-start | bytes 6148
  0.0 30.2 %copy-start.8 = (s32[24,32,32]{2,1,0:T(8,128)S(1)}, s32[24,32,32]{2,1,0:T(8,128)}, u32[]{:S(2)}) copy-start(s32[24,32,32]{2,1,0:T(8,128)} %mask_ref.2) | copy-start | bytes 294916
  4.3 17.8 %collective-permute-start = (bf16[4,3,128,128]{3,2,1,0:T(8,128)(2,1)S(1)}, bf16[4,3,128,128]{3,2,1,0:T(8,128)(2,1)S(1)}, u32[]{:S(2)}, u32[]{:S(2)}) collective-permute-start(bf16[4,3,128,128]{3,2,1,0:T(8,128)(2,1)S(1)} %pad_maximum_fusion.4), channel_id=1, source_target_pairs={{0,2},{2,0},{1,3},{3,1},{4,6},{6,4},{5,7},{7,5},{8,10},{10,8},{9,1... | collective-permute-start | bytes 1179656 | tf_op jit(solution)/shard_map/ppermute | solution.py:206
  7.8 29.3 %copy-start.12 = (bf16[2,1,2,128,128]{4,3,2,0,1:T(8,128)(2,1)}, bf16[2,1,2,128,128]{4,3,2,0,1:T(8,128)(2,1)S(1)}, u32[]{:S(2)}) copy-start(bf16[2,1,2,128,128]{4,3,2,0,1:T(8,128)(2,1)S(1)} %copy.61) | copy-start | bytes 393220
  7.8 29.3 %copy-start.13 = (bf16[2,1,2,128,128]{4,3,2,0,1:T(8,128)(2,1)}, bf16[2,1,2,128,128]{4,3,2,0,1:T(8,128)(2,1)S(1)}, u32[]{:S(2)}) copy-start(bf16[2,1,2,128,128]{4,3,2,0,1:T(8,128)(2,1)S(1)} %copy.62) | copy-start | bytes 393220
  8.6 21.6 %collective-permute-start.1 = (bf16[4,2,128,128]{3,2,1,0:T(8,128)(2,1)}, bf16[4,2,128,128]{3,2,1,0:T(8,128)(2,1)S(1)}, u32[]{:S(2)}, u32[]{:S(2)}) collective-permute-start(bf16[4,2,128,128]{3,2,1,0:T(8,128)(2,1)} %pad_maximum_fusion.8), channel_id=1, source_target_pairs={{0,4},{2,6},{4,0},{6,2},{1,5},{3,7},{5,1},{7,3},{8,12},{10,14},{12... | collective-permute-start | bytes 786440 | tf_op jit(solution)/shard_map/ppermute | solution.py:206
  11.9 18.2 %collective-permute-start.2 = (bf16[4,2,128,128]{3,2,1,0:T(8,128)(2,1)}, bf16[4,2,128,128]{3,2,1,0:T(8,128)(2,1)S(1)}, u32[]{:S(2)}, u32[]{:S(2)}) collective-permute-start(bf16[4,2,128,128]{3,2,1,0:T(8,128)(2,1)} %pad_maximum_fusion.9), channel_id=1, source_target_pairs={{0,6},{2,4},{4,2},{6,0},{1,7},{3,5},{5,3},{7,1},{8,14},{10,12},{12... | collective-permute-start | bytes 786440 | tf_op jit(solution)/shard_map/ppermute | solution.py:206
  23.0 14.0 %all-to-all-start = ((bf16[4,6,128,128]{3,2,1,0:T(8,128)(2,1)}), bf16[4,6,128,128]{3,2,1,0:T(8,128)(2,1)S(1)}, u32[]{:S(2)}, u32[]{:S(2)}) async-start(bf16[4,6,128,128]{3,2,1,0:T(8,128)(2,1)} %pad_maximum_fusion), calls=%async_computation | async-start | bytes 1572864 | tf_op jit(solution)/shard_map/all_to_all | solution.py:209
  27.7 16.6 %collective-permute-start.4 = (bf16[4,3,128,128]{3,2,1,0:T(8,128)(2,1)}, bf16[4,3,128,128]{3,2,1,0:T(8,128)(2,1)}, u32[]{:S(2)}, u32[]{:S(2)}) collective-permute-start(bf16[4,3,128,128]{3,2,1,0:T(8,128)(2,1)} %pad_maximum_fusion.5), channel_id=1, source_target_pairs={{0,2},{2,0},{1,3},{3,1},{4,6},{6,4},{5,7},{7,5},{8,10},{10,8},{9,1... | collective-permute-start | bytes 1179656 | tf_op jit(solution)/shard_map/ppermute | solution.py:206
  37.1 31.5 %copy-start.14 = (s32[2,4]{1,0:T(2,128)S(1)}, s32[2,4]{1,0:T(2,128)}, u32[]{:S(2)}) copy-start(s32[2,4]{1,0:T(2,128)} %constant.96.clone) | copy-start | bytes 100
  37.2 24.7 %collective-permute-start.3 = (bf16[4,4,128,128]{3,2,1,0:T(8,128)(2,1)S(1)}, bf16[4,4,128,128]{3,2,1,0:T(8,128)(2,1)}, u32[]{:S(2)}, u32[]{:S(2)}) collective-permute-start(bf16[4,4,128,128]{3,2,1,0:T(8,128)(2,1)S(1)} %pad_maximum_fusion.2.refs_0_), channel_id=1, source_target_pairs={{0,4},{4,0},{1,5},{5,1},{2,6},{6,2},{3,7},{7,3},{8,12},{12,8},{9,1... | collective-permute-start | bytes 1572872 | tf_op jit(solution)/shard_map/ppermute | solution.py:206
  39.0 17.6 %collective-permute-start.5 = (bf16[4,3,128,128]{3,2,1,0:T(8,128)(2,1)}, bf16[4,3,128,128]{3,2,1,0:T(8,128)(2,1)S(1)}, u32[]{:S(2)}, u32[]{:S(2)}) collective-permute-start(bf16[4,3,128,128]{3,2,1,0:T(8,128)(2,1)} %pad_maximum_fusion.7), channel_id=1, source_target_pairs={{0,2},{2,0},{1,3},{3,1},{4,6},{6,4},{5,7},{7,5},{8,10},{10,8},{9,1... | collective-permute-start | bytes 1179656 | tf_op jit(solution)/shard_map/ppermute | solution.py:206
  46.2 17.2 %all-to-all-start.1 = ((bf16[4,6,128,128]{3,2,1,0:T(8,128)(2,1)}), bf16[4,6,128,128]{3,2,1,0:T(8,128)(2,1)S(1)}, u32[]{:S(2)}, u32[]{:S(2)}) async-start(bf16[4,6,128,128]{3,2,1,0:T(8,128)(2,1)} %pad_maximum_fusion.1), calls=%async_computation.1 | async-start | bytes 1572864 | tf_op jit(solution)/shard_map/all_to_all | solution.py:209
  56.7 1.1 copy-start
  57.8 12.2 %collective-permute-start.10 = (bf16[4,4,128,128]{3,2,1,0:T(8,128)(2,1)S(1)}, bf16[4,4,128,128]{3,2,1,0:T(8,128)(2,1)}, u32[]{:S(2)}, u32[]{:S(2)}) collective-permute-start(bf16[4,4,128,128]{3,2,1,0:T(8,128)(2,1)S(1)} %pad_maximum_fusion.2.refs_0_), channel_id=1, source_target_pairs={{0,8},{8,0},{1,9},{9,1},{2,10},{10,2},{3,11},{11,3},{4,12},{12,4},... | collective-permute-start | bytes 1572872 | tf_op jit(solution)/shard_map/ppermute | solution.py:206
  61.9 12.6 %collective-permute-start.9 = (bf16[4,4,128,128]{3,2,1,0:T(8,128)(2,1)}, bf16[4,4,128,128]{3,2,1,0:T(8,128)(2,1)}, u32[]{:S(2)}, u32[]{:S(2)}) collective-permute-start(bf16[4,4,128,128]{3,2,1,0:T(8,128)(2,1)} %collective-permute-done.3.refs_0_), channel_id=1, source_target_pairs={{0,8},{8,0},{1,9},{9,1},{2,10},{10,2},{3,11},{11,3},{4,12},{12,4},... | collective-permute-start | bytes 1572872 | tf_op jit(solution)/shard_map/ppermute | solution.py:206
  64.4 14.9 %collective-permute-start.8 = (bf16[4,4,128,128]{3,2,1,0:T(8,128)(2,1)}, bf16[4,4,128,128]{3,2,1,0:T(8,128)(2,1)}, u32[]{:S(2)}, u32[]{:S(2)}) collective-permute-start(bf16[4,4,128,128]{3,2,1,0:T(8,128)(2,1)} %pad_maximum_fusion.3.refs_0_), channel_id=1, source_target_pairs={{0,8},{8,0},{1,9},{9,1},{2,10},{10,2},{3,11},{11,3},{4,12},{12,4},... | collective-permute-start | bytes 1572872 | tf_op jit(solution)/shard_map/ppermute | solution.py:206
  64.9 25.4 %collective-permute-start.6 = (bf16[4,4,128,128]{3,2,1,0:T(8,128)(2,1)}, bf16[4,4,128,128]{3,2,1,0:T(8,128)(2,1)}, u32[]{:S(2)}, u32[]{:S(2)}) collective-permute-start(bf16[4,4,128,128]{3,2,1,0:T(8,128)(2,1)} %pad_maximum_fusion.3.refs_0_), channel_id=1, source_target_pairs={{0,4},{4,0},{1,5},{5,1},{2,6},{6,2},{3,7},{7,3},{8,12},{12,8},{9,1... | collective-permute-start | bytes 1572872 | tf_op jit(solution)/shard_map/ppermute | solution.py:206
  64.9 27.4 %all-to-all-start.2 = ((bf16[4,10,128,128]{3,2,1,0:T(8,128)(2,1)}), bf16[4,10,128,128]{3,2,1,0:T(8,128)(2,1)S(1)}, u32[]{:S(2)}, u32[]{:S(2)}) async-start(bf16[4,10,128,128]{3,2,1,0:T(8,128)(2,1)} %copy-done), calls=%async_computation.2 | async-start | bytes 2621440 | tf_op jit(solution)/shard_map/all_to_all | solution.py:209
  79.3 0.9 copy-start.4
  84.8 1.0 copy-start.1
  85.8 22.0 %copy-start.5 = (f32[2,4,4096]{2,1,0:T(4,128)S(1)}, f32[2,4,4096]{2,1,0:T(4,128)}, u32[]{:S(2)}) copy-start(f32[2,4,4096]{2,1,0:T(4,128)} %copy-done.3) | copy-start | bytes 393220
  90.3 1.0 copy-start.9
  92.2 4.5 %collective-permute-start.11 = (bf16[4,10,128,128]{3,2,1,0:T(8,128)(2,1)S(1)}, bf16[4,10,128,128]{3,2,1,0:T(8,128)(2,1)S(1)}, u32[]{:S(2)}, u32[]{:S(2)}) collective-permute-start(bf16[4,10,128,128]{3,2,1,0:T(8,128)(2,1)S(1)} %all-to-all-done.2.q_ref.refs_0_), channel_id=1, source_target_pairs={{0,8},{8,0},{1,9},{9,1},{2,10},{10,2},{3,11},{11,3},{4,12},{12,4},... | collective-permute-start | bytes 3932168 | tf_op jit(solution)/shard_map/ppermute | solution.py:206
  92.3 3.6 %collective-permute-start.7 = (bf16[4,4,128,128]{3,2,1,0:T(8,128)(2,1)}, bf16[4,4,128,128]{3,2,1,0:T(8,128)(2,1)S(1)}, u32[]{:S(2)}, u32[]{:S(2)}) collective-permute-start(bf16[4,4,128,128]{3,2,1,0:T(8,128)(2,1)} %collective-permute-done.6.refs_0_), channel_id=1, source_target_pairs={{0,8},{8,0},{1,9},{9,1},{2,10},{10,2},{3,11},{11,3},{4,12},{12,4},... | collective-permute-start | bytes 1572872 | tf_op jit(solution)/shard_map/ppermute | solution.py:206
  96.0 0.8 copy-start.6
  104.0 14.0 %all-to-all-start.4 = ((bf16[8,2,128,128]{3,2,1,0:T(8,128)(2,1)}), bf16[8,2,128,128]{3,2,1,0:T(8,128)(2,1)S(1)}, u32[]{:S(2)}, u32[]{:S(2)}) async-start(bf16[8,2,128,128]{3,2,1,0:T(8,128)(2,1)} %shard_map.170), calls=%async_computation.4 | async-start | bytes 1048576 | tf_op jit(solution)/shard_map/all_to_all | solution.py:209
  107.8 1.2 copy-start.2
  109.0 1.0 copy-start.7
  118.1 10.3 %all-to-all-start.3 = ((bf16[8,128,128]{2,1,0:T(8,128)(2,1)}), bf16[8,128,128]{2,1,0:T(8,128)(2,1)S(1)}, u32[]{:S(2)}, u32[]{:S(2)}) async-start(bf16[8,128,128]{2,1,0:T(8,128)(2,1)} %shard_map.171), calls=%async_computation.3 | async-start | bytes 524288 | tf_op jit(solution)/shard_map/all_to_all | solution.py:209
  (1 other events, 0.7 us)
